TPU v7x, 32 devices: a whole 2x2x4 slice. The times are simulated.
32 devices in a mesh: section: 2 (over core), dp: 4 (over z), expert: 4 (over y, x).
Axes of the slice: x: 2, y: 2, z: 4, core: 2. Of those that a mesh axis runs over, the one named last changes fastest.
Arguments:
- edge_in: bfloat16 [2, 2, 4, 512, 1536], P('section', None, 'expert', 'dp'), may hold values from -6 to 6
- seg_lengths: int32 [2, 4, 13], P(None, 'expert'), may hold values from 1 to 204, 512 in all within a row
- routes: int32 [2, 2, 4, 512, 4], P('section', None, 'expert', 'dp'), may hold values from 0 to 31, all different within a row
- turns: int32 [2, 2, 4, 4, 128], P('section', None, 'expert', 'dp'), may hold values from 0 to 127, each once within a row
- attn_gain: float32 [2, 1536], P('section'), may hold values from 0.5 to 1.5
- w_query: bfloat16 [2, 1536, 1536], P('section'), may hold values from -0.3125 to 0.3125
- w_key: bfloat16 [2, 1536, 256], P('section'), may hold values from -0.15625 to 0.15625
- w_value: bfloat16 [2, 1536, 256], P('section'), may hold values from -0.15625 to 0.15625
- w_out: bfloat16 [2, 1536, 1536], P('section'), may hold values from -1.25 to 1.25
- ffn_gain: float32 [2, 1536], P('section'), may hold values from 0.5 to 1.5
- w_router: bfloat16 [2, 1536, 32], P('section'), may hold values from -0.078125 to 0.078125
- w_gate: bfloat16 [2, 32, 1536, 768], P('section', 'expert', 'dp'), may hold values from -0.15625 to 0.15625
- w_up: bfloat16 [2, 32, 1536, 768], P('section', 'expert', 'dp'), may hold values from -0.15625 to 0.15625
- w_down: bfloat16 [2, 32, 768, 1536], P('section', 'expert', 'dp'), may hold values from -0.4375 to 0.4375
Outputs:
- edge_out: float32 [2, 2, 4, 512, 1536], P('section', None, 'expert', 'dp')
- grad_attn_gain: float32 [2, 1536], P('section')
- grad_query: float32 [2, 1536, 1536], P('section')
- grad_key: float32 [2, 1536, 256], P('section')
- grad_value: float32 [2, 1536, 256], P('section')
- grad_out: float32 [2, 1536, 1536], P('section')
- grad_ffn_gain: float32 [2, 1536], P('section')
- grad_router: float32 [2, 1536, 32], P('section')
- grad_gate: float32 [2, 32, 1536, 768], P('section', 'expert', 'dp')
- grad_up: float32 [2, 32, 1536, 768], P('section', 'expert', 'dp')
- grad_down: float32 [2, 32, 768, 1536], P('section', 'expert', 'dp')
Inputs may be any that keep to these rules, and one draw needn't show every extreme that they name: `seg_lengths`: each row gives the lengths of a tree's 13 segments in depth-first order: the trunk, then for each of four branches the branch followed by its two leaves; a row sums to 512. `routes`: each row names 4 different experts. `turns`: the 128 numbers of one block form a permutation.
All inputs are finite; a program needn't handle non-finite values.
Results may differ from a plain program's by a relative error of at most 0.03.
Values may be sent and summed in bfloat16 or wider, within the bound.
No kernel may reach another device: no remote copies, remote signals or barrier semaphores. Data moves between devices by JAX's collectives and lax.ppermute only.
A program may use at most 384 MiB of HBM per device.

v0:
```python
import jax
import jax.numpy as jnp
import numpy as np
from jax import lax
from jax.sharding import PartitionSpec as P

HEAD_SIZE = 128
SCALE = HEAD_SIZE ** (-0.5)
epsilon = 1e-06
masked_score = -1e30
BF = jnp.bfloat16
F32 = jnp.float32

SWAP = [(0, 1), (1, 0)]
UP = [(0, 1)]
DOWN = [(1, 0)]
OWNERS = ("expert", "dp", "section")
LINE = ("dp", "section")
REPLICAS = ("dp", "expert")


def ancestry():
    parents = [-1]
    for branch_index in range(4):
        parents += [0, 1 + 3 * branch_index, 1 + 3 * branch_index]
    lineage = np.zeros((13, 13), np.float32)
    for segment in range(13):
        current = segment
        while current >= 0:
            lineage[current, segment] = 1.0
            current = parents[current]
    return lineage


def dot(left, right):
    return jnp.dot(left, right, preferred_element_type=F32)


def dot_t(left, right):
    return lax.dot_general(left, right, (((1,), (1,)), ((), ())), preferred_element_type=F32)


def t_dot(left, right):
    return lax.dot_general(left, right, (((0,), (0,)), ((), ())), preferred_element_type=F32)


def normalize(values, gain_vec):
    factor = lax.rsqrt(jnp.mean(values * values, -1, keepdims=True) + epsilon)
    return (values * factor * gain_vec, factor)


def norm_back(values, factor, gain_vec, upstream):
    scaled = upstream * gain_vec
    grad_gain = jnp.sum(upstream * values * factor, 0)
    inner_mean = jnp.mean(scaled * values, -1, keepdims=True)
    return (scaled * factor - values * factor * factor * factor * inner_mean, grad_gain)


def tree_mask(lengths_row, first_row, local_len, tree_length):
    seg_ends = jnp.cumsum(lengths_row)
    key_spots = jnp.arange(tree_length, dtype=jnp.int32)
    query_spots = first_row + jnp.arange(local_len, dtype=jnp.int32)
    seg_ids = jnp.arange(13, dtype=jnp.int32)
    key_seg = jnp.sum((key_spots[:, None] >= seg_ends[None, :]).astype(jnp.int32), 1)
    query_seg = jnp.sum((query_spots[:, None] >= seg_ends[None, :]).astype(jnp.int32), 1)
    key_hot = (key_seg[:, None] == seg_ids[None, :]).astype(BF)
    query_hot = (query_seg[:, None] == seg_ids[None, :]).astype(BF)
    allowed = dot(query_hot, jnp.asarray(ancestry(), BF)).astype(BF)
    linked = dot_t(allowed, key_hot) > 0.5
    return linked & (key_spots[None, :] <= query_spots[:, None])


def exchange(shard, axes):
    return lax.all_to_all(shard, axes, split_axis=0, concat_axis=0, tiled=True)


def swapped(shard):
    return lax.ppermute(shard, "section", SWAP)


def gather_rows(shard):
    size = lax.axis_size("dp")
    copies = jnp.broadcast_to(shard[None], (size,) + shard.shape)
    return exchange(copies, "dp").reshape((-1,) + shard.shape[1:])


def sum_to_owner(partial):
    size = lax.axis_size("dp")
    blocks = exchange(partial.reshape((size, -1) + partial.shape[1:]), "dp")
    return jnp.sum(blocks.astype(F32), 0)


def layer_forward(layer_in, visible, route_rows, turn_row, dense_set, expert_set):
    attn_gain, w_query, w_key, w_value, w_out, ffn_gain, w_router = dense_set
    w_gate, w_up, w_down = expert_set
    local_len, width = layer_in.shape
    heads_kv = w_key.shape[1] // HEAD_SIZE
    experts_all = w_router.shape[1]
    pick_count = route_rows.shape[1]
    capacity = local_len * pick_count // experts_all
    slots = experts_all * capacity
    normed, factor_one = normalize(layer_in, attn_gain)
    hidden_one = normed.astype(BF)
    queries = dot(hidden_one, w_query).astype(BF)
    key_rows = dot(hidden_one, w_key).astype(BF)
    value_rows = dot(hidden_one, w_value).astype(BF)
    kv_all = gather_rows(jnp.concatenate([key_rows, value_rows], 1))
    key_width = w_key.shape[1]
    key_all = kv_all[:, :key_width].reshape(-1, heads_kv, HEAD_SIZE)
    value_all = kv_all[:, key_width:].reshape(-1, heads_kv, HEAD_SIZE)
    grouped_query = queries.reshape(local_len, heads_kv, -1, HEAD_SIZE)
    raw = jnp.einsum("tkgd,skd->kgts", grouped_query, key_all, preferred_element_type=F32) * SCALE
    scores = jnp.where(visible[None, None], raw, masked_score)
    log_total = jax.nn.logsumexp(scores, -1, keepdims=True)
    attn_prob = jnp.exp(scores - log_total)
    attn_mix = jnp.einsum(
        "kgts,skd->tkgd", attn_prob.astype(BF), value_all, preferred_element_type=F32
    )
    attn_mix = attn_mix.reshape(local_len, -1).astype(BF)
    middle = layer_in + dot(attn_mix, w_out)
    normed_two, factor_two = normalize(middle, ffn_gain)
    hidden_two = normed_two.astype(BF)
    logits = dot(hidden_two, w_router)
    expert_ids = jnp.arange(experts_all, dtype=jnp.int32)
    chosen = jnp.any(route_rows[:, :, None] == expert_ids[None, None, :], 1)
    masked_logits = jnp.where(chosen, logits, masked_score)
    top = jnp.max(masked_logits, -1, keepdims=True)
    powers = jnp.where(chosen, jnp.exp(masked_logits - top), 0.0)
    gate_share = powers / jnp.sum(powers, -1, keepdims=True)
    earlier = (turn_row[None, :] < turn_row[:, None]).astype(BF)
    places = dot(earlier, chosen.astype(BF))
    place_of = jnp.where(chosen & (places < capacity), places, -1.0).astype(BF)
    slot_ids = jnp.arange(slots, dtype=jnp.int32)
    spread = (slot_ids[None, :] // capacity == expert_ids[:, None]).astype(BF)
    rank = (slot_ids % capacity).astype(F32)
    selected = dot(place_of, spread) == rank[None, :]
    selector = selected.astype(BF)
    weighting = jnp.where(selected, dot(gate_share.astype(BF), spread), 0.0).astype(BF)
    outgoing = t_dot(selector, hidden_two).astype(BF)
    arrived = send_out(outgoing, experts_all, capacity)
    gate_pre = dot(arrived, w_gate)
    up_pre = dot(arrived, w_up)
    inner_act = (jax.nn.silu(gate_pre) * up_pre).astype(BF)
    produced = dot(inner_act, w_down).astype(BF)
    returned = send_back(produced, experts_all, capacity)
    result = middle + dot(weighting, returned)
    stored = {
        "layer_in": layer_in,
        "factor_one": factor_one,
        "hidden_one": hidden_one,
        "queries": queries,
        "key_all": key_all,
        "value_all": value_all,
        "attn_prob": attn_prob,
        "attn_mix": attn_mix,
        "middle": middle,
        "factor_two": factor_two,
        "hidden_two": hidden_two,
        "gate_share": gate_share,
        "selected": selected,
        "spread": spread,
        "weighting": weighting,
        "arrived": arrived,
        "gate_pre": gate_pre,
        "up_pre": up_pre,
        "inner_act": inner_act,
        "returned": returned,
    }
    return (result, stored)


def copies_of_expert(experts_all):
    owners = lax.axis_size("expert") * lax.axis_size("dp") * lax.axis_size("section")
    return owners // experts_all


def send_out(slot_rows, experts_all, capacity):
    width = slot_rows.shape[-1]
    copies = copies_of_expert(experts_all)
    rows = slot_rows.reshape(experts_all, capacity, width)
    if copies > 1:
        mine = jnp.arange(copies) == lax.axis_index("dp") % copies
        rows = jnp.where(mine[None, :, None, None], rows[:, None], 0).reshape(-1, capacity, width)
    return exchange(rows, OWNERS).reshape(-1, width)


def send_back(rows, experts_all, capacity):
    width = rows.shape[-1]
    copies = copies_of_expert(experts_all)
    rows = exchange(rows.reshape(-1, capacity, width), OWNERS)
    if copies > 1:
        mine = lax.axis_index("dp") % copies
        rows = lax.dynamic_index_in_dim(
            rows.reshape(experts_all, copies, capacity, width), mine, 1, False
        )
    return rows.reshape(-1, width)


def layer_backward(stored, grad_top, dense_set, expert_set):
    attn_gain, w_query, w_key, w_value, w_out, ffn_gain, w_router = dense_set
    w_gate, w_up, w_down = expert_set
    local_len = grad_top.shape[0]
    experts_all = w_router.shape[1]
    slots = stored["selected"].shape[1]
    capacity = slots // experts_all
    gate_share = stored["gate_share"]
    slot_grads = t_dot(stored["weighting"], grad_top).astype(BF)
    slot_owed = send_out(slot_grads, experts_all, capacity)
    match = jnp.where(stored["selected"], dot_t(grad_top, stored["returned"]), 0.0)
    grad_weighting = lax.dot_general(
        match,
        stored["spread"].astype(F32),
        (((1,), (1,)), ((), ())),
        precision=lax.Precision.HIGHEST,
        preferred_element_type=F32,
    )
    grad_logits = (
        gate_share * (grad_weighting - jnp.sum(gate_share * grad_weighting, -1, keepdims=True))
    ).astype(BF)
    grad_router = t_dot(stored["hidden_two"], grad_logits)
    grad_hidden = dot_t(grad_logits, w_router)
    gate_pre = stored["gate_pre"]
    up_pre = stored["up_pre"]
    grad_inner = dot_t(slot_owed, w_down)
    sigmoid_a = jax.nn.sigmoid(gate_pre)
    grad_gate_pre = (grad_inner * up_pre * sigmoid_a * (1.0 + gate_pre * (1.0 - sigmoid_a))).astype(
        BF
    )
    grad_up_pre = (grad_inner * gate_pre * sigmoid_a).astype(BF)
    grad_arrived = (dot_t(grad_gate_pre, w_gate) + dot_t(grad_up_pre, w_up)).astype(BF)
    sent_back = send_back(grad_arrived, experts_all, capacity)
    arrived = stored["arrived"]
    grad_down = t_dot(stored["inner_act"], slot_owed)
    grad_gate = t_dot(arrived, grad_gate_pre)
    grad_up = t_dot(arrived, grad_up_pre)
    grad_hidden = grad_hidden + dot(stored["selected"].astype(BF), sent_back)
    grad_normed_two, grad_ffn_gain = norm_back(
        stored["middle"], stored["factor_two"], ffn_gain, grad_hidden
    )
    grad_middle = grad_top.astype(F32) + grad_normed_two
    grad_branch = grad_middle.astype(BF)
    grad_w_out = t_dot(stored["attn_mix"], grad_branch)
    grad_mix = dot_t(grad_branch, w_out).astype(BF)
    key_all = stored["key_all"]
    value_all = stored["value_all"]
    heads_kv = key_all.shape[1]
    attn_prob = stored["attn_prob"]
    grouped_grad = grad_mix.reshape(local_len, heads_kv, -1, HEAD_SIZE)
    grad_prob = jnp.einsum("tkgd,skd->kgts", grouped_grad, value_all, preferred_element_type=F32)
    centre = jnp.sum(attn_prob * grad_prob, -1, keepdims=True)
    grad_scores = (attn_prob * (grad_prob - centre)).astype(BF)
    grad_queries = (
        jnp.einsum("kgts,skd->tkgd", grad_scores, key_all, preferred_element_type=F32) * SCALE
    )
    grad_queries = grad_queries.reshape(local_len, -1).astype(BF)
    grouped_query = stored["queries"].reshape(local_len, heads_kv, -1, HEAD_SIZE)
    grad_keys_all = (
        jnp.einsum("kgts,tkgd->skd", grad_scores, grouped_query, preferred_element_type=F32) * SCALE
    )
    grad_values_all = jnp.einsum(
        "kgts,tkgd->skd", attn_prob.astype(BF), grouped_grad, preferred_element_type=F32
    )
    tree_length = key_all.shape[0]
    grad_kv = sum_to_owner(
        jnp.concatenate(
            [grad_keys_all.reshape(tree_length, -1), grad_values_all.reshape(tree_length, -1)], 1
        ).astype(BF)
    ).astype(BF)
    key_width = w_key.shape[1]
    grad_keys, grad_values = grad_kv[:, :key_width], grad_kv[:, key_width:]
    hidden_one = stored["hidden_one"]
    grad_query_w = t_dot(hidden_one, grad_queries)
    grad_key_w = t_dot(hidden_one, grad_keys)
    grad_value_w = t_dot(hidden_one, grad_values)
    grad_hidden_one = dot_t(grad_queries, w_query)
    grad_hidden_one = grad_hidden_one + dot_t(grad_keys, w_key)
    grad_hidden_one = grad_hidden_one + dot_t(grad_values, w_value)
    grad_normed_one, grad_attn_gain = norm_back(
        stored["layer_in"], stored["factor_one"], attn_gain, grad_hidden_one
    )
    grad_input = grad_middle + grad_normed_one
    dense_grads = (
        grad_attn_gain,
        grad_query_w,
        grad_key_w,
        grad_value_w,
        grad_w_out,
        grad_ffn_gain,
        grad_router,
    )
    return (grad_input, dense_grads, (grad_gate, grad_up, grad_down))


def experts_in(own, is_first):
    experts, rows, columns = own.shape
    copies = lax.axis_size("dp") * lax.axis_size("section") // experts
    half = rows // 2
    low_half, high_half = own[:, :half], own[:, half:]
    kept = jnp.where(is_first, low_half, high_half)
    received = swapped(jnp.where(is_first, high_half, low_half))
    layers = (jnp.where(is_first, kept, received), jnp.where(is_first, received, kept))
    whole = []
    for piece in layers:
        if copies > 1:
            piece = jnp.repeat(piece, copies, 0)
        whole.append(exchange(piece, LINE).reshape(-1, columns))
    return whole


def experts_out(grad, experts):
    size = lax.axis_size("dp") * lax.axis_size("section")
    columns = grad.shape[1]
    pieces = exchange(grad.astype(BF).reshape(size, -1, columns), LINE)
    copies = size // experts
    if copies > 1:
        pieces = jnp.sum(
            pieces.reshape(experts, copies, -1, columns).astype(F32), 1
        ).astype(BF)
    return pieces


def dense_total(grads, shift):
    attn_gain, query, key, value, out, ffn_gain, router = grads
    small = jnp.concatenate([router, attn_gain[:, None], ffn_gain[:, None]], 1)
    widths = [a.shape[1] for a in (query, key, value, out, small)]
    packed = jnp.concatenate([a.astype(BF) for a in (query, key, value, out, small)], 1)
    rows = packed.shape[0]
    other = lax.ppermute(packed, "section", shift)
    both = (packed.astype(F32) + other.astype(F32)).astype(BF)
    part = lax.psum_scatter(both, REPLICAS, scatter_dimension=0, tiled=True)
    total = lax.all_gather(part, REPLICAS, axis=0, tiled=True).astype(F32)
    offsets = np.cumsum(widths)[:-1]
    query, key, value, out, small = jnp.split(total, offsets, 1)
    experts = small.shape[1] - 2
    return (small[:, experts], query, key, value, out, small[:, experts + 1], small[:, :experts])


def local(
    edge_in,
    seg_lengths,
    routes,
    turns,
    attn_gain,
    w_query,
    w_key,
    w_value,
    w_out,
    ffn_gain,
    w_router,
    w_gate,
    w_up,
    w_down,
):
    edge_rows = edge_in[0, :, 0]
    local_len = edge_rows.shape[1]
    lengths_all = seg_lengths[:, 0]
    route_all = routes[0, :, 0]
    turn_all = turns[0, :, 0, 0]
    tree_length = local_len * lax.axis_size("dp")
    first_row = lax.axis_index("dp") * local_len
    section_index = lax.axis_index("section")
    is_first = section_index == 0

    def both_layers(own, received):
        return (jnp.where(is_first, own, received), jnp.where(is_first, received, own))

    def of_micro(pair):
        mine = jnp.where(is_first, pair[0], pair[1])
        others = jnp.where(is_first, pair[1], pair[0])
        return both_layers(mine, swapped(others))

    layer_rows, cotangent = of_micro(edge_rows)
    route_pair = of_micro(route_all)
    turn_pair = of_micro(turn_all)
    lengths_row = jnp.where(is_first, lengths_all[0], lengths_all[1])
    dense_own = (attn_gain[0], w_query[0], w_key[0], w_value[0], w_out[0], ffn_gain[0], w_router[0])
    dense_pairs = [both_layers(a, swapped(a)) for a in dense_own]
    expert_own = (w_gate[0], w_up[0], w_down[0])
    expert_pairs = [experts_in(a, is_first) for a in expert_own]
    dense_sets = [tuple(p[i] for p in dense_pairs) for i in range(2)]
    expert_sets = [tuple(p[i] for p in expert_pairs) for i in range(2)]
    visible = tree_mask(lengths_row, first_row, local_len, tree_length)

    stored = []
    state = layer_rows
    for layer in range(2):
        state, kept = layer_forward(
            state.astype(F32),
            visible,
            route_pair[layer],
            turn_pair[layer],
            dense_sets[layer],
            expert_sets[layer],
        )
        stored.append(kept)
        if layer == 0:
            state = state.astype(BF)
    top = state
    top_other = lax.ppermute(top, "section", UP)

    grad = cotangent
    dense_totals = [None, None]
    expert_halves = [None, None]
    for layer in (1, 0):
        grad, dense_grads, expert_grads = layer_backward(
            stored[layer], grad, dense_sets[layer], expert_sets[layer]
        )
        expert_halves[layer] = [experts_out(g, w_gate.shape[1]) for g in expert_grads]
        dense_totals[layer] = dense_total(dense_grads, SWAP)
        if layer == 1:
            grad = grad.astype(BF)
    grad_other = lax.ppermute(grad, "section", DOWN)
    edge_out = jnp.where(
        is_first, jnp.stack([grad, grad_other]), jnp.stack([top_other, top])
    )[None, :, None]
    expert_total = []
    for first, second in zip(*expert_halves, strict=True):
        low_half = jnp.where(is_first, first, lax.ppermute(second, "section", UP))
        high_half = jnp.where(is_first, lax.ppermute(first, "section", DOWN), second)
        expert_total.append(jnp.concatenate([low_half, high_half], 1).astype(F32))
    dense_out = [jnp.where(is_first, a, b) for a, b in zip(*dense_totals, strict=True)]
    return (
        (edge_out,)
        + tuple((piece[None] for piece in dense_out))
        + tuple((piece[None] for piece in expert_total))
    )


def solution(mesh):
    placed = (
        P("section", None, "expert", "dp", None),
        P(None, "expert", None),
        P("section", None, "expert", "dp", None),
        P("section", None, "expert", "dp", None),
        P("section", None),
        P("section", None, None),
        P("section", None, None),
        P("section", None, None),
        P("section", None, None),
        P("section", None),
        P("section", None, None),
        P("section", "expert", "dp", None),
        P("section", "expert", "dp", None),
        P("section", "expert", "dp", None),
    )
    return jax.shard_map(
        local,
        mesh=mesh,
        in_specs=placed,
        out_specs=(
            P("section", None, "expert", "dp", None),
            P("section", None),
            P("section", None, None),
            P("section", None, None),
            P("section", None, None),
            P("section", None, None),
            P("section", None),
            P("section", None, None),
            P("section", "expert", "dp", None),
            P("section", "expert", "dp", None),
            P("section", "expert", "dp", None),
        ),
        check_vma=False,
    )
```

profile of v0, /device:TPU:1, one launch (start us, length us, event | category | flops | bytes accessed | tf_op | source)
XLA Modules:
  0.0 1848.3 jit_solution(17782384590444426093)
XLA Ops:
  27.4 5.7 broadcast_select_fusion.9
  33.1 9.3 all-to-all-done
  62.1 5.7 broadcast_select_fusion.8
  67.8 33.4 %all-to-all-done.2 = bf16[8,192,768]{2,1,0:T(8,128)(2,1)} async-done(((bf16[8,192,768]{2,1,0:T(8,128)(2,1)}), bf16[8,192,768]{2,1,0:T(8,128)(2,1)}, u32[]{:S(2)}, u32[]{:S(2)}) %all-to-all-start.2) | async-done | bytes 2359328 | tf_op jit(solution)/shard_map/all_to_all | solution.py:74
  125.9 34.5 %all-to-all-done.3 = bf16[8,192,768]{2,1,0:T(8,128)(2,1)} async-done(((bf16[8,192,768]{2,1,0:T(8,128)(2,1)}), bf16[8,192,768]{2,1,0:T(8,128)(2,1)}, u32[]{:S(2)}, u32[]{:S(2)}) %all-to-all-start.3) | async-done | bytes 2359328 | tf_op jit(solution)/shard_map/all_to_all | solution.py:74
  164.6 5.7 broadcast_select_fusion.4
  170.3 32.6 %all-to-all-done.1 = bf16[32,16,1536]{2,1,0:T(8,128)(2,1)} async-done(((bf16[32,16,1536]{2,1,0:T(8,128)(2,1)}), bf16[32,16,1536]{2,1,0:T(8,128)(2,1)}, u32[]{:S(2)}, u32[]{:S(2)}) %all-to-all-start.1) | async-done | bytes 1572896 | tf_op jit(solution)/shard_map/all_to_all | solution.py:74
  217.9 44.2 %all-to-all-done.4 = bf16[8,96,1536]{2,1,0:T(8,128)(2,1)} async-done(((bf16[8,96,1536]{2,1,0:T(8,128)(2,1)}), bf16[8,96,1536]{2,1,0:T(8,128)(2,1)}, u32[]{:S(2)}, u32[]{:S(2)}) %all-to-all-start.4) | async-done | bytes 2359328 | tf_op jit(solution)/shard_map/all_to_all | solution.py:74
  265.5 41.6 %all_to_all.120 = bf16[32,16,1536]{2,1,0:T(8,128)(2,1)} all-to-all(bf16[32,16,1536]{2,1,0:T(8,128)(2,1)S(1)} %bitcast.467), channel_id=1, replica_groups=mesh['section'=2,'dp'=4,'expert'=4] {'expert','dp','section'}, dimensions={0} | all-to-all | bytes 3145728 | tf_op jit(solution)/shard_map/all_to_all | solution.py:74
  325.7 40.0 %all-to-all-done.8 = bf16[8,192,768]{2,1,0:T(8,128)(2,1)} async-done(((bf16[8,192,768]{2,1,0:T(8,128)(2,1)}), bf16[8,192,768]{2,1,0:T(8,128)(2,1)}, u32[]{:S(2)}, u32[]{:S(2)}) %all-to-all-start.8) | async-done | bytes 2359328 | tf_op jit(solution)/shard_map/all_to_all | solution.py:74
  373.0 12.8 all-to-all-done.6
  385.7 5.7 all-to-all-start.10
  411.5 33.8 %all-to-all-done.10 = bf16[8,96,1536]{2,1,0:T(8,128)(2,1)} async-done(((bf16[8,96,1536]{2,1,0:T(8,128)(2,1)}), bf16[8,96,1536]{2,1,0:T(8,128)(2,1)}, u32[]{:S(2)}, u32[]{:S(2)}) %all-to-all-start.10) | async-done | bytes 2359328 | tf_op jit(solution)/shard_map/all_to_all | solution.py:74
  455.8 31.9 %all-to-all-done.7 = bf16[32,16,1536]{2,1,0:T(8,128)(2,1)} async-done(((bf16[32,16,1536]{2,1,0:T(8,128)(2,1)}), bf16[32,16,1536]{2,1,0:T(8,128)(2,1)}, u32[]{:S(2)}, u32[]{:S(2)}) %all-to-all-start.7) | async-done | bytes 1572896 | tf_op jit(solution)/shard_map/all_to_all | solution.py:74
  487.7 42.6 %all_to_all.121 = bf16[32,16,1536]{2,1,0:T(8,128)(2,1)} all-to-all(bf16[32,16,1536]{2,1,0:T(8,128)(2,1)} %bitcast.423), channel_id=1, replica_groups=mesh['section'=2,'dp'=4,'expert'=4] {'expert','dp','section'}, dimensions={0} | all-to-all | bytes 3145728 | tf_op jit(solution)/shard_map/all_to_all | solution.py:74
  544.6 44.9 %all-to-all-done.9 = bf16[8,192,768]{2,1,0:T(8,128)(2,1)} async-done(((bf16[8,192,768]{2,1,0:T(8,128)(2,1)}), bf16[8,192,768]{2,1,0:T(8,128)(2,1)}, u32[]{:S(2)}, u32[]{:S(2)}) %all-to-all-start.9) | async-done | bytes 2359328 | tf_op jit(solution)/shard_map/all_to_all | solution.py:74
  589.4 5.8 multiply_convert_fusion.4
  611.4 34.0 %all-to-all-done.13 = bf16[32,16,1536]{2,1,0:T(8,128)(2,1)} async-done(((bf16[32,16,1536]{2,1,0:T(8,128)(2,1)}), bf16[32,16,1536]{2,1,0:T(8,128)(2,1)}, u32[]{:S(2)}, u32[]{:S(2)}) %all-to-all-start.13) | async-done | bytes 1572896 | tf_op jit(solution)/shard_map/all_to_all | solution.py:74
  651.9 35.8 %all-to-all-done.11 = bf16[32,16,1536]{2,1,0:T(8,128)(2,1)} async-done(((bf16[32,16,1536]{2,1,0:T(8,128)(2,1)}), bf16[32,16,1536]{2,1,0:T(8,128)(2,1)}, u32[]{:S(2)}, u32[]{:S(2)}) %all-to-all-start.11) | async-done | bytes 1572896 | tf_op jit(solution)/shard_map/all_to_all | solution.py:74
  747.9 51.6 %concatenate.101 = bf16[1536,3618]{0,1:T(8,128)(2,1)} concatenate(bf16[1536,1536]{0,1:T(8,128)(2,1)} %convolution_convert_fusion, bf16[1536,256]{0,1:T(8,128)(2,1)} %convolution_convert_fusion.17, bf16[1536,256]{0,1:T(8,128)(2,1)} %convolution_convert_fusion.16, bf16[1536,1536]{0,1:T(8,128)(2,1)} %convolution_convert_fusion.2, bf16[1536,32]{0,1:T(8,128)(2,1)} %convolution_convert_fusion.24, ...), dimensions={1} | concatenate | bytes 22228992 | tf_op jit(solution)/shard_map/concatenate | solution.py:326
  806.3 40.7 %all_to_all.122 = bf16[32,16,1536]{2,1,0:T(8,128)(2,1)S(1)} all-to-all(bf16[32,16,1536]{2,1,0:T(8,128)(2,1)S(1)} %bitcast.424), channel_id=1, replica_groups=mesh['section'=2,'dp'=4,'expert'=4] {'expert','dp','section'}, dimensions={0} | all-to-all | bytes 3145728 | tf_op jit(solution)/shard_map/all_to_all | solution.py:74
  862.5 12.8 add_convert_fusion
  875.3 14.7 copy.235
  894.6 6.3 all-to-all-done.16
  905.1 6.3 convolution_convert_fusion.20
  937.4 18.8 %all-to-all-done.17 = bf16[4,128,512]{1,2,0:T(8,128)(2,1)} async-done(((bf16[4,128,512]{1,2,0:T(8,128)(2,1)}), bf16[4,128,512]{1,2,0:T(8,128)(2,1)}, u32[]{:S(2)}, u32[]{:S(2)}) %all-to-all-start.17) | async-done | bytes 524320 | tf_op jit(solution)/shard_map/all_to_all | solution.py:74
  959.8 7.3 fusion.43
  968.1 46.1 %concatenate.100 = bf16[1536,3618]{0,1:T(8,128)(2,1)} concatenate(bf16[1536,1536]{0,1:T(8,128)(2,1)} %convolution_convert_fusion.1, bf16[1536,256]{0,1:T(8,128)(2,1)S(1)} %convolution_convert_fusion.19, bf16[1536,256]{0,1:T(8,128)(2,1)S(1)} %convolution_convert_fusion.18, bf16[1536,1536]{0,1:T(8,128)(2,1)} %convolution_convert_fusion.3, bf16[1536,32]{0,1:T(8,128)(2,1)S(1)} %copy-done.83, ...), dimensions={1} | concatenate | bytes 22228992 | tf_op jit(solution)/shard_map/concatenate | solution.py:326
  1014.2 17.3 collective-permute-done.15
  1031.5 11.4 add_convert_fusion.1
  1042.8 14.8 copy.233
  1057.8 32.7 %reduce-scatter.9.cloned.1.call-done = bf16[96,3618]{1,0:T(8,128)(2,1)} async-done(((bf16[1536,3618]{1,0:T(8,128)(2,1)}), bf16[96,3618]{1,0:T(8,128)(2,1)}) %reduce-scatter.9.cloned.1.call-update) | async-done | bytes 694672 | tf_op jit(solution)/shard_map/reduce_scatter | solution.py:330
  1103.9 97.4 %all-to-all-done.19 = bf16[8,192,768]{2,1,0:T(8,128)(2,1)S(1)} async-done(((bf16[8,192,768]{2,1,0:T(8,128)(2,1)}), bf16[8,192,768]{2,1,0:T(8,128)(2,1)S(1)}, u32[]{:S(2)}, u32[]{:S(2)}) %all-to-all-start.19) | async-done | bytes 2359328 | tf_op jit(solution)/shard_map/all_to_all | solution.py:74
  1201.3 6.9 all-to-all-start.21
  1208.2 133.6 %reduce-scatter.7.cloned.1.call-done = bf16[96,3618]{1,0:T(8,128)(2,1)} async-done(((bf16[1536,3618]{1,0:T(8,128)(2,1)}), bf16[96,3618]{1,0:T(8,128)(2,1)}) %reduce-scatter.7.cloned.1.call-update) | async-done | bytes 694672 | tf_op jit(solution)/shard_map/reduce_scatter | solution.py:330
  1346.1 6.1 all-to-all-start.23
  1356.5 91.3 %all-to-all-done.23 = bf16[8,96,1536]{2,1,0:T(8,128)(2,1)} async-done(((bf16[8,96,1536]{2,1,0:T(8,128)(2,1)}), bf16[8,96,1536]{2,1,0:T(8,128)(2,1)}, u32[]{:S(2)}, u32[]{:S(2)}) %all-to-all-start.23) | async-done | bytes 2359328 | tf_op jit(solution)/shard_map/all_to_all | solution.py:74
  1447.8 6.1 all-to-all-start.18
  1458.3 103.4 %all-to-all-done.18 = bf16[8,192,768]{2,1,0:T(8,128)(2,1)} async-done(((bf16[8,192,768]{2,1,0:T(8,128)(2,1)}), bf16[8,192,768]{2,1,0:T(8,128)(2,1)}, u32[]{:S(2)}, u32[]{:S(2)}) %all-to-all-start.18) | async-done | bytes 2359328 | tf_op jit(solution)/shard_map/all_to_all | solution.py:74
  1561.7 6.2 all-to-all-start.20
  1572.1 72.9 %all-to-all-done.20 = bf16[8,192,768]{2,1,0:T(8,128)(2,1)} async-done(((bf16[8,192,768]{2,1,0:T(8,128)(2,1)}), bf16[8,192,768]{2,1,0:T(8,128)(2,1)}, u32[]{:S(2)}, u32[]{:S(2)}) %all-to-all-start.20) | async-done | bytes 2359328 | tf_op jit(solution)/shard_map/all_to_all | solution.py:74
  1645.0 7.6 all-to-all-start.22
  1660.7 7.0 collective-permute-start.18
  1674.9 79.6 %all-to-all-done.22 = bf16[8,96,1536]{2,1,0:T(8,128)(2,1)} async-done(((bf16[8,96,1536]{2,1,0:T(8,128)(2,1)}), bf16[8,96,1536]{2,1,0:T(8,128)(2,1)}, u32[]{:S(2)}, u32[]{:S(2)}) %all-to-all-start.22) | async-done | bytes 2359328 | tf_op jit(solution)/shard_map/all_to_all | solution.py:74
  1783.0 12.9 convert_element_type.392
  1795.8 6.1 convert_element_type.384
  1801.9 7.6 copy-done.2
  1812.5 20.6 %fusion = (f32[1,1536,1536]{2,1,0:T(8,128)}, f32[1,1536,1536]{2,1,0:T(8,128)}) fusion(f32[1536,3618]{1,0:T(8,128)} %convert_element_type.392, f32[1536,3618]{1,0:T(8,128)} %copy-done.2, pred[]{:T(512)S(6)} %eq.124), kind=kLoop, calls=%fused_computation.3 | loop fusion | flops 4718592 | bytes 56623104 | tf_op jit(solution)/shard_map/broadcast_in_dim | solution.py:424
  (533 shorter events, 386.4 us)
Async XLA Ops:
  11.4 16.0 collective-permute-start.10
  11.5 6.7 collective-permute-start
  12.0 7.5 collective-permute-start.4
  12.2 5.5 collective-permute-start.2
  12.6 7.3 collective-permute-start.3
  21.8 20.5 %all-to-all-start = ((bf16[4,128,512]{1,2,0:T(8,128)(2,1)}), bf16[4,128,512]{1,2,0:T(8,128)(2,1)S(1)}, u32[]{:S(2)}, u32[]{:S(2)}) async-start(bf16[4,128,512]{1,2,0:T(8,128)(2,1)} %broadcast_in_dim.62), calls=%async_computation | async-start | bytes 1048576 | tf_op jit(solution)/shard_map/all_to_all | solution.py:74
  42.4 58.8 %all-to-all-start.2 = ((bf16[8,192,768]{2,1,0:T(8,128)(2,1)}), bf16[8,192,768]{2,1,0:T(8,128)(2,1)}, u32[]{:S(2)}, u32[]{:S(2)}) async-start(bf16[8,192,768]{2,1,0:T(8,128)(2,1)} %get-tuple-element.85), calls=%async_computation.2 | async-start | bytes 4718592 | tf_op jit(solution)/shard_map/all_to_all | solution.py:74
  47.3 60.7 %collective-permute-start.5 = (bf16[1536,1536]{1,0:T(8,128)(2,1)}, bf16[1536,1536]{1,0:T(8,128)(2,1)}, u32[]{:S(2)}, u32[]{:S(2)}) collective-permute-start(bf16[1536,1536]{1,0:T(8,128)(2,1)} %bitcast.433), channel_id=1, source_target_pairs={{0,16},{16,0},{1,17},{17,1},{2,18},{18,2},{3,19},{19,3},{4,20},{20... | collective-permute-start | bytes 14155784 | tf_op jit(solution)/shard_map/ppermute | solution.py:78
  47.5 69.7 %collective-permute-start.6 = (bf16[1536,1536]{1,0:T(8,128)(2,1)}, bf16[1536,1536]{1,0:T(8,128)(2,1)}, u32[]{:S(2)}, u32[]{:S(2)}) collective-permute-start(bf16[1536,1536]{1,0:T(8,128)(2,1)} %bitcast.419), channel_id=1, source_target_pairs={{0,16},{16,0},{1,17},{17,1},{2,18},{18,2},{3,19},{19,3},{4,20},{20... | collective-permute-start | bytes 14155784 | tf_op jit(solution)/shard_map/ppermute | solution.py:78
  47.8 10.1 collective-permute-start.1
  50.7 11.5 collective-permute-start.11
  51.0 5.9 collective-permute-start.7
  57.0 49.5 %collective-permute-start.8 = (f32[1536]{0:T(1024)S(1)}, f32[1536]{0:T(1024)S(1)}, u32[]{:S(2)}, u32[]{:S(2)}) collective-permute-start(f32[1536]{0:T(1024)S(1)} %reduce.3), channel_id=1, source_target_pairs={{0,16},{16,0},{1,17},{17,1},{2,18},{18,2},{3,19},{19,3},{4,20},{20... | collective-permute-start | bytes 18440 | tf_op jit(solution)/shard_map/ppermute | solution.py:78
  57.9 106.7 %collective-permute-start.12 = (bf16[8,96,1536]{2,1,0:T(8,128)(2,1)}, bf16[8,96,1536]{2,1,0:T(8,128)(2,1)}, u32[]{:S(2)}, u32[]{:S(2)}) collective-permute-start(bf16[8,96,1536]{2,1,0:T(8,128)(2,1)} %broadcast_select_fusion.6), channel_id=1, source_target_pairs={{0,16},{16,0},{1,17},{17,1},{2,18},{18,2},{3,19},{19,3},{4,20},{20... | collective-permute-start | bytes 7077896 | tf_op jit(solution)/shard_map/ppermute | solution.py:78
  101.2 59.2 %all-to-all-start.3 = ((bf16[8,192,768]{2,1,0:T(8,128)(2,1)}), bf16[8,192,768]{2,1,0:T(8,128)(2,1)}, u32[]{:S(2)}, u32[]{:S(2)}) async-start(bf16[8,192,768]{2,1,0:T(8,128)(2,1)} %get-tuple-element.83), calls=%async_computation.3 | async-start | bytes 4718592 | tf_op jit(solution)/shard_map/all_to_all | solution.py:74
  160.4 42.5 %all-to-all-start.1 = ((bf16[32,16,1536]{2,1,0:T(8,128)(2,1)}), bf16[32,16,1536]{2,1,0:T(8,128)(2,1)}, u32[]{:S(2)}, u32[]{:S(2)}) async-start(bf16[32,16,1536]{2,1,0:T(8,128)(2,1)} %bitcast.426), calls=%async_computation.1 | async-start | bytes 3145728 | tf_op jit(solution)/shard_map/all_to_all | solution.py:74
  202.9 59.3 %all-to-all-start.4 = ((bf16[8,96,1536]{2,1,0:T(8,128)(2,1)}), bf16[8,96,1536]{2,1,0:T(8,128)(2,1)}, u32[]{:S(2)}, u32[]{:S(2)}) async-start(bf16[8,96,1536]{2,1,0:T(8,128)(2,1)} %get-tuple-element.87), calls=%async_computation.4 | async-start | bytes 4718592 | tf_op jit(solution)/shard_map/all_to_all | solution.py:74
  307.1 58.7 %all-to-all-start.8 = ((bf16[8,192,768]{2,1,0:T(8,128)(2,1)}), bf16[8,192,768]{2,1,0:T(8,128)(2,1)}, u32[]{:S(2)}, u32[]{:S(2)}) async-start(bf16[8,192,768]{2,1,0:T(8,128)(2,1)} %get-tuple-element.84), calls=%async_computation.8 | async-start | bytes 4718592 | tf_op jit(solution)/shard_map/all_to_all | solution.py:74
  313.7 1.9 collective-permute-start.9
  367.5 18.2 all-to-all-start.6
  385.7 59.6 %all-to-all-start.10 = ((bf16[8,96,1536]{2,1,0:T(8,128)(2,1)}), bf16[8,96,1536]{2,1,0:T(8,128)(2,1)}, u32[]{:S(2)}, u32[]{:S(2)}) async-start(bf16[8,96,1536]{2,1,0:T(8,128)(2,1)} %get-tuple-element.86), calls=%async_computation.10 | async-start | bytes 4718592 | tf_op jit(solution)/shard_map/all_to_all | solution.py:74
  445.3 42.3 %all-to-all-start.7 = ((bf16[32,16,1536]{2,1,0:T(8,128)(2,1)}), bf16[32,16,1536]{2,1,0:T(8,128)(2,1)}, u32[]{:S(2)}, u32[]{:S(2)}) async-start(bf16[32,16,1536]{2,1,0:T(8,128)(2,1)} %bitcast.425), calls=%async_computation.7 | async-start | bytes 3145728 | tf_op jit(solution)/shard_map/all_to_all | solution.py:74
  530.2 59.2 %all-to-all-start.9 = ((bf16[8,192,768]{2,1,0:T(8,128)(2,1)}), bf16[8,192,768]{2,1,0:T(8,128)(2,1)}, u32[]{:S(2)}, u32[]{:S(2)}) async-start(bf16[8,192,768]{2,1,0:T(8,128)(2,1)} %get-tuple-element.82), calls=%async_computation.9 | async-start | bytes 4718592 | tf_op jit(solution)/shard_map/all_to_all | solution.py:74
  603.1 42.3 %all-to-all-start.13 = ((bf16[32,16,1536]{2,1,0:T(8,128)(2,1)}), bf16[32,16,1536]{2,1,0:T(8,128)(2,1)}, u32[]{:S(2)}, u32[]{:S(2)}) async-start(bf16[32,16,1536]{2,1,0:T(8,128)(2,1)} %bitcast.466), calls=%async_computation.13 | async-start | bytes 3145728 | tf_op jit(solution)/shard_map/all_to_all | solution.py:74
  645.4 42.3 %all-to-all-start.11 = ((bf16[32,16,1536]{2,1,0:T(8,128)(2,1)}), bf16[32,16,1536]{2,1,0:T(8,128)(2,1)}, u32[]{:S(2)}, u32[]{:S(2)}) async-start(bf16[32,16,1536]{2,1,0:T(8,128)(2,1)} %bitcast.465), calls=%async_computation.11 | async-start | bytes 3145728 | tf_op jit(solution)/shard_map/all_to_all | solution.py:74
  715.6 17.7 all-to-all-start.14
  799.5 62.9 %collective-permute-start.16 = (bf16[1536,3618]{0,1:T(8,128)(2,1)}, bf16[1536,3618]{0,1:T(8,128)(2,1)}, u32[]{:S(2)}, u32[]{:S(2)}) collective-permute-start(bf16[1536,3618]{0,1:T(8,128)(2,1)} %concatenate.101), channel_id=1, source_target_pairs={{0,16},{16,0},{1,17},{17,1},{2,18},{18,2},{3,19},{19,3},{4,20},{20... | collective-permute-start | bytes 33343496 | tf_op jit(solution)/shard_map/ppermute | solution.py:328
  858.9 41.9 %all-to-all-start.16 = ((bf16[32,16,1536]{2,1,0:T(8,128)(2,1)}), bf16[32,16,1536]{2,1,0:T(8,128)(2,1)}, u32[]{:S(2)}, u32[]{:S(2)}) async-start(bf16[32,16,1536]{2,1,0:T(8,128)(2,1)} %bitcast.464), calls=%async_computation.16 | async-start | bytes 3145728 | tf_op jit(solution)/shard_map/all_to_all | solution.py:74
  862.4 228.1 %reduce-scatter.9.cloned.1.call-start = ((), (), s32[]{:S(2)}) async-start(), calls=%async_computation.29 | async-start | bytes 12115968 | tf_op jit(solution)/shard_map/reduce_scatter | solution.py:330
  924.5 31.7 %all-to-all-start.17 = ((bf16[4,128,512]{1,2,0:T(8,128)(2,1)}), bf16[4,128,512]{1,2,0:T(8,128)(2,1)}, u32[]{:S(2)}, u32[]{:S(2)}) async-start(bf16[4,128,512]{1,2,0:T(8,128)(2,1)} %pad_maximum_fusion.1), calls=%async_computation.17 | async-start | bytes 1048576 | tf_op jit(solution)/shard_map/all_to_all | solution.py:74
  928.7 413.1 %reduce-scatter.7.cloned.1.call-start = ((), (), s32[]{:S(2)}) async-start(), calls=%async_computation.28 | async-start | bytes 12115968 | tf_op jit(solution)/shard_map/reduce_scatter | solution.py:330
  1014.2 17.3 collective-permute-start.15
  1057.7 725.3 %all-gather.5.cloned.1.call-start = ((), (), s32[]{:S(2)}) async-start(), calls=%async_computation.27 | async-start | bytes 12115968 | tf_op jit(solution)/shard_map/all_gather | solution.py:331
  1094.8 106.5 %all-to-all-start.19 = ((bf16[8,192,768]{2,1,0:T(8,128)(2,1)}), bf16[8,192,768]{2,1,0:T(8,128)(2,1)S(1)}, u32[]{:S(2)}, u32[]{:S(2)}) async-start(bf16[8,192,768]{2,1,0:T(8,128)(2,1)} %bitcast.451), calls=%async_computation.19 | async-start | bytes 4718592 | tf_op jit(solution)/shard_map/all_to_all | solution.py:74
  1201.3 144.8 %all-to-all-start.21 = ((bf16[8,192,768]{2,1,0:T(8,128)(2,1)}), bf16[8,192,768]{2,1,0:T(8,128)(2,1)}, u32[]{:S(2)}, u32[]{:S(2)}) async-start(bf16[8,192,768]{2,1,0:T(8,128)(2,1)} %bitcast.447), calls=%async_computation.21 | async-start | bytes 4718592 | tf_op jit(solution)/shard_map/all_to_all | solution.py:74
  1208.2 587.7 %all-gather.3.cloned.1.call-start = ((), (), s32[]{:S(2)}) async-start(), calls=%async_computation.26 | async-start | bytes 12115968 | tf_op jit(solution)/shard_map/all_gather | solution.py:331
  1346.1 101.8 %all-to-all-start.23 = ((bf16[8,96,1536]{2,1,0:T(8,128)(2,1)}), bf16[8,96,1536]{2,1,0:T(8,128)(2,1)}, u32[]{:S(2)}, u32[]{:S(2)}) async-start(bf16[8,96,1536]{2,1,0:T(8,128)(2,1)} %bitcast.449), calls=%async_computation.23 | async-start | bytes 4718592 | tf_op jit(solution)/shard_map/all_to_all | solution.py:74
  1447.8 113.8 %all-to-all-start.18 = ((bf16[8,192,768]{2,1,0:T(8,128)(2,1)}), bf16[8,192,768]{2,1,0:T(8,128)(2,1)}, u32[]{:S(2)}, u32[]{:S(2)}) async-start(bf16[8,192,768]{2,1,0:T(8,128)(2,1)} %bitcast.450), calls=%async_computation.18 | async-start | bytes 4718592 | tf_op jit(solution)/shard_map/all_to_all | solution.py:74
  1561.7 83.3 %all-to-all-start.20 = ((bf16[8,192,768]{2,1,0:T(8,128)(2,1)}), bf16[8,192,768]{2,1,0:T(8,128)(2,1)}, u32[]{:S(2)}, u32[]{:S(2)}) async-start(bf16[8,192,768]{2,1,0:T(8,128)(2,1)} %bitcast.448), calls=%async_computation.20 | async-start | bytes 4718592 | tf_op jit(solution)/shard_map/all_to_all | solution.py:74
  1645.0 109.5 %all-to-all-start.22 = ((bf16[8,96,1536]{2,1,0:T(8,128)(2,1)}), bf16[8,96,1536]{2,1,0:T(8,128)(2,1)}, u32[]{:S(2)}, u32[]{:S(2)}) async-start(bf16[8,96,1536]{2,1,0:T(8,128)(2,1)} %bitcast.446), calls=%async_computation.22 | async-start | bytes 4718592 | tf_op jit(solution)/shard_map/all_to_all | solution.py:74
  1652.6 16.3 collective-permute-start.17
  1654.0 19.2 %collective-permute-start.19 = (bf16[8,192,768]{2,1,0:T(8,128)(2,1)}, bf16[8,192,768]{2,1,0:T(8,128)(2,1)S(1)}, u32[]{:S(2)}, u32[]{:S(2)}) collective-permute-start(bf16[8,192,768]{2,1,0:T(8,128)(2,1)} %all-to-all-done.21), channel_id=1, source_target_pairs={{0,16},{1,17},{2,18},{3,19},{4,20},{5,21},{6,22},{7,23},{8,24},{9,... | collective-permute-start | bytes 7077896 | tf_op jit(solution)/shard_map/ppermute | solution.py:418
  1655.3 19.5 %collective-permute-start.21 = (bf16[8,96,1536]{2,1,0:T(8,128)(2,1)}, bf16[8,96,1536]{2,1,0:T(8,128)(2,1)}, u32[]{:S(2)}, u32[]{:S(2)}) collective-permute-start(bf16[8,96,1536]{2,1,0:T(8,128)(2,1)} %all-to-all-done.23), channel_id=1, source_target_pairs={{0,16},{1,17},{2,18},{3,19},{4,20},{5,21},{6,22},{7,23},{8,24},{9,... | collective-permute-start | bytes 7077896 | tf_op jit(solution)/shard_map/ppermute | solution.py:418
  1659.4 100.5 %collective-permute-start.14 = (f32[128,1536]{1,0:T(8,128)}, f32[128,1536]{1,0:T(8,128)}, u32[]{:S(2)}, u32[]{:S(2)}) collective-permute-start(f32[128,1536]{1,0:T(8,128)} %convolution_add_fusion.2), channel_id=1, source_target_pairs={{0,16},{1,17},{2,18},{3,19},{4,20},{5,21},{6,22},{7,23},{8,24},{9,... | collective-permute-start | bytes 2359304 | tf_op jit(solution)/shard_map/ppermute | solution.py:399
  1660.7 102.4 %collective-permute-start.18 = (bf16[8,192,768]{2,1,0:T(8,128)(2,1)}, bf16[8,192,768]{2,1,0:T(8,128)(2,1)}, u32[]{:S(2)}, u32[]{:S(2)}) collective-permute-start(bf16[8,192,768]{2,1,0:T(8,128)(2,1)} %all-to-all-done.18), channel_id=1, source_target_pairs={{16,0},{17,1},{18,2},{19,3},{20,4},{21,5},{22,6},{23,7},{24,8},{25... | collective-permute-start | bytes 7077896 | tf_op jit(solution)/shard_map/ppermute | solution.py:419
  1668.9 100.5 %collective-permute-start.20 = (bf16[8,192,768]{2,1,0:T(8,128)(2,1)}, bf16[8,192,768]{2,1,0:T(8,128)(2,1)}, u32[]{:S(2)}, u32[]{:S(2)}) collective-permute-start(bf16[8,192,768]{2,1,0:T(8,128)(2,1)} %all-to-all-done.20), channel_id=1, source_target_pairs={{16,0},{17,1},{18,2},{19,3},{20,4},{21,5},{22,6},{23,7},{24,8},{25... | collective-permute-start | bytes 7077896 | tf_op jit(solution)/shard_map/ppermute | solution.py:419
  1673.2 86.7 %collective-permute-start.13 = (f32[128,1536]{1,0:T(8,128)}, f32[128,1536]{1,0:T(8,128)S(1)}, u32[]{:S(2)}, u32[]{:S(2)}) collective-permute-start(f32[128,1536]{1,0:T(8,128)} %fusion.39), channel_id=1, source_target_pairs={{16,0},{17,1},{18,2},{19,3},{20,4},{21,5},{22,6},{23,7},{24,8},{25... | collective-permute-start | bytes 2359304 | tf_op jit(solution)/shard_map/ppermute | solution.py:412
  1754.5 21.4 %collective-permute-start.22 = (bf16[8,96,1536]{2,1,0:T(8,128)(2,1)}, bf16[8,96,1536]{2,1,0:T(8,128)(2,1)S(1)}, u32[]{:S(2)}, u32[]{:S(2)}) collective-permute-start(bf16[8,96,1536]{2,1,0:T(8,128)(2,1)} %all-to-all-done.22), channel_id=1, source_target_pairs={{16,0},{17,1},{18,2},{19,3},{20,4},{21,5},{22,6},{23,7},{24,8},{25... | collective-permute-start | bytes 7077896 | tf_op jit(solution)/shard_map/ppermute | solution.py:419
  (146 other events, 1500.8 us)
Sparse Core Ops, SparseCore 0:
  890.1 200.3 reduce-scatter.8
  1096.3 245.4 reduce-scatter.6
  1344.6 225.2 all-gather.4
  1572.5 207.9 all-gather.2
where the time goes:
time: 1860 us; the launch traced here: 1850 us
  waiting for transfers between devices  1050 us (56%)
  matrix products  195 us (10%)
  local copies, waits for them, and re-layouts  180 us (10%)
  other arithmetic  147 us (8%)
  starting transfers between devices  133 us (7%)
  blocking collectives  125 us (7%)
    all_to_all x21, waiting for transfers between devices, exchange(): return lax.all_to_all(shard, axes, split_axis=0, concat_axis=0, tiled=True)  859 us
    reduce_scatter x2, waiting for transfers between devices, dense_total(): part = lax.psum_scatter(both, REPLICAS, scatter_dimension=0, tiled=True)  166 us
    all_to_all x3, blocking collectives, exchange(): return lax.all_to_all(shard, axes, split_axis=0, concat_axis=0, tiled=True)  125 us
    all_to_all x21, starting transfers between devices, exchange(): return lax.all_to_all(shard, axes, split_axis=0, concat_axis=0, tiled=True)  106 us
    concatenate x2, local copies, waits for them, and re-layouts, dense_total(): jnp.concatenate([a.astype(BF) for a in (query, key, value, out, small)], 1)  97.8 us
    dot_general x24, matrix products, dot(): return jnp.dot(left, right, preferred_element_type=F32)  62.7 us
    dot_general x19, matrix products, dot_t(): lax.dot_general(left, right, (((1,), (1,)), ((), ())), preferred_element_...  58.3 us
    unnamed x296, local copies, waits for them, and re-layouts  55.9 us
  transfers between devices with their start and end apart: 48, of which 26 were waited for; matrix products, arithmetic and copies ran while one was open for 19% of the time, Pallas kernels for 0%

commit v1 on v0

--- a/solution.py
+++ b/solution.py
@@ -56,9 +56,15 @@
     return (scaled * factor - values * factor * factor * factor * inner_mean, grad_gain)
 
 
-def tree_mask(lengths_row, first_row, local_len, tree_length):
+def tree_mask(lengths_row, local_len):
+    size = lax.axis_size("dp")
+    own = lax.axis_index("dp")
+    first_row = own * local_len
     seg_ends = jnp.cumsum(lengths_row)
-    key_spots = jnp.arange(tree_length, dtype=jnp.int32)
+    blocks = (own - jnp.arange(size, dtype=jnp.int32)) % size
+    key_spots = (
+        blocks[:, None] * local_len + jnp.arange(local_len, dtype=jnp.int32)[None, :]
+    ).reshape(-1)
     query_spots = first_row + jnp.arange(local_len, dtype=jnp.int32)
     seg_ids = jnp.arange(13, dtype=jnp.int32)
     key_seg = jnp.sum((key_spots[:, None] >= seg_ends[None, :]).astype(jnp.int32), 1)
@@ -80,14 +86,20 @@
 
 def gather_rows(shard):
     size = lax.axis_size("dp")
-    copies = jnp.broadcast_to(shard[None], (size,) + shard.shape)
-    return exchange(copies, "dp").reshape((-1,) + shard.shape[1:])
+    blocks = [shard]
+    for step in range(1, size):
+        blocks.append(lax.ppermute(shard, "dp", [(i, (i + step) % size) for i in range(size)]))
+    return jnp.concatenate(blocks, 0)
 
 
 def sum_to_owner(partial):
     size = lax.axis_size("dp")
-    blocks = exchange(partial.reshape((size, -1) + partial.shape[1:]), "dp")
-    return jnp.sum(blocks.astype(F32), 0)
+    blocks = jnp.split(partial, size, 0)
+    total = blocks[0].astype(F32)
+    for step in range(1, size):
+        back = [((i + step) % size, i) for i in range(size)]
+        total = total + lax.ppermute(blocks[step], "dp", back).astype(F32)
+    return total
 
 
 def layer_forward(layer_in, visible, route_rows, turn_row, dense_set, expert_set):
@@ -165,6 +177,8 @@
         "up_pre": up_pre,
         "inner_act": inner_act,
         "returned": returned,
+        "early_hidden": early_operand(hidden_one),
+        "early_mix": early_operand(attn_mix),
     }
     return (result, stored)
 
@@ -217,7 +231,7 @@
     grad_logits = (
         gate_share * (grad_weighting - jnp.sum(gate_share * grad_weighting, -1, keepdims=True))
     ).astype(BF)
-    grad_router = t_dot(stored["hidden_two"], grad_logits)
+    grad_router = t_dot(grad_logits, stored["hidden_two"])
     grad_hidden = dot_t(grad_logits, w_router)
     gate_pre = stored["gate_pre"]
     up_pre = stored["up_pre"]
@@ -239,7 +253,7 @@
     )
     grad_middle = grad_top.astype(F32) + grad_normed_two
     grad_branch = grad_middle.astype(BF)
-    grad_w_out = t_dot(stored["attn_mix"], grad_branch)
+    grad_w_out = dense_total(stored["early_mix"], late_operand(grad_branch))
     grad_mix = dot_t(grad_branch, w_out).astype(BF)
     key_all = stored["key_all"]
     value_all = stored["value_all"]
@@ -268,10 +282,9 @@
     ).astype(BF)
     key_width = w_key.shape[1]
     grad_keys, grad_values = grad_kv[:, :key_width], grad_kv[:, key_width:]
-    hidden_one = stored["hidden_one"]
-    grad_query_w = t_dot(hidden_one, grad_queries)
-    grad_key_w = t_dot(hidden_one, grad_keys)
-    grad_value_w = t_dot(hidden_one, grad_values)
+    grad_qkv_w = dense_total(
+        stored["early_hidden"], late_operand(jnp.concatenate([grad_queries, grad_kv], 1))
+    )
     grad_hidden_one = dot_t(grad_queries, w_query)
     grad_hidden_one = grad_hidden_one + dot_t(grad_keys, w_key)
     grad_hidden_one = grad_hidden_one + dot_t(grad_values, w_value)
@@ -279,15 +292,9 @@
         stored["layer_in"], stored["factor_one"], attn_gain, grad_hidden_one
     )
     grad_input = grad_middle + grad_normed_one
-    dense_grads = (
-        grad_attn_gain,
-        grad_query_w,
-        grad_key_w,
-        grad_value_w,
-        grad_w_out,
-        grad_ffn_gain,
-        grad_router,
-    )
+    small = jnp.concatenate([grad_router, grad_attn_gain[None], grad_ffn_gain[None]], 0)
+    small = small_total(jnp.pad(small, ((0, -small.shape[0] % 16), (0, 0))))
+    dense_grads = (grad_w_out, grad_qkv_w, small)
     return (grad_input, dense_grads, (grad_gate, grad_up, grad_down))
 
 
@@ -319,20 +326,91 @@
     return pieces
 
 
-def dense_total(grads, shift):
-    attn_gain, query, key, value, out, ffn_gain, router = grads
-    small = jnp.concatenate([router, attn_gain[:, None], ffn_gain[:, None]], 1)
-    widths = [a.shape[1] for a in (query, key, value, out, small)]
-    packed = jnp.concatenate([a.astype(BF) for a in (query, key, value, out, small)], 1)
-    rows = packed.shape[0]
-    other = lax.ppermute(packed, "section", shift)
-    both = (packed.astype(F32) + other.astype(F32)).astype(BF)
-    part = lax.psum_scatter(both, REPLICAS, scatter_dimension=0, tiled=True)
-    total = lax.all_gather(part, REPLICAS, axis=0, tiled=True).astype(F32)
-    offsets = np.cumsum(widths)[:-1]
-    query, key, value, out, small = jnp.split(total, offsets, 1)
-    experts = small.shape[1] - 2
-    return (small[:, experts], query, key, value, out, small[:, experts + 1], small[:, :experts])
+def ring(axis, step):
+    size = lax.axis_size(axis)
+    return [(i, (i + step) % size) for i in range(size)]
+
+
+def partners(axis, flip):
+    return [(i, i ^ flip) for i in range(lax.axis_size(axis))]
+
+
+def early_operand(rows):
+    half = rows.shape[1] // 2
+    section = lax.axis_index("section")
+    mine = lax.dynamic_slice_in_dim(rows, section * half, half, 1)
+    others = lax.dynamic_slice_in_dim(rows, (1 - section) * half, half, 1)
+    gathered = jnp.stack([mine, swapped(others)])
+    flip = 1
+    while flip < lax.axis_size("expert"):
+        others = lax.ppermute(gathered, "expert", partners("expert", flip))
+        gathered = jnp.concatenate([gathered, others], 1)
+        flip *= 2
+    return gathered.reshape(-1, half)
+
+
+def late_operand(rows):
+    groups = lax.axis_size("expert")
+    own = lax.axis_index("expert")
+    share = rows.shape[1] // groups
+    blocks = []
+    for flip in range(groups):
+        block = lax.dynamic_slice_in_dim(rows, (own ^ flip) * share, share, 1)
+        if flip > 0:
+            block = lax.ppermute(block, "expert", partners("expert", flip))
+        blocks.append(block)
+    gathered = jnp.concatenate(blocks, 0)
+    return jnp.concatenate([gathered, swapped(gathered)], 0)
+
+
+def rows_of(array, index, count):
+    return lax.dynamic_slice_in_dim(array, index * count, count, 0)
+
+
+def dense_total(early, late):
+    partial = t_dot(early, late)
+    size = lax.axis_size("dp")
+    own = lax.axis_index("dp")
+    count = partial.shape[0] // size
+    total = rows_of(partial, own, count)
+    rounded = partial.astype(BF)
+    for step in range(1, size):
+        block = rows_of(rounded, (own + step) % size, count)
+        total = total + lax.ppermute(block, "dp", ring("dp", step)).astype(F32)
+    total = total.astype(BF)
+    blocks = [total] + [lax.ppermute(total, "dp", ring("dp", -step)) for step in range(1, size)]
+    total = jnp.concatenate(blocks + blocks[:-1], 0)
+    total = lax.dynamic_slice_in_dim(total, ((size - own) % size) * count, size * count, 0)
+    group = lax.axis_index("expert")
+    flip = 1
+    while flip < lax.axis_size("expert"):
+        others = lax.ppermute(total, "expert", partners("expert", flip))
+        first = (group & flip) == 0
+        total = jnp.concatenate(
+            [jnp.where(first, total, others), jnp.where(first, others, total)], 1
+        )
+        flip *= 2
+    return total
+
+
+def small_total(partial):
+    total = partial + swapped(partial.astype(BF)).astype(F32)
+    flip = 1
+    while flip < lax.axis_size("expert"):
+        total = total + lax.ppermute(
+            total.astype(BF), "expert", partners("expert", flip)
+        ).astype(F32)
+        flip *= 2
+    rounded = total.astype(BF)
+    for step in range(1, lax.axis_size("dp")):
+        total = total + lax.ppermute(rounded, "dp", ring("dp", step)).astype(F32)
+    return total
+
+
+def at_home(first, second, is_first, axis):
+    low_half = jnp.where(is_first, first, lax.ppermute(second, "section", UP))
+    high_half = jnp.where(is_first, lax.ppermute(first, "section", DOWN), second)
+    return jnp.concatenate([low_half, high_half], axis).astype(F32)
 
 
 def local(
@@ -356,8 +434,6 @@
     lengths_all = seg_lengths[:, 0]
     route_all = routes[0, :, 0]
     turn_all = turns[0, :, 0, 0]
-    tree_length = local_len * lax.axis_size("dp")
-    first_row = lax.axis_index("dp") * local_len
     section_index = lax.axis_index("section")
     is_first = section_index == 0
 
@@ -379,7 +455,7 @@
     expert_pairs = [experts_in(a, is_first) for a in expert_own]
     dense_sets = [tuple(p[i] for p in dense_pairs) for i in range(2)]
     expert_sets = [tuple(p[i] for p in expert_pairs) for i in range(2)]
-    visible = tree_mask(lengths_row, first_row, local_len, tree_length)
+    visible = tree_mask(lengths_row, local_len)
 
     stored = []
     state = layer_rows
@@ -406,19 +482,29 @@
             stored[layer], grad, dense_sets[layer], expert_sets[layer]
         )
         expert_halves[layer] = [experts_out(g, w_gate.shape[1]) for g in expert_grads]
-        dense_totals[layer] = dense_total(dense_grads, SWAP)
+        dense_totals[layer] = dense_grads
         if layer == 1:
             grad = grad.astype(BF)
+            grad, expert_halves[1] = lax.optimization_barrier((grad, expert_halves[1]))
     grad_other = lax.ppermute(grad, "section", DOWN)
     edge_out = jnp.where(
         is_first, jnp.stack([grad, grad_other]), jnp.stack([top_other, top])
     )[None, :, None]
-    expert_total = []
-    for first, second in zip(*expert_halves, strict=True):
-        low_half = jnp.where(is_first, first, lax.ppermute(second, "section", UP))
-        high_half = jnp.where(is_first, lax.ppermute(first, "section", DOWN), second)
-        expert_total.append(jnp.concatenate([low_half, high_half], 1).astype(F32))
-    dense_out = [jnp.where(is_first, a, b) for a, b in zip(*dense_totals, strict=True)]
+    expert_total = [at_home(*pair, is_first, 1) for pair in zip(*expert_halves, strict=True)]
+    out, qkv = [at_home(a, b, is_first, 0) for a, b in list(zip(*dense_totals, strict=True))[:2]]
+    small = jnp.where(is_first, dense_totals[0][2], dense_totals[1][2])
+    query_width, key_width = w_query.shape[2], w_key.shape[2]
+    query, key, value = jnp.split(qkv, [query_width, query_width + key_width], 1)
+    experts_all = w_router.shape[2]
+    dense_out = (
+        small[experts_all],
+        query,
+        key,
+        value,
+        out,
+        small[experts_all + 1],
+        small[:experts_all].T,
+    )
     return (
         (edge_out,)
         + tuple((piece[None] for piece in dense_out))

time: 1860 us -> 1520 us (0.82)
  waiting for transfers between devices: 1050 us -> 762 us
  starting transfers between devices: 133 us -> 250 us
  local copies, waits for them, and re-layouts: 180 us -> 74.5 us
  blocking collectives: 125 us -> 84.2 us
    all_to_all x21 -> x18, waiting for transfers between devices: 859 us -> 297 us  [exchange(): return lax.all_to_all(shard, axes, split_axis=0, concat_axis=0, tiled=True)]
    ppermute x8 -> x84, waiting for transfers between devices: 17.3 us -> 464 us  [the longest x12 121 us: dense_total(): total = total + lax.ppermute(block, 'dp', ring('dp', step)).astype(F32)]
    reduce_scatter x2 -> x0, waiting for transfers between devices: 166 us -> none  [dense_total(): part = lax.psum_scatter(both, REPLICAS, scatter_dimension=0, tiled=True)]
    ppermute x8 -> x84, starting transfers between devices: 20.8 us -> 127 us  [the longest x12 34.6 us: dense_total(): lax.ppermute(total, 'dp', ring('dp', -step))]
    concatenate x12 -> x8, local copies, waits for them, and re-layouts: 109 us -> 5.68 us  [the longest x4 4.04 us: late_operand(): return jnp.concatenate([gathered, swapped(gathered)], 0)]
    all_to_all x3 -> x2, blocking collectives: 125 us -> 84.2 us  [exchange(): return lax.all_to_all(shard, axes, split_axis=0, concat_axis=0, tiled=True)]
    concatenate x6 -> x28, other arithmetic: 7.98 us -> 45.6 us  [the longest x8 17.4 us: early_operand(): gathered = jnp.concatenate([gathered, others], 1)]
    convert_element_type x7 -> x17, other arithmetic: 57.3 us -> 27.9 us  [the longest x5 23.8 us: at_home(): return jnp.concatenate([low_half, high_half], axis).astype(F32)]
  transfers between devices with their start and end apart: 48 -> 127, of which waited for: 26 -> 45; matrix products, arithmetic and copies ran while one was open for 19% -> 23% of each run, Pallas kernels for 0% -> 0%
where the time goes in v1:
time: 1520 us; the launch traced here: 1510 us
  waiting for transfers between devices  762 us (50%)
  starting transfers between devices  250 us (16%)
  matrix products  178 us (12%)
  other arithmetic  156 us (10%)
  blocking collectives  84.2 us (6%)
  local copies, waits for them, and re-layouts  74.5 us (5%)
    all_to_all x18, waiting for transfers between devices, exchange(): return lax.all_to_all(shard, axes, split_axis=0, concat_axis=0, tiled=True)  297 us
    ppermute x12, waiting for transfers between devices, dense_total(): total = total + lax.ppermute(block, 'dp', ring('dp', step)).astype(F32)  121 us
    all_to_all x18, starting transfers between devices, exchange(): return lax.all_to_all(shard, axes, split_axis=0, concat_axis=0, tiled=True)  101 us
    all_to_all x2, blocking collectives, exchange(): return lax.all_to_all(shard, axes, split_axis=0, concat_axis=0, tiled=True)  84.2 us
    ppermute x8, waiting for transfers between devices, dense_total(): others = lax.ppermute(total, 'expert', partners('expert', flip))  79 us
    ppermute x12, waiting for transfers between devices, dense_total(): lax.ppermute(total, 'dp', ring('dp', -step))  78.7 us
    dot_general x24, matrix products, dot(): return jnp.dot(left, right, preferred_element_type=F32)  64 us
    ppermute x8, waiting for transfers between devices, early_operand(): others = lax.ppermute(gathered, 'expert', partners('expert', flip))  58.4 us
  transfers between devices with their start and end apart: 127, of which 45 were waited for; matrix products, arithmetic and copies ran while one was open for 23% of the time, Pallas kernels for 0%

profile of v1, /device:TPU:1, one launch (start us, length us, event | category | flops | bytes accessed | tf_op | source)
XLA Modules:
  0.0 1509.0 jit_solution(10385712672223011701)
XLA Ops:
  17.2 6.5 all-to-all-start.1
  51.5 31.7 %all-to-all-done.1 = bf16[8,192,768]{2,1,0:T(8,128)(2,1)} async-done(((bf16[8,192,768]{2,1,0:T(8,128)(2,1)}), bf16[8,192,768]{2,1,0:T(8,128)(2,1)}, u32[]{:S(2)}, u32[]{:S(2)}) %all-to-all-start.1) | async-done | bytes 2359328 | tf_op jit(solution)/shard_map/all_to_all | solution.py:80
  83.2 5.7 all-to-all-start.2
  108.5 34.3 %all-to-all-done.2 = bf16[8,192,768]{2,1,0:T(8,128)(2,1)} async-done(((bf16[8,192,768]{2,1,0:T(8,128)(2,1)}), bf16[8,192,768]{2,1,0:T(8,128)(2,1)}, u32[]{:S(2)}, u32[]{:S(2)}) %all-to-all-start.2) | async-done | bytes 2359328 | tf_op jit(solution)/shard_map/all_to_all | solution.py:80
  147.0 5.7 broadcast_select_fusion.6
  152.7 32.6 %all-to-all-done = bf16[32,16,1536]{2,1,0:T(8,128)(2,1)} async-done(((bf16[32,16,1536]{2,1,0:T(8,128)(2,1)}), bf16[32,16,1536]{2,1,0:T(8,128)(2,1)}, u32[]{:S(2)}, u32[]{:S(2)}) %all-to-all-start) | async-done | bytes 1572896 | tf_op jit(solution)/shard_map/all_to_all | solution.py:80
  200.4 44.2 %all-to-all-done.3 = bf16[8,96,1536]{2,1,0:T(8,128)(2,1)} async-done(((bf16[8,96,1536]{2,1,0:T(8,128)(2,1)}), bf16[8,96,1536]{2,1,0:T(8,128)(2,1)}, u32[]{:S(2)}, u32[]{:S(2)}) %all-to-all-start.3) | async-done | bytes 2359328 | tf_op jit(solution)/shard_map/all_to_all | solution.py:80
  247.9 41.6 %all_to_all.100 = bf16[32,16,1536]{2,1,0:T(8,128)(2,1)} all-to-all(bf16[32,16,1536]{2,1,0:T(8,128)(2,1)S(1)} %bitcast.457), channel_id=1, replica_groups=mesh['section'=2,'dp'=4,'expert'=4] {'expert','dp','section'}, dimensions={0} | all-to-all | bytes 3145728 | tf_op jit(solution)/shard_map/all_to_all | solution.py:80
  304.5 43.9 %all-to-all-done.6 = bf16[8,192,768]{2,1,0:T(8,128)(2,1)} async-done(((bf16[8,192,768]{2,1,0:T(8,128)(2,1)}), bf16[8,192,768]{2,1,0:T(8,128)(2,1)}, u32[]{:S(2)}, u32[]{:S(2)}) %all-to-all-start.6) | async-done | bytes 2359328 | tf_op jit(solution)/shard_map/all_to_all | solution.py:80
  366.2 28.8 %collective-permute-done.18 = bf16[128,512]{1,0:T(8,128)(2,1)} collective-permute-done((bf16[128,512]{1,0:T(8,128)(2,1)}, bf16[128,512]{1,0:T(8,128)(2,1)}, u32[]{:S(2)}, u32[]{:S(2)}) %collective-permute-start.18) | collective-permute-done | bytes 131104 | tf_op jit(solution)/shard_map/ppermute | solution.py:91
  394.9 23.8 %collective-permute-done.17 = bf16[128,512]{1,0:T(8,128)(2,1)} collective-permute-done((bf16[128,512]{1,0:T(8,128)(2,1)}, bf16[128,512]{1,0:T(8,128)(2,1)}, u32[]{:S(2)}, u32[]{:S(2)}) %collective-permute-start.17) | collective-permute-done | bytes 131104 | tf_op jit(solution)/shard_map/ppermute | solution.py:91
  449.5 31.1 %all-to-all-done.5 = bf16[32,16,1536]{2,1,0:T(8,128)(2,1)} async-done(((bf16[32,16,1536]{2,1,0:T(8,128)(2,1)}), bf16[32,16,1536]{2,1,0:T(8,128)(2,1)}, u32[]{:S(2)}, u32[]{:S(2)}) %all-to-all-start.5) | async-done | bytes 1572896 | tf_op jit(solution)/shard_map/all_to_all | solution.py:80
  480.6 42.6 %all_to_all.101 = bf16[32,16,1536]{2,1,0:T(8,128)(2,1)} all-to-all(bf16[32,16,1536]{2,1,0:T(8,128)(2,1)} %bitcast.397), channel_id=1, replica_groups=mesh['section'=2,'dp'=4,'expert'=4] {'expert','dp','section'}, dimensions={0} | all-to-all | bytes 3145728 | tf_op jit(solution)/shard_map/all_to_all | solution.py:80
  537.4 44.9 %all-to-all-done.7 = bf16[8,192,768]{2,1,0:T(8,128)(2,1)} async-done(((bf16[8,192,768]{2,1,0:T(8,128)(2,1)}), bf16[8,192,768]{2,1,0:T(8,128)(2,1)}, u32[]{:S(2)}, u32[]{:S(2)}) %all-to-all-start.7) | async-done | bytes 2359328 | tf_op jit(solution)/shard_map/all_to_all | solution.py:80
  582.3 5.7 multiply_convert_fusion.4
  604.2 34.0 %all-to-all-done.11 = bf16[32,16,1536]{2,1,0:T(8,128)(2,1)} async-done(((bf16[32,16,1536]{2,1,0:T(8,128)(2,1)}), bf16[32,16,1536]{2,1,0:T(8,128)(2,1)}, u32[]{:S(2)}, u32[]{:S(2)}) %all-to-all-start.11) | async-done | bytes 1572896 | tf_op jit(solution)/shard_map/all_to_all | solution.py:80
  646.2 18.7 %collective-permute-done.40 = bf16[2,128,768]{2,1,0:T(8,128)(2,1)S(1)} collective-permute-done((bf16[2,128,768]{2,1,0:T(8,128)(2,1)S(1)}, bf16[2,128,768]{2,1,0:T(8,128)(2,1)S(1)}, u32[]{:S(2)}, u32[]{:S(2)}) %collective-permute-start.40) | collective-permute-done | bytes 393248 | tf_op jit(solution)/shard_map/ppermute | solution.py:346
  691.7 8.5 all-to-all-start.12
  712.9 8.9 collective-permute-done.73
  724.4 14.3 collective-permute-done.56
  741.2 14.3 collective-permute-done.88
  772.8 6.5 all-to-all-start.13
  809.3 15.0 collective-permute-done.21
  824.3 17.3 %collective-permute-done.20 = bf16[128,512]{0,1:T(8,128)(2,1)S(1)} collective-permute-done((bf16[128,512]{0,1:T(8,128)(2,1)S(1)}, bf16[128,512]{0,1:T(8,128)(2,1)S(1)}, u32[]{:S(2)}, u32[]{:S(2)}) %collective-permute-start.20) | collective-permute-done | bytes 131104 | tf_op jit(solution)/shard_map/ppermute | solution.py:101
  844.2 6.6 all-to-all-start.14
  878.3 14.2 collective-permute-done.95
  892.4 24.8 %collective-permute-done.94 = bf16[192,384]{1,0:T(8,128)(2,1)S(1)} collective-permute-done((bf16[192,384]{1,0:T(8,128)(2,1)S(1)}, bf16[192,384]{1,0:T(8,128)(2,1)S(1)}, u32[]{:S(2)}, u32[]{:S(2)}) %collective-permute-start.94) | collective-permute-done | bytes 147488 | tf_op jit(solution)/shard_map/ppermute | solution.py:379
  941.5 12.9 collective-permute-done.62
  954.4 13.3 collective-permute-done.61
  970.7 21.5 %collective-permute-start.65 = (bf16[192,512]{1,0:T(8,128)(2,1)S(1)}, bf16[192,512]{1,0:T(8,128)(2,1)S(1)}, u32[]{:S(2)}, u32[]{:S(2)}) collective-permute-start(bf16[192,512]{1,0:T(8,128)(2,1)S(1)} %get-tuple-element.36), channel_id=1, source_target_pairs={{0,8},{4,12},{8,0},{12,4},{1,9},{5,13},{9,1},{13,5},{2,10},{6,14},... | collective-permute-start | bytes 589832 | tf_op jit(solution)/shard_map/ppermute | solution.py:381
  996.1 12.0 collective-permute-done.65
  1014.8 11.6 collective-permute-done.67
  1055.0 34.8 %collective-permute-done.68 = bf16[768,1024]{1,0:T(8,128)(2,1)} collective-permute-done((bf16[768,1024]{1,0:T(8,128)(2,1)}, bf16[768,1024]{1,0:T(8,128)(2,1)}, u32[]{:S(2)}, u32[]{:S(2)}) %collective-permute-start.68) | collective-permute-done | bytes 1572896 | tf_op jit(solution)/shard_map/ppermute | solution.py:387
  1107.5 7.9 all-to-all-start.17
  1121.1 6.2 convolution_convert_fusion.12
  1150.9 9.3 collective-permute-done.24
  1161.6 15.9 %collective-permute-done.23 = bf16[128,512]{0,1:T(8,128)(2,1)S(1)} collective-permute-done((bf16[128,512]{0,1:T(8,128)(2,1)S(1)}, bf16[128,512]{0,1:T(8,128)(2,1)S(1)}, u32[]{:S(2)}, u32[]{:S(2)}) %collective-permute-start.23) | collective-permute-done | bytes 131104 | tf_op jit(solution)/shard_map/ppermute | solution.py:101
  1186.7 6.3 all-to-all-start.18
  1215.5 19.1 %collective-permute-done.80 = bf16[192,384]{1,0:T(8,128)(2,1)S(1)} collective-permute-done((bf16[192,384]{1,0:T(8,128)(2,1)S(1)}, bf16[192,384]{1,0:T(8,128)(2,1)S(1)}, u32[]{:S(2)}, u32[]{:S(2)}) %collective-permute-start.80) | collective-permute-done | bytes 147488 | tf_op jit(solution)/shard_map/ppermute | solution.py:379
  1238.6 24.0 %collective-permute-done.79 = bf16[192,384]{1,0:T(8,128)(2,1)S(1)} collective-permute-done((bf16[192,384]{1,0:T(8,128)(2,1)S(1)}, bf16[192,384]{1,0:T(8,128)(2,1)S(1)}, u32[]{:S(2)}, u32[]{:S(2)}) %collective-permute-start.79) | collective-permute-done | bytes 147488 | tf_op jit(solution)/shard_map/ppermute | solution.py:379
  1266.1 6.8 collective-permute-start.25
  1292.5 54.4 %collective-permute-done.82 = bf16[192,384]{1,0:T(8,128)(2,1)S(1)} collective-permute-done((bf16[192,384]{1,0:T(8,128)(2,1)S(1)}, bf16[192,384]{1,0:T(8,128)(2,1)S(1)}, u32[]{:S(2)}, u32[]{:S(2)}) %collective-permute-start.82) | collective-permute-done | bytes 147488 | tf_op jit(solution)/shard_map/ppermute | solution.py:381
  1356.1 8.8 collective-permute-done.47
  1374.0 12.3 collective-permute-done.50
  1392.5 7.6 collective-permute-done.84
  1407.0 10.3 collective-permute-done.52
  1418.2 6.1 collective-permute-start.106
  1447.6 13.5 collective-permute-done.53
  (879 shorter events, 583.6 us)
Async XLA Ops:
  7.3 84.2 %collective-permute-start.8 = (bf16[1536,1536]{1,0:T(8,128)(2,1)}, bf16[1536,1536]{1,0:T(8,128)(2,1)}, u32[]{:S(2)}, u32[]{:S(2)}) collective-permute-start(bf16[1536,1536]{1,0:T(8,128)(2,1)} %bitcast.400), channel_id=1, source_target_pairs={{0,16},{16,0},{1,17},{17,1},{2,18},{18,2},{3,19},{19,3},{4,20},{20... | collective-permute-start | bytes 14155784 | tf_op jit(solution)/shard_map/ppermute | solution.py:84
  17.2 66.1 %all-to-all-start.1 = ((bf16[8,192,768]{2,1,0:T(8,128)(2,1)}), bf16[8,192,768]{2,1,0:T(8,128)(2,1)}, u32[]{:S(2)}, u32[]{:S(2)}) async-start(bf16[8,192,768]{2,1,0:T(8,128)(2,1)} %get-tuple-element.48), calls=%async_computation.1 | async-start | bytes 4718592 | tf_op jit(solution)/shard_map/all_to_all | solution.py:80
  38.1 62.5 %collective-permute-start.9 = (bf16[1536,1536]{1,0:T(8,128)(2,1)}, bf16[1536,1536]{1,0:T(8,128)(2,1)}, u32[]{:S(2)}, u32[]{:S(2)}) collective-permute-start(bf16[1536,1536]{1,0:T(8,128)(2,1)} %bitcast.393), channel_id=1, source_target_pairs={{0,16},{16,0},{1,17},{17,1},{2,18},{18,2},{3,19},{19,3},{4,20},{20... | collective-permute-start | bytes 14155784 | tf_op jit(solution)/shard_map/ppermute | solution.py:84
  41.4 48.1 %collective-permute-start.7 = (bf16[128,512]{1,0:T(8,128)(2,1)S(1)}, bf16[128,512]{1,0:T(8,128)(2,1)S(1)}, u32[]{:S(2)}, u32[]{:S(2)}) collective-permute-start(bf16[128,512]{1,0:T(8,128)(2,1)S(1)} %pad_maximum_fusion.28), channel_id=1, source_target_pairs={{0,12},{4,0},{8,4},{12,8},{1,13},{5,1},{9,5},{13,9},{2,14},{6,2},{... | collective-permute-start | bytes 393224 | tf_op jit(solution)/shard_map/ppermute | solution.py:91
  44.7 45.0 %collective-permute-start.6 = (bf16[128,512]{1,0:T(8,128)(2,1)S(1)}, bf16[128,512]{1,0:T(8,128)(2,1)S(1)}, u32[]{:S(2)}, u32[]{:S(2)}) collective-permute-start(bf16[128,512]{1,0:T(8,128)(2,1)S(1)} %pad_maximum_fusion.28), channel_id=1, source_target_pairs={{0,8},{4,12},{8,0},{12,4},{1,9},{5,13},{9,1},{13,5},{2,10},{6,14},... | collective-permute-start | bytes 393224 | tf_op jit(solution)/shard_map/ppermute | solution.py:91
  83.2 59.7 %all-to-all-start.2 = ((bf16[8,192,768]{2,1,0:T(8,128)(2,1)}), bf16[8,192,768]{2,1,0:T(8,128)(2,1)}, u32[]{:S(2)}, u32[]{:S(2)}) async-start(bf16[8,192,768]{2,1,0:T(8,128)(2,1)} %get-tuple-element.46), calls=%async_computation.2 | async-start | bytes 4718592 | tf_op jit(solution)/shard_map/all_to_all | solution.py:80
  89.6 57.5 %collective-permute-start.15 = (bf16[8,96,1536]{2,1,0:T(8,128)(2,1)}, bf16[8,96,1536]{2,1,0:T(8,128)(2,1)}, u32[]{:S(2)}, u32[]{:S(2)}) collective-permute-start(bf16[8,96,1536]{2,1,0:T(8,128)(2,1)} %broadcast_select_fusion.8), channel_id=1, source_target_pairs={{0,16},{16,0},{1,17},{17,1},{2,18},{18,2},{3,19},{19,3},{4,20},{20... | collective-permute-start | bytes 7077896 | tf_op jit(solution)/shard_map/ppermute | solution.py:84
  142.9 42.5 %all-to-all-start = ((bf16[32,16,1536]{2,1,0:T(8,128)(2,1)}), bf16[32,16,1536]{2,1,0:T(8,128)(2,1)}, u32[]{:S(2)}, u32[]{:S(2)}) async-start(bf16[32,16,1536]{2,1,0:T(8,128)(2,1)} %bitcast.399), calls=%async_computation | async-start | bytes 3145728 | tf_op jit(solution)/shard_map/all_to_all | solution.py:80
  185.4 59.3 %all-to-all-start.3 = ((bf16[8,96,1536]{2,1,0:T(8,128)(2,1)}), bf16[8,96,1536]{2,1,0:T(8,128)(2,1)}, u32[]{:S(2)}, u32[]{:S(2)}) async-start(bf16[8,96,1536]{2,1,0:T(8,128)(2,1)} %get-tuple-element.50), calls=%async_computation.3 | async-start | bytes 4718592 | tf_op jit(solution)/shard_map/all_to_all | solution.py:80
  289.5 58.8 %all-to-all-start.6 = ((bf16[8,192,768]{2,1,0:T(8,128)(2,1)}), bf16[8,192,768]{2,1,0:T(8,128)(2,1)}, u32[]{:S(2)}, u32[]{:S(2)}) async-start(bf16[8,192,768]{2,1,0:T(8,128)(2,1)} %get-tuple-element.47), calls=%async_computation.6 | async-start | bytes 4718592 | tf_op jit(solution)/shard_map/all_to_all | solution.py:80
  348.4 88.5 %all-to-all-start.8 = ((bf16[8,96,1536]{2,1,0:T(8,128)(2,1)}), bf16[8,96,1536]{2,1,0:T(8,128)(2,1)}, u32[]{:S(2)}, u32[]{:S(2)}) async-start(bf16[8,96,1536]{2,1,0:T(8,128)(2,1)} %get-tuple-element.49), calls=%async_computation.8 | async-start | bytes 4718592 | tf_op jit(solution)/shard_map/all_to_all | solution.py:80
  360.3 58.4 %collective-permute-start.17 = (bf16[128,512]{1,0:T(8,128)(2,1)}, bf16[128,512]{1,0:T(8,128)(2,1)}, u32[]{:S(2)}, u32[]{:S(2)}) collective-permute-start(bf16[128,512]{1,0:T(8,128)(2,1)} %pad_maximum_fusion.29), channel_id=1, source_target_pairs={{0,8},{4,12},{8,0},{12,4},{1,9},{5,13},{9,1},{13,5},{2,10},{6,14},... | collective-permute-start | bytes 393224 | tf_op jit(solution)/shard_map/ppermute | solution.py:91
  360.3 58.4 %collective-permute-start.16 = (bf16[128,512]{1,0:T(8,128)(2,1)}, bf16[128,512]{1,0:T(8,128)(2,1)}, u32[]{:S(2)}, u32[]{:S(2)}) collective-permute-start(bf16[128,512]{1,0:T(8,128)(2,1)} %pad_maximum_fusion.29), channel_id=1, source_target_pairs={{0,4},{4,8},{8,12},{12,0},{1,5},{5,9},{9,13},{13,1},{2,6},{6,10},{... | collective-permute-start | bytes 393224 | tf_op jit(solution)/shard_map/ppermute | solution.py:91
  436.9 43.7 %all-to-all-start.5 = ((bf16[32,16,1536]{2,1,0:T(8,128)(2,1)}), bf16[32,16,1536]{2,1,0:T(8,128)(2,1)}, u32[]{:S(2)}, u32[]{:S(2)}) async-start(bf16[32,16,1536]{2,1,0:T(8,128)(2,1)} %bitcast.398), calls=%async_computation.5 | async-start | bytes 3145728 | tf_op jit(solution)/shard_map/all_to_all | solution.py:80
  523.2 59.1 %all-to-all-start.7 = ((bf16[8,192,768]{2,1,0:T(8,128)(2,1)}), bf16[8,192,768]{2,1,0:T(8,128)(2,1)}, u32[]{:S(2)}, u32[]{:S(2)}) async-start(bf16[8,192,768]{2,1,0:T(8,128)(2,1)} %get-tuple-element.45), calls=%async_computation.7 | async-start | bytes 4718592 | tf_op jit(solution)/shard_map/all_to_all | solution.py:80
  638.2 53.5 %all-to-all-start.9 = ((bf16[32,16,1536]{2,1,0:T(8,128)(2,1)}), bf16[32,16,1536]{2,1,0:T(8,128)(2,1)}, u32[]{:S(2)}, u32[]{:S(2)}) async-start(bf16[32,16,1536]{2,1,0:T(8,128)(2,1)} %bitcast.454), calls=%async_computation.9 | async-start | bytes 3145728 | tf_op jit(solution)/shard_map/all_to_all | solution.py:80
  665.9 44.4 %collective-permute-start.41 = (bf16[2,256,768]{2,1,0:T(8,128)(2,1)}, bf16[2,256,768]{2,1,0:T(8,128)(2,1)}, u32[]{:S(2)}, u32[]{:S(2)}) collective-permute-start(bf16[2,256,768]{2,1,0:T(8,128)(2,1)} %pad_maximum_fusion.12), channel_id=1, source_target_pairs={{0,2},{1,3},{2,0},{3,1},{4,6},{5,7},{6,4},{7,5},{8,10},{9,11},{10,... | collective-permute-start | bytes 2359304 | tf_op jit(solution)/shard_map/ppermute | solution.py:346
  691.7 81.1 %all-to-all-start.12 = ((bf16[8,192,768]{2,1,0:T(8,128)(2,1)}), bf16[8,192,768]{2,1,0:T(8,128)(2,1)}, u32[]{:S(2)}, u32[]{:S(2)}) async-start(bf16[8,192,768]{2,1,0:T(8,128)(2,1)} %bitcast.434), calls=%async_computation.12 | async-start | bytes 4718592 | tf_op jit(solution)/shard_map/all_to_all | solution.py:80
  710.0 45.5 %collective-permute-start.88 = (bf16[2,256,768]{2,1,0:T(8,128)(2,1)}, bf16[2,256,768]{2,1,0:T(8,128)(2,1)}, u32[]{:S(2)}, u32[]{:S(2)}) collective-permute-start(bf16[2,256,768]{2,1,0:T(8,128)(2,1)} %pad_maximum_fusion.15), channel_id=1, source_target_pairs={{0,2},{1,3},{2,0},{3,1},{4,6},{5,7},{6,4},{7,5},{8,10},{9,11},{10,... | collective-permute-start | bytes 2359304 | tf_op jit(solution)/shard_map/ppermute | solution.py:346
  772.8 71.5 %all-to-all-start.13 = ((bf16[8,192,768]{2,1,0:T(8,128)(2,1)}), bf16[8,192,768]{2,1,0:T(8,128)(2,1)}, u32[]{:S(2)}, u32[]{:S(2)}) async-start(bf16[8,192,768]{2,1,0:T(8,128)(2,1)} %bitcast.436), calls=%async_computation.13 | async-start | bytes 4718592 | tf_op jit(solution)/shard_map/all_to_all | solution.py:80
  805.8 64.6 %collective-permute-start.92 = (bf16[512,384]{1,0:T(8,128)(2,1)}, bf16[512,384]{1,0:T(8,128)(2,1)}, u32[]{:S(2)}, u32[]{:S(2)}) collective-permute-start(bf16[512,384]{1,0:T(8,128)(2,1)} %pad_maximum_fusion.25), channel_id=1, source_target_pairs={{0,16},{16,0},{1,17},{17,1},{2,18},{18,2},{3,19},{19,3},{4,20},{20... | collective-permute-start | bytes 1179656 | tf_op jit(solution)/shard_map/ppermute | solution.py:84
  844.2 82.0 %all-to-all-start.14 = ((bf16[8,96,1536]{2,1,0:T(8,128)(2,1)}), bf16[8,96,1536]{2,1,0:T(8,128)(2,1)}, u32[]{:S(2)}, u32[]{:S(2)}) async-start(bf16[8,96,1536]{2,1,0:T(8,128)(2,1)} %bitcast.433), calls=%async_computation.14 | async-start | bytes 4718592 | tf_op jit(solution)/shard_map/all_to_all | solution.py:80
  868.6 51.4 %collective-permute-start.60 = (bf16[512,512]{0,1:T(8,128)(2,1)S(1)}, bf16[512,512]{0,1:T(8,128)(2,1)S(1)}, u32[]{:S(2)}, u32[]{:S(2)}) collective-permute-start(bf16[512,512]{0,1:T(8,128)(2,1)S(1)} %pad_maximum_fusion.19), channel_id=1, source_target_pairs={{0,16},{16,0},{1,17},{17,1},{2,18},{18,2},{3,19},{19,3},{4,20},{20... | collective-permute-start | bytes 1572872 | tf_op jit(solution)/shard_map/ppermute | solution.py:84
  877.4 132.1 %collective-permute-start.35 = (bf16[48,1536]{1,0:T(8,128)(2,1)}, bf16[48,1536]{1,0:T(8,128)(2,1)}, u32[]{:S(2)}, u32[]{:S(2)}) collective-permute-start(bf16[48,1536]{1,0:T(8,128)(2,1)} %fusion.153), channel_id=1, source_target_pairs={{0,2},{1,3},{2,0},{3,1},{4,6},{5,7},{6,4},{7,5},{8,10},{9,11},{10,... | collective-permute-start | bytes 442376 | tf_op jit(solution)/shard_map/ppermute | solution.py:400
  928.8 100.3 %all-to-all-start.15 = ((bf16[32,16,1536]{2,1,0:T(8,128)(2,1)}), bf16[32,16,1536]{2,1,0:T(8,128)(2,1)}, u32[]{:S(2)}, u32[]{:S(2)}) async-start(bf16[32,16,1536]{2,1,0:T(8,128)(2,1)} %bitcast.396), calls=%async_computation.15 | async-start | bytes 3145728 | tf_op jit(solution)/shard_map/all_to_all | solution.py:80
  1011.2 202.0 %collective-permute-start.38 = (bf16[48,1536]{1,0:T(8,128)(2,1)}, bf16[48,1536]{1,0:T(8,128)(2,1)}, u32[]{:S(2)}, u32[]{:S(2)}) collective-permute-start(bf16[48,1536]{1,0:T(8,128)(2,1)} %fusion.53), channel_id=1, source_target_pairs={{0,12},{4,0},{8,4},{12,8},{1,13},{5,1},{9,5},{13,9},{2,14},{6,2},{... | collective-permute-start | bytes 442376 | tf_op jit(solution)/shard_map/ppermute | solution.py:406
  1011.6 251.8 %collective-permute-start.37 = (bf16[48,1536]{1,0:T(8,128)(2,1)}, bf16[48,1536]{1,0:T(8,128)(2,1)}, u32[]{:S(2)}, u32[]{:S(2)}) collective-permute-start(bf16[48,1536]{1,0:T(8,128)(2,1)} %fusion.53), channel_id=1, source_target_pairs={{0,8},{4,12},{8,0},{12,4},{1,9},{5,13},{9,1},{13,5},{2,10},{6,14},... | collective-permute-start | bytes 442376 | tf_op jit(solution)/shard_map/ppermute | solution.py:406
  1029.1 60.7 %collective-permute-start.68 = (bf16[768,1024]{1,0:T(8,128)(2,1)}, bf16[768,1024]{1,0:T(8,128)(2,1)}, u32[]{:S(2)}, u32[]{:S(2)}) collective-permute-start(bf16[768,1024]{1,0:T(8,128)(2,1)} %pad_maximum_fusion.7), channel_id=1, source_target_pairs={{0,2},{1,3},{2,0},{3,1},{4,6},{5,7},{6,4},{7,5},{8,10},{9,11},{10,... | collective-permute-start | bytes 4718600 | tf_op jit(solution)/shard_map/ppermute | solution.py:387
  1041.8 65.6 %all-to-all-start.16 = ((bf16[32,16,1536]{2,1,0:T(8,128)(2,1)}), bf16[32,16,1536]{2,1,0:T(8,128)(2,1)}, u32[]{:S(2)}, u32[]{:S(2)}) async-start(bf16[32,16,1536]{2,1,0:T(8,128)(2,1)} %bitcast.455), calls=%async_computation.16 | async-start | bytes 3145728 | tf_op jit(solution)/shard_map/all_to_all | solution.py:80
  1107.5 79.2 %all-to-all-start.17 = ((bf16[8,192,768]{2,1,0:T(8,128)(2,1)}), bf16[8,192,768]{2,1,0:T(8,128)(2,1)}, u32[]{:S(2)}, u32[]{:S(2)}) async-start(bf16[8,192,768]{2,1,0:T(8,128)(2,1)} %bitcast.435), calls=%async_computation.17 | async-start | bytes 4718592 | tf_op jit(solution)/shard_map/all_to_all | solution.py:80
  1160.3 46.1 %collective-permute-start.77 = (bf16[512,384]{1,0:T(8,128)(2,1)}, bf16[512,384]{1,0:T(8,128)(2,1)}, u32[]{:S(2)}, u32[]{:S(2)}) collective-permute-start(bf16[512,384]{1,0:T(8,128)(2,1)} %pad_maximum_fusion.23), channel_id=1, source_target_pairs={{0,16},{16,0},{1,17},{17,1},{2,18},{18,2},{3,19},{19,3},{4,20},{20... | collective-permute-start | bytes 1179656 | tf_op jit(solution)/shard_map/ppermute | solution.py:84
  1186.7 91.8 %all-to-all-start.18 = ((bf16[8,192,768]{2,1,0:T(8,128)(2,1)}), bf16[8,192,768]{2,1,0:T(8,128)(2,1)}, u32[]{:S(2)}, u32[]{:S(2)}) async-start(bf16[8,192,768]{2,1,0:T(8,128)(2,1)} %bitcast.432), calls=%async_computation.18 | async-start | bytes 4718592 | tf_op jit(solution)/shard_map/all_to_all | solution.py:80
  1212.7 49.9 %collective-permute-start.79 = (bf16[192,384]{1,0:T(8,128)(2,1)S(1)}, bf16[192,384]{1,0:T(8,128)(2,1)S(1)}, u32[]{:S(2)}, u32[]{:S(2)}) collective-permute-start(bf16[192,384]{1,0:T(8,128)(2,1)S(1)} %get-tuple-element.89), channel_id=1, source_target_pairs={{0,8},{4,12},{8,0},{12,4},{1,9},{5,13},{9,1},{13,5},{2,10},{6,14},... | collective-permute-start | bytes 442376 | tf_op jit(solution)/shard_map/ppermute | solution.py:379
  1212.7 49.9 %collective-permute-start.78 = (bf16[192,384]{1,0:T(8,128)(2,1)S(1)}, bf16[192,384]{1,0:T(8,128)(2,1)S(1)}, u32[]{:S(2)}, u32[]{:S(2)}) collective-permute-start(bf16[192,384]{1,0:T(8,128)(2,1)S(1)} %get-tuple-element.87), channel_id=1, source_target_pairs={{0,4},{4,8},{8,12},{12,0},{1,5},{5,9},{9,13},{13,1},{2,6},{6,10},{... | collective-permute-start | bytes 442376 | tf_op jit(solution)/shard_map/ppermute | solution.py:379
  1213.2 51.4 %collective-permute-start.36 = (bf16[48,1536]{1,0:T(8,128)(2,1)}, bf16[48,1536]{1,0:T(8,128)(2,1)S(1)}, u32[]{:S(2)}, u32[]{:S(2)}) collective-permute-start(bf16[48,1536]{1,0:T(8,128)(2,1)} %fusion.53), channel_id=1, source_target_pairs={{0,4},{4,8},{8,12},{12,0},{1,5},{5,9},{9,13},{13,1},{2,6},{6,10},{... | collective-permute-start | bytes 442376 | tf_op jit(solution)/shard_map/ppermute | solution.py:406
  1263.4 85.1 %collective-permute-start.26 = (f32[128,1536]{1,0:T(8,128)S(1)}, f32[128,1536]{1,0:T(8,128)}, u32[]{:S(2)}, u32[]{:S(2)}) collective-permute-start(f32[128,1536]{1,0:T(8,128)S(1)} %copy-done.56), channel_id=1, source_target_pairs={{0,16},{1,17},{2,18},{3,19},{4,20},{5,21},{6,22},{7,23},{8,24},{9,... | collective-permute-start | bytes 2359304 | tf_op jit(solution)/shard_map/ppermute | solution.py:475
  1264.7 102.2 %collective-permute-start.103 = (bf16[8,192,768]{2,1,0:T(8,128)(2,1)}, bf16[8,192,768]{2,1,0:T(8,128)(2,1)}, u32[]{:S(2)}, u32[]{:S(2)}) collective-permute-start(bf16[8,192,768]{2,1,0:T(8,128)(2,1)} %all-to-all-done.12), channel_id=1, source_target_pairs={{0,16},{1,17},{2,18},{3,19},{4,20},{5,21},{6,22},{7,23},{8,24},{9,... | collective-permute-start | bytes 7077896 | tf_op jit(solution)/shard_map/ppermute | solution.py:411
  1266.1 83.7 %collective-permute-start.25 = (f32[128,1536]{1,0:T(8,128)S(1)}, f32[128,1536]{1,0:T(8,128)}, u32[]{:S(2)}, u32[]{:S(2)}) collective-permute-start(f32[128,1536]{1,0:T(8,128)S(1)} %fusion.31), channel_id=1, source_target_pairs={{16,0},{17,1},{18,2},{19,3},{20,4},{21,5},{22,6},{23,7},{24,8},{25... | collective-permute-start | bytes 2359304 | tf_op jit(solution)/shard_map/ppermute | solution.py:489
  1278.6 145.8 %all-to-all-start.19 = ((bf16[8,96,1536]{2,1,0:T(8,128)(2,1)}), bf16[8,96,1536]{2,1,0:T(8,128)(2,1)}, u32[]{:S(2)}, u32[]{:S(2)}) async-start(bf16[8,96,1536]{2,1,0:T(8,128)(2,1)} %bitcast.431), calls=%async_computation.19 | async-start | bytes 4718592 | tf_op jit(solution)/shard_map/all_to_all | solution.py:80
  1284.1 62.7 %collective-permute-start.82 = (bf16[192,384]{1,0:T(8,128)(2,1)S(1)}, bf16[192,384]{1,0:T(8,128)(2,1)S(1)}, u32[]{:S(2)}, u32[]{:S(2)}) collective-permute-start(bf16[192,384]{1,0:T(8,128)(2,1)S(1)} %get-tuple-element.32), channel_id=1, source_target_pairs={{0,8},{4,12},{8,0},{12,4},{1,9},{5,13},{9,1},{13,5},{2,10},{6,14},... | collective-permute-start | bytes 442376 | tf_op jit(solution)/shard_map/ppermute | solution.py:381
  1291.2 57.0 %collective-permute-start.83 = (bf16[192,384]{1,0:T(8,128)(2,1)S(1)}, bf16[192,384]{1,0:T(8,128)(2,1)S(1)}, u32[]{:S(2)}, u32[]{:S(2)}) collective-permute-start(bf16[192,384]{1,0:T(8,128)(2,1)S(1)} %get-tuple-element.32), channel_id=1, source_target_pairs={{0,4},{4,8},{8,12},{12,0},{1,5},{5,9},{9,13},{13,1},{2,6},{6,10},{... | collective-permute-start | bytes 442376 | tf_op jit(solution)/shard_map/ppermute | solution.py:381
  1346.9 56.0 %collective-permute-start.105 = (bf16[8,192,768]{2,1,0:T(8,128)(2,1)}, bf16[8,192,768]{2,1,0:T(8,128)(2,1)S(1)}, u32[]{:S(2)}, u32[]{:S(2)}) collective-permute-start(bf16[8,192,768]{2,1,0:T(8,128)(2,1)} %all-to-all-done.13), channel_id=1, source_target_pairs={{0,16},{1,17},{2,18},{3,19},{4,20},{5,21},{6,22},{7,23},{8,24},{9,... | collective-permute-start | bytes 7077896 | tf_op jit(solution)/shard_map/ppermute | solution.py:411
  1348.5 57.3 %collective-permute-start.107 = (bf16[8,96,1536]{2,1,0:T(8,128)(2,1)}, bf16[8,96,1536]{2,1,0:T(8,128)(2,1)}, u32[]{:S(2)}, u32[]{:S(2)}) collective-permute-start(bf16[8,96,1536]{2,1,0:T(8,128)(2,1)} %all-to-all-done.14), channel_id=1, source_target_pairs={{0,16},{1,17},{2,18},{3,19},{4,20},{5,21},{6,22},{7,23},{8,24},{9,... | collective-permute-start | bytes 7077896 | tf_op jit(solution)/shard_map/ppermute | solution.py:411
  1364.9 66.4 %collective-permute-start.101 = (bf16[768,1536]{1,0:T(8,128)(2,1)}, bf16[768,1536]{1,0:T(8,128)(2,1)}, u32[]{:S(2)}, u32[]{:S(2)}) collective-permute-start(bf16[768,1536]{1,0:T(8,128)(2,1)} %pad_maximum_fusion.3), channel_id=1, source_target_pairs={{0,16},{1,17},{2,18},{3,19},{4,20},{5,21},{6,22},{7,23},{8,24},{9,... | collective-permute-start | bytes 7077896 | tf_op jit(solution)/shard_map/ppermute | solution.py:411
  1387.7 53.1 %collective-permute-start.104 = (bf16[8,192,768]{2,1,0:T(8,128)(2,1)}, bf16[8,192,768]{2,1,0:T(8,128)(2,1)}, u32[]{:S(2)}, u32[]{:S(2)}) collective-permute-start(bf16[8,192,768]{2,1,0:T(8,128)(2,1)} %all-to-all-done.17), channel_id=1, source_target_pairs={{16,0},{17,1},{18,2},{19,3},{20,4},{21,5},{22,6},{23,7},{24,8},{25... | collective-permute-start | bytes 7077896 | tf_op jit(solution)/shard_map/ppermute | solution.py:412
  1405.7 56.2 %collective-permute-start.69 = (bf16[768,2048]{1,0:T(8,128)(2,1)}, bf16[768,2048]{1,0:T(8,128)(2,1)}, u32[]{:S(2)}, u32[]{:S(2)}) collective-permute-start(bf16[768,2048]{1,0:T(8,128)(2,1)} %pad_maximum_fusion.1), channel_id=1, source_target_pairs={{0,16},{1,17},{2,18},{3,19},{4,20},{5,21},{6,22},{7,23},{8,24},{9,... | collective-permute-start | bytes 9437192 | tf_op jit(solution)/shard_map/ppermute | solution.py:411
  1431.3 48.7 %collective-permute-start.108 = (bf16[8,96,1536]{2,1,0:T(8,128)(2,1)}, bf16[8,96,1536]{2,1,0:T(8,128)(2,1)S(1)}, u32[]{:S(2)}, u32[]{:S(2)}) collective-permute-start(bf16[8,96,1536]{2,1,0:T(8,128)(2,1)} %all-to-all-done.19), channel_id=1, source_target_pairs={{16,0},{17,1},{18,2},{19,3},{20,4},{21,5},{22,6},{23,7},{24,8},{25... | collective-permute-start | bytes 7077896 | tf_op jit(solution)/shard_map/ppermute | solution.py:412
  1440.7 46.4 %collective-permute-start.102 = (bf16[768,1536]{1,0:T(8,128)(2,1)}, bf16[768,1536]{1,0:T(8,128)(2,1)}, u32[]{:S(2)}, u32[]{:S(2)}) collective-permute-start(bf16[768,1536]{1,0:T(8,128)(2,1)} %get-tuple-element.65), channel_id=1, source_target_pairs={{16,0},{17,1},{18,2},{19,3},{20,4},{21,5},{22,6},{23,7},{24,8},{25... | collective-permute-start | bytes 7077896 | tf_op jit(solution)/shard_map/ppermute | solution.py:412
  (276 other events, 4624.9 us)

commit v2 on v0

v2 whole, which is shorter than its diff:
```python
import jax
import jax.numpy as jnp
import numpy as np
from jax import lax
from jax.experimental import pallas as pl
from jax.experimental.pallas import tpu as pltpu
from jax.sharding import PartitionSpec as P

HEAD_SIZE = 128
SCALE = HEAD_SIZE ** (-0.5)
epsilon = 1e-06
masked_score = -1e30
BF = jnp.bfloat16
F32 = jnp.float32

SWAP = [(0, 1), (1, 0)]
UP = [(0, 1)]
DOWN = [(1, 0)]
OWNERS = ("expert", "dp", "section")
LINE = ("dp", "section")


def ancestry():
    parents = [-1]
    for branch_index in range(4):
        parents += [0, 1 + 3 * branch_index, 1 + 3 * branch_index]
    lineage = np.zeros((13, 13), np.float32)
    for segment in range(13):
        current = segment
        while current >= 0:
            lineage[current, segment] = 1.0
            current = parents[current]
    return lineage


def dot(left, right):
    return jnp.dot(left, right, preferred_element_type=F32)


def dot_t(left, right):
    return lax.dot_general(left, right, (((1,), (1,)), ((), ())), preferred_element_type=F32)


def t_dot(left, right):
    return lax.dot_general(left, right, (((0,), (0,)), ((), ())), preferred_element_type=F32)


def t_dot_t(left, right):
    return lax.dot_general(left, right, (((0,), (1,)), ((), ())), preferred_element_type=F32)


def normalize(values, gain_vec):
    factor = lax.rsqrt(jnp.mean(values * values, -1, keepdims=True) + epsilon)
    return (values * factor * gain_vec, factor)


def norm_back(values, factor, gain_vec, upstream):
    scaled = upstream * gain_vec
    grad_gain = jnp.sum(upstream * values * factor, 0)
    inner_mean = jnp.mean(scaled * values, -1, keepdims=True)
    return (scaled * factor - values * factor * factor * factor * inner_mean, grad_gain)


def tree_mask(lengths_row, local_len):
    own = lax.axis_index("dp")
    first_row = own * local_len
    seg_ends = jnp.cumsum(lengths_row)
    blocks = own ^ jnp.asarray(block_order(), jnp.int32)
    key_spots = (
        blocks[:, None] * local_len + jnp.arange(local_len, dtype=jnp.int32)[None, :]
    ).reshape(-1)
    query_spots = first_row + jnp.arange(local_len, dtype=jnp.int32)
    seg_ids = jnp.arange(13, dtype=jnp.int32)
    key_seg = jnp.sum((key_spots[:, None] >= seg_ends[None, :]).astype(jnp.int32), 1)
    query_seg = jnp.sum((query_spots[:, None] >= seg_ends[None, :]).astype(jnp.int32), 1)
    key_hot = (key_seg[:, None] == seg_ids[None, :]).astype(BF)
    query_hot = (query_seg[:, None] == seg_ids[None, :]).astype(BF)
    allowed = dot(query_hot, jnp.asarray(ancestry(), BF)).astype(BF)
    linked = dot_t(allowed, key_hot) > 0.5
    return linked & (key_spots[None, :] <= query_spots[:, None])


def tie(*values):
    return lax.optimization_barrier(values)


def swapped(shard):
    return lax.ppermute(shard, "section", SWAP)


def partners(axis, flip):
    return [(i, i ^ flip) for i in range(lax.axis_size(axis))]


def flips(axis):
    found = [1]
    while 2 * found[-1] < lax.axis_size(axis):
        found.append(2 * found[-1])
    return found


def block_order():
    order = [0]
    for flip in reversed(flips("dp")):
        order = order + [k ^ flip for k in order]
    return order


def gathered(shard, axis, over="dp"):
    for flip in reversed(flips(over)):
        shard = jnp.concatenate([shard, lax.ppermute(shard, over, partners(over, flip))], axis)
    return shard


def sum_to_owner(partial, axis):
    sent_as = partial.dtype
    for flip in flips("dp"):
        kept, sent = jnp.split(partial, 2, axis)
        sent = lax.ppermute(sent.astype(sent_as), "dp", partners("dp", flip))
        partial = kept.astype(F32) + sent.astype(F32)
    return partial


def pick_blocks(sources, blocks, pick, count, kernel, out_shapes, out_blocks):
    where = jnp.stack([lax.axis_index(axis) for axis in ("section", "dp")]).astype(jnp.int32)

    def spec(at):
        def index(k, where):
            return pick(k, where)[at]

        return pl.BlockSpec(blocks[at], index)

    def body(where, *refs):
        kernel(pl.program_id(0), where, refs[: len(sources)], refs[len(sources) :])

    return pl.pallas_call(
        body,
        grid_spec=pltpu.PrefetchScalarGridSpec(
            num_scalar_prefetch=1,
            grid=(count,),
            in_specs=[spec(at) for at in range(len(sources))],
            out_specs=[
                pl.BlockSpec(shape, lambda k, where: (k,) + (0,) * (len(shape) - 1))
                for shape in out_blocks
            ],
        ),
        out_shape=[jax.ShapeDtypeStruct(shape, F32) for shape in out_shapes],
        compiler_params=pltpu.CompilerParams(vmem_limit_bytes=48 * 1024 * 1024),
    )(where, *sources)


def two_homes(first, second):
    return (
        first,
        second,
        lax.ppermute(first, "section", DOWN),
        lax.ppermute(second, "section", UP),
    )


def source_of(section, core):
    return jnp.where(core == section, section, 2 + section)


def dense_home(homes, out_widths):
    parts, groups, rows, width = homes[0].shape
    block = rows // 2

    def pick(k, where):
        used = source_of(where[0], k // (2 * parts))
        return [
            (jnp.where(used == source, k // 2 % parts, 0), 0, jnp.where(used == source, k % 2, 0), 0)
            for source in range(4)
        ]

    def kernel(k, where, sources, outs):
        used = source_of(where[0], k // (2 * parts))
        for source in range(4):

            @pl.when(used == source)
            def _():
                out, at = 0, 0
                for group in range(groups):
                    start = 0
                    while start < width:
                        piece = min(width - start, out_widths[out] - at)
                        outs[out][:, at : at + piece] = sources[source][
                            0, group, :, start : start + piece
                        ].astype(F32)
                        start, at = start + piece, at + piece
                        if at == out_widths[out]:
                            out, at = out + 1, 0

    count = 4 * parts
    shapes = [(count * block, w) for w in out_widths]
    blocks = [(1, groups, block, width)] * 4
    return pick_blocks(
        homes, blocks, pick, count, kernel, shapes, [(block, w) for w in out_widths]
    )


def two_parts(array, index, axis=0):
    half = array.shape[axis] // 2
    return (
        lax.dynamic_slice_in_dim(array, index * half, half, axis),
        lax.dynamic_slice_in_dim(array, (1 - index) * half, half, axis),
    )


def in_order(mine, others, index, axis):
    first = index == 0
    return jnp.concatenate(
        [jnp.where(first, mine, others), jnp.where(first, others, mine)], axis
    )


def early_operand(rows):
    mine, others = two_parts(rows, lax.axis_index("section"), 1)
    half = mine.shape[1]
    joined = jnp.stack([mine.reshape(2, -1, half), swapped(others).reshape(2, -1, half)], 1)
    return gathered(joined[:, None], 1, "expert").reshape(2, -1, half)


def late_operands(operands):
    groups = lax.axis_size("expert")
    own = lax.axis_index("expert")
    blocks = []
    order = [0]
    for flip in reversed(flips("expert")):
        order = order + [k ^ flip for k in order]
    for flip in order:
        shares = []
        for rows in operands:
            share = rows.shape[1] // groups
            shares.append(lax.dynamic_slice_in_dim(rows, (own ^ flip) * share, share, 1))
        block = jnp.concatenate(shares, 1)
        if flip > 0:
            block = lax.ppermute(block, "expert", partners("expert", flip))
        blocks.append(block)
    joined = jnp.stack(blocks)
    joined = jnp.stack([joined, swapped(joined)], 1)
    joined = joined.reshape(-1, joined.shape[-1])
    return jnp.split(joined, np.cumsum([a.shape[1] // groups for a in operands])[:-1], 1)


def dense_partial(early, late):
    return jnp.concatenate([t_dot(e, p) for e, p in zip(early, late, strict=True)], 1)


def dense_rows(partial):
    own = lax.axis_index("dp")
    for flip in flips("dp"):
        kept, sent = two_parts(partial, jnp.where((own & flip) == 0, 0, 1))
        sent = lax.ppermute(sent.astype(BF), "dp", partners("dp", flip))
        partial = kept.astype(F32) + sent.astype(F32)
    return partial.astype(BF)


def dense_line(total):
    own = lax.axis_index("dp")
    for flip in reversed(flips("dp")):
        others = lax.ppermute(total, "dp", partners("dp", flip))
        total = in_order(total, others, own & flip, 0)
    return total


def dense_groups(total):
    own = lax.axis_index("expert")
    order = flips("expert")
    parts = []
    for part, way in zip(jnp.split(total, 2, 0), (order, order[::-1]), strict=True):
        part = part.reshape((1,) * len(order) + part.shape)
        for flip in way:
            others = lax.ppermute(part, "expert", partners("expert", flip))
            part = in_order(part, others, own & flip, len(order) - 1 - order.index(flip))
        parts.append(part.reshape((-1,) + part.shape[-2:]))
    return jnp.stack(parts)


def small_total(partial):
    for axis in ("section", "expert", "dp"):
        for flip in flips(axis):
            others = lax.ppermute(partial.astype(BF), axis, partners(axis, flip))
            partial = partial + others.astype(F32)
    return partial


def exchange(rows, axes):
    return lax.all_to_all(rows, axes, split_axis=0, concat_axis=0, tiled=True)


def copies_of_expert(experts_all):
    owners = lax.axis_size("expert") * lax.axis_size("dp") * lax.axis_size("section")
    return owners // experts_all


def send_out(slot_rows, experts_all):
    width = slot_rows.shape[-1]
    copies = copies_of_expert(experts_all)
    rows = slot_rows.reshape(experts_all, -1, width)
    if copies > 1:
        mine = jnp.arange(copies) == lax.axis_index("dp") % copies
        rows = jnp.where(mine[None, :, None, None], rows[:, None], 0)
        rows = rows.reshape(experts_all * copies, -1, width)
    return exchange(rows, OWNERS).reshape(-1, width)


def send_back(rows, experts_all):
    width = rows.shape[-1]
    copies = copies_of_expert(experts_all)
    rows = exchange(rows.reshape(experts_all * copies, -1, width), OWNERS)
    if copies > 1:
        rows = rows.reshape(experts_all, copies, -1, width)
        rows = lax.dynamic_index_in_dim(rows, lax.axis_index("dp") % copies, 1, False)
    return rows.reshape(-1, width)


def row_halves(own, is_first):
    half = own.shape[1] // 2
    low_half, high_half = own[:, :half], own[:, half:]
    kept = jnp.where(is_first, low_half, high_half)
    received = swapped(jnp.where(is_first, high_half, low_half))
    return (jnp.where(is_first, kept, received), jnp.where(is_first, received, kept))


def expert_in(rows):
    copies = lax.axis_size("dp") * lax.axis_size("section") // rows.shape[0]
    if copies > 1:
        rows = jnp.repeat(rows, copies, 0)
    return exchange(rows, LINE).reshape(-1, rows.shape[-1])


def expert_out(grad, experts):
    size = lax.axis_size("dp") * lax.axis_size("section")
    columns = grad.shape[1]
    pieces = exchange(grad.reshape(size, -1, columns), LINE)
    copies = size // experts
    if copies > 1:
        pieces = pieces.reshape(experts, copies, -1, columns).astype(F32)
        pieces = jnp.sum(pieces, 1).astype(BF)
    return pieces


def expert_home(homes):
    experts, rows, columns = homes[0].shape

    def pick(k, where):
        section = where[0]
        used = [section, 2 + section]
        return [
            (jnp.where((used[0] == source) | (used[1] == source), k, 0), 0, 0)
            for source in range(4)
        ]

    def kernel(k, where, sources, outs):
        for core in range(2):
            used = source_of(where[0], core)
            for source in range(4):

                @pl.when(used == source)
                def _():
                    outs[0][0, core * rows : (core + 1) * rows] = sources[source][0].astype(F32)

    shape = (experts, 2 * rows, columns)
    blocks = [(1, rows, columns)] * 4
    return pick_blocks(homes, blocks, pick, experts, kernel, [shape], [(1,) + shape[1:]])[0]


def routing(route_rows, turn_row, experts_all, capacity):
    expert_ids = jnp.arange(experts_all, dtype=jnp.int32)
    chosen = jnp.any(route_rows[:, :, None] == expert_ids[None, None, :], 1)
    earlier = (turn_row[None, :] < turn_row[:, None]).astype(BF)
    places = dot(earlier, chosen.astype(BF))
    place_of = jnp.where(chosen & (places < capacity), places, -1.0).astype(BF)
    slot_ids = jnp.arange(experts_all * capacity, dtype=jnp.int32)
    spread = (slot_ids[None, :] // capacity == expert_ids[:, None]).astype(BF)
    selected = dot(place_of, spread) == (slot_ids % capacity).astype(F32)[None, :]
    return chosen, selected, spread


def attention_forward(layer_in, visible, routed, dense_set, hook):
    attn_gain, w_query, w_key, w_value, w_out, ffn_gain, w_router = dense_set
    local_len = layer_in.shape[0]
    heads_kv = w_key.shape[1] // HEAD_SIZE
    normed, factor_one = normalize(layer_in, attn_gain)
    hidden_one = normed.astype(BF)
    key_rows = dot(hidden_one, w_key).astype(BF)
    value_rows = dot(hidden_one, w_value).astype(BF)
    kv_all = hook(gathered(jnp.concatenate([key_rows, value_rows], 1), 0))
    queries = dot(hidden_one, w_query).astype(BF)
    key_width = w_key.shape[1]
    key_all = kv_all[:, :key_width].reshape(-1, heads_kv, HEAD_SIZE)
    value_all = kv_all[:, key_width:].reshape(-1, heads_kv, HEAD_SIZE)
    grouped_query = queries.reshape(local_len, heads_kv, -1, HEAD_SIZE)
    raw = jnp.einsum("tkgd,skd->kgts", grouped_query, key_all, preferred_element_type=F32) * SCALE
    scores = jnp.where(visible[None, None], raw, masked_score)
    log_total = jax.nn.logsumexp(scores, -1, keepdims=True)
    attn_prob = jnp.exp(scores - log_total)
    attn_mix = jnp.einsum(
        "kgts,skd->tkgd", attn_prob.astype(BF), value_all, preferred_element_type=F32
    )
    attn_mix = attn_mix.reshape(local_len, -1).astype(BF)
    middle = layer_in + dot(attn_mix, w_out)
    normed_two, factor_two = normalize(middle, ffn_gain)
    hidden_two = normed_two.astype(BF)
    chosen, selected, spread = routed
    logits = dot(hidden_two, w_router)
    masked_logits = jnp.where(chosen, logits, masked_score)
    top = jnp.max(masked_logits, -1, keepdims=True)
    powers = jnp.where(chosen, jnp.exp(masked_logits - top), 0.0)
    gate_share = powers / jnp.sum(powers, -1, keepdims=True)
    weighting = jnp.where(selected, dot(gate_share.astype(BF), spread), 0.0).astype(BF)
    return {
        "layer_in": layer_in,
        "factor_one": factor_one,
        "hidden_one": hidden_one,
        "queries": queries,
        "key_all": key_all,
        "value_all": value_all,
        "attn_prob": attn_prob,
        "attn_mix": attn_mix,
        "middle": middle,
        "factor_two": factor_two,
        "hidden_two": hidden_two,
        "gate_share": gate_share,
        "selected": selected,
        "selector": selected.astype(BF),
        "spread": spread,
        "weighting": weighting,
    }


def expert_forward(arrived, w_gate, w_up):
    gate_pre = dot(arrived, w_gate)
    up_pre = dot(arrived, w_up)
    return gate_pre, up_pre, (jax.nn.silu(gate_pre) * up_pre).astype(BF)


def expert_backward(owed, gate_pre, up_pre, w_down):
    grad_inner = dot_t(owed, w_down)
    sigmoid_a = jax.nn.sigmoid(gate_pre)
    grad_gate_pre = grad_inner * up_pre * sigmoid_a * (1.0 + gate_pre * (1.0 - sigmoid_a))
    return grad_gate_pre.astype(BF), (grad_inner * gate_pre * sigmoid_a).astype(BF)


def router_backward(stored, grad_top, returned, w_router):
    match = jnp.where(stored["selected"], dot_t(grad_top, returned), 0.0)
    grad_weighting = lax.dot_general(
        match,
        stored["spread"].astype(F32),
        (((1,), (1,)), ((), ())),
        precision=lax.Precision.HIGHEST,
        preferred_element_type=F32,
    )
    gate_share = stored["gate_share"]
    grad_logits = (
        gate_share * (grad_weighting - jnp.sum(gate_share * grad_weighting, -1, keepdims=True))
    ).astype(BF)
    return t_dot(grad_logits, stored["hidden_two"]), dot_t(grad_logits, w_router)


def attention_backward(stored, grad_top, grad_router, grad_hidden, dense_set, hook):
    attn_gain, w_query, w_key, w_value, w_out, ffn_gain, w_router = dense_set
    local_len = grad_top.shape[0]
    grad_normed_two, grad_ffn_gain = norm_back(
        stored["middle"], stored["factor_two"], ffn_gain, grad_hidden
    )
    grad_middle = grad_top.astype(F32) + grad_normed_two
    grad_branch = hook("branch", grad_middle.astype(BF))
    grad_mix = dot_t(grad_branch, w_out).astype(BF)
    key_all = stored["key_all"]
    value_all = stored["value_all"]
    heads_kv = key_all.shape[1]
    attn_prob = stored["attn_prob"]
    grouped_grad = grad_mix.reshape(local_len, heads_kv, -1, HEAD_SIZE)
    grad_prob = jnp.einsum("tkgd,skd->kgts", grouped_grad, value_all, preferred_element_type=F32)
    centre = jnp.sum(attn_prob * grad_prob, -1, keepdims=True)
    grad_scores = (attn_prob * (grad_prob - centre)).astype(BF)
    grouped_query = stored["queries"].reshape(local_len, heads_kv, -1, HEAD_SIZE)
    grad_keys_all = (
        jnp.einsum("kgts,tkgd->skd", grad_scores, grouped_query, preferred_element_type=F32) * SCALE
    )
    grad_values_all = jnp.einsum(
        "kgts,tkgd->skd", attn_prob.astype(BF), grouped_grad, preferred_element_type=F32
    )
    tree_length = key_all.shape[0]
    grad_kv_all = jnp.concatenate(
        [grad_keys_all.reshape(tree_length, -1), grad_values_all.reshape(tree_length, -1)], 1
    ).astype(BF)
    grad_kv_all = hook("kv_all", grad_kv_all)
    grad_kv = sum_to_owner(grad_kv_all, 0).astype(BF)
    grad_queries = (
        jnp.einsum("kgts,skd->tkgd", grad_scores, key_all, preferred_element_type=F32) * SCALE
    )
    grad_queries = grad_queries.reshape(local_len, -1).astype(BF)
    key_width = w_key.shape[1]
    grad_keys, grad_values = grad_kv[:, :key_width], grad_kv[:, key_width:]
    grad_hidden_one = dot_t(grad_queries, w_query)
    grad_hidden_one = grad_hidden_one + dot_t(grad_keys, w_key)
    grad_hidden_one = grad_hidden_one + dot_t(grad_values, w_value)
    grad_normed_one, grad_attn_gain = norm_back(
        stored["layer_in"], stored["factor_one"], attn_gain, grad_hidden_one
    )
    grad_input = grad_middle + grad_normed_one
    small = jnp.concatenate([grad_router, grad_attn_gain[None], grad_ffn_gain[None]], 0)
    return {
        "input": grad_input,
        "branch": grad_branch,
        "qkv": jnp.concatenate([grad_queries, grad_kv], 1),
        "small": jnp.pad(small, ((0, -small.shape[0] % 16), (0, 0))),
    }


def local(
    edge_in,
    seg_lengths,
    routes,
    turns,
    attn_gain,
    w_query,
    w_key,
    w_value,
    w_out,
    ffn_gain,
    w_router,
    w_gate,
    w_up,
    w_down,
):
    edge_rows = edge_in[0, :, 0]
    local_len = edge_rows.shape[1]
    lengths_all = seg_lengths[:, 0]
    is_first = lax.axis_index("section") == 0

    def both_layers(own, received):
        return (jnp.where(is_first, own, received), jnp.where(is_first, received, own))

    def of_micro(pair):
        mine = jnp.where(is_first, pair[0], pair[1])
        others = jnp.where(is_first, pair[1], pair[0])
        return both_layers(mine, swapped(others))

    layer_rows, cotangent = of_micro(edge_rows)
    dense_own = (attn_gain[0], w_query[0], w_key[0], w_value[0], w_out[0], ffn_gain[0], w_router[0])
    dense_pairs = [both_layers(a, swapped(a)) for a in dense_own]
    dense_sets = [tuple(p[i] for p in dense_pairs) for i in range(2)]
    lengths_row = jnp.where(is_first, lengths_all[0], lengths_all[1])
    visible = tree_mask(lengths_row, local_len)
    experts_all, experts = w_router.shape[2], w_gate.shape[1]
    picks = routes.shape[4]
    capacity = local_len * picks // experts_all
    orders = of_micro(
        jnp.concatenate([jnp.swapaxes(routes[0, :, 0], 1, 2), turns[0, :, 0]], 1)
    )
    routed = [routing(o[:picks].T, o[picks], experts_all, capacity) for o in orders]
    gates, ups, downs = (row_halves(a[0], is_first) for a in (w_gate, w_up, w_down))

    gate_first, up_first = expert_in(gates[0]), expert_in(ups[0])
    first = attention_forward(
        layer_rows.astype(F32), visible, routed[0], dense_sets[0], lambda value: value
    )
    outgoing = t_dot(first["selector"], first["hidden_two"]).astype(BF)
    arrived_first = send_out(outgoing, experts_all)
    down_first = expert_in(downs[0])
    gate_pre, up_pre, inner_first = expert_forward(arrived_first, gate_first, up_first)
    pres_first = (gate_pre, up_pre)
    returned_first = send_back(dot(inner_first, down_first).astype(BF), experts_all)
    early = jnp.concatenate([first["hidden_one"], first["attn_mix"]], 0)
    early, returned_first = tie(early, returned_first)
    kept = {"early": early_operand(early)}

    def end(name, value):
        kept[name], value = tie(kept[name], value)
        return value

    state = (first["middle"] + dot(first["weighting"], returned_first)).astype(BF)

    gate_second, up_second = expert_in(gates[1]), expert_in(ups[1])
    second = attention_forward(
        state.astype(F32), visible, routed[1], dense_sets[1], lambda value: end("early", value)
    )
    outgoing = t_dot(second["selector"], second["hidden_two"]).astype(BF)
    early_first = kept["early"]
    arrived_second = send_out(outgoing, experts_all)
    early = jnp.concatenate([second["hidden_one"], second["attn_mix"]], 0)
    early, arrived_second = tie(early, arrived_second)
    early_second = early_operand(early)
    owed_second = send_out(t_dot(second["weighting"], cotangent).astype(BF), experts_all)
    down_second = expert_in(downs[1])
    gate_pre, up_pre, inner_second = expert_forward(arrived_second, gate_second, up_second)
    grad_gate_pre, grad_up_pre = expert_backward(owed_second, gate_pre, up_pre, down_second)
    grad_arrived = (dot_t(grad_gate_pre, gate_second) + dot_t(grad_up_pre, up_second)).astype(BF)
    early_second, grad_arrived = tie(early_second, grad_arrived)
    returned_second = send_back(dot(inner_second, down_second).astype(BF), experts_all)
    sent_second = send_back(grad_arrived, experts_all)
    top = second["middle"] + dot(second["weighting"], returned_second)
    top_other = lax.ppermute(top, "section", UP)
    expert_grads = [t_dot(arrived_second, g).astype(BF) for g in (grad_gate_pre, grad_up_pre)]
    expert_grads.append(t_dot(inner_second, owed_second).astype(BF))
    sent_second, expert_grads = tie(sent_second, expert_grads)

    kept["gate"] = expert_out(expert_grads[0], experts)
    grad_router, grad_hidden = router_backward(
        second, cotangent, returned_second, dense_sets[1][6]
    )
    grad_hidden = grad_hidden + dot(second["selector"], sent_second)

    def later_hook(name, value):
        return end("gate", value) if name == "kv_all" else value

    later = attention_backward(
        second, cotangent, grad_router, grad_hidden, dense_sets[1], later_hook
    )
    grad = later["input"].astype(BF)
    branch, qkv, grad = tie(later["branch"], later["qkv"], grad)
    late = late_operands([branch, qkv])
    width = late[0].shape[1]
    outgoing = t_dot(first["weighting"], grad).astype(BF)
    owed_first = send_out(outgoing, experts_all)
    late, owed_first, up_grad = tie(late, owed_first, expert_grads[1])
    kept["up"] = expert_out(up_grad, experts)
    hidden_early, mix_early = early_second
    kept["dense"] = dense_rows(dense_partial([mix_early, hidden_early], late))
    grad_gate_pre, grad_up_pre = expert_backward(owed_first, *pres_first, down_first)
    grad_arrived = (dot_t(grad_gate_pre, gate_first) + dot_t(grad_up_pre, up_first)).astype(BF)
    first_grads = [t_dot(arrived_first, g).astype(BF) for g in (grad_gate_pre, grad_up_pre)]
    first_grads.append(t_dot(inner_first, owed_first).astype(BF))
    grad_arrived, first_grads = tie(grad_arrived, first_grads)
    sent_first = send_back(end("dense", end("up", grad_arrived)), experts_all)
    down_grad, sent_first = tie(expert_grads[2], sent_first)
    kept["down"] = expert_out(down_grad, experts)
    kept["dense"], sent_first = tie(kept["dense"], sent_first)
    kept["dense"] = dense_line(kept["dense"])
    grad_router, grad_hidden = router_backward(first, grad, returned_first, dense_sets[0][6])
    grad_hidden = grad_hidden + dot(first["selector"], sent_first)

    def hook(name, value):
        if name == "branch":
            kept["late"] = late_operands([value])
        if name == "kv_all":
            value = end("dense", end("down", end("late", value)))
            kept["dense"] = dense_groups(kept["dense"])
            kept["out"] = dense_partial([early_first[1]], kept["late"])
            return end("out", value)
        return value

    earlier = attention_backward(
        first, grad, grad_router, grad_hidden, dense_sets[0], hook
    )
    out_second = [kept[name] for name in ("gate", "up", "down")]
    ending, gate_grad = tie(earlier["qkv"], first_grads[0])
    gate_part = expert_out(gate_grad, experts)
    out_total = dense_line(dense_rows(kept["out"]))
    qkv_total = dense_partial([early_first[0]], late_operands([ending]))
    smalls = small_total(jnp.concatenate([earlier["small"], later["small"]], 0))
    gate_part, qkv_total, out_total, smalls = tie(gate_part, qkv_total, out_total, smalls)
    out_total = dense_groups(out_total)
    qkv_total = dense_line(dense_rows(qkv_total))
    qkv_total, up_grad, second_total = tie(qkv_total, first_grads[1], kept["dense"])
    up_part = expert_out(up_grad, experts)
    qkv_total = dense_groups(qkv_total)
    gate_total = expert_home(two_homes(gate_part, out_second[0]))
    out = dense_home(two_homes(out_total, second_total[..., :width]), [w_out.shape[2]])[0]
    up_part, down_grad, gate_total, out, qkv_total, smalls = tie(
        up_part, first_grads[2], gate_total, out, qkv_total, smalls
    )
    down_part = expert_out(down_grad, experts)
    up_total = expert_home(two_homes(up_part, out_second[1]))
    query, key, value = dense_home(
        two_homes(qkv_total, second_total[..., width:]),
        [w_query.shape[2], w_key.shape[2], w_value.shape[2]],
    )
    small = jnp.where(is_first, *jnp.split(smalls, 2, 0))
    grad = earlier["input"]
    grad_other = lax.ppermute(grad, "section", DOWN)
    edge_out = jnp.where(
        is_first, jnp.stack([grad, grad_other]), jnp.stack([top_other, top])
    )[None, :, None]
    down_part, up_total, query, key, value, edge_out = tie(
        down_part, up_total, query, key, value, edge_out
    )
    expert_total = [gate_total, up_total, expert_home(two_homes(down_part, out_second[2]))]
    dense_out = (
        small[experts_all],
        query,
        key,
        value,
        out,
        small[experts_all + 1],
        small[:experts_all].T,
    )
    return (
        (edge_out,)
        + tuple((piece[None] for piece in dense_out))
        + tuple((piece[None] for piece in expert_total))
    )


def solution(mesh):
    placed = (
        P("section", None, "expert", "dp", None),
        P(None, "expert", None),
        P("section", None, "expert", "dp", None),
        P("section", None, "expert", "dp", None),
        P("section", None),
        P("section", None, None),
        P("section", None, None),
        P("section", None, None),
        P("section", None, None),
        P("section", None),
        P("section", None, None),
        P("section", "expert", "dp", None),
        P("section", "expert", "dp", None),
        P("section", "expert", "dp", None),
    )
    return jax.shard_map(
        local,
        mesh=mesh,
        in_specs=placed,
        out_specs=(
            P("section", None, "expert", "dp", None),
            P("section", None),
            P("section", None, None),
            P("section", None, None),
            P("section", None, None),
            P("section", None, None),
            P("section", None),
            P("section", None, None),
            P("section", "expert", "dp", None),
            P("section", "expert", "dp", None),
            P("section", "expert", "dp", None),
        ),
        check_vma=False,
    )
```

time: 1860 us -> 1390 us (0.75)
  waiting for transfers between devices: 1050 us -> 791 us
  local copies, waits for them, and re-layouts: 180 us -> 61.7 us
  blocking collectives: 125 us -> 42.6 us
  other arithmetic: 147 us -> 86.4 us
  starting transfers between devices: 133 us -> 184 us
  Pallas kernels: 0 us -> 42.9 us
  matrix products: 195 us -> 163 us
    all_to_all x21 -> x19, waiting for transfers between devices: 859 us -> 383 us  [exchange(): return lax.all_to_all(rows, axes, split_axis=0, concat_axis=0, tiled=True)]
    ppermute x8 -> x60, waiting for transfers between devices: 17.3 us -> 397 us  [the longest x6 130 us: dense_line(): others = lax.ppermute(total, 'dp', partners('dp', flip))]
    reduce_scatter x2 -> x0, waiting for transfers between devices: 166 us -> none  [dense_total(): part = lax.psum_scatter(both, REPLICAS, scatter_dimension=0, tiled=True)]
    concatenate x12 -> x2, local copies, waits for them, and re-layouts: 109 us -> 7.76 us  [in_order(): jnp.concatenate([jnp.where(first, mine, others), jnp.where(first, others,...]
    all_to_all x3 -> x1, blocking collectives: 125 us -> 42.6 us  [exchange(): return lax.all_to_all(rows, axes, split_axis=0, concat_axis=0, tiled=True)]
    ppermute x8 -> x60, starting transfers between devices: 20.8 us -> 77.1 us  [the longest x5 19.8 us: two_homes(): lax.ppermute(first, 'section', DOWN)]
    convert_element_type x15 -> x22, other arithmetic: 60.9 us -> 7.98 us  [the longest x3 2.08 us: dense_rows(): return partial.astype(BF)]
    pallas_call x0 -> x5, Pallas kernels: none -> 42.9 us  [pick_blocks(): pl.pallas_call(body, grid_spec=pltpu.PrefetchScalarGridSpec(num_scalar_pr...]
  transfers between devices with their start and end apart: 48 -> 98, of which waited for: 26 -> 47; matrix products, arithmetic and copies ran while one was open for 19% -> 19% of each run, Pallas kernels for 0% -> 3%
where the time goes in v2:
time: 1390 us; the launch traced here: 1380 us
  waiting for transfers between devices  791 us (57%)
  starting transfers between devices  184 us (13%)
  matrix products  163 us (12%)
  other arithmetic  86.4 us (6%)
  local copies, waits for them, and re-layouts  61.7 us (4%)
  Pallas kernels  42.9 us (3%)
  blocking collectives  42.6 us (3%)
    all_to_all x19, waiting for transfers between devices, exchange(): return lax.all_to_all(rows, axes, split_axis=0, concat_axis=0, tiled=True)  383 us
    ppermute x6, waiting for transfers between devices, dense_line(): others = lax.ppermute(total, 'dp', partners('dp', flip))  130 us
    ppermute x8, waiting for transfers between devices, gathered(): lax.ppermute(shard, over, partners(over, flip))  106 us
    all_to_all x19, starting transfers between devices, exchange(): return lax.all_to_all(rows, axes, split_axis=0, concat_axis=0, tiled=True)  97.3 us
    ppermute x6, waiting for transfers between devices, dense_rows(): sent = lax.ppermute(sent.astype(BF), 'dp', partners('dp', flip))  61.7 us
    dot_general x19, matrix products, dot_t(): lax.dot_general(left, right, (((1,), (1,)), ((), ())), preferred_element_...  57.3 us
    dot_general x24, matrix products, dot(): return jnp.dot(left, right, preferred_element_type=F32)  54.2 us
    pallas_call x5, Pallas kernels, pick_blocks(): pl.pallas_call(body, grid_spec=pltpu.PrefetchScalarGridSpec(num_scalar_pr...  42.9 us
  transfers between devices with their start and end apart: 98, of which 47 were waited for; matrix products, arithmetic and copies ran while one was open for 19% of the time, Pallas kernels for 3%

profile of v2, /device:TPU:1, one launch (start us, length us, event | category | flops | bytes accessed | tf_op | source)
XLA Modules:
  0.0 1375.9 jit_solution(6044246804507607346)
XLA Ops:
  17.6 6.6 all-to-all-start.1
  37.9 45.7 %collective-permute-done.4 = bf16[128,512]{1,0:T(8,128)(2,1)S(1)} collective-permute-done((bf16[128,512]{1,0:T(8,128)(2,1)S(1)}, bf16[128,512]{1,0:T(8,128)(2,1)S(1)}, u32[]{:S(2)}, u32[]{:S(2)}) %collective-permute-start.4) | collective-permute-done | bytes 131104 | tf_op jit(solution)/shard_map/ppermute | solution.py:111
  85.4 5.7 broadcast_select_fusion.8
  111.3 38.1 %all-to-all-done.2 = bf16[8,192,768]{2,1,0:T(8,128)(2,1)} async-done(((bf16[8,192,768]{2,1,0:T(8,128)(2,1)}), bf16[8,192,768]{2,1,0:T(8,128)(2,1)}, u32[]{:S(2)}, u32[]{:S(2)}) %all-to-all-start.2) | async-done | bytes 2359328 | tf_op jit(solution)/shard_map/all_to_all | solution.py:289
  153.5 5.7 broadcast_select_fusion.4
  159.2 32.6 %all-to-all-done = bf16[32,16,1536]{2,1,0:T(8,128)(2,1)S(1)} async-done(((bf16[32,16,1536]{2,1,0:T(8,128)(2,1)}), bf16[32,16,1536]{2,1,0:T(8,128)(2,1)S(1)}, u32[]{:S(2)}, u32[]{:S(2)}) %all-to-all-start) | async-done | bytes 1572896 | tf_op jit(solution)/shard_map/all_to_all | solution.py:289
  191.8 5.6 all-to-all-start.3
  206.1 45.2 %all-to-all-done.3 = bf16[8,96,1536]{2,1,0:T(8,128)(2,1)} async-done(((bf16[8,96,1536]{2,1,0:T(8,128)(2,1)}), bf16[8,96,1536]{2,1,0:T(8,128)(2,1)}, u32[]{:S(2)}, u32[]{:S(2)}) %all-to-all-start.3) | async-done | bytes 2359328 | tf_op jit(solution)/shard_map/all_to_all | solution.py:289
  264.5 33.0 %all-to-all-done.4 = bf16[32,16,1536]{2,1,0:T(8,128)(2,1)S(1)} async-done(((bf16[32,16,1536]{2,1,0:T(8,128)(2,1)}), bf16[32,16,1536]{2,1,0:T(8,128)(2,1)S(1)}, u32[]{:S(2)}, u32[]{:S(2)}) %all-to-all-start.4) | async-done | bytes 1572896 | tf_op jit(solution)/shard_map/all_to_all | solution.py:289
  307.8 18.3 %collective-permute-done.15 = bf16[2,1,2,128,768]{4,3,2,1,0:T(8,128)(2,1)S(1)} collective-permute-done((bf16[2,1,2,128,768]{4,3,2,1,0:T(8,128)(2,1)S(1)}, bf16[2,1,2,128,768]{4,3,2,1,0:T(8,128)(2,1)S(1)}, u32[]{:S(2)}, u32[]{:S(2)}) %collective-permute-start.15) | collective-permute-done | bytes 786464 | tf_op jit(solution)/shard_map/ppermute | solution.py:111
  330.1 32.0 %collective-permute-done.17 = bf16[128,512]{1,0:T(8,128)(2,1)S(1)} collective-permute-done((bf16[128,512]{1,0:T(8,128)(2,1)S(1)}, bf16[128,512]{1,0:T(8,128)(2,1)S(1)}, u32[]{:S(2)}, u32[]{:S(2)}) %collective-permute-start.17) | collective-permute-done | bytes 131104 | tf_op jit(solution)/shard_map/ppermute | solution.py:111
  364.3 7.6 all-to-all-start.6
  390.0 35.9 %all-to-all-done.6 = bf16[8,192,768]{2,1,0:T(8,128)(2,1)} async-done(((bf16[8,192,768]{2,1,0:T(8,128)(2,1)}), bf16[8,192,768]{2,1,0:T(8,128)(2,1)}, u32[]{:S(2)}, u32[]{:S(2)}) %all-to-all-start.6) | async-done | bytes 2359328 | tf_op jit(solution)/shard_map/all_to_all | solution.py:289
  432.5 35.7 %all-to-all-done.10 = bf16[32,16,1536]{2,1,0:T(8,128)(2,1)} async-done(((bf16[32,16,1536]{2,1,0:T(8,128)(2,1)}), bf16[32,16,1536]{2,1,0:T(8,128)(2,1)}, u32[]{:S(2)}, u32[]{:S(2)}) %all-to-all-start.10) | async-done | bytes 1572896 | tf_op jit(solution)/shard_map/all_to_all | solution.py:289
  468.1 42.6 %all_to_all.100 = bf16[32,16,1536]{2,1,0:T(8,128)(2,1)} all-to-all(bf16[32,16,1536]{2,1,0:T(8,128)(2,1)} %bitcast.482), channel_id=1, replica_groups=mesh['section'=2,'dp'=4,'expert'=4] {'expert','dp','section'}, dimensions={0} | all-to-all | bytes 3145728 | tf_op jit(solution)/shard_map/all_to_all | solution.py:289
  530.0 9.8 collective-permute-done.20
  541.4 28.2 %all-to-all-done.7 = bf16[8,192,768]{2,1,0:T(8,128)(2,1)} async-done(((bf16[8,192,768]{2,1,0:T(8,128)(2,1)}), bf16[8,192,768]{2,1,0:T(8,128)(2,1)}, u32[]{:S(2)}, u32[]{:S(2)}) %all-to-all-start.7) | async-done | bytes 2359328 | tf_op jit(solution)/shard_map/all_to_all | solution.py:289
  569.6 5.7 multiply_convert_fusion.4
  595.0 34.0 %all-to-all-done.11 = bf16[32,16,1536]{2,1,0:T(8,128)(2,1)} async-done(((bf16[32,16,1536]{2,1,0:T(8,128)(2,1)}), bf16[32,16,1536]{2,1,0:T(8,128)(2,1)}, u32[]{:S(2)}, u32[]{:S(2)}) %all-to-all-start.11) | async-done | bytes 1572896 | tf_op jit(solution)/shard_map/all_to_all | solution.py:289
  643.3 28.0 %all-to-all-done.9 = bf16[32,16,1536]{2,1,0:T(8,128)(2,1)} async-done(((bf16[32,16,1536]{2,1,0:T(8,128)(2,1)}), bf16[32,16,1536]{2,1,0:T(8,128)(2,1)}, u32[]{:S(2)}, u32[]{:S(2)}) %all-to-all-start.9) | async-done | bytes 1572896 | tf_op jit(solution)/shard_map/all_to_all | solution.py:289
  700.9 29.7 %all-to-all-done.12.refs_1_ = bf16[8,192,768]{2,1,0:T(8,128)(2,1)} async-done(((bf16[8,192,768]{2,1,0:T(8,128)(2,1)}), bf16[8,192,768]{2,1,0:T(8,128)(2,1)}, u32[]{:S(2)}, u32[]{:S(2)}) %all-to-all-start.12) | async-done | bytes 2359328 | tf_op jit(solution)/shard_map/all_to_all | solution.py:289
  730.7 6.9 collective-permute-done.22
  740.9 6.6 collective-permute-done.23
  757.3 5.7 all-to-all-start.13
  766.1 15.1 %collective-permute-done.24 = bf16[128,896]{1,0:T(8,128)(2,1)S(1)} collective-permute-done((bf16[128,896]{1,0:T(8,128)(2,1)S(1)}, bf16[128,896]{1,0:T(8,128)(2,1)S(1)}, u32[]{:S(2)}, u32[]{:S(2)}) %collective-permute-start.24) | collective-permute-done | bytes 229408 | tf_op jit(solution)/shard_map/ppermute | solution.py:238
  781.2 9.8 collective-permute-done.26
  795.6 5.8 all-to-all-done.13
  826.7 35.7 %collective-permute-done.28 = bf16[384,896]{0,1:T(8,128)(2,1)S(1)} collective-permute-done((bf16[384,896]{0,1:T(8,128)(2,1)S(1)}, bf16[384,896]{0,1:T(8,128)(2,1)S(1)}, u32[]{:S(2)}, u32[]{:S(2)}) %collective-permute-start.28) | collective-permute-done | bytes 688160 | tf_op jit(solution)/shard_map/ppermute | solution.py:254
  870.6 15.2 %collective-permute-done.29 = bf16[192,896]{0,1:T(8,128)(2,1)S(1)} collective-permute-done((bf16[192,896]{0,1:T(8,128)(2,1)S(1)}, bf16[192,896]{0,1:T(8,128)(2,1)S(1)}, u32[]{:S(2)}, u32[]{:S(2)}) %collective-permute-start.29) | collective-permute-done | bytes 344096 | tf_op jit(solution)/shard_map/ppermute | solution.py:254
  897.4 31.6 %all-to-all-done.15 = bf16[32,16,1536]{2,1,0:T(8,128)(2,1)} async-done(((bf16[32,16,1536]{2,1,0:T(8,128)(2,1)}), bf16[32,16,1536]{2,1,0:T(8,128)(2,1)}, u32[]{:S(2)}, u32[]{:S(2)}) %all-to-all-start.15) | async-done | bytes 1572896 | tf_op jit(solution)/shard_map/all_to_all | solution.py:289
  938.5 6.3 convolution_convert_fusion.12
  957.9 52.9 %collective-permute-done.34 = bf16[192,896]{0,1:T(8,128)(2,1)S(1)} collective-permute-done((bf16[192,896]{0,1:T(8,128)(2,1)}, bf16[192,896]{0,1:T(8,128)(2,1)S(1)}, u32[]{:S(2)}, u32[]{:S(2)}) %collective-permute-start.34) | collective-permute-done | bytes 344096 | tf_op jit(solution)/shard_map/ppermute | solution.py:262
  1018.6 9.8 collective-permute-done.35
  1039.2 5.8 collective-permute-done.42
  1048.5 7.2 fusion.51
  1079.1 50.5 %collective-permute-done.44 = bf16[192,384]{1,0:T(8,128)(2,1)S(1)} collective-permute-done((bf16[192,384]{1,0:T(8,128)(2,1)S(1)}, bf16[192,384]{1,0:T(8,128)(2,1)S(1)}, u32[]{:S(2)}, u32[]{:S(2)}) %collective-permute-start.44) | collective-permute-done | bytes 147488 | tf_op jit(solution)/shard_map/ppermute | solution.py:262
  1147.9 11.0 collective-permute-done.50
  1159.7 7.4 collective-permute-done.56
  1198.5 9.8 collective-permute-done.53
  1212.2 6.5 collective-permute-done.54
  1245.0 15.9 %collective-permute-done.68 = bf16[1,2,384,512]{3,2,1,0:T(8,128)(2,1)S(1)} collective-permute-done((bf16[1,2,384,512]{3,2,1,0:T(8,128)(2,1)S(1)}, bf16[1,2,384,512]{3,2,1,0:T(8,128)(2,1)S(1)}, u32[]{:S(2)}, u32[]{:S(2)}) %collective-permute-start.68) | collective-permute-done | bytes 786464 | tf_op jit(solution)/shard_map/ppermute | solution.py:274
  1262.1 14.6 %collective-permute-done.70 = bf16[2,1,384,512]{3,2,1,0:T(8,128)(2,1)S(1)} collective-permute-done((bf16[2,1,384,512]{3,2,1,0:T(8,128)(2,1)S(1)}, bf16[2,1,384,512]{3,2,1,0:T(8,128)(2,1)S(1)}, u32[]{:S(2)}, u32[]{:S(2)}) %collective-permute-start.70) | collective-permute-done | bytes 786464 | tf_op jit(solution)/shard_map/ppermute | solution.py:274
  1278.6 8.4 shard_map.239
  1287.1 8.1 shard_map.240
  1295.2 9.5 all-to-all-start.19
  1333.4 7.8 shard_map.241
  1343.0 10.1 shard_map.242
  1367.0 8.4 shard_map.243
  (799 shorter events, 463.4 us)
Async XLA Ops:
  5.0 24.0 %collective-permute-start = (bf16[128,1536]{1,0:T(8,128)(2,1)S(1)}, bf16[128,1536]{1,0:T(8,128)(2,1)S(1)}, u32[]{:S(2)}, u32[]{:S(2)}) collective-permute-start(bf16[128,1536]{1,0:T(8,128)(2,1)S(1)} %select_bitcast_fusion), channel_id=1, source_target_pairs={{0,16},{16,0},{1,17},{17,1},{2,18},{18,2},{3,19},{19,3},{4,20},{20... | collective-permute-start | bytes 1179656 | tf_op jit(solution)/shard_map/ppermute | solution.py:88
  6.1 90.6 %collective-permute-start.6 = (bf16[1536,1536]{1,0:T(8,128)(2,1)}, bf16[1536,1536]{1,0:T(8,128)(2,1)}, u32[]{:S(2)}, u32[]{:S(2)}) collective-permute-start(bf16[1536,1536]{1,0:T(8,128)(2,1)} %bitcast.484), channel_id=1, source_target_pairs={{0,16},{16,0},{1,17},{17,1},{2,18},{18,2},{3,19},{19,3},{4,20},{20... | collective-permute-start | bytes 14155784 | tf_op jit(solution)/shard_map/ppermute | solution.py:88
  17.6 73.5 %all-to-all-start.1 = ((bf16[8,192,768]{2,1,0:T(8,128)(2,1)}), bf16[8,192,768]{2,1,0:T(8,128)(2,1)}, u32[]{:S(2)}, u32[]{:S(2)}) async-start(bf16[8,192,768]{2,1,0:T(8,128)(2,1)} %get-tuple-element.158), calls=%async_computation.1 | async-start | bytes 4718592 | tf_op jit(solution)/shard_map/all_to_all | solution.py:289
  26.6 58.6 %collective-permute-start.12 = (bf16[8,192,768]{2,1,0:T(8,128)(2,1)}, bf16[8,192,768]{2,1,0:T(8,128)(2,1)}, u32[]{:S(2)}, u32[]{:S(2)}) collective-permute-start(bf16[8,192,768]{2,1,0:T(8,128)(2,1)} %broadcast_select_fusion.11), channel_id=1, source_target_pairs={{0,16},{16,0},{1,17},{17,1},{2,18},{18,2},{3,19},{19,3},{4,20},{20... | collective-permute-start | bytes 7077896 | tf_op jit(solution)/shard_map/ppermute | solution.py:88
  29.0 75.2 %collective-permute-start.8 = (bf16[1536,1536]{1,0:T(8,128)(2,1)}, bf16[1536,1536]{1,0:T(8,128)(2,1)}, u32[]{:S(2)}, u32[]{:S(2)}) collective-permute-start(bf16[1536,1536]{1,0:T(8,128)(2,1)} %bitcast.469), channel_id=1, source_target_pairs={{0,16},{16,0},{1,17},{17,1},{2,18},{18,2},{3,19},{19,3},{4,20},{20... | collective-permute-start | bytes 14155784 | tf_op jit(solution)/shard_map/ppermute | solution.py:88
  30.0 65.6 %collective-permute-start.9 = (f32[1536]{0:T(1024)}, f32[1536]{0:T(1024)}, u32[]{:S(2)}, u32[]{:S(2)}) collective-permute-start(f32[1536]{0:T(1024)} %reduce.1), channel_id=1, source_target_pairs={{0,16},{16,0},{1,17},{17,1},{2,18},{18,2},{3,19},{19,3},{4,20},{20... | collective-permute-start | bytes 18440 | tf_op jit(solution)/shard_map/ppermute | solution.py:88
  34.3 49.2 %collective-permute-start.4 = (bf16[128,512]{1,0:T(8,128)(2,1)S(1)}, bf16[128,512]{1,0:T(8,128)(2,1)S(1)}, u32[]{:S(2)}, u32[]{:S(2)}) collective-permute-start(bf16[128,512]{1,0:T(8,128)(2,1)S(1)} %pad_maximum_fusion.45), channel_id=1, source_target_pairs={{0,8},{4,12},{8,0},{12,4},{1,9},{5,13},{9,1},{13,5},{2,10},{6,14},... | collective-permute-start | bytes 393224 | tf_op jit(solution)/shard_map/ppermute | solution.py:111
  83.5 70.0 %collective-permute-start.13 = (bf16[8,96,1536]{2,1,0:T(8,128)(2,1)}, bf16[8,96,1536]{2,1,0:T(8,128)(2,1)}, u32[]{:S(2)}, u32[]{:S(2)}) collective-permute-start(bf16[8,96,1536]{2,1,0:T(8,128)(2,1)} %broadcast_select_fusion.6), channel_id=1, source_target_pairs={{0,16},{16,0},{1,17},{17,1},{2,18},{18,2},{3,19},{19,3},{4,20},{20... | collective-permute-start | bytes 7077896 | tf_op jit(solution)/shard_map/ppermute | solution.py:88
  91.1 58.3 %all-to-all-start.2 = ((bf16[8,192,768]{2,1,0:T(8,128)(2,1)}), bf16[8,192,768]{2,1,0:T(8,128)(2,1)}, u32[]{:S(2)}, u32[]{:S(2)}) async-start(bf16[8,192,768]{2,1,0:T(8,128)(2,1)} %get-tuple-element.156), calls=%async_computation.2 | async-start | bytes 4718592 | tf_op jit(solution)/shard_map/all_to_all | solution.py:289
  149.4 42.4 %all-to-all-start = ((bf16[32,16,1536]{2,1,0:T(8,128)(2,1)}), bf16[32,16,1536]{2,1,0:T(8,128)(2,1)S(1)}, u32[]{:S(2)}, u32[]{:S(2)}) async-start(bf16[32,16,1536]{2,1,0:T(8,128)(2,1)} %bitcast.28), calls=%async_computation | async-start | bytes 3145728 | tf_op jit(solution)/shard_map/all_to_all | solution.py:289
  191.8 59.5 %all-to-all-start.3 = ((bf16[8,96,1536]{2,1,0:T(8,128)(2,1)}), bf16[8,96,1536]{2,1,0:T(8,128)(2,1)}, u32[]{:S(2)}, u32[]{:S(2)}) async-start(bf16[8,96,1536]{2,1,0:T(8,128)(2,1)} %get-tuple-element.160), calls=%async_computation.3 | async-start | bytes 4718592 | tf_op jit(solution)/shard_map/all_to_all | solution.py:289
  255.8 41.7 %all-to-all-start.4 = ((bf16[32,16,1536]{2,1,0:T(8,128)(2,1)}), bf16[32,16,1536]{2,1,0:T(8,128)(2,1)S(1)}, u32[]{:S(2)}, u32[]{:S(2)}) async-start(bf16[32,16,1536]{2,1,0:T(8,128)(2,1)} %bitcast.532), calls=%async_computation.4 | async-start | bytes 3145728 | tf_op jit(solution)/shard_map/all_to_all | solution.py:289
  259.1 43.5 %collective-permute-start.10 = (bf16[1536,32]{0,1:T(8,128)(2,1)}, bf16[1536,32]{0,1:T(8,128)(2,1)}, u32[]{:S(2)}, u32[]{:S(2)}) collective-permute-start(bf16[1536,32]{0,1:T(8,128)(2,1)} %bitcast.539), channel_id=1, source_target_pairs={{0,16},{16,0},{1,17},{17,1},{2,18},{18,2},{3,19},{19,3},{4,20},{20... | collective-permute-start | bytes 294920 | tf_op jit(solution)/shard_map/ppermute | solution.py:88
  297.5 66.8 %all-to-all-start.8 = ((bf16[8,96,1536]{2,1,0:T(8,128)(2,1)}), bf16[8,96,1536]{2,1,0:T(8,128)(2,1)}, u32[]{:S(2)}, u32[]{:S(2)}) async-start(bf16[8,96,1536]{2,1,0:T(8,128)(2,1)} %get-tuple-element.159), calls=%async_computation.8 | async-start | bytes 4718592 | tf_op jit(solution)/shard_map/all_to_all | solution.py:289
  327.4 44.5 %collective-permute-start.16 = (bf16[2,2,2,128,768]{4,3,2,1,0:T(8,128)(2,1)}, bf16[2,2,2,128,768]{4,3,2,1,0:T(8,128)(2,1)}, u32[]{:S(2)}, u32[]{:S(2)}) collective-permute-start(bf16[2,2,2,128,768]{4,3,2,1,0:T(8,128)(2,1)} %pad_maximum_fusion.8), channel_id=1, source_target_pairs={{0,1},{1,0},{2,3},{3,2},{4,5},{5,4},{6,7},{7,6},{8,9},{9,8},{10,11... | collective-permute-start | bytes 4718600 | tf_op jit(solution)/shard_map/ppermute | solution.py:111
  328.0 34.1 %collective-permute-start.17 = (bf16[128,512]{1,0:T(8,128)(2,1)S(1)}, bf16[128,512]{1,0:T(8,128)(2,1)S(1)}, u32[]{:S(2)}, u32[]{:S(2)}) collective-permute-start(bf16[128,512]{1,0:T(8,128)(2,1)S(1)} %pad_maximum_fusion.46), channel_id=1, source_target_pairs={{0,8},{4,12},{8,0},{12,4},{1,9},{5,13},{9,1},{13,5},{2,10},{6,14},... | collective-permute-start | bytes 393224 | tf_op jit(solution)/shard_map/ppermute | solution.py:111
  364.3 61.5 %all-to-all-start.6 = ((bf16[8,192,768]{2,1,0:T(8,128)(2,1)}), bf16[8,192,768]{2,1,0:T(8,128)(2,1)}, u32[]{:S(2)}, u32[]{:S(2)}) async-start(bf16[8,192,768]{2,1,0:T(8,128)(2,1)} %get-tuple-element.157), calls=%async_computation.6 | async-start | bytes 4718592 | tf_op jit(solution)/shard_map/all_to_all | solution.py:289
  425.8 42.3 %all-to-all-start.10 = ((bf16[32,16,1536]{2,1,0:T(8,128)(2,1)}), bf16[32,16,1536]{2,1,0:T(8,128)(2,1)}, u32[]{:S(2)}, u32[]{:S(2)}) async-start(bf16[32,16,1536]{2,1,0:T(8,128)(2,1)} %bitcast.480), calls=%async_computation.10 | async-start | bytes 3145728 | tf_op jit(solution)/shard_map/all_to_all | solution.py:289
  510.7 58.9 %all-to-all-start.7 = ((bf16[8,192,768]{2,1,0:T(8,128)(2,1)}), bf16[8,192,768]{2,1,0:T(8,128)(2,1)}, u32[]{:S(2)}, u32[]{:S(2)}) async-start(bf16[8,192,768]{2,1,0:T(8,128)(2,1)} %get-tuple-element.155), calls=%async_computation.7 | async-start | bytes 4718592 | tf_op jit(solution)/shard_map/all_to_all | solution.py:289
  541.3 42.1 %collective-permute-start.21 = (bf16[2,2,2,128,768]{4,3,2,1,0:T(8,128)(2,1)}, bf16[2,2,2,128,768]{4,3,2,1,0:T(8,128)(2,1)}, u32[]{:S(2)}, u32[]{:S(2)}) collective-permute-start(bf16[2,2,2,128,768]{4,3,2,1,0:T(8,128)(2,1)} %pad_maximum_fusion.9), channel_id=1, source_target_pairs={{0,1},{1,0},{2,3},{3,2},{4,5},{5,4},{6,7},{7,6},{8,9},{9,8},{10,11... | collective-permute-start | bytes 4718600 | tf_op jit(solution)/shard_map/ppermute | solution.py:111
  586.8 42.3 %all-to-all-start.11 = ((bf16[32,16,1536]{2,1,0:T(8,128)(2,1)}), bf16[32,16,1536]{2,1,0:T(8,128)(2,1)}, u32[]{:S(2)}, u32[]{:S(2)}) async-start(bf16[32,16,1536]{2,1,0:T(8,128)(2,1)} %bitcast.534), calls=%async_computation.11 | async-start | bytes 3145728 | tf_op jit(solution)/shard_map/all_to_all | solution.py:289
  629.1 42.3 %all-to-all-start.9 = ((bf16[32,16,1536]{2,1,0:T(8,128)(2,1)}), bf16[32,16,1536]{2,1,0:T(8,128)(2,1)}, u32[]{:S(2)}, u32[]{:S(2)}) async-start(bf16[32,16,1536]{2,1,0:T(8,128)(2,1)} %bitcast.533), calls=%async_computation.9 | async-start | bytes 3145728 | tf_op jit(solution)/shard_map/all_to_all | solution.py:289
  671.3 59.3 %all-to-all-start.12 = ((bf16[8,192,768]{2,1,0:T(8,128)(2,1)}), bf16[8,192,768]{2,1,0:T(8,128)(2,1)}, u32[]{:S(2)}, u32[]{:S(2)}) async-start(bf16[8,192,768]{2,1,0:T(8,128)(2,1)} %bitcast.516), calls=%async_computation.12 | async-start | bytes 4718592 | tf_op jit(solution)/shard_map/all_to_all | solution.py:289
  757.3 44.1 %all-to-all-start.13 = ((bf16[32,16,1536]{2,1,0:T(8,128)(2,1)}), bf16[32,16,1536]{2,1,0:T(8,128)(2,1)S(1)}, u32[]{:S(2)}, u32[]{:S(2)}) async-start(bf16[32,16,1536]{2,1,0:T(8,128)(2,1)} %bitcast.92), calls=%async_computation.13 | async-start | bytes 3145728 | tf_op jit(solution)/shard_map/all_to_all | solution.py:289
  766.0 25.0 %collective-permute-start.26 = (bf16[128,896]{1,0:T(8,128)(2,1)S(1)}, bf16[128,896]{1,0:T(8,128)(2,1)S(1)}, u32[]{:S(2)}, u32[]{:S(2)}) collective-permute-start(bf16[128,896]{1,0:T(8,128)(2,1)S(1)} %pad_maximum_fusion.44), channel_id=1, source_target_pairs={{0,3},{1,2},{2,1},{3,0},{4,7},{5,6},{6,5},{7,4},{8,11},{9,10},{10,... | collective-permute-start | bytes 688136 | tf_op jit(solution)/shard_map/ppermute | solution.py:238
  802.6 84.4 %all-to-all-start.14 = ((bf16[8,192,768]{2,1,0:T(8,128)(2,1)}), bf16[8,192,768]{2,1,0:T(8,128)(2,1)S(1)}, u32[]{:S(2)}, u32[]{:S(2)}) async-start(bf16[8,192,768]{2,1,0:T(8,128)(2,1)} %bitcast.515), calls=%async_computation.14 | async-start | bytes 4718592 | tf_op jit(solution)/shard_map/all_to_all | solution.py:289
  811.2 51.2 %collective-permute-start.28 = (bf16[384,896]{0,1:T(8,128)(2,1)S(1)}, bf16[384,896]{0,1:T(8,128)(2,1)S(1)}, u32[]{:S(2)}, u32[]{:S(2)}) collective-permute-start(bf16[384,896]{0,1:T(8,128)(2,1)S(1)} %fusion.27), channel_id=1, source_target_pairs={{0,4},{4,0},{8,12},{12,8},{1,5},{5,1},{9,13},{13,9},{2,6},{6,2},{1... | collective-permute-start | bytes 2064392 | tf_op jit(solution)/shard_map/ppermute | solution.py:254
  887.0 42.1 %all-to-all-start.15 = ((bf16[32,16,1536]{2,1,0:T(8,128)(2,1)}), bf16[32,16,1536]{2,1,0:T(8,128)(2,1)}, u32[]{:S(2)}, u32[]{:S(2)}) async-start(bf16[32,16,1536]{2,1,0:T(8,128)(2,1)} %bitcast.531), calls=%async_computation.15 | async-start | bytes 3145728 | tf_op jit(solution)/shard_map/all_to_all | solution.py:289
  932.9 97.1 %all-to-all-start.16 = ((bf16[8,96,1536]{2,1,0:T(8,128)(2,1)}), bf16[8,96,1536]{2,1,0:T(8,128)(2,1)}, u32[]{:S(2)}, u32[]{:S(2)}) async-start(bf16[8,96,1536]{2,1,0:T(8,128)(2,1)} %bitcast.513), calls=%async_computation.16 | async-start | bytes 4718592 | tf_op jit(solution)/shard_map/all_to_all | solution.py:289
  950.6 60.2 %collective-permute-start.34 = (bf16[192,896]{0,1:T(8,128)(2,1)}, bf16[192,896]{0,1:T(8,128)(2,1)S(1)}, u32[]{:S(2)}, u32[]{:S(2)}) collective-permute-start(bf16[192,896]{0,1:T(8,128)(2,1)} %add_convert_fusion), channel_id=1, source_target_pairs={{0,8},{4,12},{8,0},{12,4},{1,9},{5,13},{9,1},{13,5},{2,10},{6,14},... | collective-permute-start | bytes 1032200 | tf_op jit(solution)/shard_map/ppermute | solution.py:262
  957.7 57.3 %collective-permute-start.33 = (bf16[4,128,384]{2,1,0:T(8,128)(2,1)S(1)}, bf16[4,128,384]{2,1,0:T(8,128)(2,1)}, u32[]{:S(2)}, u32[]{:S(2)}) collective-permute-start(bf16[4,128,384]{2,1,0:T(8,128)(2,1)S(1)} %get-tuple-element.233), channel_id=1, source_target_pairs={{0,16},{16,0},{1,17},{17,1},{2,18},{18,2},{3,19},{19,3},{4,20},{20... | collective-permute-start | bytes 1179656 | tf_op jit(solution)/shard_map/ppermute | solution.py:88
  1035.0 95.2 %collective-permute-start.55 = (bf16[1,1,384,896]{2,3,1,0:T(8,128)(2,1)}, bf16[1,1,384,896]{2,3,1,0:T(8,128)(2,1)}, u32[]{:S(2)}, u32[]{:S(2)}) collective-permute-start(bf16[1,1,384,896]{2,3,1,0:T(8,128)(2,1)} %get-tuple-element.180), channel_id=1, source_target_pairs={{0,1},{1,0},{2,3},{3,2},{4,5},{5,4},{6,7},{7,6},{8,9},{9,8},{10,11... | collective-permute-start | bytes 2064392 | tf_op jit(solution)/shard_map/ppermute | solution.py:274
  1064.3 108.3 %all-to-all-start.17 = ((bf16[8,192,768]{2,1,0:T(8,128)(2,1)}), bf16[8,192,768]{2,1,0:T(8,128)(2,1)}, u32[]{:S(2)}, u32[]{:S(2)}) async-start(bf16[8,192,768]{2,1,0:T(8,128)(2,1)} %bitcast.514), calls=%async_computation.17 | async-start | bytes 4718592 | tf_op jit(solution)/shard_map/all_to_all | solution.py:289
  1071.1 59.1 %collective-permute-start.57 = (bf16[1,1,384,896]{2,3,1,0:T(8,128)(2,1)}, bf16[1,1,384,896]{2,3,1,0:T(8,128)(2,1)S(1)}, u32[]{:S(2)}, u32[]{:S(2)}) collective-permute-start(bf16[1,1,384,896]{2,3,1,0:T(8,128)(2,1)} %get-tuple-element.181), channel_id=1, source_target_pairs={{0,2},{1,3},{2,0},{3,1},{4,6},{5,7},{6,4},{7,5},{8,10},{9,11},{10,... | collective-permute-start | bytes 2064392 | tf_op jit(solution)/shard_map/ppermute | solution.py:274
  1072.9 56.7 %collective-permute-start.44 = (bf16[192,384]{1,0:T(8,128)(2,1)S(1)}, bf16[192,384]{1,0:T(8,128)(2,1)S(1)}, u32[]{:S(2)}, u32[]{:S(2)}) collective-permute-start(bf16[192,384]{1,0:T(8,128)(2,1)S(1)} %add_convert_fusion.3), channel_id=1, source_target_pairs={{0,8},{4,12},{8,0},{12,4},{1,9},{5,13},{9,1},{13,5},{2,10},{6,14},... | collective-permute-start | bytes 442376 | tf_op jit(solution)/shard_map/ppermute | solution.py:262
  1076.9 63.1 %collective-permute-start.41 = (bf16[4,128,512]{2,1,0:T(8,128)(2,1)S(1)}, bf16[4,128,512]{2,1,0:T(8,128)(2,1)S(1)}, u32[]{:S(2)}, u32[]{:S(2)}) collective-permute-start(bf16[4,128,512]{2,1,0:T(8,128)(2,1)S(1)} %get-tuple-element.217), channel_id=1, source_target_pairs={{0,16},{16,0},{1,17},{17,1},{2,18},{18,2},{3,19},{19,3},{4,20},{20... | collective-permute-start | bytes 1572872 | tf_op jit(solution)/shard_map/ppermute | solution.py:88
  1077.9 51.9 %collective-permute-start.47 = (bf16[96,1536]{1,0:T(8,128)(2,1)S(1)}, bf16[96,1536]{1,0:T(8,128)(2,1)S(1)}, u32[]{:S(2)}, u32[]{:S(2)}) collective-permute-start(bf16[96,1536]{1,0:T(8,128)(2,1)S(1)} %fusion.104), channel_id=1, source_target_pairs={{0,1},{1,0},{2,3},{3,2},{4,5},{5,4},{6,7},{7,6},{8,9},{9,8},{10,11... | collective-permute-start | bytes 884744 | tf_op jit(solution)/shard_map/ppermute | solution.py:283
  1131.8 35.3 %collective-permute-start.56 = (bf16[1,2,384,896]{2,3,1,0:T(8,128)(2,1)S(1)}, bf16[1,2,384,896]{2,3,1,0:T(8,128)(2,1)S(1)}, u32[]{:S(2)}, u32[]{:S(2)}) collective-permute-start(bf16[1,2,384,896]{2,3,1,0:T(8,128)(2,1)S(1)} %pad_maximum_fusion.13), channel_id=1, source_target_pairs={{0,2},{1,3},{2,0},{3,1},{4,6},{5,7},{6,4},{7,5},{8,10},{9,11},{10,... | collective-permute-start | bytes 4128776 | tf_op jit(solution)/shard_map/ppermute | solution.py:274
  1134.3 41.4 %collective-permute-start.58 = (bf16[2,1,384,896]{2,3,1,0:T(8,128)(2,1)}, bf16[2,1,384,896]{2,3,1,0:T(8,128)(2,1)}, u32[]{:S(2)}, u32[]{:S(2)}) collective-permute-start(bf16[2,1,384,896]{2,3,1,0:T(8,128)(2,1)} %pad_maximum_fusion.14), channel_id=1, source_target_pairs={{0,1},{1,0},{2,3},{3,2},{4,5},{5,4},{6,7},{7,6},{8,9},{9,8},{10,11... | collective-permute-start | bytes 4128776 | tf_op jit(solution)/shard_map/ppermute | solution.py:274
  1218.9 76.2 %all-to-all-start.18 = ((bf16[8,192,768]{2,1,0:T(8,128)(2,1)}), bf16[8,192,768]{2,1,0:T(8,128)(2,1)}, u32[]{:S(2)}, u32[]{:S(2)}) async-start(bf16[8,192,768]{2,1,0:T(8,128)(2,1)} %bitcast.512), calls=%async_computation.18 | async-start | bytes 4718592 | tf_op jit(solution)/shard_map/all_to_all | solution.py:289
  1224.4 52.8 %collective-permute-start.60 = (bf16[8,192,768]{2,1,0:T(8,128)(2,1)}, bf16[8,192,768]{2,1,0:T(8,128)(2,1)S(1)}, u32[]{:S(2)}, u32[]{:S(2)}) collective-permute-start(bf16[8,192,768]{2,1,0:T(8,128)(2,1)} %all-to-all-done.12.refs_1_), channel_id=1, source_target_pairs={{0,16},{1,17},{2,18},{3,19},{4,20},{5,21},{6,22},{7,23},{8,24},{9,... | collective-permute-start | bytes 7077896 | tf_op jit(solution)/shard_map/ppermute | solution.py:157
  1225.7 51.5 %collective-permute-start.59 = (bf16[8,192,768]{2,1,0:T(8,128)(2,1)}, bf16[8,192,768]{2,1,0:T(8,128)(2,1)}, u32[]{:S(2)}, u32[]{:S(2)}) collective-permute-start(bf16[8,192,768]{2,1,0:T(8,128)(2,1)} %all-to-all-done.17.refs_0_), channel_id=1, source_target_pairs={{16,0},{17,1},{18,2},{19,3},{20,4},{21,5},{22,6},{23,7},{24,8},{25... | collective-permute-start | bytes 7077896 | tf_op jit(solution)/shard_map/ppermute | solution.py:156
  1235.2 51.8 %collective-permute-start.65 = (bf16[2,4,384,384]{3,2,1,0:T(8,128)(2,1)S(1)}, bf16[2,4,384,384]{3,2,1,0:T(8,128)(2,1)}, u32[]{:S(2)}, u32[]{:S(2)}) collective-permute-start(bf16[2,4,384,384]{3,2,1,0:T(8,128)(2,1)S(1)} %pad_maximum_fusion.6.refs_0_), channel_id=1, source_target_pairs={{16,0},{17,1},{18,2},{19,3},{20,4},{21,5},{22,6},{23,7},{24,8},{25... | collective-permute-start | bytes 7077896 | tf_op jit(solution)/shard_map/ppermute | solution.py:156
  1242.5 44.5 %collective-permute-start.66 = (bf16[2,4,384,384]{3,2,1,0:T(8,128)(2,1)S(1)}, bf16[2,4,384,384]{3,2,1,0:T(8,128)(2,1)}, u32[]{:S(2)}, u32[]{:S(2)}) collective-permute-start(bf16[2,4,384,384]{3,2,1,0:T(8,128)(2,1)S(1)} %slice.127.refs_1_), channel_id=1, source_target_pairs={{0,16},{1,17},{2,18},{3,19},{4,20},{5,21},{6,22},{7,23},{8,24},{9,... | collective-permute-start | bytes 7077896 | tf_op jit(solution)/shard_map/ppermute | solution.py:157
  1295.2 63.4 %all-to-all-start.19 = ((bf16[8,96,1536]{2,1,0:T(8,128)(2,1)}), bf16[8,96,1536]{2,1,0:T(8,128)(2,1)}, u32[]{:S(2)}, u32[]{:S(2)}) async-start(bf16[8,96,1536]{2,1,0:T(8,128)(2,1)} %bitcast.511), calls=%async_computation.19 | async-start | bytes 4718592 | tf_op jit(solution)/shard_map/all_to_all | solution.py:289
  1307.1 34.2 %collective-permute-start.74 = (bf16[2,4,384,512]{3,2,1,0:T(8,128)(2,1)S(1)}, bf16[2,4,384,512]{3,2,1,0:T(8,128)(2,1)S(1)}, u32[]{:S(2)}, u32[]{:S(2)}) collective-permute-start(bf16[2,4,384,512]{3,2,1,0:T(8,128)(2,1)S(1)} %slice.128.refs_1_), channel_id=1, source_target_pairs={{0,16},{1,17},{2,18},{3,19},{4,20},{5,21},{6,22},{7,23},{8,24},{9,... | collective-permute-start | bytes 9437192 | tf_op jit(solution)/shard_map/ppermute | solution.py:157
  1308.6 32.6 %collective-permute-start.73 = (bf16[2,4,384,512]{3,2,1,0:T(8,128)(2,1)S(1)}, bf16[2,4,384,512]{3,2,1,0:T(8,128)(2,1)}, u32[]{:S(2)}, u32[]{:S(2)}) collective-permute-start(bf16[2,4,384,512]{3,2,1,0:T(8,128)(2,1)S(1)} %pad_maximum_fusion.3.refs_0_), channel_id=1, source_target_pairs={{16,0},{17,1},{18,2},{19,3},{20,4},{21,5},{22,6},{23,7},{24,8},{25... | collective-permute-start | bytes 9437192 | tf_op jit(solution)/shard_map/ppermute | solution.py:156
  1329.3 34.5 %collective-permute-start.78 = (bf16[8,96,1536]{2,1,0:T(8,128)(2,1)}, bf16[8,96,1536]{2,1,0:T(8,128)(2,1)}, u32[]{:S(2)}, u32[]{:S(2)}) collective-permute-start(bf16[8,96,1536]{2,1,0:T(8,128)(2,1)} %all-to-all-done.16.refs_1_), channel_id=1, source_target_pairs={{0,16},{1,17},{2,18},{3,19},{4,20},{5,21},{6,22},{7,23},{8,24},{9,... | collective-permute-start | bytes 7077896 | tf_op jit(solution)/shard_map/ppermute | solution.py:157
  (237 other events, 3856.9 us)

commit v3 on v2

--- a/solution.py
+++ b/solution.py
@@ -1,3 +1,5 @@
+from types import SimpleNamespace
+
 import jax
 import jax.numpy as jnp
 import numpy as np
@@ -162,8 +164,8 @@
     return jnp.where(core == section, section, 2 + section)
 
 
-def dense_home(homes, out_widths):
-    parts, groups, rows, width = homes[0].shape
+def dense_home(homes, offsets, width, out_widths):
+    parts, groups, rows, _ = homes[0].shape
     block = rows // 2
 
     def pick(k, where):
@@ -181,9 +183,10 @@
             def _():
                 out, at = 0, 0
                 for group in range(groups):
-                    start = 0
-                    while start < width:
-                        piece = min(width - start, out_widths[out] - at)
+                    start = offsets[source]
+                    stop = start + width
+                    while start < stop:
+                        piece = min(stop - start, out_widths[out] - at)
                         outs[out][:, at : at + piece] = sources[source][
                             0, group, :, start : start + piece
                         ].astype(F32)
@@ -193,7 +196,7 @@
 
     count = 4 * parts
     shapes = [(count * block, w) for w in out_widths]
-    blocks = [(1, groups, block, width)] * 4
+    blocks = [(1, groups, block, home.shape[3]) for home in homes]
     return pick_blocks(
         homes, blocks, pick, count, kernel, shapes, [(block, w) for w in out_widths]
     )
@@ -248,12 +251,16 @@
 
 
 def dense_rows(partial):
+    for flip in flips("dp"):
+        partial = dense_rows_step(partial, flip)
+    return partial.astype(BF)
+
+
+def dense_rows_step(partial, flip):
     own = lax.axis_index("dp")
-    for flip in flips("dp"):
-        kept, sent = two_parts(partial, jnp.where((own & flip) == 0, 0, 1))
-        sent = lax.ppermute(sent.astype(BF), "dp", partners("dp", flip))
-        partial = kept.astype(F32) + sent.astype(F32)
-    return partial.astype(BF)
+    kept, sent = two_parts(partial, jnp.where((own & flip) == 0, 0, 1))
+    sent = lax.ppermute(sent.astype(BF), "dp", partners("dp", flip))
+    return kept.astype(F32) + sent.astype(F32)
 
 
 def dense_line(total):
@@ -264,25 +271,36 @@
     return total
 
 
-def dense_groups(total):
+def group_parts(total):
+    axes = (1,) * len(flips("expert"))
+    return [part.reshape(axes + part.shape) for part in jnp.split(total, 2, 0)]
+
+
+def group_step(parts, index):
     own = lax.axis_index("expert")
     order = flips("expert")
-    parts = []
-    for part, way in zip(jnp.split(total, 2, 0), (order, order[::-1]), strict=True):
-        part = part.reshape((1,) * len(order) + part.shape)
-        for flip in way:
-            others = lax.ppermute(part, "expert", partners("expert", flip))
-            part = in_order(part, others, own & flip, len(order) - 1 - order.index(flip))
-        parts.append(part.reshape((-1,) + part.shape[-2:]))
-    return jnp.stack(parts)
-
-
-def small_total(partial):
-    for axis in ("section", "expert", "dp"):
-        for flip in flips(axis):
-            others = lax.ppermute(partial.astype(BF), axis, partners(axis, flip))
-            partial = partial + others.astype(F32)
-    return partial
+    stepped = []
+    for part, way in zip(parts, (order, order[::-1]), strict=True):
+        flip = way[index]
+        others = lax.ppermute(part, "expert", partners("expert", flip))
+        axis = len(order) - 1 - order.index(flip)
+        stepped.append(in_order(part, others, own & flip, axis))
+    return stepped
+
+
+def group_join(parts):
+    return jnp.stack([part.reshape((-1,) + part.shape[-2:]) for part in parts])
+
+
+def dense_groups(total):
+    parts = group_parts(total)
+    for index in range(len(flips("expert"))):
+        parts = group_step(parts, index)
+    return group_join(parts)
+
+
+def small_step(partial, axis, flip):
+    return partial + lax.ppermute(partial.astype(BF), axis, partners(axis, flip)).astype(F32)
 
 
 def exchange(rows, axes):
@@ -317,10 +335,11 @@
 
 def row_halves(own, is_first):
     half = own.shape[1] // 2
-    low_half, high_half = own[:, :half], own[:, half:]
-    kept = jnp.where(is_first, low_half, high_half)
-    received = swapped(jnp.where(is_first, high_half, low_half))
-    return (jnp.where(is_first, kept, received), jnp.where(is_first, received, kept))
+    received = swapped(two_parts(own, lax.axis_index("section"), 1)[1])
+    return (
+        jnp.where(is_first, own[:, :half], received),
+        jnp.where(is_first, received, own[:, half:]),
+    )
 
 
 def expert_in(rows):
@@ -341,8 +360,9 @@
     return pieces
 
 
-def expert_home(homes):
-    experts, rows, columns = homes[0].shape
+def expert_home(homes, count=1):
+    experts, rows, width = homes[0].shape
+    columns = width // count
 
     def pick(k, where):
         section = where[0]
@@ -359,11 +379,16 @@
 
                 @pl.when(used == source)
                 def _():
-                    outs[0][0, core * rows : (core + 1) * rows] = sources[source][0].astype(F32)
+                    for part, out in enumerate(outs):
+                        out[0, core * rows : (core + 1) * rows] = sources[source][
+                            0, :, part * columns : (part + 1) * columns
+                        ].astype(F32)
 
     shape = (experts, 2 * rows, columns)
-    blocks = [(1, rows, columns)] * 4
-    return pick_blocks(homes, blocks, pick, experts, kernel, [shape], [(1,) + shape[1:]])[0]
+    blocks = [(1, rows, width)] * 4
+    return list(
+        pick_blocks(homes, blocks, pick, experts, kernel, [shape] * count, [(1,) + shape[1:]] * count)
+    )
 
 
 def routing(route_rows, turn_row, experts_all, capacity):
@@ -410,24 +435,24 @@
     powers = jnp.where(chosen, jnp.exp(masked_logits - top), 0.0)
     gate_share = powers / jnp.sum(powers, -1, keepdims=True)
     weighting = jnp.where(selected, dot(gate_share.astype(BF), spread), 0.0).astype(BF)
-    return {
-        "layer_in": layer_in,
-        "factor_one": factor_one,
-        "hidden_one": hidden_one,
-        "queries": queries,
-        "key_all": key_all,
-        "value_all": value_all,
-        "attn_prob": attn_prob,
-        "attn_mix": attn_mix,
-        "middle": middle,
-        "factor_two": factor_two,
-        "hidden_two": hidden_two,
-        "gate_share": gate_share,
-        "selected": selected,
-        "selector": selected.astype(BF),
-        "spread": spread,
-        "weighting": weighting,
-    }
+    return SimpleNamespace(
+        layer_in=layer_in,
+        factor_one=factor_one,
+        hidden_one=hidden_one,
+        queries=queries,
+        key_all=key_all,
+        value_all=value_all,
+        attn_prob=attn_prob,
+        attn_mix=attn_mix,
+        middle=middle,
+        factor_two=factor_two,
+        hidden_two=hidden_two,
+        gate_share=gate_share,
+        selected=selected,
+        selector=selected.astype(BF),
+        spread=spread,
+        weighting=weighting,
+    )
 
 
 def expert_forward(arrived, w_gate, w_up):
@@ -440,43 +465,48 @@
     grad_inner = dot_t(owed, w_down)
     sigmoid_a = jax.nn.sigmoid(gate_pre)
     grad_gate_pre = grad_inner * up_pre * sigmoid_a * (1.0 + gate_pre * (1.0 - sigmoid_a))
-    return grad_gate_pre.astype(BF), (grad_inner * gate_pre * sigmoid_a).astype(BF)
+    return jnp.concatenate([grad_gate_pre, grad_inner * gate_pre * sigmoid_a], 1).astype(BF)
+
+
+def expert_input(grad_pre, w_gate, w_up):
+    width = w_gate.shape[1]
+    return dot_t(grad_pre[:, :width], w_gate) + dot_t(grad_pre[:, width:], w_up)
 
 
 def router_backward(stored, grad_top, returned, w_router):
-    match = jnp.where(stored["selected"], dot_t(grad_top, returned), 0.0)
+    match = jnp.where(stored.selected, dot_t(grad_top, returned), 0.0)
     grad_weighting = lax.dot_general(
         match,
-        stored["spread"].astype(F32),
+        stored.spread.astype(F32),
         (((1,), (1,)), ((), ())),
         precision=lax.Precision.HIGHEST,
         preferred_element_type=F32,
     )
-    gate_share = stored["gate_share"]
+    gate_share = stored.gate_share
     grad_logits = (
         gate_share * (grad_weighting - jnp.sum(gate_share * grad_weighting, -1, keepdims=True))
     ).astype(BF)
-    return t_dot(grad_logits, stored["hidden_two"]), dot_t(grad_logits, w_router)
+    return t_dot(grad_logits, stored.hidden_two), dot_t(grad_logits, w_router)
 
 
 def attention_backward(stored, grad_top, grad_router, grad_hidden, dense_set, hook):
     attn_gain, w_query, w_key, w_value, w_out, ffn_gain, w_router = dense_set
     local_len = grad_top.shape[0]
     grad_normed_two, grad_ffn_gain = norm_back(
-        stored["middle"], stored["factor_two"], ffn_gain, grad_hidden
+        stored.middle, stored.factor_two, ffn_gain, grad_hidden
     )
     grad_middle = grad_top.astype(F32) + grad_normed_two
     grad_branch = hook("branch", grad_middle.astype(BF))
     grad_mix = dot_t(grad_branch, w_out).astype(BF)
-    key_all = stored["key_all"]
-    value_all = stored["value_all"]
+    key_all = stored.key_all
+    value_all = stored.value_all
     heads_kv = key_all.shape[1]
-    attn_prob = stored["attn_prob"]
+    attn_prob = stored.attn_prob
     grouped_grad = grad_mix.reshape(local_len, heads_kv, -1, HEAD_SIZE)
     grad_prob = jnp.einsum("tkgd,skd->kgts", grouped_grad, value_all, preferred_element_type=F32)
     centre = jnp.sum(attn_prob * grad_prob, -1, keepdims=True)
     grad_scores = (attn_prob * (grad_prob - centre)).astype(BF)
-    grouped_query = stored["queries"].reshape(local_len, heads_kv, -1, HEAD_SIZE)
+    grouped_query = stored.queries.reshape(local_len, heads_kv, -1, HEAD_SIZE)
     grad_keys_all = (
         jnp.einsum("kgts,tkgd->skd", grad_scores, grouped_query, preferred_element_type=F32) * SCALE
     )
@@ -488,7 +518,7 @@
         [grad_keys_all.reshape(tree_length, -1), grad_values_all.reshape(tree_length, -1)], 1
     ).astype(BF)
     grad_kv_all = hook("kv_all", grad_kv_all)
-    grad_kv = sum_to_owner(grad_kv_all, 0).astype(BF)
+    grad_kv = hook("kv", sum_to_owner(grad_kv_all, 0).astype(BF))
     grad_queries = (
         jnp.einsum("kgts,skd->tkgd", grad_scores, key_all, preferred_element_type=F32) * SCALE
     )
@@ -499,16 +529,16 @@
     grad_hidden_one = grad_hidden_one + dot_t(grad_keys, w_key)
     grad_hidden_one = grad_hidden_one + dot_t(grad_values, w_value)
     grad_normed_one, grad_attn_gain = norm_back(
-        stored["layer_in"], stored["factor_one"], attn_gain, grad_hidden_one
+        stored.layer_in, stored.factor_one, attn_gain, grad_hidden_one
     )
     grad_input = grad_middle + grad_normed_one
     small = jnp.concatenate([grad_router, grad_attn_gain[None], grad_ffn_gain[None]], 0)
-    return {
-        "input": grad_input,
-        "branch": grad_branch,
-        "qkv": jnp.concatenate([grad_queries, grad_kv], 1),
-        "small": jnp.pad(small, ((0, -small.shape[0] % 16), (0, 0))),
-    }
+    return SimpleNamespace(
+        input=grad_input,
+        branch=grad_branch,
+        qkv=jnp.concatenate([grad_queries, grad_kv], 1),
+        small=jnp.pad(small, ((0, -small.shape[0] % 16), (0, 0))),
+    )
 
 
 def local(
@@ -559,127 +589,138 @@
     first = attention_forward(
         layer_rows.astype(F32), visible, routed[0], dense_sets[0], lambda value: value
     )
-    outgoing = t_dot(first["selector"], first["hidden_two"]).astype(BF)
+    outgoing = t_dot(first.selector, first.hidden_two).astype(BF)
     arrived_first = send_out(outgoing, experts_all)
     down_first = expert_in(downs[0])
     gate_pre, up_pre, inner_first = expert_forward(arrived_first, gate_first, up_first)
     pres_first = (gate_pre, up_pre)
     returned_first = send_back(dot(inner_first, down_first).astype(BF), experts_all)
-    early = jnp.concatenate([first["hidden_one"], first["attn_mix"]], 0)
+    early = jnp.concatenate([first.hidden_one, first.attn_mix], 0)
     early, returned_first = tie(early, returned_first)
-    kept = {"early": early_operand(early)}
+    kept = SimpleNamespace(early=early_operand(early))
 
     def end(name, value):
-        kept[name], value = tie(kept[name], value)
+        got, value = tie(getattr(kept, name), value)
+        setattr(kept, name, got)
         return value
 
-    state = (first["middle"] + dot(first["weighting"], returned_first)).astype(BF)
-
+    state = (first.middle + dot(first.weighting, returned_first)).astype(BF)
     gate_second, up_second = expert_in(gates[1]), expert_in(ups[1])
     second = attention_forward(
         state.astype(F32), visible, routed[1], dense_sets[1], lambda value: end("early", value)
     )
-    outgoing = t_dot(second["selector"], second["hidden_two"]).astype(BF)
-    early_first = kept["early"]
-    arrived_second = send_out(outgoing, experts_all)
-    early = jnp.concatenate([second["hidden_one"], second["attn_mix"]], 0)
-    early, arrived_second = tie(early, arrived_second)
+    early_first = kept.early
+    outgoing = jnp.concatenate(
+        [t_dot(second.selector, second.hidden_two), t_dot(second.weighting, cotangent)], 1
+    ).astype(BF)
+    outgoing = send_out(outgoing, experts_all)
+    early = jnp.concatenate([second.hidden_one, second.attn_mix], 0)
+    early, outgoing = tie(early, outgoing)
     early_second = early_operand(early)
-    owed_second = send_out(t_dot(second["weighting"], cotangent).astype(BF), experts_all)
+    arrived_second, owed_second = jnp.split(outgoing, 2, 1)
     down_second = expert_in(downs[1])
     gate_pre, up_pre, inner_second = expert_forward(arrived_second, gate_second, up_second)
-    grad_gate_pre, grad_up_pre = expert_backward(owed_second, gate_pre, up_pre, down_second)
-    grad_arrived = (dot_t(grad_gate_pre, gate_second) + dot_t(grad_up_pre, up_second)).astype(BF)
-    early_second, grad_arrived = tie(early_second, grad_arrived)
-    returned_second = send_back(dot(inner_second, down_second).astype(BF), experts_all)
-    sent_second = send_back(grad_arrived, experts_all)
-    top = second["middle"] + dot(second["weighting"], returned_second)
+    grad_pre = expert_backward(owed_second, gate_pre, up_pre, down_second)
+    early_second, grad_pre = tie(early_second, grad_pre)
+    produced = jnp.concatenate(
+        [dot(inner_second, down_second), expert_input(grad_pre, gate_second, up_second)], 1
+    ).astype(BF)
+    produced = send_back(produced, experts_all)
+    gate_up_grad = t_dot(arrived_second, grad_pre).astype(BF)
+    down_grad = t_dot(inner_second, owed_second).astype(BF)
+    produced, gate_up_grad, down_grad = tie(produced, gate_up_grad, down_grad)
+    kept.down1 = expert_out(down_grad, experts)
+    returned_second, sent_second = jnp.split(produced, 2, 1)
+    top = second.middle + dot(second.weighting, returned_second)
     top_other = lax.ppermute(top, "section", UP)
-    expert_grads = [t_dot(arrived_second, g).astype(BF) for g in (grad_gate_pre, grad_up_pre)]
-    expert_grads.append(t_dot(inner_second, owed_second).astype(BF))
-    sent_second, expert_grads = tie(sent_second, expert_grads)
-
-    kept["gate"] = expert_out(expert_grads[0], experts)
+
     grad_router, grad_hidden = router_backward(
         second, cotangent, returned_second, dense_sets[1][6]
     )
-    grad_hidden = grad_hidden + dot(second["selector"], sent_second)
-
-    def later_hook(name, value):
-        return end("gate", value) if name == "kv_all" else value
-
+    grad_hidden = grad_hidden + dot(second.selector, sent_second)
     later = attention_backward(
-        second, cotangent, grad_router, grad_hidden, dense_sets[1], later_hook
-    )
-    grad = later["input"].astype(BF)
-    branch, qkv, grad = tie(later["branch"], later["qkv"], grad)
+        second,
+        cotangent,
+        grad_router,
+        grad_hidden,
+        dense_sets[1],
+        lambda name, value: end("down1", value) if name == "kv_all" else value,
+    )
+    grad = later.input.astype(BF)
+    branch, qkv, grad = tie(later.branch, later.qkv, grad)
     late = late_operands([branch, qkv])
     width = late[0].shape[1]
-    outgoing = t_dot(first["weighting"], grad).astype(BF)
-    owed_first = send_out(outgoing, experts_all)
-    late, owed_first, up_grad = tie(late, owed_first, expert_grads[1])
-    kept["up"] = expert_out(up_grad, experts)
+    owed_first = send_out(t_dot(first.weighting, grad).astype(BF), experts_all)
+    late, owed_first = tie(late, owed_first)
     hidden_early, mix_early = early_second
-    kept["dense"] = dense_rows(dense_partial([mix_early, hidden_early], late))
-    grad_gate_pre, grad_up_pre = expert_backward(owed_first, *pres_first, down_first)
-    grad_arrived = (dot_t(grad_gate_pre, gate_first) + dot_t(grad_up_pre, up_first)).astype(BF)
-    first_grads = [t_dot(arrived_first, g).astype(BF) for g in (grad_gate_pre, grad_up_pre)]
+    kept.dense = dense_rows(dense_partial([mix_early, hidden_early], late))
+    grad_pre = expert_backward(owed_first, *pres_first, down_first)
+    grad_arrived = expert_input(grad_pre, gate_first, up_first).astype(BF)
+    first_grads = [t_dot(arrived_first, grad_pre).astype(BF)]
     first_grads.append(t_dot(inner_first, owed_first).astype(BF))
-    grad_arrived, first_grads = tie(grad_arrived, first_grads)
-    sent_first = send_back(end("dense", end("up", grad_arrived)), experts_all)
-    down_grad, sent_first = tie(expert_grads[2], sent_first)
-    kept["down"] = expert_out(down_grad, experts)
-    kept["dense"], sent_first = tie(kept["dense"], sent_first)
-    kept["dense"] = dense_line(kept["dense"])
+    sent_first = send_back(end("dense", grad_arrived), experts_all)
+    kept.dense, sent_first = tie(kept.dense, sent_first)
+    kept.dense, gate_up_grad = tie(dense_line(kept.dense), gate_up_grad)
+    kept.gate_up1 = expert_out(gate_up_grad, experts)
     grad_router, grad_hidden = router_backward(first, grad, returned_first, dense_sets[0][6])
-    grad_hidden = grad_hidden + dot(first["selector"], sent_first)
+    grad_hidden = grad_hidden + dot(first.selector, sent_first)
 
     def hook(name, value):
         if name == "branch":
-            kept["late"] = late_operands([value])
+            kept.late = late_operands([value])
         if name == "kv_all":
-            value = end("dense", end("down", end("late", value)))
-            kept["dense"] = dense_groups(kept["dense"])
-            kept["out"] = dense_partial([early_first[1]], kept["late"])
-            return end("out", value)
+            value = end("late", value)
+            kept.out = dense_partial([early_first[1]], kept.late)
+            kept.dense = dense_groups(kept.dense)
+            value = end("dense", end("out", end("gate_up1", value)))
+        if name == "kv":
+            down_grad, value, kept.out = tie(first_grads[1], value, kept.out)
+            kept.down0 = expert_out(down_grad, experts)
         return value
 
     earlier = attention_backward(
         first, grad, grad_router, grad_hidden, dense_sets[0], hook
     )
-    out_second = [kept[name] for name in ("gate", "up", "down")]
-    ending, gate_grad = tie(earlier["qkv"], first_grads[0])
-    gate_part = expert_out(gate_grad, experts)
-    out_total = dense_line(dense_rows(kept["out"]))
-    qkv_total = dense_partial([early_first[0]], late_operands([ending]))
-    smalls = small_total(jnp.concatenate([earlier["small"], later["small"]], 0))
-    gate_part, qkv_total, out_total, smalls = tie(gate_part, qkv_total, out_total, smalls)
+    smalls = jnp.concatenate([earlier.small, later.small], 0)
+    for axis in ("section", "expert"):
+        for flip in flips(axis):
+            smalls = small_step(smalls, axis, flip)
+    qkv_total = dense_partial([early_first[0]], late_operands([earlier.qkv]))
+    qkv_total, smalls, down_part, out_total = tie(qkv_total, smalls, kept.down0, kept.out)
+    for flip in flips("dp"):
+        qkv_total = dense_rows_step(qkv_total, flip)
+        out_total = dense_rows_step(out_total, flip)
+        smalls = small_step(smalls, "dp", flip)
+        qkv_total, out_total, smalls = tie(qkv_total, out_total, smalls)
+    qkv_total, out_total = dense_line(qkv_total.astype(BF)), dense_line(out_total.astype(BF))
+    qkv_total, out_total, gate_up_grad = tie(qkv_total, out_total, first_grads[0])
+    gate_up_part = expert_out(gate_up_grad, experts)
+    second_total = kept.dense
+    second_other = lax.ppermute(second_total, "section", UP)
+    down_total = expert_home(two_homes(down_part, kept.down1))
     out_total = dense_groups(out_total)
-    qkv_total = dense_line(dense_rows(qkv_total))
-    qkv_total, up_grad, second_total = tie(qkv_total, first_grads[1], kept["dense"])
-    up_part = expert_out(up_grad, experts)
+    out_other = lax.ppermute(out_total, "section", DOWN)
+    homes = (out_total, second_total, out_other, second_other)
+    out = dense_home(homes, [0] * 4, width, [w_out.shape[2]])[0]
     qkv_total = dense_groups(qkv_total)
-    gate_total = expert_home(two_homes(gate_part, out_second[0]))
-    out = dense_home(two_homes(out_total, second_total[..., :width]), [w_out.shape[2]])[0]
-    up_part, down_grad, gate_total, out, qkv_total, smalls = tie(
-        up_part, first_grads[2], gate_total, out, qkv_total, smalls
-    )
-    down_part = expert_out(down_grad, experts)
-    up_total = expert_home(two_homes(up_part, out_second[1]))
+    qkv_other = lax.ppermute(qkv_total, "section", DOWN)
+    homes = (qkv_total, second_total, qkv_other, second_other)
     query, key, value = dense_home(
-        two_homes(qkv_total, second_total[..., width:]),
+        homes,
+        [0, width, 0, width],
+        qkv_total.shape[3],
         [w_query.shape[2], w_key.shape[2], w_value.shape[2]],
     )
     small = jnp.where(is_first, *jnp.split(smalls, 2, 0))
-    grad = earlier["input"]
+    grad = earlier.input
     grad_other = lax.ppermute(grad, "section", DOWN)
     edge_out = jnp.where(
         is_first, jnp.stack([grad, grad_other]), jnp.stack([top_other, top])
     )[None, :, None]
-    down_part, up_total, query, key, value, edge_out = tie(
-        down_part, up_total, query, key, value, edge_out
-    )
-    expert_total = [gate_total, up_total, expert_home(two_homes(down_part, out_second[2]))]
+    gate_up_part, down_total, out, query, key, value, edge_out = tie(
+        gate_up_part, down_total, out, query, key, value, edge_out
+    )
+    expert_total = expert_home(two_homes(gate_up_part, kept.gate_up1), 2) + down_total
     dense_out = (
         small[experts_all],
         query,
@@ -697,38 +738,15 @@
 
 
 def solution(mesh):
-    placed = (
-        P("section", None, "expert", "dp", None),
-        P(None, "expert", None),
-        P("section", None, "expert", "dp", None),
-        P("section", None, "expert", "dp", None),
-        P("section", None),
-        P("section", None, None),
-        P("section", None, None),
-        P("section", None, None),
-        P("section", None, None),
-        P("section", None),
-        P("section", None, None),
-        P("section", "expert", "dp", None),
-        P("section", "expert", "dp", None),
-        P("section", "expert", "dp", None),
-    )
+    section, expert, dp = "section", "expert", "dp"
+    tokens = P(section, None, expert, dp, None)
+    vector, matrix = P(section, None), P(section, None, None)
+    rows = P(section, expert, dp, None)
+    dense = (vector, matrix, matrix, matrix, matrix, vector, matrix)
     return jax.shard_map(
         local,
         mesh=mesh,
-        in_specs=placed,
-        out_specs=(
-            P("section", None, "expert", "dp", None),
-            P("section", None),
-            P("section", None, None),
-            P("section", None, None),
-            P("section", None, None),
-            P("section", None, None),
-            P("section", None),
-            P("section", None, None),
-            P("section", "expert", "dp", None),
-            P("section", "expert", "dp", None),
-            P("section", "expert", "dp", None),
-        ),
+        in_specs=(tokens, P(None, expert, None), tokens, tokens) + dense + (rows, rows, rows),
+        out_specs=(tokens,) + dense + (rows, rows, rows),
         check_vma=False,
     )

time: 1390 us -> 1350 us (0.971)
  waiting for transfers between devices: 791 us -> 687 us
  blocking collectives: 42.6 us -> 119 us
  starting transfers between devices: 184 us -> 147 us
  local copies, waits for them, and re-layouts: 61.7 us -> 77.6 us
    all_to_all x1 -> x2, blocking collectives: 42.6 us -> 119 us  [exchange(): return lax.all_to_all(rows, axes, split_axis=0, concat_axis=0, tiled=True)]
    ppermute x6, waiting for transfers between devices: 130 us -> 63.1 us  [dense_line(): others = lax.ppermute(total, 'dp', partners('dp', flip))]
    all_to_all x19 -> x14, waiting for transfers between devices: 383 us -> 322 us  [exchange(): return lax.all_to_all(rows, axes, split_axis=0, concat_axis=0, tiled=True)]
    all_to_all x19 -> x14, starting transfers between devices: 97.3 us -> 71.4 us  [exchange(): return lax.all_to_all(rows, axes, split_axis=0, concat_axis=0, tiled=True)]
    ppermute x23 -> x26, waiting for transfers between devices: 119 us -> 138 us  [the longest x12 60.4 us: group_step(): others = lax.ppermute(part, 'expert', partners('expert', flip))]
    dot_general x16 -> x14, matrix products: 36.5 us -> 32.3 us  [t_dot(): lax.dot_general(left, right, (((0,), (0,)), ((), ())), preferred_element_...]
    ppermute x23 -> x26, starting transfers between devices: 28.7 us -> 27.8 us  [the longest x12 11.9 us: group_step(): others = lax.ppermute(part, 'expert', partners('expert', flip))]
    pallas_call x5 -> x4, Pallas kernels: 42.9 us -> 43.4 us  [pick_blocks(): pl.pallas_call(body, grid_spec=pltpu.PrefetchScalarGridSpec(num_scalar_pr...]
  transfers between devices with their start and end apart: 98 -> 90, of which waited for: 47 -> 52; matrix products, arithmetic and copies ran while one was open for 19% -> 20% of each run, Pallas kernels for 3% -> 2%
where the time goes in v3:
time: 1350 us; the launch traced here: 1340 us
  waiting for transfers between devices  687 us (51%)
  matrix products  163 us (12%)
  starting transfers between devices  147 us (11%)
  blocking collectives  119 us (9%)
  other arithmetic  99.4 us (7%)
  local copies, waits for them, and re-layouts  77.6 us (6%)
  Pallas kernels  43.4 us (3%)
    all_to_all x14, waiting for transfers between devices, exchange(): return lax.all_to_all(rows, axes, split_axis=0, concat_axis=0, tiled=True)  322 us
    all_to_all x2, blocking collectives, exchange(): return lax.all_to_all(rows, axes, split_axis=0, concat_axis=0, tiled=True)  119 us
    ppermute x8, waiting for transfers between devices, gathered(): lax.ppermute(shard, over, partners(over, flip))  107 us
    all_to_all x14, starting transfers between devices, exchange(): return lax.all_to_all(rows, axes, split_axis=0, concat_axis=0, tiled=True)  71.4 us
    ppermute x6, waiting for transfers between devices, dense_line(): others = lax.ppermute(total, 'dp', partners('dp', flip))  63.1 us
    ppermute x12, waiting for transfers between devices, group_step(): others = lax.ppermute(part, 'expert', partners('expert', flip))  60.4 us
    dot_general x19, matrix products, dot_t(): lax.dot_general(left, right, (((1,), (1,)), ((), ())), preferred_element_...  57.4 us
    ppermute x6, waiting for transfers between devices, dense_rows_step(): sent = lax.ppermute(sent.astype(BF), 'dp', partners('dp', flip))  57.3 us
  transfers between devices with their start and end apart: 90, of which 52 were waited for; matrix products, arithmetic and copies ran while one was open for 20% of the time, Pallas kernels for 2%

profile of v3, /device:TPU:1, one launch (start us, length us, event | category | flops | bytes accessed | tf_op | source)
XLA Modules:
  0.0 1339.6 jit_solution(11808381253134775340)
XLA Ops:
  9.2 5.6 slice_select_fusion.4
  14.8 6.4 all-to-all-start.2
  42.4 38.3 %collective-permute-done.4 = bf16[128,512]{1,0:T(8,128)(2,1)S(1)} collective-permute-done((bf16[128,512]{1,0:T(8,128)(2,1)S(1)}, bf16[128,512]{1,0:T(8,128)(2,1)S(1)}, u32[]{:S(2)}, u32[]{:S(2)}) %collective-permute-start.4) | collective-permute-done | bytes 131104 | tf_op jit(solution)/shard_map/ppermute | solution.py:113
  81.6 5.7 slice_select_fusion.2
  111.3 34.3 %all-to-all-done.1 = bf16[8,192,768]{2,1,0:T(8,128)(2,1)} async-done(((bf16[8,192,768]{2,1,0:T(8,128)(2,1)}), bf16[8,192,768]{2,1,0:T(8,128)(2,1)}, u32[]{:S(2)}, u32[]{:S(2)}) %all-to-all-start.1) | async-done | bytes 2359328 | tf_op jit(solution)/shard_map/all_to_all | solution.py:307
  149.8 5.7 slice_select_fusion
  155.4 32.6 %all-to-all-done = bf16[32,16,1536]{2,1,0:T(8,128)(2,1)S(1)} async-done(((bf16[32,16,1536]{2,1,0:T(8,128)(2,1)}), bf16[32,16,1536]{2,1,0:T(8,128)(2,1)S(1)}, u32[]{:S(2)}, u32[]{:S(2)}) %all-to-all-start) | async-done | bytes 1572896 | tf_op jit(solution)/shard_map/all_to_all | solution.py:307
  202.4 45.2 %all-to-all-done.3 = bf16[8,96,1536]{2,1,0:T(8,128)(2,1)} async-done(((bf16[8,96,1536]{2,1,0:T(8,128)(2,1)}), bf16[8,96,1536]{2,1,0:T(8,128)(2,1)}, u32[]{:S(2)}, u32[]{:S(2)}) %all-to-all-start.3) | async-done | bytes 2359328 | tf_op jit(solution)/shard_map/all_to_all | solution.py:307
  261.7 32.0 %all-to-all-done.4 = bf16[32,16,1536]{2,1,0:T(8,128)(2,1)S(1)} async-done(((bf16[32,16,1536]{2,1,0:T(8,128)(2,1)}), bf16[32,16,1536]{2,1,0:T(8,128)(2,1)S(1)}, u32[]{:S(2)}, u32[]{:S(2)}) %all-to-all-start.4) | async-done | bytes 1572896 | tf_op jit(solution)/shard_map/all_to_all | solution.py:307
  303.3 18.0 %collective-permute-done.14 = bf16[2,1,2,128,768]{4,3,2,1,0:T(8,128)(2,1)S(1)} collective-permute-done((bf16[2,1,2,128,768]{4,3,2,1,0:T(8,128)(2,1)S(1)}, bf16[2,1,2,128,768]{4,3,2,1,0:T(8,128)(2,1)S(1)}, u32[]{:S(2)}, u32[]{:S(2)}) %collective-permute-start.14) | collective-permute-done | bytes 786464 | tf_op jit(solution)/shard_map/ppermute | solution.py:113
  325.2 34.2 %collective-permute-done.17 = bf16[128,512]{1,0:T(8,128)(2,1)S(1)} collective-permute-done((bf16[128,512]{1,0:T(8,128)(2,1)S(1)}, bf16[128,512]{1,0:T(8,128)(2,1)S(1)}, u32[]{:S(2)}, u32[]{:S(2)}) %collective-permute-start.17) | collective-permute-done | bytes 131104 | tf_op jit(solution)/shard_map/ppermute | solution.py:113
  372.4 6.2 all-to-all-start.8
  391.5 41.1 %all-to-all-done.8 = bf16[8,96,1536]{2,1,0:T(8,128)(2,1)} async-done(((bf16[8,96,1536]{2,1,0:T(8,128)(2,1)}), bf16[8,96,1536]{2,1,0:T(8,128)(2,1)}, u32[]{:S(2)}, u32[]{:S(2)}) %all-to-all-start.8) | async-done | bytes 2359328 | tf_op jit(solution)/shard_map/all_to_all | solution.py:307
  432.6 76.2 %all_to_all.80 = bf16[32,16,3072]{2,1,0:T(8,128)(2,1)} all-to-all(bf16[32,16,3072]{2,1,0:T(8,128)(2,1)} %pad_maximum_fusion.2), channel_id=1, replica_groups=mesh['section'=2,'dp'=4,'expert'=4] {'expert','dp','section'}, dimensions={0} | all-to-all | bytes 6291456 | tf_op jit(solution)/shard_map/all_to_all | solution.py:307
  520.8 14.6 %collective-permute-done.20 = bf16[2,1,2,128,768]{4,3,2,1,0:T(8,128)(2,1)S(1)} collective-permute-done((bf16[2,1,2,128,768]{4,3,2,1,0:T(8,128)(2,1)S(1)}, bf16[2,1,2,128,768]{4,3,2,1,0:T(8,128)(2,1)S(1)}, u32[]{:S(2)}, u32[]{:S(2)}) %collective-permute-start.20) | collective-permute-done | bytes 786464 | tf_op jit(solution)/shard_map/ppermute | solution.py:113
  541.1 26.9 %all-to-all-done.7 = bf16[8,192,768]{2,1,0:T(8,128)(2,1)} async-done(((bf16[8,192,768]{2,1,0:T(8,128)(2,1)}), bf16[8,192,768]{2,1,0:T(8,128)(2,1)}, u32[]{:S(2)}, u32[]{:S(2)}) %all-to-all-start.7) | async-done | bytes 2359328 | tf_op jit(solution)/shard_map/all_to_all | solution.py:307
  601.2 63.6 %all-to-all-done.9 = bf16[32,16,3072]{2,1,0:T(8,128)(2,1)} async-done(((bf16[32,16,3072]{2,1,0:T(8,128)(2,1)}), bf16[32,16,3072]{2,1,0:T(8,128)(2,1)}, u32[]{:S(2)}, u32[]{:S(2)}) %all-to-all-start.9) | async-done | bytes 3145760 | tf_op jit(solution)/shard_map/all_to_all | solution.py:307
  696.9 26.3 %all-to-all-done.10.refs_1_ = bf16[8,96,1536]{2,1,0:T(8,128)(2,1)S(1)} async-done(((bf16[8,96,1536]{2,1,0:T(8,128)(2,1)}), bf16[8,96,1536]{2,1,0:T(8,128)(2,1)S(1)}, u32[]{:S(2)}, u32[]{:S(2)}) %all-to-all-start.10) | async-done | bytes 2359328 | tf_op jit(solution)/shard_map/all_to_all | solution.py:307
  724.2 6.9 collective-permute-done.22
  754.6 6.2 all-to-all-start.11
  766.0 13.3 collective-permute-done.24
  779.3 9.3 collective-permute-done.26
  812.4 6.9 collective-permute-done.28
  824.6 17.9 %collective-permute-done.29 = bf16[192,896]{0,1:T(8,128)(2,1)S(1)} collective-permute-done((bf16[192,896]{0,1:T(8,128)(2,1)S(1)}, bf16[192,896]{0,1:T(8,128)(2,1)S(1)}, u32[]{:S(2)}, u32[]{:S(2)}) %collective-permute-start.29) | collective-permute-done | bytes 344096 | tf_op jit(solution)/shard_map/ppermute | solution.py:262
  842.8 42.6 %all_to_all.81 = bf16[32,16,1536]{2,1,0:T(8,128)(2,1)} all-to-all(bf16[32,16,1536]{2,1,0:T(8,128)(2,1)S(1)} %bitcast.510), channel_id=1, replica_groups=mesh['section'=2,'dp'=4,'expert'=4] {'expert','dp','section'}, dimensions={0} | all-to-all | bytes 3145728 | tf_op jit(solution)/shard_map/all_to_all | solution.py:307
  885.4 21.9 %collective-permute-done.30 = bf16[192,896]{0,1:T(8,128)(2,1)S(1)} collective-permute-done((bf16[192,896]{0,1:T(8,128)(2,1)S(1)}, bf16[192,896]{0,1:T(8,128)(2,1)S(1)}, u32[]{:S(2)}, u32[]{:S(2)}) %collective-permute-start.30) | collective-permute-done | bytes 344096 | tf_op jit(solution)/shard_map/ppermute | solution.py:269
  907.7 16.5 %collective-permute-done.31 = bf16[384,896]{0,1:T(8,128)(2,1)S(1)} collective-permute-done((bf16[384,896]{0,1:T(8,128)(2,1)S(1)}, bf16[384,896]{0,1:T(8,128)(2,1)S(1)}, u32[]{:S(2)}, u32[]{:S(2)}) %collective-permute-start.31) | collective-permute-done | bytes 688160 | tf_op jit(solution)/shard_map/ppermute | solution.py:269
  925.8 6.0 all-to-all-start.13
  942.4 6.2 convolution_convert_fusion.10
  965.5 9.8 collective-permute-done.32
  994.8 16.4 %collective-permute-done.35 = bf16[2,1,384,896]{2,3,1,0:T(8,128)(2,1)} collective-permute-done((bf16[2,1,384,896]{2,3,1,0:T(8,128)(2,1)}, bf16[2,1,384,896]{2,3,1,0:T(8,128)(2,1)}, u32[]{:S(2)}, u32[]{:S(2)}) %collective-permute-start.35) | collective-permute-done | bytes 1376288 | tf_op jit(solution)/shard_map/ppermute | solution.py:285
  1046.8 6.2 collective-permute-done.41
  1062.3 6.6 fusion.70
  1097.8 15.1 %all-to-all-done.14.refs_0_ = bf16[8,96,1536]{2,1,0:T(8,128)(2,1)} async-done(((bf16[8,96,1536]{2,1,0:T(8,128)(2,1)}), bf16[8,96,1536]{2,1,0:T(8,128)(2,1)}, u32[]{:S(2)}, u32[]{:S(2)}) %all-to-all-start.14) | async-done | bytes 2359328 | tf_op jit(solution)/shard_map/all_to_all | solution.py:307
  1122.0 6.3 collective-permute-done.51
  1128.3 8.4 collective-permute-done.49
  1140.4 16.4 %collective-permute-done.53 = bf16[192,384]{1,0:T(8,128)(2,1)S(1)} collective-permute-done((bf16[192,384]{1,0:T(8,128)(2,1)S(1)}, bf16[192,384]{1,0:T(8,128)(2,1)S(1)}, u32[]{:S(2)}, u32[]{:S(2)}) %collective-permute-start.53) | collective-permute-done | bytes 147488 | tf_op jit(solution)/shard_map/ppermute | solution.py:262
  1161.1 6.3 collective-permute-done.54
  1170.7 11.5 collective-permute-done.57
  1193.7 7.4 collective-permute-done.56
  1225.8 10.4 collective-permute-start.72
  1244.2 11.6 collective-permute-done.68
  1262.1 8.7 collective-permute-done.62
  1282.9 7.8 shard_map.239
  1290.7 11.0 shard_map.240
  1303.3 12.3 shard_map.241
  1318.6 6.1 collective-permute-done.74.refs_2_
  1326.9 12.3 shard_map.242
  (779 shorter events, 478.2 us)
Async XLA Ops:
  4.7 26.5 %collective-permute-start.7 = (s32[5,128]{1,0:T(8,128)}, s32[5,128]{1,0:T(8,128)S(1)}, u32[]{:S(2)}, u32[]{:S(2)}) collective-permute-start(s32[5,128]{1,0:T(8,128)} %select_bitcast_fusion.1), channel_id=1, source_target_pairs={{0,16},{16,0},{1,17},{17,1},{2,18},{18,2},{3,19},{19,3},{4,20},{20... | collective-permute-start | bytes 7688 | tf_op jit(solution)/shard_map/ppermute | solution.py:90
  5.8 27.2 %collective-permute-start.1 = (f32[1536]{0:T(1024)}, f32[1536]{0:T(1024)}, u32[]{:S(2)}, u32[]{:S(2)}) collective-permute-start(f32[1536]{0:T(1024)} %reduce), channel_id=1, source_target_pairs={{0,16},{16,0},{1,17},{17,1},{2,18},{18,2},{3,19},{19,3},{4,20},{20... | collective-permute-start | bytes 18440 | tf_op jit(solution)/shard_map/ppermute | solution.py:90
  6.7 28.3 %collective-permute-start = (bf16[128,1536]{1,0:T(8,128)(2,1)}, bf16[128,1536]{1,0:T(8,128)(2,1)S(1)}, u32[]{:S(2)}, u32[]{:S(2)}) collective-permute-start(bf16[128,1536]{1,0:T(8,128)(2,1)} %select_bitcast_fusion), channel_id=1, source_target_pairs={{0,16},{16,0},{1,17},{17,1},{2,18},{18,2},{3,19},{19,3},{4,20},{20... | collective-permute-start | bytes 1179656 | tf_op jit(solution)/shard_map/ppermute | solution.py:90
  7.1 30.1 %collective-permute-start.3 = (bf16[1536,256]{1,0:T(8,128)(2,1)S(1)}, bf16[1536,256]{1,0:T(8,128)(2,1)S(1)}, u32[]{:S(2)}, u32[]{:S(2)}) collective-permute-start(bf16[1536,256]{1,0:T(8,128)(2,1)S(1)} %bitcast.498), channel_id=1, source_target_pairs={{0,16},{16,0},{1,17},{17,1},{2,18},{18,2},{3,19},{19,3},{4,20},{20... | collective-permute-start | bytes 2359304 | tf_op jit(solution)/shard_map/ppermute | solution.py:90
  9.0 86.0 %collective-permute-start.6 = (bf16[1536,1536]{1,0:T(8,128)(2,1)}, bf16[1536,1536]{1,0:T(8,128)(2,1)}, u32[]{:S(2)}, u32[]{:S(2)}) collective-permute-start(bf16[1536,1536]{1,0:T(8,128)(2,1)} %bitcast.468), channel_id=1, source_target_pairs={{0,16},{16,0},{1,17},{17,1},{2,18},{18,2},{3,19},{19,3},{4,20},{20... | collective-permute-start | bytes 14155784 | tf_op jit(solution)/shard_map/ppermute | solution.py:90
  14.8 72.5 %all-to-all-start.2 = ((bf16[8,192,768]{2,1,0:T(8,128)(2,1)}), bf16[8,192,768]{2,1,0:T(8,128)(2,1)}, u32[]{:S(2)}, u32[]{:S(2)}) async-start(bf16[8,192,768]{2,1,0:T(8,128)(2,1)} %get-tuple-element.149), calls=%async_computation.2 | async-start | bytes 4718592 | tf_op jit(solution)/shard_map/all_to_all | solution.py:307
  31.2 50.3 %collective-permute-start.10 = (bf16[8,192,768]{2,1,0:T(8,128)(2,1)}, bf16[8,192,768]{2,1,0:T(8,128)(2,1)}, u32[]{:S(2)}, u32[]{:S(2)}) collective-permute-start(bf16[8,192,768]{2,1,0:T(8,128)(2,1)} %dynamic-slice_bitcast_fusion.2), channel_id=1, source_target_pairs={{0,16},{16,0},{1,17},{17,1},{2,18},{18,2},{3,19},{19,3},{4,20},{20... | collective-permute-start | bytes 7077896 | tf_op jit(solution)/shard_map/ppermute | solution.py:90
  35.7 68.5 %collective-permute-start.8 = (bf16[1536,1536]{1,0:T(8,128)(2,1)}, bf16[1536,1536]{1,0:T(8,128)(2,1)}, u32[]{:S(2)}, u32[]{:S(2)}) collective-permute-start(bf16[1536,1536]{1,0:T(8,128)(2,1)} %bitcast.450), channel_id=1, source_target_pairs={{0,16},{16,0},{1,17},{17,1},{2,18},{18,2},{3,19},{19,3},{4,20},{20... | collective-permute-start | bytes 14155784 | tf_op jit(solution)/shard_map/ppermute | solution.py:90
  37.3 54.5 %collective-permute-start.9 = (f32[1536]{0:T(1024)}, f32[1536]{0:T(1024)}, u32[]{:S(2)}, u32[]{:S(2)}) collective-permute-start(f32[1536]{0:T(1024)} %reduce.1), channel_id=1, source_target_pairs={{0,16},{16,0},{1,17},{17,1},{2,18},{18,2},{3,19},{19,3},{4,20},{20... | collective-permute-start | bytes 18440 | tf_op jit(solution)/shard_map/ppermute | solution.py:90
  38.6 42.1 %collective-permute-start.4 = (bf16[128,512]{1,0:T(8,128)(2,1)S(1)}, bf16[128,512]{1,0:T(8,128)(2,1)S(1)}, u32[]{:S(2)}, u32[]{:S(2)}) collective-permute-start(bf16[128,512]{1,0:T(8,128)(2,1)S(1)} %pad_maximum_fusion.47), channel_id=1, source_target_pairs={{0,8},{4,12},{8,0},{12,4},{1,9},{5,13},{9,1},{13,5},{2,10},{6,14},... | collective-permute-start | bytes 393224 | tf_op jit(solution)/shard_map/ppermute | solution.py:113
  80.7 69.1 %collective-permute-start.12 = (bf16[8,96,1536]{2,1,0:T(8,128)(2,1)}, bf16[8,96,1536]{2,1,0:T(8,128)(2,1)}, u32[]{:S(2)}, u32[]{:S(2)}) collective-permute-start(bf16[8,96,1536]{2,1,0:T(8,128)(2,1)} %dynamic-slice_bitcast_fusion), channel_id=1, source_target_pairs={{0,16},{16,0},{1,17},{17,1},{2,18},{18,2},{3,19},{19,3},{4,20},{20... | collective-permute-start | bytes 7077896 | tf_op jit(solution)/shard_map/ppermute | solution.py:90
  87.3 58.3 %all-to-all-start.1 = ((bf16[8,192,768]{2,1,0:T(8,128)(2,1)}), bf16[8,192,768]{2,1,0:T(8,128)(2,1)}, u32[]{:S(2)}, u32[]{:S(2)}) async-start(bf16[8,192,768]{2,1,0:T(8,128)(2,1)} %get-tuple-element.146), calls=%async_computation.1 | async-start | bytes 4718592 | tf_op jit(solution)/shard_map/all_to_all | solution.py:307
  145.7 42.4 %all-to-all-start = ((bf16[32,16,1536]{2,1,0:T(8,128)(2,1)}), bf16[32,16,1536]{2,1,0:T(8,128)(2,1)S(1)}, u32[]{:S(2)}, u32[]{:S(2)}) async-start(bf16[32,16,1536]{2,1,0:T(8,128)(2,1)} %bitcast.24), calls=%async_computation | async-start | bytes 3145728 | tf_op jit(solution)/shard_map/all_to_all | solution.py:307
  188.1 59.5 %all-to-all-start.3 = ((bf16[8,96,1536]{2,1,0:T(8,128)(2,1)}), bf16[8,96,1536]{2,1,0:T(8,128)(2,1)}, u32[]{:S(2)}, u32[]{:S(2)}) async-start(bf16[8,96,1536]{2,1,0:T(8,128)(2,1)} %get-tuple-element.148), calls=%async_computation.3 | async-start | bytes 4718592 | tf_op jit(solution)/shard_map/all_to_all | solution.py:307
  252.0 41.7 %all-to-all-start.4 = ((bf16[32,16,1536]{2,1,0:T(8,128)(2,1)}), bf16[32,16,1536]{2,1,0:T(8,128)(2,1)S(1)}, u32[]{:S(2)}, u32[]{:S(2)}) async-start(bf16[32,16,1536]{2,1,0:T(8,128)(2,1)} %bitcast.509), calls=%async_computation.4 | async-start | bytes 3145728 | tf_op jit(solution)/shard_map/all_to_all | solution.py:307
  294.9 77.6 %all-to-all-start.6 = ((bf16[8,192,768]{2,1,0:T(8,128)(2,1)}), bf16[8,192,768]{2,1,0:T(8,128)(2,1)}, u32[]{:S(2)}, u32[]{:S(2)}) async-start(bf16[8,192,768]{2,1,0:T(8,128)(2,1)} %get-tuple-element.145), calls=%async_computation.6 | async-start | bytes 4718592 | tf_op jit(solution)/shard_map/all_to_all | solution.py:307
  302.1 19.2 %collective-permute-start.14 = (bf16[2,1,2,128,768]{4,3,2,1,0:T(8,128)(2,1)S(1)}, bf16[2,1,2,128,768]{4,3,2,1,0:T(8,128)(2,1)S(1)}, u32[]{:S(2)}, u32[]{:S(2)}) collective-permute-start(bf16[2,1,2,128,768]{4,3,2,1,0:T(8,128)(2,1)S(1)} %maximum_bitcast_fusion), channel_id=1, source_target_pairs={{0,2},{1,3},{2,0},{3,1},{4,6},{5,7},{6,4},{7,5},{8,10},{9,11},{10,... | collective-permute-start | bytes 2359304 | tf_op jit(solution)/shard_map/ppermute | solution.py:113
  322.7 45.8 %collective-permute-start.15 = (bf16[2,2,2,128,768]{4,3,2,1,0:T(8,128)(2,1)}, bf16[2,2,2,128,768]{4,3,2,1,0:T(8,128)(2,1)}, u32[]{:S(2)}, u32[]{:S(2)}) collective-permute-start(bf16[2,2,2,128,768]{4,3,2,1,0:T(8,128)(2,1)} %pad_maximum_fusion.10), channel_id=1, source_target_pairs={{0,1},{1,0},{2,3},{3,2},{4,5},{5,4},{6,7},{7,6},{8,9},{9,8},{10,11... | collective-permute-start | bytes 4718600 | tf_op jit(solution)/shard_map/ppermute | solution.py:113
  323.3 36.1 %collective-permute-start.17 = (bf16[128,512]{1,0:T(8,128)(2,1)S(1)}, bf16[128,512]{1,0:T(8,128)(2,1)S(1)}, u32[]{:S(2)}, u32[]{:S(2)}) collective-permute-start(bf16[128,512]{1,0:T(8,128)(2,1)S(1)} %pad_maximum_fusion.48), channel_id=1, source_target_pairs={{0,8},{4,12},{8,0},{12,4},{1,9},{5,13},{9,1},{13,5},{2,10},{6,14},... | collective-permute-start | bytes 393224 | tf_op jit(solution)/shard_map/ppermute | solution.py:113
  372.4 60.1 %all-to-all-start.8 = ((bf16[8,96,1536]{2,1,0:T(8,128)(2,1)}), bf16[8,96,1536]{2,1,0:T(8,128)(2,1)}, u32[]{:S(2)}, u32[]{:S(2)}) async-start(bf16[8,96,1536]{2,1,0:T(8,128)(2,1)} %get-tuple-element.147), calls=%async_computation.8 | async-start | bytes 4718592 | tf_op jit(solution)/shard_map/all_to_all | solution.py:307
  508.8 59.2 %all-to-all-start.7 = ((bf16[8,192,768]{2,1,0:T(8,128)(2,1)}), bf16[8,192,768]{2,1,0:T(8,128)(2,1)}, u32[]{:S(2)}, u32[]{:S(2)}) async-start(bf16[8,192,768]{2,1,0:T(8,128)(2,1)} %get-tuple-element.150), calls=%async_computation.7 | async-start | bytes 4718592 | tf_op jit(solution)/shard_map/all_to_all | solution.py:307
  516.2 19.2 %collective-permute-start.20 = (bf16[2,1,2,128,768]{4,3,2,1,0:T(8,128)(2,1)S(1)}, bf16[2,1,2,128,768]{4,3,2,1,0:T(8,128)(2,1)S(1)}, u32[]{:S(2)}, u32[]{:S(2)}) collective-permute-start(bf16[2,1,2,128,768]{4,3,2,1,0:T(8,128)(2,1)S(1)} %maximum_bitcast_fusion.1), channel_id=1, source_target_pairs={{0,2},{1,3},{2,0},{3,1},{4,6},{5,7},{6,4},{7,5},{8,10},{9,11},{10,... | collective-permute-start | bytes 2359304 | tf_op jit(solution)/shard_map/ppermute | solution.py:113
  536.7 40.0 %collective-permute-start.21 = (bf16[2,2,2,128,768]{4,3,2,1,0:T(8,128)(2,1)}, bf16[2,2,2,128,768]{4,3,2,1,0:T(8,128)(2,1)}, u32[]{:S(2)}, u32[]{:S(2)}) collective-permute-start(bf16[2,2,2,128,768]{4,3,2,1,0:T(8,128)(2,1)} %pad_maximum_fusion.11), channel_id=1, source_target_pairs={{0,1},{1,0},{2,3},{3,2},{4,5},{5,4},{6,7},{7,6},{8,9},{9,8},{10,11... | collective-permute-start | bytes 4718600 | tf_op jit(solution)/shard_map/ppermute | solution.py:113
  588.4 76.3 %all-to-all-start.9 = ((bf16[32,16,3072]{2,1,0:T(8,128)(2,1)}), bf16[32,16,3072]{2,1,0:T(8,128)(2,1)}, u32[]{:S(2)}, u32[]{:S(2)}) async-start(bf16[32,16,3072]{2,1,0:T(8,128)(2,1)} %pad_maximum_fusion.4), calls=%async_computation.9 | async-start | bytes 6291456 | tf_op jit(solution)/shard_map/all_to_all | solution.py:307
  664.7 58.4 %all-to-all-start.10 = ((bf16[8,96,1536]{2,1,0:T(8,128)(2,1)}), bf16[8,96,1536]{2,1,0:T(8,128)(2,1)S(1)}, u32[]{:S(2)}, u32[]{:S(2)}) async-start(bf16[8,96,1536]{2,1,0:T(8,128)(2,1)} %bitcast.501), calls=%async_computation.10 | async-start | bytes 4718592 | tf_op jit(solution)/shard_map/all_to_all | solution.py:307
  754.6 44.5 %all-to-all-start.11 = ((bf16[32,16,1536]{2,1,0:T(8,128)(2,1)}), bf16[32,16,1536]{2,1,0:T(8,128)(2,1)}, u32[]{:S(2)}, u32[]{:S(2)}) async-start(bf16[32,16,1536]{2,1,0:T(8,128)(2,1)} %bitcast.462), calls=%async_computation.11 | async-start | bytes 3145728 | tf_op jit(solution)/shard_map/all_to_all | solution.py:307
  765.9 22.8 %collective-permute-start.26 = (bf16[128,896]{1,0:T(8,128)(2,1)S(1)}, bf16[128,896]{1,0:T(8,128)(2,1)S(1)}, u32[]{:S(2)}, u32[]{:S(2)}) collective-permute-start(bf16[128,896]{1,0:T(8,128)(2,1)S(1)} %pad_maximum_fusion.46), channel_id=1, source_target_pairs={{0,3},{1,2},{2,1},{3,0},{4,7},{5,6},{6,5},{7,4},{8,11},{9,10},{10,... | collective-permute-start | bytes 688136 | tf_op jit(solution)/shard_map/ppermute | solution.py:241
  819.6 22.8 %collective-permute-start.29 = (bf16[192,896]{0,1:T(8,128)(2,1)S(1)}, bf16[192,896]{0,1:T(8,128)(2,1)S(1)}, u32[]{:S(2)}, u32[]{:S(2)}) collective-permute-start(bf16[192,896]{0,1:T(8,128)(2,1)S(1)} %dynamic-slice_convert_fusion), channel_id=1, source_target_pairs={{0,8},{4,12},{8,0},{12,4},{1,9},{5,13},{9,1},{13,5},{2,10},{6,14},... | collective-permute-start | bytes 1032200 | tf_op jit(solution)/shard_map/ppermute | solution.py:262
  885.4 21.9 %collective-permute-start.30 = (bf16[192,896]{0,1:T(8,128)(2,1)S(1)}, bf16[192,896]{0,1:T(8,128)(2,1)S(1)}, u32[]{:S(2)}, u32[]{:S(2)}) collective-permute-start(bf16[192,896]{0,1:T(8,128)(2,1)S(1)} %add_convert_fusion), channel_id=1, source_target_pairs={{0,8},{4,12},{8,0},{12,4},{1,9},{5,13},{9,1},{13,5},{2,10},{6,14},... | collective-permute-start | bytes 1032200 | tf_op jit(solution)/shard_map/ppermute | solution.py:269
  925.8 110.5 %all-to-all-start.13 = ((bf16[8,192,1536]{2,1,0:T(8,128)(2,1)}), bf16[8,192,1536]{2,1,0:T(8,128)(2,1)}, u32[]{:S(2)}, u32[]{:S(2)}) async-start(bf16[8,192,1536]{2,1,0:T(8,128)(2,1)} %bitcast.469), calls=%async_computation.13 | async-start | bytes 9437184 | tf_op jit(solution)/shard_map/all_to_all | solution.py:307
  952.5 30.6 %collective-permute-start.38 = (bf16[128,384]{1,0:T(8,128)(2,1)}, bf16[128,384]{1,0:T(8,128)(2,1)}, u32[]{:S(2)}, u32[]{:S(2)}) collective-permute-start(bf16[128,384]{1,0:T(8,128)(2,1)} %get-tuple-element.225), channel_id=1, source_target_pairs={{0,3},{1,2},{2,1},{3,0},{4,7},{5,6},{6,5},{7,4},{8,11},{9,10},{10,... | collective-permute-start | bytes 294920 | tf_op jit(solution)/shard_map/ppermute | solution.py:241
  954.0 29.0 %collective-permute-start.37 = (bf16[128,384]{1,0:T(8,128)(2,1)}, bf16[128,384]{1,0:T(8,128)(2,1)}, u32[]{:S(2)}, u32[]{:S(2)}) collective-permute-start(bf16[128,384]{1,0:T(8,128)(2,1)} %get-tuple-element.226), channel_id=1, source_target_pairs={{0,1},{1,0},{2,3},{3,2},{4,5},{5,4},{6,7},{7,6},{8,9},{9,8},{10,11... | collective-permute-start | bytes 294920 | tf_op jit(solution)/shard_map/ppermute | solution.py:241
  955.0 28.1 %collective-permute-start.36 = (bf16[128,384]{1,0:T(8,128)(2,1)}, bf16[128,384]{1,0:T(8,128)(2,1)}, u32[]{:S(2)}, u32[]{:S(2)}) collective-permute-start(bf16[128,384]{1,0:T(8,128)(2,1)} %get-tuple-element.227), channel_id=1, source_target_pairs={{0,2},{1,3},{2,0},{3,1},{4,6},{5,7},{6,4},{7,5},{8,10},{9,11},{10,... | collective-permute-start | bytes 294920 | tf_op jit(solution)/shard_map/ppermute | solution.py:241
  979.7 31.5 %collective-permute-start.35 = (bf16[2,1,384,896]{2,3,1,0:T(8,128)(2,1)}, bf16[2,1,384,896]{2,3,1,0:T(8,128)(2,1)}, u32[]{:S(2)}, u32[]{:S(2)}) collective-permute-start(bf16[2,1,384,896]{2,3,1,0:T(8,128)(2,1)} %pad_maximum_fusion.17), channel_id=1, source_target_pairs={{0,1},{1,0},{2,3},{3,2},{4,5},{5,4},{6,7},{7,6},{8,9},{9,8},{10,11... | collective-permute-start | bytes 4128776 | tf_op jit(solution)/shard_map/ppermute | solution.py:285
  981.8 37.4 %collective-permute-start.33 = (bf16[1,2,384,896]{2,3,1,0:T(8,128)(2,1)}, bf16[1,2,384,896]{2,3,1,0:T(8,128)(2,1)}, u32[]{:S(2)}, u32[]{:S(2)}) collective-permute-start(bf16[1,2,384,896]{2,3,1,0:T(8,128)(2,1)} %pad_maximum_fusion.16), channel_id=1, source_target_pairs={{0,2},{1,3},{2,0},{3,1},{4,6},{5,7},{6,4},{7,5},{8,10},{9,11},{10,... | collective-permute-start | bytes 4128776 | tf_op jit(solution)/shard_map/ppermute | solution.py:285
  1053.7 59.2 %all-to-all-start.14 = ((bf16[8,96,1536]{2,1,0:T(8,128)(2,1)}), bf16[8,96,1536]{2,1,0:T(8,128)(2,1)}, u32[]{:S(2)}, u32[]{:S(2)}) async-start(bf16[8,96,1536]{2,1,0:T(8,128)(2,1)} %bitcast.500), calls=%async_computation.14 | async-start | bytes 4718592 | tf_op jit(solution)/shard_map/all_to_all | solution.py:307
  1118.1 18.6 %collective-permute-start.49 = (bf16[384,512]{1,0:T(8,128)(2,1)S(1)}, bf16[384,512]{1,0:T(8,128)(2,1)S(1)}, u32[]{:S(2)}, u32[]{:S(2)}) collective-permute-start(bf16[384,512]{1,0:T(8,128)(2,1)S(1)} %dynamic-slice_convert_fusion.1), channel_id=1, source_target_pairs={{0,4},{4,0},{8,12},{12,8},{1,5},{5,1},{9,13},{13,9},{2,6},{6,2},{1... | collective-permute-start | bytes 1179656 | tf_op jit(solution)/shard_map/ppermute | solution.py:262
  1136.8 20.1 %collective-permute-start.53 = (bf16[192,384]{1,0:T(8,128)(2,1)S(1)}, bf16[192,384]{1,0:T(8,128)(2,1)S(1)}, u32[]{:S(2)}, u32[]{:S(2)}) collective-permute-start(bf16[192,384]{1,0:T(8,128)(2,1)S(1)} %dynamic-slice_convert_fusion.4), channel_id=1, source_target_pairs={{0,8},{4,12},{8,0},{12,4},{1,9},{5,13},{9,1},{13,5},{2,10},{6,14},... | collective-permute-start | bytes 442376 | tf_op jit(solution)/shard_map/ppermute | solution.py:262
  1137.9 23.2 %collective-permute-start.52 = (bf16[192,512]{1,0:T(8,128)(2,1)S(1)}, bf16[192,512]{1,0:T(8,128)(2,1)S(1)}, u32[]{:S(2)}, u32[]{:S(2)}) collective-permute-start(bf16[192,512]{1,0:T(8,128)(2,1)S(1)} %dynamic-slice_convert_fusion.3), channel_id=1, source_target_pairs={{0,8},{4,12},{8,0},{12,4},{1,9},{5,13},{9,1},{13,5},{2,10},{6,14},... | collective-permute-start | bytes 589832 | tf_op jit(solution)/shard_map/ppermute | solution.py:262
  1139.3 28.1 %collective-permute-start.54 = (bf16[96,1536]{1,0:T(8,128)(2,1)S(1)}, bf16[96,1536]{1,0:T(8,128)(2,1)S(1)}, u32[]{:S(2)}, u32[]{:S(2)}) collective-permute-start(bf16[96,1536]{1,0:T(8,128)(2,1)S(1)} %convert_element_type.393), channel_id=1, source_target_pairs={{0,8},{4,12},{8,0},{12,4},{1,9},{5,13},{9,1},{13,5},{2,10},{6,14},... | collective-permute-start | bytes 884744 | tf_op jit(solution)/shard_map/ppermute | solution.py:303
  1202.2 113.4 %all-to-all-start.15 = ((bf16[8,192,1536]{2,1,0:T(8,128)(2,1)}), bf16[8,192,1536]{2,1,0:T(8,128)(2,1)}, u32[]{:S(2)}, u32[]{:S(2)}) async-start(bf16[8,192,1536]{2,1,0:T(8,128)(2,1)} %bitcast.470), calls=%async_computation.15 | async-start | bytes 9437184 | tf_op jit(solution)/shard_map/all_to_all | solution.py:307
  1209.4 63.0 %collective-permute-start.73 = (f32[128,1536]{1,0:T(8,128)S(1)}, f32[128,1536]{1,0:T(8,128)S(1)}, u32[]{:S(2)}, u32[]{:S(2)}) collective-permute-start(f32[128,1536]{1,0:T(8,128)S(1)} %convolution_add_fusion.2), channel_id=1, source_target_pairs={{0,16},{1,17},{2,18},{3,19},{4,20},{5,21},{6,22},{7,23},{8,24},{9,... | collective-permute-start | bytes 2359304 | tf_op jit(solution)/shard_map/ppermute | solution.py:635
  1210.7 80.1 %collective-permute-start.66 = (bf16[2,4,384,896]{3,2,1,0:T(8,128)(2,1)}, bf16[2,4,384,896]{3,2,1,0:T(8,128)(2,1)}, u32[]{:S(2)}, u32[]{:S(2)}) collective-permute-start(bf16[2,4,384,896]{3,2,1,0:T(8,128)(2,1)} %pad_maximum_fusion.refs_1_), channel_id=1, source_target_pairs={{0,16},{1,17},{2,18},{3,19},{4,20},{5,21},{6,22},{7,23},{8,24},{9,... | collective-permute-start | bytes 16515080 | tf_op jit(solution)/shard_map/ppermute | solution.py:699
  1221.0 21.6 %collective-permute-start.70 = (bf16[2,1,384,512]{3,2,1,0:T(8,128)(2,1)S(1)}, bf16[2,1,384,512]{3,2,1,0:T(8,128)(2,1)S(1)}, u32[]{:S(2)}, u32[]{:S(2)}) collective-permute-start(bf16[2,1,384,512]{3,2,1,0:T(8,128)(2,1)S(1)} %pad_maximum_fusion.27), channel_id=1, source_target_pairs={{0,1},{1,0},{2,3},{3,2},{4,5},{5,4},{6,7},{7,6},{8,9},{9,8},{10,11... | collective-permute-start | bytes 2359304 | tf_op jit(solution)/shard_map/ppermute | solution.py:285
  1225.8 51.5 %collective-permute-start.72 = (f32[128,1536]{1,0:T(8,128)S(1)}, f32[128,1536]{1,0:T(8,128)S(1)}, u32[]{:S(2)}, u32[]{:S(2)}) collective-permute-start(f32[128,1536]{1,0:T(8,128)S(1)} %fusion.66), channel_id=1, source_target_pairs={{16,0},{17,1},{18,2},{19,3},{20,4},{21,5},{22,6},{23,7},{24,8},{25... | collective-permute-start | bytes 2359304 | tf_op jit(solution)/shard_map/ppermute | solution.py:716
  1236.3 19.5 %collective-permute-start.68 = (bf16[1,2,384,512]{3,2,1,0:T(8,128)(2,1)S(1)}, bf16[1,2,384,512]{3,2,1,0:T(8,128)(2,1)S(1)}, u32[]{:S(2)}, u32[]{:S(2)}) collective-permute-start(bf16[1,2,384,512]{3,2,1,0:T(8,128)(2,1)S(1)} %pad_maximum_fusion.26), channel_id=1, source_target_pairs={{0,2},{1,3},{2,0},{3,1},{4,6},{5,7},{6,4},{7,5},{8,10},{9,11},{10,... | collective-permute-start | bytes 2359304 | tf_op jit(solution)/shard_map/ppermute | solution.py:285
  1257.6 44.1 %collective-permute-start.71 = (bf16[2,4,384,512]{3,2,1,0:T(8,128)(2,1)S(1)}, bf16[2,4,384,512]{3,2,1,0:T(8,128)(2,1)S(1)}, u32[]{:S(2)}, u32[]{:S(2)}) collective-permute-start(bf16[2,4,384,512]{3,2,1,0:T(8,128)(2,1)S(1)} %pad_maximum_fusion.5.refs_0_), channel_id=1, source_target_pairs={{16,0},{17,1},{18,2},{19,3},{20,4},{21,5},{22,6},{23,7},{24,8},{25... | collective-permute-start | bytes 9437192 | tf_op jit(solution)/shard_map/ppermute | solution.py:706
  1281.6 37.0 %collective-permute-start.75 = (bf16[8,192,1536]{2,1,0:T(8,128)(2,1)}, bf16[8,192,1536]{2,1,0:T(8,128)(2,1)}, u32[]{:S(2)}, u32[]{:S(2)}) collective-permute-start(bf16[8,192,1536]{2,1,0:T(8,128)(2,1)} %all-to-all-done.13.refs_1_), channel_id=1, source_target_pairs={{0,16},{1,17},{2,18},{3,19},{4,20},{5,21},{6,22},{7,23},{8,24},{9,... | collective-permute-start | bytes 14155784 | tf_op jit(solution)/shard_map/ppermute | solution.py:159
  (228 other events, 2496.6 us)

commit v4 on v3

--- a/solution.py
+++ b/solution.py
@@ -165,7 +165,7 @@
 
 
 def dense_home(homes, offsets, width, out_widths):
-    parts, groups, rows, _ = homes[0].shape
+    parts, groups, rows, _ = homes[1].shape
     block = rows // 2
 
     def pick(k, where):
@@ -299,8 +299,27 @@
     return group_join(parts)
 
 
-def small_step(partial, axis, flip):
-    return partial + lax.ppermute(partial.astype(BF), axis, partners(axis, flip)).astype(F32)
+def small_sum(mine, others):
+    total = mine + swapped(others.astype(BF)).astype(F32)
+    for flip in flips("expert"):
+        total = total + lax.ppermute(
+            total.astype(BF), "expert", partners("expert", flip)
+        ).astype(F32)
+    return total
+
+
+def with_small(partial, small):
+    width = partial.shape[1]
+    share = lax.dynamic_slice_in_dim(small, lax.axis_index("expert") * width, width, 1)
+    share = jnp.pad(share, ((0, -small.shape[0] % 64), (0, 0)))
+    halves = [jnp.split(a, 2, 0) for a in (partial, share)]
+    return jnp.concatenate([a[k] for k in range(2) for a in halves], 0)
+
+
+def small_of(total, rows):
+    first = total.shape[2] - (rows + -rows % 64) // 2
+    part = jnp.transpose(total[:, :, first:], (0, 2, 1, 3))
+    return part.reshape(-1, part.shape[2] * part.shape[3])[:rows].astype(F32)
 
 
 def exchange(rows, axes):
@@ -681,17 +700,18 @@
     earlier = attention_backward(
         first, grad, grad_router, grad_hidden, dense_sets[0], hook
     )
-    smalls = jnp.concatenate([earlier.small, later.small], 0)
-    for axis in ("section", "expert"):
-        for flip in flips(axis):
-            smalls = small_step(smalls, axis, flip)
+    smalls = small_sum(
+        jnp.where(is_first, earlier.small, later.small),
+        jnp.where(is_first, later.small, earlier.small),
+    )
     qkv_total = dense_partial([early_first[0]], late_operands([earlier.qkv]))
     qkv_total, smalls, down_part, out_total = tie(qkv_total, smalls, kept.down0, kept.out)
+    small_rows = smalls.shape[0]
+    out_total = with_small(out_total, smalls)
     for flip in flips("dp"):
         qkv_total = dense_rows_step(qkv_total, flip)
         out_total = dense_rows_step(out_total, flip)
-        smalls = small_step(smalls, "dp", flip)
-        qkv_total, out_total, smalls = tie(qkv_total, out_total, smalls)
+        qkv_total, out_total = tie(qkv_total, out_total)
     qkv_total, out_total = dense_line(qkv_total.astype(BF)), dense_line(out_total.astype(BF))
     qkv_total, out_total, gate_up_grad = tie(qkv_total, out_total, first_grads[0])
     gate_up_part = expert_out(gate_up_grad, experts)
@@ -699,6 +719,7 @@
     second_other = lax.ppermute(second_total, "section", UP)
     down_total = expert_home(two_homes(down_part, kept.down1))
     out_total = dense_groups(out_total)
+    small = small_of(out_total, small_rows)
     out_other = lax.ppermute(out_total, "section", DOWN)
     homes = (out_total, second_total, out_other, second_other)
     out = dense_home(homes, [0] * 4, width, [w_out.shape[2]])[0]
@@ -711,14 +732,13 @@
         qkv_total.shape[3],
         [w_query.shape[2], w_key.shape[2], w_value.shape[2]],
     )
-    small = jnp.where(is_first, *jnp.split(smalls, 2, 0))
     grad = earlier.input
     grad_other = lax.ppermute(grad, "section", DOWN)
     edge_out = jnp.where(
         is_first, jnp.stack([grad, grad_other]), jnp.stack([top_other, top])
     )[None, :, None]
-    gate_up_part, down_total, out, query, key, value, edge_out = tie(
-        gate_up_part, down_total, out, query, key, value, edge_out
+    gate_up_part, down_total, out, query, key, value, edge_out, small = tie(
+        gate_up_part, down_total, out, query, key, value, edge_out, small
     )
     expert_total = expert_home(two_homes(gate_up_part, kept.gate_up1), 2) + down_total
     dense_out = (

time: 1350 us -> 1340 us (level)
  waiting for transfers between devices: 687 us -> 660 us
    ppermute x5 -> x2, waiting for transfers between devices: 20.3 us -> 0.9 us  [small_sum(): lax.ppermute(total.astype(BF), 'expert', partners('expert', flip))]
  transfers between devices with their start and end apart: 90 -> 88, of which waited for: 52 -> 52; matrix products, arithmetic and copies ran while one was open for 20% -> 21% of each run, Pallas kernels for 2% -> 2%
where the time goes in v4:
time: 1340 us; the launch traced here: 1330 us
  waiting for transfers between devices  660 us (49%)
  matrix products  167 us (12%)
  starting transfers between devices  153 us (11%)
  blocking collectives  119 us (9%)
  other arithmetic  105 us (8%)
  local copies, waits for them, and re-layouts  81.1 us (6%)
  Pallas kernels  43.5 us (3%)
    all_to_all x14, waiting for transfers between devices, exchange(): return lax.all_to_all(rows, axes, split_axis=0, concat_axis=0, tiled=True)  327 us
    all_to_all x2, blocking collectives, exchange(): return lax.all_to_all(rows, axes, split_axis=0, concat_axis=0, tiled=True)  119 us
    ppermute x8, waiting for transfers between devices, gathered(): lax.ppermute(shard, over, partners(over, flip))  107 us
    all_to_all x14, starting transfers between devices, exchange(): return lax.all_to_all(rows, axes, split_axis=0, concat_axis=0, tiled=True)  71.9 us
    ppermute x6, waiting for transfers between devices, dense_line(): others = lax.ppermute(total, 'dp', partners('dp', flip))  63.9 us
    dot_general x19, matrix products, dot_t(): lax.dot_general(left, right, (((1,), (1,)), ((), ())), preferred_element_...  57.6 us
    ppermute x12, waiting for transfers between devices, group_step(): others = lax.ppermute(part, 'expert', partners('expert', flip))  56.6 us
    dot_general x24, matrix products, dot(): return jnp.dot(left, right, preferred_element_type=F32)  53.5 us
  transfers between devices with their start and end apart: 88, of which 52 were waited for; matrix products, arithmetic and copies ran while one was open for 21% of the time, Pallas kernels for 2%

profile of v4, /device:TPU:1, one launch (start us, length us, event | category | flops | bytes accessed | tf_op | source)
XLA Modules:
  0.0 1332.3 jit_solution(18139334841519807609)
XLA Ops:
  9.2 5.6 slice_select_fusion.4
  14.8 6.4 all-to-all-start.2
  42.3 38.3 %collective-permute-done.4 = bf16[128,512]{1,0:T(8,128)(2,1)S(1)} collective-permute-done((bf16[128,512]{1,0:T(8,128)(2,1)S(1)}, bf16[128,512]{1,0:T(8,128)(2,1)S(1)}, u32[]{:S(2)}, u32[]{:S(2)}) %collective-permute-start.4) | collective-permute-done | bytes 131104 | tf_op jit(solution)/shard_map/ppermute | solution.py:113
  81.6 5.7 slice_select_fusion.2
  111.3 34.4 %all-to-all-done.1 = bf16[8,192,768]{2,1,0:T(8,128)(2,1)} async-done(((bf16[8,192,768]{2,1,0:T(8,128)(2,1)}), bf16[8,192,768]{2,1,0:T(8,128)(2,1)}, u32[]{:S(2)}, u32[]{:S(2)}) %all-to-all-start.1) | async-done | bytes 2359328 | tf_op jit(solution)/shard_map/all_to_all | solution.py:326
  149.8 5.7 slice_select_fusion
  155.4 32.6 %all-to-all-done = bf16[32,16,1536]{2,1,0:T(8,128)(2,1)S(1)} async-done(((bf16[32,16,1536]{2,1,0:T(8,128)(2,1)}), bf16[32,16,1536]{2,1,0:T(8,128)(2,1)S(1)}, u32[]{:S(2)}, u32[]{:S(2)}) %all-to-all-start) | async-done | bytes 1572896 | tf_op jit(solution)/shard_map/all_to_all | solution.py:326
  202.4 45.2 %all-to-all-done.3 = bf16[8,96,1536]{2,1,0:T(8,128)(2,1)} async-done(((bf16[8,96,1536]{2,1,0:T(8,128)(2,1)}), bf16[8,96,1536]{2,1,0:T(8,128)(2,1)}, u32[]{:S(2)}, u32[]{:S(2)}) %all-to-all-start.3) | async-done | bytes 2359328 | tf_op jit(solution)/shard_map/all_to_all | solution.py:326
  261.7 32.0 %all-to-all-done.4 = bf16[32,16,1536]{2,1,0:T(8,128)(2,1)S(1)} async-done(((bf16[32,16,1536]{2,1,0:T(8,128)(2,1)}), bf16[32,16,1536]{2,1,0:T(8,128)(2,1)S(1)}, u32[]{:S(2)}, u32[]{:S(2)}) %all-to-all-start.4) | async-done | bytes 1572896 | tf_op jit(solution)/shard_map/all_to_all | solution.py:326
  303.3 18.0 %collective-permute-done.14 = bf16[2,1,2,128,768]{4,3,2,1,0:T(8,128)(2,1)S(1)} collective-permute-done((bf16[2,1,2,128,768]{4,3,2,1,0:T(8,128)(2,1)S(1)}, bf16[2,1,2,128,768]{4,3,2,1,0:T(8,128)(2,1)S(1)}, u32[]{:S(2)}, u32[]{:S(2)}) %collective-permute-start.14) | collective-permute-done | bytes 786464 | tf_op jit(solution)/shard_map/ppermute | solution.py:113
  325.2 34.2 %collective-permute-done.17 = bf16[128,512]{1,0:T(8,128)(2,1)S(1)} collective-permute-done((bf16[128,512]{1,0:T(8,128)(2,1)S(1)}, bf16[128,512]{1,0:T(8,128)(2,1)S(1)}, u32[]{:S(2)}, u32[]{:S(2)}) %collective-permute-start.17) | collective-permute-done | bytes 131104 | tf_op jit(solution)/shard_map/ppermute | solution.py:113
  372.5 6.2 all-to-all-start.8
  391.5 41.1 %all-to-all-done.8 = bf16[8,96,1536]{2,1,0:T(8,128)(2,1)} async-done(((bf16[8,96,1536]{2,1,0:T(8,128)(2,1)}), bf16[8,96,1536]{2,1,0:T(8,128)(2,1)}, u32[]{:S(2)}, u32[]{:S(2)}) %all-to-all-start.8) | async-done | bytes 2359328 | tf_op jit(solution)/shard_map/all_to_all | solution.py:326
  432.6 76.2 %all_to_all.80 = bf16[32,16,3072]{2,1,0:T(8,128)(2,1)} all-to-all(bf16[32,16,3072]{2,1,0:T(8,128)(2,1)} %pad_maximum_fusion.2), channel_id=1, replica_groups=mesh['section'=2,'dp'=4,'expert'=4] {'expert','dp','section'}, dimensions={0} | all-to-all | bytes 6291456 | tf_op jit(solution)/shard_map/all_to_all | solution.py:326
  520.8 14.6 %collective-permute-done.20 = bf16[2,1,2,128,768]{4,3,2,1,0:T(8,128)(2,1)S(1)} collective-permute-done((bf16[2,1,2,128,768]{4,3,2,1,0:T(8,128)(2,1)S(1)}, bf16[2,1,2,128,768]{4,3,2,1,0:T(8,128)(2,1)S(1)}, u32[]{:S(2)}, u32[]{:S(2)}) %collective-permute-start.20) | collective-permute-done | bytes 786464 | tf_op jit(solution)/shard_map/ppermute | solution.py:113
  541.1 26.9 %all-to-all-done.7 = bf16[8,192,768]{2,1,0:T(8,128)(2,1)} async-done(((bf16[8,192,768]{2,1,0:T(8,128)(2,1)}), bf16[8,192,768]{2,1,0:T(8,128)(2,1)}, u32[]{:S(2)}, u32[]{:S(2)}) %all-to-all-start.7) | async-done | bytes 2359328 | tf_op jit(solution)/shard_map/all_to_all | solution.py:326
  601.2 63.6 %all-to-all-done.9 = bf16[32,16,3072]{2,1,0:T(8,128)(2,1)} async-done(((bf16[32,16,3072]{2,1,0:T(8,128)(2,1)}), bf16[32,16,3072]{2,1,0:T(8,128)(2,1)}, u32[]{:S(2)}, u32[]{:S(2)}) %all-to-all-start.9) | async-done | bytes 3145760 | tf_op jit(solution)/shard_map/all_to_all | solution.py:326
  696.9 26.3 %all-to-all-done.10.refs_1_ = bf16[8,96,1536]{2,1,0:T(8,128)(2,1)S(1)} async-done(((bf16[8,96,1536]{2,1,0:T(8,128)(2,1)}), bf16[8,96,1536]{2,1,0:T(8,128)(2,1)S(1)}, u32[]{:S(2)}, u32[]{:S(2)}) %all-to-all-start.10) | async-done | bytes 2359328 | tf_op jit(solution)/shard_map/all_to_all | solution.py:326
  724.2 6.9 collective-permute-done.22
  754.6 6.2 all-to-all-start.11
  766.1 13.3 collective-permute-done.24
  779.4 9.3 collective-permute-done.26
  812.5 6.9 collective-permute-done.28
  824.7 17.9 %collective-permute-done.29 = bf16[192,896]{0,1:T(8,128)(2,1)S(1)} collective-permute-done((bf16[192,896]{0,1:T(8,128)(2,1)S(1)}, bf16[192,896]{0,1:T(8,128)(2,1)S(1)}, u32[]{:S(2)}, u32[]{:S(2)}) %collective-permute-start.29) | collective-permute-done | bytes 344096 | tf_op jit(solution)/shard_map/ppermute | solution.py:262
  842.9 42.6 %all_to_all.81 = bf16[32,16,1536]{2,1,0:T(8,128)(2,1)} all-to-all(bf16[32,16,1536]{2,1,0:T(8,128)(2,1)S(1)} %bitcast.517), channel_id=1, replica_groups=mesh['section'=2,'dp'=4,'expert'=4] {'expert','dp','section'}, dimensions={0} | all-to-all | bytes 3145728 | tf_op jit(solution)/shard_map/all_to_all | solution.py:326
  885.4 21.9 %collective-permute-done.30 = bf16[192,896]{0,1:T(8,128)(2,1)S(1)} collective-permute-done((bf16[192,896]{0,1:T(8,128)(2,1)S(1)}, bf16[192,896]{0,1:T(8,128)(2,1)S(1)}, u32[]{:S(2)}, u32[]{:S(2)}) %collective-permute-start.30) | collective-permute-done | bytes 344096 | tf_op jit(solution)/shard_map/ppermute | solution.py:269
  907.7 16.5 %collective-permute-done.31 = bf16[384,896]{0,1:T(8,128)(2,1)S(1)} collective-permute-done((bf16[384,896]{0,1:T(8,128)(2,1)S(1)}, bf16[384,896]{0,1:T(8,128)(2,1)S(1)}, u32[]{:S(2)}, u32[]{:S(2)}) %collective-permute-start.31) | collective-permute-done | bytes 688160 | tf_op jit(solution)/shard_map/ppermute | solution.py:269
  925.8 6.0 all-to-all-start.13
  939.5 6.2 convolution_convert_fusion.10
  962.6 9.8 collective-permute-done.32
  991.7 16.5 %collective-permute-done.35 = bf16[2,1,384,896]{2,3,1,0:T(8,128)(2,1)} collective-permute-done((bf16[2,1,384,896]{2,3,1,0:T(8,128)(2,1)}, bf16[2,1,384,896]{2,3,1,0:T(8,128)(2,1)}, u32[]{:S(2)}, u32[]{:S(2)}) %collective-permute-start.35) | collective-permute-done | bytes 1376288 | tf_op jit(solution)/shard_map/ppermute | solution.py:285
  1030.2 6.1 all-to-all-done.13.refs_1_
  1054.6 5.7 all-to-all-start.14
  1064.6 7.2 fusion.70
  1097.3 16.9 %all-to-all-done.14.refs_0_ = bf16[8,96,1536]{2,1,0:T(8,128)(2,1)} async-done(((bf16[8,96,1536]{2,1,0:T(8,128)(2,1)}), bf16[8,96,1536]{2,1,0:T(8,128)(2,1)}, u32[]{:S(2)}, u32[]{:S(2)}) %all-to-all-start.14) | async-done | bytes 2359328 | tf_op jit(solution)/shard_map/all_to_all | solution.py:326
  1128.9 7.2 collective-permute-done.49
  1142.6 11.1 collective-permute-done.52
  1161.3 11.8 collective-permute-done.55
  1185.2 7.4 collective-permute-done.54
  1220.7 10.0 collective-permute-start.70
  1232.8 15.3 %collective-permute-done.68 = bf16[2,1,384,512]{3,2,1,0:T(8,128)(2,1)S(1)} collective-permute-done((bf16[2,1,384,512]{3,2,1,0:T(8,128)(2,1)S(1)}, bf16[2,1,384,512]{3,2,1,0:T(8,128)(2,1)S(1)}, u32[]{:S(2)}, u32[]{:S(2)}) %collective-permute-start.68) | collective-permute-done | bytes 786464 | tf_op jit(solution)/shard_map/ppermute | solution.py:285
  1250.2 8.3 collective-permute-start.69
  1261.4 6.7 collective-permute-start.63
  1277.2 7.8 shard_map.239
  1285.0 11.1 shard_map.240
  1296.0 12.3 shard_map.241
  1311.2 6.1 collective-permute-done.72.refs_2_
  1319.5 12.3 shard_map.242
  (773 shorter events, 471.9 us)
Async XLA Ops:
  4.7 26.5 %collective-permute-start.7 = (s32[5,128]{1,0:T(8,128)}, s32[5,128]{1,0:T(8,128)S(1)}, u32[]{:S(2)}, u32[]{:S(2)}) collective-permute-start(s32[5,128]{1,0:T(8,128)} %select_bitcast_fusion.1), channel_id=1, source_target_pairs={{0,16},{16,0},{1,17},{17,1},{2,18},{18,2},{3,19},{19,3},{4,20},{20... | collective-permute-start | bytes 7688 | tf_op jit(solution)/shard_map/ppermute | solution.py:90
  5.8 27.2 %collective-permute-start.1 = (f32[1536]{0:T(1024)}, f32[1536]{0:T(1024)}, u32[]{:S(2)}, u32[]{:S(2)}) collective-permute-start(f32[1536]{0:T(1024)} %reduce), channel_id=1, source_target_pairs={{0,16},{16,0},{1,17},{17,1},{2,18},{18,2},{3,19},{19,3},{4,20},{20... | collective-permute-start | bytes 18440 | tf_op jit(solution)/shard_map/ppermute | solution.py:90
  6.7 28.3 %collective-permute-start = (bf16[128,1536]{1,0:T(8,128)(2,1)}, bf16[128,1536]{1,0:T(8,128)(2,1)S(1)}, u32[]{:S(2)}, u32[]{:S(2)}) collective-permute-start(bf16[128,1536]{1,0:T(8,128)(2,1)} %select_bitcast_fusion), channel_id=1, source_target_pairs={{0,16},{16,0},{1,17},{17,1},{2,18},{18,2},{3,19},{19,3},{4,20},{20... | collective-permute-start | bytes 1179656 | tf_op jit(solution)/shard_map/ppermute | solution.py:90
  7.1 30.1 %collective-permute-start.3 = (bf16[1536,256]{1,0:T(8,128)(2,1)S(1)}, bf16[1536,256]{1,0:T(8,128)(2,1)S(1)}, u32[]{:S(2)}, u32[]{:S(2)}) collective-permute-start(bf16[1536,256]{1,0:T(8,128)(2,1)S(1)} %bitcast.505), channel_id=1, source_target_pairs={{0,16},{16,0},{1,17},{17,1},{2,18},{18,2},{3,19},{19,3},{4,20},{20... | collective-permute-start | bytes 2359304 | tf_op jit(solution)/shard_map/ppermute | solution.py:90
  9.0 86.0 %collective-permute-start.6 = (bf16[1536,1536]{1,0:T(8,128)(2,1)}, bf16[1536,1536]{1,0:T(8,128)(2,1)}, u32[]{:S(2)}, u32[]{:S(2)}) collective-permute-start(bf16[1536,1536]{1,0:T(8,128)(2,1)} %bitcast.477), channel_id=1, source_target_pairs={{0,16},{16,0},{1,17},{17,1},{2,18},{18,2},{3,19},{19,3},{4,20},{20... | collective-permute-start | bytes 14155784 | tf_op jit(solution)/shard_map/ppermute | solution.py:90
  14.8 72.5 %all-to-all-start.2 = ((bf16[8,192,768]{2,1,0:T(8,128)(2,1)}), bf16[8,192,768]{2,1,0:T(8,128)(2,1)}, u32[]{:S(2)}, u32[]{:S(2)}) async-start(bf16[8,192,768]{2,1,0:T(8,128)(2,1)} %get-tuple-element.149), calls=%async_computation.2 | async-start | bytes 4718592 | tf_op jit(solution)/shard_map/all_to_all | solution.py:326
  31.2 50.3 %collective-permute-start.10 = (bf16[8,192,768]{2,1,0:T(8,128)(2,1)}, bf16[8,192,768]{2,1,0:T(8,128)(2,1)}, u32[]{:S(2)}, u32[]{:S(2)}) collective-permute-start(bf16[8,192,768]{2,1,0:T(8,128)(2,1)} %dynamic-slice_bitcast_fusion.2), channel_id=1, source_target_pairs={{0,16},{16,0},{1,17},{17,1},{2,18},{18,2},{3,19},{19,3},{4,20},{20... | collective-permute-start | bytes 7077896 | tf_op jit(solution)/shard_map/ppermute | solution.py:90
  35.7 68.5 %collective-permute-start.8 = (bf16[1536,1536]{1,0:T(8,128)(2,1)}, bf16[1536,1536]{1,0:T(8,128)(2,1)}, u32[]{:S(2)}, u32[]{:S(2)}) collective-permute-start(bf16[1536,1536]{1,0:T(8,128)(2,1)} %bitcast.455), channel_id=1, source_target_pairs={{0,16},{16,0},{1,17},{17,1},{2,18},{18,2},{3,19},{19,3},{4,20},{20... | collective-permute-start | bytes 14155784 | tf_op jit(solution)/shard_map/ppermute | solution.py:90
  37.3 54.5 %collective-permute-start.9 = (f32[1536]{0:T(1024)}, f32[1536]{0:T(1024)}, u32[]{:S(2)}, u32[]{:S(2)}) collective-permute-start(f32[1536]{0:T(1024)} %reduce.1), channel_id=1, source_target_pairs={{0,16},{16,0},{1,17},{17,1},{2,18},{18,2},{3,19},{19,3},{4,20},{20... | collective-permute-start | bytes 18440 | tf_op jit(solution)/shard_map/ppermute | solution.py:90
  38.6 42.1 %collective-permute-start.4 = (bf16[128,512]{1,0:T(8,128)(2,1)S(1)}, bf16[128,512]{1,0:T(8,128)(2,1)S(1)}, u32[]{:S(2)}, u32[]{:S(2)}) collective-permute-start(bf16[128,512]{1,0:T(8,128)(2,1)S(1)} %pad_maximum_fusion.47), channel_id=1, source_target_pairs={{0,8},{4,12},{8,0},{12,4},{1,9},{5,13},{9,1},{13,5},{2,10},{6,14},... | collective-permute-start | bytes 393224 | tf_op jit(solution)/shard_map/ppermute | solution.py:113
  80.6 69.1 %collective-permute-start.12 = (bf16[8,96,1536]{2,1,0:T(8,128)(2,1)}, bf16[8,96,1536]{2,1,0:T(8,128)(2,1)}, u32[]{:S(2)}, u32[]{:S(2)}) collective-permute-start(bf16[8,96,1536]{2,1,0:T(8,128)(2,1)} %dynamic-slice_bitcast_fusion), channel_id=1, source_target_pairs={{0,16},{16,0},{1,17},{17,1},{2,18},{18,2},{3,19},{19,3},{4,20},{20... | collective-permute-start | bytes 7077896 | tf_op jit(solution)/shard_map/ppermute | solution.py:90
  87.3 58.3 %all-to-all-start.1 = ((bf16[8,192,768]{2,1,0:T(8,128)(2,1)}), bf16[8,192,768]{2,1,0:T(8,128)(2,1)}, u32[]{:S(2)}, u32[]{:S(2)}) async-start(bf16[8,192,768]{2,1,0:T(8,128)(2,1)} %get-tuple-element.146), calls=%async_computation.1 | async-start | bytes 4718592 | tf_op jit(solution)/shard_map/all_to_all | solution.py:326
  145.6 42.4 %all-to-all-start = ((bf16[32,16,1536]{2,1,0:T(8,128)(2,1)}), bf16[32,16,1536]{2,1,0:T(8,128)(2,1)S(1)}, u32[]{:S(2)}, u32[]{:S(2)}) async-start(bf16[32,16,1536]{2,1,0:T(8,128)(2,1)} %bitcast.24), calls=%async_computation | async-start | bytes 3145728 | tf_op jit(solution)/shard_map/all_to_all | solution.py:326
  188.1 59.5 %all-to-all-start.3 = ((bf16[8,96,1536]{2,1,0:T(8,128)(2,1)}), bf16[8,96,1536]{2,1,0:T(8,128)(2,1)}, u32[]{:S(2)}, u32[]{:S(2)}) async-start(bf16[8,96,1536]{2,1,0:T(8,128)(2,1)} %get-tuple-element.148), calls=%async_computation.3 | async-start | bytes 4718592 | tf_op jit(solution)/shard_map/all_to_all | solution.py:326
  252.0 41.7 %all-to-all-start.4 = ((bf16[32,16,1536]{2,1,0:T(8,128)(2,1)}), bf16[32,16,1536]{2,1,0:T(8,128)(2,1)S(1)}, u32[]{:S(2)}, u32[]{:S(2)}) async-start(bf16[32,16,1536]{2,1,0:T(8,128)(2,1)} %bitcast.516), calls=%async_computation.4 | async-start | bytes 3145728 | tf_op jit(solution)/shard_map/all_to_all | solution.py:326
  294.9 77.6 %all-to-all-start.6 = ((bf16[8,192,768]{2,1,0:T(8,128)(2,1)}), bf16[8,192,768]{2,1,0:T(8,128)(2,1)}, u32[]{:S(2)}, u32[]{:S(2)}) async-start(bf16[8,192,768]{2,1,0:T(8,128)(2,1)} %get-tuple-element.145), calls=%async_computation.6 | async-start | bytes 4718592 | tf_op jit(solution)/shard_map/all_to_all | solution.py:326
  302.1 19.2 %collective-permute-start.14 = (bf16[2,1,2,128,768]{4,3,2,1,0:T(8,128)(2,1)S(1)}, bf16[2,1,2,128,768]{4,3,2,1,0:T(8,128)(2,1)S(1)}, u32[]{:S(2)}, u32[]{:S(2)}) collective-permute-start(bf16[2,1,2,128,768]{4,3,2,1,0:T(8,128)(2,1)S(1)} %maximum_bitcast_fusion), channel_id=1, source_target_pairs={{0,2},{1,3},{2,0},{3,1},{4,6},{5,7},{6,4},{7,5},{8,10},{9,11},{10,... | collective-permute-start | bytes 2359304 | tf_op jit(solution)/shard_map/ppermute | solution.py:113
  322.7 45.8 %collective-permute-start.15 = (bf16[2,2,2,128,768]{4,3,2,1,0:T(8,128)(2,1)}, bf16[2,2,2,128,768]{4,3,2,1,0:T(8,128)(2,1)}, u32[]{:S(2)}, u32[]{:S(2)}) collective-permute-start(bf16[2,2,2,128,768]{4,3,2,1,0:T(8,128)(2,1)} %pad_maximum_fusion.10), channel_id=1, source_target_pairs={{0,1},{1,0},{2,3},{3,2},{4,5},{5,4},{6,7},{7,6},{8,9},{9,8},{10,11... | collective-permute-start | bytes 4718600 | tf_op jit(solution)/shard_map/ppermute | solution.py:113
  323.3 36.1 %collective-permute-start.17 = (bf16[128,512]{1,0:T(8,128)(2,1)S(1)}, bf16[128,512]{1,0:T(8,128)(2,1)S(1)}, u32[]{:S(2)}, u32[]{:S(2)}) collective-permute-start(bf16[128,512]{1,0:T(8,128)(2,1)S(1)} %pad_maximum_fusion.48), channel_id=1, source_target_pairs={{0,8},{4,12},{8,0},{12,4},{1,9},{5,13},{9,1},{13,5},{2,10},{6,14},... | collective-permute-start | bytes 393224 | tf_op jit(solution)/shard_map/ppermute | solution.py:113
  372.5 60.1 %all-to-all-start.8 = ((bf16[8,96,1536]{2,1,0:T(8,128)(2,1)}), bf16[8,96,1536]{2,1,0:T(8,128)(2,1)}, u32[]{:S(2)}, u32[]{:S(2)}) async-start(bf16[8,96,1536]{2,1,0:T(8,128)(2,1)} %get-tuple-element.147), calls=%async_computation.8 | async-start | bytes 4718592 | tf_op jit(solution)/shard_map/all_to_all | solution.py:326
  508.8 59.2 %all-to-all-start.7 = ((bf16[8,192,768]{2,1,0:T(8,128)(2,1)}), bf16[8,192,768]{2,1,0:T(8,128)(2,1)}, u32[]{:S(2)}, u32[]{:S(2)}) async-start(bf16[8,192,768]{2,1,0:T(8,128)(2,1)} %get-tuple-element.150), calls=%async_computation.7 | async-start | bytes 4718592 | tf_op jit(solution)/shard_map/all_to_all | solution.py:326
  516.3 19.2 %collective-permute-start.20 = (bf16[2,1,2,128,768]{4,3,2,1,0:T(8,128)(2,1)S(1)}, bf16[2,1,2,128,768]{4,3,2,1,0:T(8,128)(2,1)S(1)}, u32[]{:S(2)}, u32[]{:S(2)}) collective-permute-start(bf16[2,1,2,128,768]{4,3,2,1,0:T(8,128)(2,1)S(1)} %maximum_bitcast_fusion.1), channel_id=1, source_target_pairs={{0,2},{1,3},{2,0},{3,1},{4,6},{5,7},{6,4},{7,5},{8,10},{9,11},{10,... | collective-permute-start | bytes 2359304 | tf_op jit(solution)/shard_map/ppermute | solution.py:113
  536.8 40.0 %collective-permute-start.21 = (bf16[2,2,2,128,768]{4,3,2,1,0:T(8,128)(2,1)}, bf16[2,2,2,128,768]{4,3,2,1,0:T(8,128)(2,1)}, u32[]{:S(2)}, u32[]{:S(2)}) collective-permute-start(bf16[2,2,2,128,768]{4,3,2,1,0:T(8,128)(2,1)} %pad_maximum_fusion.11), channel_id=1, source_target_pairs={{0,1},{1,0},{2,3},{3,2},{4,5},{5,4},{6,7},{7,6},{8,9},{9,8},{10,11... | collective-permute-start | bytes 4718600 | tf_op jit(solution)/shard_map/ppermute | solution.py:113
  588.5 76.3 %all-to-all-start.9 = ((bf16[32,16,3072]{2,1,0:T(8,128)(2,1)}), bf16[32,16,3072]{2,1,0:T(8,128)(2,1)}, u32[]{:S(2)}, u32[]{:S(2)}) async-start(bf16[32,16,3072]{2,1,0:T(8,128)(2,1)} %pad_maximum_fusion.4), calls=%async_computation.9 | async-start | bytes 6291456 | tf_op jit(solution)/shard_map/all_to_all | solution.py:326
  664.8 58.4 %all-to-all-start.10 = ((bf16[8,96,1536]{2,1,0:T(8,128)(2,1)}), bf16[8,96,1536]{2,1,0:T(8,128)(2,1)S(1)}, u32[]{:S(2)}, u32[]{:S(2)}) async-start(bf16[8,96,1536]{2,1,0:T(8,128)(2,1)} %bitcast.508), calls=%async_computation.10 | async-start | bytes 4718592 | tf_op jit(solution)/shard_map/all_to_all | solution.py:326
  754.6 44.5 %all-to-all-start.11 = ((bf16[32,16,1536]{2,1,0:T(8,128)(2,1)}), bf16[32,16,1536]{2,1,0:T(8,128)(2,1)}, u32[]{:S(2)}, u32[]{:S(2)}) async-start(bf16[32,16,1536]{2,1,0:T(8,128)(2,1)} %bitcast.471), calls=%async_computation.11 | async-start | bytes 3145728 | tf_op jit(solution)/shard_map/all_to_all | solution.py:326
  765.9 22.8 %collective-permute-start.26 = (bf16[128,896]{1,0:T(8,128)(2,1)S(1)}, bf16[128,896]{1,0:T(8,128)(2,1)S(1)}, u32[]{:S(2)}, u32[]{:S(2)}) collective-permute-start(bf16[128,896]{1,0:T(8,128)(2,1)S(1)} %pad_maximum_fusion.46), channel_id=1, source_target_pairs={{0,3},{1,2},{2,1},{3,0},{4,7},{5,6},{6,5},{7,4},{8,11},{9,10},{10,... | collective-permute-start | bytes 688136 | tf_op jit(solution)/shard_map/ppermute | solution.py:241
  819.7 22.9 %collective-permute-start.29 = (bf16[192,896]{0,1:T(8,128)(2,1)S(1)}, bf16[192,896]{0,1:T(8,128)(2,1)S(1)}, u32[]{:S(2)}, u32[]{:S(2)}) collective-permute-start(bf16[192,896]{0,1:T(8,128)(2,1)S(1)} %dynamic-slice_convert_fusion), channel_id=1, source_target_pairs={{0,8},{4,12},{8,0},{12,4},{1,9},{5,13},{9,1},{13,5},{2,10},{6,14},... | collective-permute-start | bytes 1032200 | tf_op jit(solution)/shard_map/ppermute | solution.py:262
  885.4 21.9 %collective-permute-start.30 = (bf16[192,896]{0,1:T(8,128)(2,1)S(1)}, bf16[192,896]{0,1:T(8,128)(2,1)S(1)}, u32[]{:S(2)}, u32[]{:S(2)}) collective-permute-start(bf16[192,896]{0,1:T(8,128)(2,1)S(1)} %add_convert_fusion), channel_id=1, source_target_pairs={{0,8},{4,12},{8,0},{12,4},{1,9},{5,13},{9,1},{13,5},{2,10},{6,14},... | collective-permute-start | bytes 1032200 | tf_op jit(solution)/shard_map/ppermute | solution.py:269
  925.8 110.5 %all-to-all-start.13 = ((bf16[8,192,1536]{2,1,0:T(8,128)(2,1)}), bf16[8,192,1536]{2,1,0:T(8,128)(2,1)}, u32[]{:S(2)}, u32[]{:S(2)}) async-start(bf16[8,192,1536]{2,1,0:T(8,128)(2,1)} %bitcast.478), calls=%async_computation.13 | async-start | bytes 9437184 | tf_op jit(solution)/shard_map/all_to_all | solution.py:326
  949.6 30.6 %collective-permute-start.38 = (bf16[128,384]{1,0:T(8,128)(2,1)}, bf16[128,384]{1,0:T(8,128)(2,1)}, u32[]{:S(2)}, u32[]{:S(2)}) collective-permute-start(bf16[128,384]{1,0:T(8,128)(2,1)} %get-tuple-element.227), channel_id=1, source_target_pairs={{0,3},{1,2},{2,1},{3,0},{4,7},{5,6},{6,5},{7,4},{8,11},{9,10},{10,... | collective-permute-start | bytes 294920 | tf_op jit(solution)/shard_map/ppermute | solution.py:241
  951.1 29.0 %collective-permute-start.37 = (bf16[128,384]{1,0:T(8,128)(2,1)}, bf16[128,384]{1,0:T(8,128)(2,1)}, u32[]{:S(2)}, u32[]{:S(2)}) collective-permute-start(bf16[128,384]{1,0:T(8,128)(2,1)} %get-tuple-element.228), channel_id=1, source_target_pairs={{0,1},{1,0},{2,3},{3,2},{4,5},{5,4},{6,7},{7,6},{8,9},{9,8},{10,11... | collective-permute-start | bytes 294920 | tf_op jit(solution)/shard_map/ppermute | solution.py:241
  952.0 28.1 %collective-permute-start.36 = (bf16[128,384]{1,0:T(8,128)(2,1)}, bf16[128,384]{1,0:T(8,128)(2,1)}, u32[]{:S(2)}, u32[]{:S(2)}) collective-permute-start(bf16[128,384]{1,0:T(8,128)(2,1)} %get-tuple-element.229), channel_id=1, source_target_pairs={{0,2},{1,3},{2,0},{3,1},{4,6},{5,7},{6,4},{7,5},{8,10},{9,11},{10,... | collective-permute-start | bytes 294920 | tf_op jit(solution)/shard_map/ppermute | solution.py:241
  954.8 17.7 %collective-permute-start.32 = (bf16[1,1,384,896]{2,3,1,0:T(8,128)(2,1)}, bf16[1,1,384,896]{2,3,1,0:T(8,128)(2,1)}, u32[]{:S(2)}, u32[]{:S(2)}) collective-permute-start(bf16[1,1,384,896]{2,3,1,0:T(8,128)(2,1)} %get-tuple-element.170), channel_id=1, source_target_pairs={{0,1},{1,0},{2,3},{3,2},{4,5},{5,4},{6,7},{7,6},{8,9},{9,8},{10,11... | collective-permute-start | bytes 2064392 | tf_op jit(solution)/shard_map/ppermute | solution.py:285
  976.7 31.5 %collective-permute-start.35 = (bf16[2,1,384,896]{2,3,1,0:T(8,128)(2,1)}, bf16[2,1,384,896]{2,3,1,0:T(8,128)(2,1)}, u32[]{:S(2)}, u32[]{:S(2)}) collective-permute-start(bf16[2,1,384,896]{2,3,1,0:T(8,128)(2,1)} %pad_maximum_fusion.17), channel_id=1, source_target_pairs={{0,1},{1,0},{2,3},{3,2},{4,5},{5,4},{6,7},{7,6},{8,9},{9,8},{10,11... | collective-permute-start | bytes 4128776 | tf_op jit(solution)/shard_map/ppermute | solution.py:285
  978.9 37.4 %collective-permute-start.33 = (bf16[1,2,384,896]{2,3,1,0:T(8,128)(2,1)}, bf16[1,2,384,896]{2,3,1,0:T(8,128)(2,1)}, u32[]{:S(2)}, u32[]{:S(2)}) collective-permute-start(bf16[1,2,384,896]{2,3,1,0:T(8,128)(2,1)} %pad_maximum_fusion.16), channel_id=1, source_target_pairs={{0,2},{1,3},{2,0},{3,1},{4,6},{5,7},{6,4},{7,5},{8,10},{9,11},{10,... | collective-permute-start | bytes 4128776 | tf_op jit(solution)/shard_map/ppermute | solution.py:285
  1054.6 59.6 %all-to-all-start.14 = ((bf16[8,96,1536]{2,1,0:T(8,128)(2,1)}), bf16[8,96,1536]{2,1,0:T(8,128)(2,1)}, u32[]{:S(2)}, u32[]{:S(2)}) async-start(bf16[8,96,1536]{2,1,0:T(8,128)(2,1)} %bitcast.507), calls=%async_computation.14 | async-start | bytes 4718592 | tf_op jit(solution)/shard_map/all_to_all | solution.py:326
  1159.0 18.4 %collective-permute-start.53 = (bf16[192,512]{1,0:T(8,128)(2,1)S(1)}, bf16[192,512]{1,0:T(8,128)(2,1)S(1)}, u32[]{:S(2)}, u32[]{:S(2)}) collective-permute-start(bf16[192,512]{1,0:T(8,128)(2,1)S(1)} %convert_add_fusion.4), channel_id=1, source_target_pairs={{0,8},{4,12},{8,0},{12,4},{1,9},{5,13},{9,1},{13,5},{2,10},{6,14},... | collective-permute-start | bytes 589832 | tf_op jit(solution)/shard_map/ppermute | solution.py:269
  1193.7 114.6 %all-to-all-start.15 = ((bf16[8,192,1536]{2,1,0:T(8,128)(2,1)}), bf16[8,192,1536]{2,1,0:T(8,128)(2,1)}, u32[]{:S(2)}, u32[]{:S(2)}) async-start(bf16[8,192,1536]{2,1,0:T(8,128)(2,1)} %bitcast.479), calls=%async_computation.15 | async-start | bytes 9437184 | tf_op jit(solution)/shard_map/all_to_all | solution.py:326
  1200.9 67.3 %collective-permute-start.71 = (f32[128,1536]{1,0:T(8,128)S(1)}, f32[128,1536]{1,0:T(8,128)S(1)}, u32[]{:S(2)}, u32[]{:S(2)}) collective-permute-start(f32[128,1536]{1,0:T(8,128)S(1)} %convolution_add_fusion.2), channel_id=1, source_target_pairs={{0,16},{1,17},{2,18},{3,19},{4,20},{5,21},{6,22},{7,23},{8,24},{9,... | collective-permute-start | bytes 2359304 | tf_op jit(solution)/shard_map/ppermute | solution.py:654
  1202.2 82.8 %collective-permute-start.64 = (bf16[2,4,384,896]{3,2,1,0:T(8,128)(2,1)}, bf16[2,4,384,896]{3,2,1,0:T(8,128)(2,1)}, u32[]{:S(2)}, u32[]{:S(2)}) collective-permute-start(bf16[2,4,384,896]{3,2,1,0:T(8,128)(2,1)} %pad_maximum_fusion.refs_1_), channel_id=1, source_target_pairs={{0,16},{1,17},{2,18},{3,19},{4,20},{5,21},{6,22},{7,23},{8,24},{9,... | collective-permute-start | bytes 16515080 | tf_op jit(solution)/shard_map/ppermute | solution.py:719
  1211.4 19.9 %collective-permute-start.62 = (bf16[2,1,416,384]{3,2,1,0:T(8,128)(2,1)S(1)}, bf16[2,1,416,384]{3,2,1,0:T(8,128)(2,1)S(1)}, u32[]{:S(2)}, u32[]{:S(2)}) collective-permute-start(bf16[2,1,416,384]{3,2,1,0:T(8,128)(2,1)S(1)} %pad_maximum_fusion.32), channel_id=1, source_target_pairs={{0,1},{1,0},{2,3},{3,2},{4,5},{5,4},{6,7},{7,6},{8,9},{9,8},{10,11... | collective-permute-start | bytes 1916936 | tf_op jit(solution)/shard_map/ppermute | solution.py:285
  1219.8 28.3 %collective-permute-start.68 = (bf16[2,1,384,512]{3,2,1,0:T(8,128)(2,1)S(1)}, bf16[2,1,384,512]{3,2,1,0:T(8,128)(2,1)S(1)}, u32[]{:S(2)}, u32[]{:S(2)}) collective-permute-start(bf16[2,1,384,512]{3,2,1,0:T(8,128)(2,1)S(1)} %pad_maximum_fusion.28), channel_id=1, source_target_pairs={{0,1},{1,0},{2,3},{3,2},{4,5},{5,4},{6,7},{7,6},{8,9},{9,8},{10,11... | collective-permute-start | bytes 2359304 | tf_op jit(solution)/shard_map/ppermute | solution.py:285
  1220.7 48.8 %collective-permute-start.70 = (f32[128,1536]{1,0:T(8,128)S(1)}, f32[128,1536]{1,0:T(8,128)S(1)}, u32[]{:S(2)}, u32[]{:S(2)}) collective-permute-start(f32[128,1536]{1,0:T(8,128)S(1)} %fusion.66), channel_id=1, source_target_pairs={{16,0},{17,1},{18,2},{19,3},{20,4},{21,5},{22,6},{23,7},{24,8},{25... | collective-permute-start | bytes 2359304 | tf_op jit(solution)/shard_map/ppermute | solution.py:736
  1231.3 18.4 %collective-permute-start.66 = (bf16[1,2,384,512]{3,2,1,0:T(8,128)(2,1)S(1)}, bf16[1,2,384,512]{3,2,1,0:T(8,128)(2,1)S(1)}, u32[]{:S(2)}, u32[]{:S(2)}) collective-permute-start(bf16[1,2,384,512]{3,2,1,0:T(8,128)(2,1)S(1)} %pad_maximum_fusion.27), channel_id=1, source_target_pairs={{0,2},{1,3},{2,0},{3,1},{4,6},{5,7},{6,4},{7,5},{8,10},{9,11},{10,... | collective-permute-start | bytes 2359304 | tf_op jit(solution)/shard_map/ppermute | solution.py:285
  1250.2 45.8 %collective-permute-start.69 = (bf16[2,4,384,512]{3,2,1,0:T(8,128)(2,1)S(1)}, bf16[2,4,384,512]{3,2,1,0:T(8,128)(2,1)}, u32[]{:S(2)}, u32[]{:S(2)}) collective-permute-start(bf16[2,4,384,512]{3,2,1,0:T(8,128)(2,1)S(1)} %pad_maximum_fusion.5.refs_0_), channel_id=1, source_target_pairs={{16,0},{17,1},{18,2},{19,3},{20,4},{21,5},{22,6},{23,7},{24,8},{25... | collective-permute-start | bytes 9437192 | tf_op jit(solution)/shard_map/ppermute | solution.py:727
  1261.4 23.6 %collective-permute-start.63 = (bf16[2,4,416,384]{3,2,1,0:T(8,128)(2,1)S(1)}, bf16[2,4,416,384]{3,2,1,0:T(8,128)(2,1)S(1)}, u32[]{:S(2)}, u32[]{:S(2)}) collective-permute-start(bf16[2,4,416,384]{3,2,1,0:T(8,128)(2,1)S(1)} %pad_maximum_fusion.6.refs_0_), channel_id=1, source_target_pairs={{16,0},{17,1},{18,2},{19,3},{20,4},{21,5},{22,6},{23,7},{24,8},{25... | collective-permute-start | bytes 7667720 | tf_op jit(solution)/shard_map/ppermute | solution.py:723
  1275.7 35.6 %collective-permute-start.73 = (bf16[8,192,1536]{2,1,0:T(8,128)(2,1)}, bf16[8,192,1536]{2,1,0:T(8,128)(2,1)}, u32[]{:S(2)}, u32[]{:S(2)}) collective-permute-start(bf16[8,192,1536]{2,1,0:T(8,128)(2,1)} %all-to-all-done.13.refs_1_), channel_id=1, source_target_pairs={{0,16},{1,17},{2,18},{3,19},{4,20},{5,21},{6,22},{7,23},{8,24},{9,... | collective-permute-start | bytes 14155784 | tf_op jit(solution)/shard_map/ppermute | solution.py:159
  (224 other events, 2444.5 us)

commit v5 on v4

--- a/solution.py
+++ b/solution.py
@@ -123,7 +123,7 @@
     return partial
 
 
-def pick_blocks(sources, blocks, pick, count, kernel, out_shapes, out_blocks):
+def pick_blocks(sources, blocks, pick, count, kernel, out_shapes, out_blocks, place=None, into=()):
     where = jnp.stack([lax.axis_index(axis) for axis in ("section", "dp")]).astype(jnp.int32)
 
     def spec(at):
@@ -133,22 +133,24 @@
         return pl.BlockSpec(blocks[at], index)
 
     def body(where, *refs):
-        kernel(pl.program_id(0), where, refs[: len(sources)], refs[len(sources) :])
+        kernel(pl.program_id(0), where, refs[: len(sources)], refs[len(sources) + len(into) :])
 
     return pl.pallas_call(
         body,
         grid_spec=pltpu.PrefetchScalarGridSpec(
             num_scalar_prefetch=1,
             grid=(count,),
-            in_specs=[spec(at) for at in range(len(sources))],
+            in_specs=[spec(at) for at in range(len(sources))]
+            + [pl.BlockSpec(memory_space=pl.ANY)] * len(into),
             out_specs=[
-                pl.BlockSpec(shape, lambda k, where: (k,) + (0,) * (len(shape) - 1))
+                pl.BlockSpec(shape, place or (lambda k, where: (k,) + (0,) * (len(shape) - 1)))
                 for shape in out_blocks
             ],
         ),
         out_shape=[jax.ShapeDtypeStruct(shape, F32) for shape in out_shapes],
+        input_output_aliases={1 + len(sources) + at: at for at in range(len(into))},
         compiler_params=pltpu.CompilerParams(vmem_limit_bytes=48 * 1024 * 1024),
-    )(where, *sources)
+    )(where, *sources, *into)
 
 
 def two_homes(first, second):
@@ -264,11 +266,14 @@
 
 
 def dense_line(total):
-    own = lax.axis_index("dp")
     for flip in reversed(flips("dp")):
-        others = lax.ppermute(total, "dp", partners("dp", flip))
-        total = in_order(total, others, own & flip, 0)
+        total = dense_line_step(total, flip)
     return total
+
+
+def dense_line_step(total, flip):
+    others = lax.ppermute(total, "dp", partners("dp", flip))
+    return in_order(total, others, lax.axis_index("dp") & flip, 0)
 
 
 def group_parts(total):
@@ -309,16 +314,16 @@
 
 
 def with_small(partial, small):
-    width = partial.shape[1]
+    width = small.shape[1] // lax.axis_size("expert")
     share = lax.dynamic_slice_in_dim(small, lax.axis_index("expert") * width, width, 1)
-    share = jnp.pad(share, ((0, -small.shape[0] % 64), (0, 0)))
+    share = jnp.pad(share, ((0, -small.shape[0] % 64), (0, partial.shape[1] - width)))
     halves = [jnp.split(a, 2, 0) for a in (partial, share)]
     return jnp.concatenate([a[k] for k in range(2) for a in halves], 0)
 
 
-def small_of(total, rows):
+def small_of(total, rows, columns):
     first = total.shape[2] - (rows + -rows % 64) // 2
-    part = jnp.transpose(total[:, :, first:], (0, 2, 1, 3))
+    part = jnp.transpose(total[:, :, first:, : columns // total.shape[1]], (0, 2, 1, 3))
     return part.reshape(-1, part.shape[2] * part.shape[3])[:rows].astype(F32)
 
 
@@ -407,6 +412,38 @@
     blocks = [(1, rows, width)] * 4
     return list(
         pick_blocks(homes, blocks, pick, experts, kernel, [shape] * count, [(1,) + shape[1:]] * count)
+    )
+
+
+def expert_rows(arrays, count, others, into=()):
+    experts, rows, width = arrays[0].shape
+    columns = width // count
+
+    def pick(k, where):
+        return [(jnp.where(where[0] == layer, k, 0), 0, 0) for layer in range(2)]
+
+    def place(k, where):
+        return (k, 1 - where[0] if others else where[0], 0)
+
+    def kernel(k, where, sources, outs):
+        for layer in range(2):
+
+            @pl.when(where[0] == layer)
+            def _():
+                for part, out in enumerate(outs):
+                    out[0] = sources[layer][0, :, part * columns : (part + 1) * columns].astype(F32)
+
+    shape = (experts, 2 * rows, columns)
+    return pick_blocks(
+        arrays,
+        [(1, rows, width)] * 2,
+        pick,
+        experts,
+        kernel,
+        [shape] * count,
+        [(1, rows, columns)] * count,
+        place,
+        into,
     )
 
 
@@ -693,6 +730,7 @@
             kept.dense = dense_groups(kept.dense)
             value = end("dense", end("out", end("gate_up1", value)))
         if name == "kv":
+            kept.out = dense_rows_step(kept.out, flips("dp")[0])
             down_grad, value, kept.out = tie(first_grads[1], value, kept.out)
             kept.down0 = expert_out(down_grad, experts)
         return value
@@ -706,24 +744,30 @@
     )
     qkv_total = dense_partial([early_first[0]], late_operands([earlier.qkv]))
     qkv_total, smalls, down_part, out_total = tie(qkv_total, smalls, kept.down0, kept.out)
-    small_rows = smalls.shape[0]
-    out_total = with_small(out_total, smalls)
-    for flip in flips("dp"):
-        qkv_total = dense_rows_step(qkv_total, flip)
-        out_total = dense_rows_step(out_total, flip)
+    small_rows, small_columns = smalls.shape
+    qkv_total = with_small(qkv_total, smalls)
+    steps = [(dense_rows_step, flip) for flip in flips("dp")]
+    steps += [(dense_line_step, flip) for flip in reversed(flips("dp"))]
+    turning = len(flips("dp"))
+    for index in range(len(steps)):
+        if index + 1 < len(steps):
+            step, flip = steps[index + 1]
+            out_total = out_total.astype(BF) if index + 1 >= turning else out_total
+            out_total = step(out_total, flip)
+        step, flip = steps[index]
+        qkv_total = step(qkv_total.astype(BF) if index >= turning else qkv_total, flip)
         qkv_total, out_total = tie(qkv_total, out_total)
-    qkv_total, out_total = dense_line(qkv_total.astype(BF)), dense_line(out_total.astype(BF))
     qkv_total, out_total, gate_up_grad = tie(qkv_total, out_total, first_grads[0])
     gate_up_part = expert_out(gate_up_grad, experts)
     second_total = kept.dense
     second_other = lax.ppermute(second_total, "section", UP)
     down_total = expert_home(two_homes(down_part, kept.down1))
     out_total = dense_groups(out_total)
-    small = small_of(out_total, small_rows)
     out_other = lax.ppermute(out_total, "section", DOWN)
     homes = (out_total, second_total, out_other, second_other)
     out = dense_home(homes, [0] * 4, width, [w_out.shape[2]])[0]
     qkv_total = dense_groups(qkv_total)
+    small = small_of(qkv_total, small_rows, small_columns)
     qkv_other = lax.ppermute(qkv_total, "section", DOWN)
     homes = (qkv_total, second_total, qkv_other, second_other)
     query, key, value = dense_home(
@@ -740,7 +784,9 @@
     gate_up_part, down_total, out, query, key, value, edge_out, small = tie(
         gate_up_part, down_total, out, query, key, value, edge_out, small
     )
-    expert_total = expert_home(two_homes(gate_up_part, kept.gate_up1), 2) + down_total
+    pair = (gate_up_part, kept.gate_up1)
+    received = two_homes(*pair)[2:]
+    expert_total = list(expert_rows(received, 2, True, expert_rows(pair, 2, False))) + down_total
     dense_out = (
         small[experts_all],
         query,

time: 1340 us -> 1320 us (0.985)
  waiting for transfers between devices: 660 us -> 639 us
    pallas_call x4 -> x5, Pallas kernels: 43.5 us -> 47.7 us  [pick_blocks(): pl.pallas_call(body, grid_spec=pltpu.PrefetchScalarGridSpec(num_scalar_pr...]
  transfers between devices with their start and end apart: 88 -> 88, of which waited for: 52 -> 47; matrix products, arithmetic and copies ran while one was open for 21% -> 22% of each run, Pallas kernels for 2% -> 3%
where the time goes in v5:
time: 1320 us; the launch traced here: 1310 us
  waiting for transfers between devices  639 us (48%)
  matrix products  165 us (12%)
  starting transfers between devices  149 us (11%)
  blocking collectives  119 us (9%)
  other arithmetic  106 us (8%)
  local copies, waits for them, and re-layouts  82.2 us (6%)
  Pallas kernels  47.7 us (4%)
    all_to_all x14, waiting for transfers between devices, exchange(): return lax.all_to_all(rows, axes, split_axis=0, concat_axis=0, tiled=True)  330 us
    all_to_all x2, blocking collectives, exchange(): return lax.all_to_all(rows, axes, split_axis=0, concat_axis=0, tiled=True)  119 us
    ppermute x8, waiting for transfers between devices, gathered(): lax.ppermute(shard, over, partners(over, flip))  107 us
    all_to_all x14, starting transfers between devices, exchange(): return lax.all_to_all(rows, axes, split_axis=0, concat_axis=0, tiled=True)  76.1 us
    dot_general x19, matrix products, dot_t(): lax.dot_general(left, right, (((1,), (1,)), ((), ())), preferred_element_...  57.5 us
    ppermute x6, waiting for transfers between devices, dense_line_step(): others = lax.ppermute(total, 'dp', partners('dp', flip))  54.6 us
    dot_general x24, matrix products, dot(): return jnp.dot(left, right, preferred_element_type=F32)  53.4 us
    ppermute x6, waiting for transfers between devices, dense_rows_step(): sent = lax.ppermute(sent.astype(BF), 'dp', partners('dp', flip))  52.3 us
  transfers between devices with their start and end apart: 88, of which 47 were waited for; matrix products, arithmetic and copies ran while one was open for 22% of the time, Pallas kernels for 3%

profile of v5, /device:TPU:1, one launch (start us, length us, event | category | flops | bytes accessed | tf_op | source)
XLA Modules:
  0.0 1312.4 jit_solution(12005939782572953242)
XLA Ops:
  9.2 5.6 slice_select_fusion.4
  14.8 6.4 all-to-all-start.2
  42.4 38.3 %collective-permute-done.4 = bf16[128,512]{1,0:T(8,128)(2,1)S(1)} collective-permute-done((bf16[128,512]{1,0:T(8,128)(2,1)S(1)}, bf16[128,512]{1,0:T(8,128)(2,1)S(1)}, u32[]{:S(2)}, u32[]{:S(2)}) %collective-permute-start.4) | collective-permute-done | bytes 131104 | tf_op jit(solution)/shard_map/ppermute | solution.py:113
  81.6 5.7 slice_select_fusion.2
  111.3 34.3 %all-to-all-done.1 = bf16[8,192,768]{2,1,0:T(8,128)(2,1)} async-done(((bf16[8,192,768]{2,1,0:T(8,128)(2,1)}), bf16[8,192,768]{2,1,0:T(8,128)(2,1)}, u32[]{:S(2)}, u32[]{:S(2)}) %all-to-all-start.1) | async-done | bytes 2359328 | tf_op jit(solution)/shard_map/all_to_all | solution.py:331
  149.8 5.7 slice_select_fusion
  155.4 32.6 %all-to-all-done = bf16[32,16,1536]{2,1,0:T(8,128)(2,1)S(1)} async-done(((bf16[32,16,1536]{2,1,0:T(8,128)(2,1)}), bf16[32,16,1536]{2,1,0:T(8,128)(2,1)S(1)}, u32[]{:S(2)}, u32[]{:S(2)}) %all-to-all-start) | async-done | bytes 1572896 | tf_op jit(solution)/shard_map/all_to_all | solution.py:331
  188.1 5.6 all-to-all-start.3
  202.4 45.2 %all-to-all-done.3 = bf16[8,96,1536]{2,1,0:T(8,128)(2,1)} async-done(((bf16[8,96,1536]{2,1,0:T(8,128)(2,1)}), bf16[8,96,1536]{2,1,0:T(8,128)(2,1)}, u32[]{:S(2)}, u32[]{:S(2)}) %all-to-all-start.3) | async-done | bytes 2359328 | tf_op jit(solution)/shard_map/all_to_all | solution.py:331
  261.7 32.0 %all-to-all-done.4 = bf16[32,16,1536]{2,1,0:T(8,128)(2,1)S(1)} async-done(((bf16[32,16,1536]{2,1,0:T(8,128)(2,1)}), bf16[32,16,1536]{2,1,0:T(8,128)(2,1)S(1)}, u32[]{:S(2)}, u32[]{:S(2)}) %all-to-all-start.4) | async-done | bytes 1572896 | tf_op jit(solution)/shard_map/all_to_all | solution.py:331
  303.3 18.0 %collective-permute-done.14 = bf16[2,1,2,128,768]{4,3,2,1,0:T(8,128)(2,1)S(1)} collective-permute-done((bf16[2,1,2,128,768]{4,3,2,1,0:T(8,128)(2,1)S(1)}, bf16[2,1,2,128,768]{4,3,2,1,0:T(8,128)(2,1)S(1)}, u32[]{:S(2)}, u32[]{:S(2)}) %collective-permute-start.14) | collective-permute-done | bytes 786464 | tf_op jit(solution)/shard_map/ppermute | solution.py:113
  325.2 34.2 %collective-permute-done.17 = bf16[128,512]{1,0:T(8,128)(2,1)S(1)} collective-permute-done((bf16[128,512]{1,0:T(8,128)(2,1)S(1)}, bf16[128,512]{1,0:T(8,128)(2,1)S(1)}, u32[]{:S(2)}, u32[]{:S(2)}) %collective-permute-start.17) | collective-permute-done | bytes 131104 | tf_op jit(solution)/shard_map/ppermute | solution.py:113
  372.4 6.2 all-to-all-start.8
  391.4 41.1 %all-to-all-done.8 = bf16[8,96,1536]{2,1,0:T(8,128)(2,1)} async-done(((bf16[8,96,1536]{2,1,0:T(8,128)(2,1)}), bf16[8,96,1536]{2,1,0:T(8,128)(2,1)}, u32[]{:S(2)}, u32[]{:S(2)}) %all-to-all-start.8) | async-done | bytes 2359328 | tf_op jit(solution)/shard_map/all_to_all | solution.py:331
  432.5 76.3 %all_to_all.80 = bf16[32,16,3072]{2,1,0:T(8,128)(2,1)} all-to-all(bf16[32,16,3072]{2,1,0:T(8,128)(2,1)} %pad_maximum_fusion.3), channel_id=1, replica_groups=mesh['section'=2,'dp'=4,'expert'=4] {'expert','dp','section'}, dimensions={0} | all-to-all | bytes 6291456 | tf_op jit(solution)/shard_map/all_to_all | solution.py:331
  520.8 14.6 %collective-permute-done.20 = bf16[2,1,2,128,768]{4,3,2,1,0:T(8,128)(2,1)S(1)} collective-permute-done((bf16[2,1,2,128,768]{4,3,2,1,0:T(8,128)(2,1)S(1)}, bf16[2,1,2,128,768]{4,3,2,1,0:T(8,128)(2,1)S(1)}, u32[]{:S(2)}, u32[]{:S(2)}) %collective-permute-start.20) | collective-permute-done | bytes 786464 | tf_op jit(solution)/shard_map/ppermute | solution.py:113
  541.1 26.9 %all-to-all-done.7 = bf16[8,192,768]{2,1,0:T(8,128)(2,1)} async-done(((bf16[8,192,768]{2,1,0:T(8,128)(2,1)}), bf16[8,192,768]{2,1,0:T(8,128)(2,1)}, u32[]{:S(2)}, u32[]{:S(2)}) %all-to-all-start.7) | async-done | bytes 2359328 | tf_op jit(solution)/shard_map/all_to_all | solution.py:331
  601.2 63.6 %all-to-all-done.9 = bf16[32,16,3072]{2,1,0:T(8,128)(2,1)} async-done(((bf16[32,16,3072]{2,1,0:T(8,128)(2,1)}), bf16[32,16,3072]{2,1,0:T(8,128)(2,1)}, u32[]{:S(2)}, u32[]{:S(2)}) %all-to-all-start.9) | async-done | bytes 3145760 | tf_op jit(solution)/shard_map/all_to_all | solution.py:331
  696.9 26.3 %all-to-all-done.10.refs_1_ = bf16[8,96,1536]{2,1,0:T(8,128)(2,1)S(1)} async-done(((bf16[8,96,1536]{2,1,0:T(8,128)(2,1)}), bf16[8,96,1536]{2,1,0:T(8,128)(2,1)S(1)}, u32[]{:S(2)}, u32[]{:S(2)}) %all-to-all-start.10) | async-done | bytes 2359328 | tf_op jit(solution)/shard_map/all_to_all | solution.py:331
  724.2 6.9 collective-permute-done.22
  754.6 6.2 all-to-all-start.11
  766.0 13.3 %collective-permute-done.24 = bf16[128,896]{1,0:T(8,128)(2,1)S(1)} collective-permute-done((bf16[128,896]{1,0:T(8,128)(2,1)S(1)}, bf16[128,896]{1,0:T(8,128)(2,1)S(1)}, u32[]{:S(2)}, u32[]{:S(2)}) %collective-permute-start.24) | collective-permute-done | bytes 229408 | tf_op jit(solution)/shard_map/ppermute | solution.py:243
  779.3 9.3 collective-permute-done.26
  812.4 6.9 collective-permute-done.28
  824.6 17.9 %collective-permute-done.29 = bf16[192,896]{0,1:T(8,128)(2,1)S(1)} collective-permute-done((bf16[192,896]{0,1:T(8,128)(2,1)S(1)}, bf16[192,896]{0,1:T(8,128)(2,1)S(1)}, u32[]{:S(2)}, u32[]{:S(2)}) %collective-permute-start.29) | collective-permute-done | bytes 344096 | tf_op jit(solution)/shard_map/ppermute | solution.py:264
  842.8 42.5 %all_to_all.81 = bf16[32,16,1536]{2,1,0:T(8,128)(2,1)} all-to-all(bf16[32,16,1536]{2,1,0:T(8,128)(2,1)S(1)} %bitcast.519), channel_id=1, replica_groups=mesh['section'=2,'dp'=4,'expert'=4] {'expert','dp','section'}, dimensions={0} | all-to-all | bytes 3145728 | tf_op jit(solution)/shard_map/all_to_all | solution.py:331
  885.4 21.9 %collective-permute-done.30 = bf16[192,896]{0,1:T(8,128)(2,1)S(1)} collective-permute-done((bf16[192,896]{0,1:T(8,128)(2,1)S(1)}, bf16[192,896]{0,1:T(8,128)(2,1)S(1)}, u32[]{:S(2)}, u32[]{:S(2)}) %collective-permute-start.30) | collective-permute-done | bytes 344096 | tf_op jit(solution)/shard_map/ppermute | solution.py:275
  907.7 16.5 %collective-permute-done.31 = bf16[384,896]{0,1:T(8,128)(2,1)S(1)} collective-permute-done((bf16[384,896]{0,1:T(8,128)(2,1)S(1)}, bf16[384,896]{0,1:T(8,128)(2,1)S(1)}, u32[]{:S(2)}, u32[]{:S(2)}) %collective-permute-start.31) | collective-permute-done | bytes 688160 | tf_op jit(solution)/shard_map/ppermute | solution.py:275
  925.8 6.0 all-to-all-start.13
  944.1 6.2 convolution_convert_fusion.10
  967.3 9.8 collective-permute-done.32
  996.5 16.5 %collective-permute-done.35 = bf16[2,1,384,896]{2,3,1,0:T(8,128)(2,1)} collective-permute-done((bf16[2,1,384,896]{2,3,1,0:T(8,128)(2,1)}, bf16[2,1,384,896]{2,3,1,0:T(8,128)(2,1)}, u32[]{:S(2)}, u32[]{:S(2)}) %collective-permute-start.35) | collective-permute-done | bytes 1376288 | tf_op jit(solution)/shard_map/ppermute | solution.py:290
  1045.5 6.8 collective-permute-done.42
  1053.9 7.1 all-to-all-start.14
  1065.2 7.2 fusion.70
  1097.6 17.3 %all-to-all-done.14.refs_0_ = bf16[8,96,1536]{2,1,0:T(8,128)(2,1)} async-done(((bf16[8,96,1536]{2,1,0:T(8,128)(2,1)}), bf16[8,96,1536]{2,1,0:T(8,128)(2,1)}, u32[]{:S(2)}, u32[]{:S(2)}) %all-to-all-start.14) | async-done | bytes 2359328 | tf_op jit(solution)/shard_map/all_to_all | solution.py:331
  1122.7 8.7 collective-permute-done.51
  1142.6 11.8 collective-permute-done.52
  1157.7 10.0 collective-permute-done.54
  1178.7 7.8 all-to-all-start.15
  1207.6 14.9 %collective-permute-done.68 = bf16[2,1,416,512]{3,2,1,0:T(8,128)(2,1)S(1)} collective-permute-done((bf16[2,1,416,512]{3,2,1,0:T(8,128)(2,1)S(1)}, bf16[2,1,416,512]{3,2,1,0:T(8,128)(2,1)S(1)}, u32[]{:S(2)}, u32[]{:S(2)}) %collective-permute-start.68) | collective-permute-done | bytes 852000 | tf_op jit(solution)/shard_map/ppermute | solution.py:290
  1225.8 7.4 collective-permute-start.69
  1251.6 7.8 shard_map.239
  1260.5 11.0 shard_map.240
  1271.5 12.3 shard_map.241
  1283.8 7.2 all-to-all-done.15.refs_0_
  1294.0 8.4 shard_map.242
  1303.7 8.2 shard_map.243
  (771 shorter events, 455.8 us)
Async XLA Ops:
  4.7 26.5 %collective-permute-start.7 = (s32[5,128]{1,0:T(8,128)}, s32[5,128]{1,0:T(8,128)S(1)}, u32[]{:S(2)}, u32[]{:S(2)}) collective-permute-start(s32[5,128]{1,0:T(8,128)} %select_bitcast_fusion.1), channel_id=1, source_target_pairs={{0,16},{16,0},{1,17},{17,1},{2,18},{18,2},{3,19},{19,3},{4,20},{20... | collective-permute-start | bytes 7688 | tf_op jit(solution)/shard_map/ppermute | solution.py:90
  5.8 27.2 %collective-permute-start.1 = (f32[1536]{0:T(1024)}, f32[1536]{0:T(1024)}, u32[]{:S(2)}, u32[]{:S(2)}) collective-permute-start(f32[1536]{0:T(1024)} %reduce), channel_id=1, source_target_pairs={{0,16},{16,0},{1,17},{17,1},{2,18},{18,2},{3,19},{19,3},{4,20},{20... | collective-permute-start | bytes 18440 | tf_op jit(solution)/shard_map/ppermute | solution.py:90
  6.7 28.3 %collective-permute-start = (bf16[128,1536]{1,0:T(8,128)(2,1)}, bf16[128,1536]{1,0:T(8,128)(2,1)S(1)}, u32[]{:S(2)}, u32[]{:S(2)}) collective-permute-start(bf16[128,1536]{1,0:T(8,128)(2,1)} %select_bitcast_fusion), channel_id=1, source_target_pairs={{0,16},{16,0},{1,17},{17,1},{2,18},{18,2},{3,19},{19,3},{4,20},{20... | collective-permute-start | bytes 1179656 | tf_op jit(solution)/shard_map/ppermute | solution.py:90
  7.1 30.1 %collective-permute-start.3 = (bf16[1536,256]{1,0:T(8,128)(2,1)S(1)}, bf16[1536,256]{1,0:T(8,128)(2,1)S(1)}, u32[]{:S(2)}, u32[]{:S(2)}) collective-permute-start(bf16[1536,256]{1,0:T(8,128)(2,1)S(1)} %bitcast.507), channel_id=1, source_target_pairs={{0,16},{16,0},{1,17},{17,1},{2,18},{18,2},{3,19},{19,3},{4,20},{20... | collective-permute-start | bytes 2359304 | tf_op jit(solution)/shard_map/ppermute | solution.py:90
  9.0 86.0 %collective-permute-start.6 = (bf16[1536,1536]{1,0:T(8,128)(2,1)}, bf16[1536,1536]{1,0:T(8,128)(2,1)}, u32[]{:S(2)}, u32[]{:S(2)}) collective-permute-start(bf16[1536,1536]{1,0:T(8,128)(2,1)} %bitcast.477), channel_id=1, source_target_pairs={{0,16},{16,0},{1,17},{17,1},{2,18},{18,2},{3,19},{19,3},{4,20},{20... | collective-permute-start | bytes 14155784 | tf_op jit(solution)/shard_map/ppermute | solution.py:90
  14.8 72.5 %all-to-all-start.2 = ((bf16[8,192,768]{2,1,0:T(8,128)(2,1)}), bf16[8,192,768]{2,1,0:T(8,128)(2,1)}, u32[]{:S(2)}, u32[]{:S(2)}) async-start(bf16[8,192,768]{2,1,0:T(8,128)(2,1)} %get-tuple-element.161), calls=%async_computation.2 | async-start | bytes 4718592 | tf_op jit(solution)/shard_map/all_to_all | solution.py:331
  31.2 50.3 %collective-permute-start.10 = (bf16[8,192,768]{2,1,0:T(8,128)(2,1)}, bf16[8,192,768]{2,1,0:T(8,128)(2,1)}, u32[]{:S(2)}, u32[]{:S(2)}) collective-permute-start(bf16[8,192,768]{2,1,0:T(8,128)(2,1)} %dynamic-slice_bitcast_fusion.2), channel_id=1, source_target_pairs={{0,16},{16,0},{1,17},{17,1},{2,18},{18,2},{3,19},{19,3},{4,20},{20... | collective-permute-start | bytes 7077896 | tf_op jit(solution)/shard_map/ppermute | solution.py:90
  35.7 68.5 %collective-permute-start.8 = (bf16[1536,1536]{1,0:T(8,128)(2,1)}, bf16[1536,1536]{1,0:T(8,128)(2,1)}, u32[]{:S(2)}, u32[]{:S(2)}) collective-permute-start(bf16[1536,1536]{1,0:T(8,128)(2,1)} %bitcast.455), channel_id=1, source_target_pairs={{0,16},{16,0},{1,17},{17,1},{2,18},{18,2},{3,19},{19,3},{4,20},{20... | collective-permute-start | bytes 14155784 | tf_op jit(solution)/shard_map/ppermute | solution.py:90
  37.3 54.5 %collective-permute-start.9 = (f32[1536]{0:T(1024)}, f32[1536]{0:T(1024)}, u32[]{:S(2)}, u32[]{:S(2)}) collective-permute-start(f32[1536]{0:T(1024)} %reduce.1), channel_id=1, source_target_pairs={{0,16},{16,0},{1,17},{17,1},{2,18},{18,2},{3,19},{19,3},{4,20},{20... | collective-permute-start | bytes 18440 | tf_op jit(solution)/shard_map/ppermute | solution.py:90
  38.6 42.1 %collective-permute-start.4 = (bf16[128,512]{1,0:T(8,128)(2,1)S(1)}, bf16[128,512]{1,0:T(8,128)(2,1)S(1)}, u32[]{:S(2)}, u32[]{:S(2)}) collective-permute-start(bf16[128,512]{1,0:T(8,128)(2,1)S(1)} %pad_maximum_fusion.47), channel_id=1, source_target_pairs={{0,8},{4,12},{8,0},{12,4},{1,9},{5,13},{9,1},{13,5},{2,10},{6,14},... | collective-permute-start | bytes 393224 | tf_op jit(solution)/shard_map/ppermute | solution.py:113
  80.6 69.1 %collective-permute-start.12 = (bf16[8,96,1536]{2,1,0:T(8,128)(2,1)}, bf16[8,96,1536]{2,1,0:T(8,128)(2,1)}, u32[]{:S(2)}, u32[]{:S(2)}) collective-permute-start(bf16[8,96,1536]{2,1,0:T(8,128)(2,1)} %dynamic-slice_bitcast_fusion), channel_id=1, source_target_pairs={{0,16},{16,0},{1,17},{17,1},{2,18},{18,2},{3,19},{19,3},{4,20},{20... | collective-permute-start | bytes 7077896 | tf_op jit(solution)/shard_map/ppermute | solution.py:90
  87.3 58.3 %all-to-all-start.1 = ((bf16[8,192,768]{2,1,0:T(8,128)(2,1)}), bf16[8,192,768]{2,1,0:T(8,128)(2,1)}, u32[]{:S(2)}, u32[]{:S(2)}) async-start(bf16[8,192,768]{2,1,0:T(8,128)(2,1)} %get-tuple-element.158), calls=%async_computation.1 | async-start | bytes 4718592 | tf_op jit(solution)/shard_map/all_to_all | solution.py:331
  145.7 42.4 %all-to-all-start = ((bf16[32,16,1536]{2,1,0:T(8,128)(2,1)}), bf16[32,16,1536]{2,1,0:T(8,128)(2,1)S(1)}, u32[]{:S(2)}, u32[]{:S(2)}) async-start(bf16[32,16,1536]{2,1,0:T(8,128)(2,1)} %bitcast.24), calls=%async_computation | async-start | bytes 3145728 | tf_op jit(solution)/shard_map/all_to_all | solution.py:331
  188.1 59.5 %all-to-all-start.3 = ((bf16[8,96,1536]{2,1,0:T(8,128)(2,1)}), bf16[8,96,1536]{2,1,0:T(8,128)(2,1)}, u32[]{:S(2)}, u32[]{:S(2)}) async-start(bf16[8,96,1536]{2,1,0:T(8,128)(2,1)} %get-tuple-element.160), calls=%async_computation.3 | async-start | bytes 4718592 | tf_op jit(solution)/shard_map/all_to_all | solution.py:331
  252.0 41.7 %all-to-all-start.4 = ((bf16[32,16,1536]{2,1,0:T(8,128)(2,1)}), bf16[32,16,1536]{2,1,0:T(8,128)(2,1)S(1)}, u32[]{:S(2)}, u32[]{:S(2)}) async-start(bf16[32,16,1536]{2,1,0:T(8,128)(2,1)} %bitcast.518), calls=%async_computation.4 | async-start | bytes 3145728 | tf_op jit(solution)/shard_map/all_to_all | solution.py:331
  294.9 77.6 %all-to-all-start.6 = ((bf16[8,192,768]{2,1,0:T(8,128)(2,1)}), bf16[8,192,768]{2,1,0:T(8,128)(2,1)}, u32[]{:S(2)}, u32[]{:S(2)}) async-start(bf16[8,192,768]{2,1,0:T(8,128)(2,1)} %get-tuple-element.157), calls=%async_computation.6 | async-start | bytes 4718592 | tf_op jit(solution)/shard_map/all_to_all | solution.py:331
  302.1 19.2 %collective-permute-start.14 = (bf16[2,1,2,128,768]{4,3,2,1,0:T(8,128)(2,1)S(1)}, bf16[2,1,2,128,768]{4,3,2,1,0:T(8,128)(2,1)S(1)}, u32[]{:S(2)}, u32[]{:S(2)}) collective-permute-start(bf16[2,1,2,128,768]{4,3,2,1,0:T(8,128)(2,1)S(1)} %maximum_bitcast_fusion), channel_id=1, source_target_pairs={{0,2},{1,3},{2,0},{3,1},{4,6},{5,7},{6,4},{7,5},{8,10},{9,11},{10,... | collective-permute-start | bytes 2359304 | tf_op jit(solution)/shard_map/ppermute | solution.py:113
  322.7 45.8 %collective-permute-start.15 = (bf16[2,2,2,128,768]{4,3,2,1,0:T(8,128)(2,1)}, bf16[2,2,2,128,768]{4,3,2,1,0:T(8,128)(2,1)}, u32[]{:S(2)}, u32[]{:S(2)}) collective-permute-start(bf16[2,2,2,128,768]{4,3,2,1,0:T(8,128)(2,1)} %pad_maximum_fusion.13), channel_id=1, source_target_pairs={{0,1},{1,0},{2,3},{3,2},{4,5},{5,4},{6,7},{7,6},{8,9},{9,8},{10,11... | collective-permute-start | bytes 4718600 | tf_op jit(solution)/shard_map/ppermute | solution.py:113
  323.3 36.1 %collective-permute-start.17 = (bf16[128,512]{1,0:T(8,128)(2,1)S(1)}, bf16[128,512]{1,0:T(8,128)(2,1)S(1)}, u32[]{:S(2)}, u32[]{:S(2)}) collective-permute-start(bf16[128,512]{1,0:T(8,128)(2,1)S(1)} %pad_maximum_fusion.48), channel_id=1, source_target_pairs={{0,8},{4,12},{8,0},{12,4},{1,9},{5,13},{9,1},{13,5},{2,10},{6,14},... | collective-permute-start | bytes 393224 | tf_op jit(solution)/shard_map/ppermute | solution.py:113
  372.4 60.1 %all-to-all-start.8 = ((bf16[8,96,1536]{2,1,0:T(8,128)(2,1)}), bf16[8,96,1536]{2,1,0:T(8,128)(2,1)}, u32[]{:S(2)}, u32[]{:S(2)}) async-start(bf16[8,96,1536]{2,1,0:T(8,128)(2,1)} %get-tuple-element.159), calls=%async_computation.8 | async-start | bytes 4718592 | tf_op jit(solution)/shard_map/all_to_all | solution.py:331
  508.8 59.2 %all-to-all-start.7 = ((bf16[8,192,768]{2,1,0:T(8,128)(2,1)}), bf16[8,192,768]{2,1,0:T(8,128)(2,1)}, u32[]{:S(2)}, u32[]{:S(2)}) async-start(bf16[8,192,768]{2,1,0:T(8,128)(2,1)} %get-tuple-element.162), calls=%async_computation.7 | async-start | bytes 4718592 | tf_op jit(solution)/shard_map/all_to_all | solution.py:331
  516.2 19.2 %collective-permute-start.20 = (bf16[2,1,2,128,768]{4,3,2,1,0:T(8,128)(2,1)S(1)}, bf16[2,1,2,128,768]{4,3,2,1,0:T(8,128)(2,1)S(1)}, u32[]{:S(2)}, u32[]{:S(2)}) collective-permute-start(bf16[2,1,2,128,768]{4,3,2,1,0:T(8,128)(2,1)S(1)} %maximum_bitcast_fusion.1), channel_id=1, source_target_pairs={{0,2},{1,3},{2,0},{3,1},{4,6},{5,7},{6,4},{7,5},{8,10},{9,11},{10,... | collective-permute-start | bytes 2359304 | tf_op jit(solution)/shard_map/ppermute | solution.py:113
  536.7 40.0 %collective-permute-start.21 = (bf16[2,2,2,128,768]{4,3,2,1,0:T(8,128)(2,1)}, bf16[2,2,2,128,768]{4,3,2,1,0:T(8,128)(2,1)}, u32[]{:S(2)}, u32[]{:S(2)}) collective-permute-start(bf16[2,2,2,128,768]{4,3,2,1,0:T(8,128)(2,1)} %pad_maximum_fusion.14), channel_id=1, source_target_pairs={{0,1},{1,0},{2,3},{3,2},{4,5},{5,4},{6,7},{7,6},{8,9},{9,8},{10,11... | collective-permute-start | bytes 4718600 | tf_op jit(solution)/shard_map/ppermute | solution.py:113
  588.4 76.3 %all-to-all-start.9 = ((bf16[32,16,3072]{2,1,0:T(8,128)(2,1)}), bf16[32,16,3072]{2,1,0:T(8,128)(2,1)}, u32[]{:S(2)}, u32[]{:S(2)}) async-start(bf16[32,16,3072]{2,1,0:T(8,128)(2,1)} %pad_maximum_fusion.5), calls=%async_computation.9 | async-start | bytes 6291456 | tf_op jit(solution)/shard_map/all_to_all | solution.py:331
  664.8 58.4 %all-to-all-start.10 = ((bf16[8,96,1536]{2,1,0:T(8,128)(2,1)}), bf16[8,96,1536]{2,1,0:T(8,128)(2,1)S(1)}, u32[]{:S(2)}, u32[]{:S(2)}) async-start(bf16[8,96,1536]{2,1,0:T(8,128)(2,1)} %bitcast.510), calls=%async_computation.10 | async-start | bytes 4718592 | tf_op jit(solution)/shard_map/all_to_all | solution.py:331
  754.6 44.5 %all-to-all-start.11 = ((bf16[32,16,1536]{2,1,0:T(8,128)(2,1)}), bf16[32,16,1536]{2,1,0:T(8,128)(2,1)}, u32[]{:S(2)}, u32[]{:S(2)}) async-start(bf16[32,16,1536]{2,1,0:T(8,128)(2,1)} %bitcast.473), calls=%async_computation.11 | async-start | bytes 3145728 | tf_op jit(solution)/shard_map/all_to_all | solution.py:331
  765.9 22.8 %collective-permute-start.26 = (bf16[128,896]{1,0:T(8,128)(2,1)S(1)}, bf16[128,896]{1,0:T(8,128)(2,1)S(1)}, u32[]{:S(2)}, u32[]{:S(2)}) collective-permute-start(bf16[128,896]{1,0:T(8,128)(2,1)S(1)} %pad_maximum_fusion.46), channel_id=1, source_target_pairs={{0,3},{1,2},{2,1},{3,0},{4,7},{5,6},{6,5},{7,4},{8,11},{9,10},{10,... | collective-permute-start | bytes 688136 | tf_op jit(solution)/shard_map/ppermute | solution.py:243
  819.6 22.9 %collective-permute-start.29 = (bf16[192,896]{0,1:T(8,128)(2,1)S(1)}, bf16[192,896]{0,1:T(8,128)(2,1)S(1)}, u32[]{:S(2)}, u32[]{:S(2)}) collective-permute-start(bf16[192,896]{0,1:T(8,128)(2,1)S(1)} %dynamic-slice_convert_fusion), channel_id=1, source_target_pairs={{0,8},{4,12},{8,0},{12,4},{1,9},{5,13},{9,1},{13,5},{2,10},{6,14},... | collective-permute-start | bytes 1032200 | tf_op jit(solution)/shard_map/ppermute | solution.py:264
  885.4 21.9 %collective-permute-start.30 = (bf16[192,896]{0,1:T(8,128)(2,1)S(1)}, bf16[192,896]{0,1:T(8,128)(2,1)S(1)}, u32[]{:S(2)}, u32[]{:S(2)}) collective-permute-start(bf16[192,896]{0,1:T(8,128)(2,1)S(1)} %add_convert_fusion), channel_id=1, source_target_pairs={{0,8},{4,12},{8,0},{12,4},{1,9},{5,13},{9,1},{13,5},{2,10},{6,14},... | collective-permute-start | bytes 1032200 | tf_op jit(solution)/shard_map/ppermute | solution.py:275
  907.6 16.6 %collective-permute-start.31 = (bf16[384,896]{0,1:T(8,128)(2,1)S(1)}, bf16[384,896]{0,1:T(8,128)(2,1)S(1)}, u32[]{:S(2)}, u32[]{:S(2)}) collective-permute-start(bf16[384,896]{0,1:T(8,128)(2,1)S(1)} %pad_maximum_fusion.29), channel_id=1, source_target_pairs={{0,4},{4,0},{8,12},{12,8},{1,5},{5,1},{9,13},{13,9},{2,6},{6,2},{1... | collective-permute-start | bytes 2064392 | tf_op jit(solution)/shard_map/ppermute | solution.py:275
  925.8 110.5 %all-to-all-start.13 = ((bf16[8,192,1536]{2,1,0:T(8,128)(2,1)}), bf16[8,192,1536]{2,1,0:T(8,128)(2,1)}, u32[]{:S(2)}, u32[]{:S(2)}) async-start(bf16[8,192,1536]{2,1,0:T(8,128)(2,1)} %bitcast.478), calls=%async_computation.13 | async-start | bytes 9437184 | tf_op jit(solution)/shard_map/all_to_all | solution.py:331
  954.2 30.6 %collective-permute-start.38 = (bf16[128,384]{1,0:T(8,128)(2,1)}, bf16[128,384]{1,0:T(8,128)(2,1)}, u32[]{:S(2)}, u32[]{:S(2)}) collective-permute-start(bf16[128,384]{1,0:T(8,128)(2,1)} %get-tuple-element.239), channel_id=1, source_target_pairs={{0,3},{1,2},{2,1},{3,0},{4,7},{5,6},{6,5},{7,4},{8,11},{9,10},{10,... | collective-permute-start | bytes 294920 | tf_op jit(solution)/shard_map/ppermute | solution.py:243
  955.8 29.0 %collective-permute-start.37 = (bf16[128,384]{1,0:T(8,128)(2,1)}, bf16[128,384]{1,0:T(8,128)(2,1)}, u32[]{:S(2)}, u32[]{:S(2)}) collective-permute-start(bf16[128,384]{1,0:T(8,128)(2,1)} %get-tuple-element.240), channel_id=1, source_target_pairs={{0,1},{1,0},{2,3},{3,2},{4,5},{5,4},{6,7},{7,6},{8,9},{9,8},{10,11... | collective-permute-start | bytes 294920 | tf_op jit(solution)/shard_map/ppermute | solution.py:243
  956.7 28.1 %collective-permute-start.36 = (bf16[128,384]{1,0:T(8,128)(2,1)}, bf16[128,384]{1,0:T(8,128)(2,1)}, u32[]{:S(2)}, u32[]{:S(2)}) collective-permute-start(bf16[128,384]{1,0:T(8,128)(2,1)} %get-tuple-element.241), channel_id=1, source_target_pairs={{0,2},{1,3},{2,0},{3,1},{4,6},{5,7},{6,4},{7,5},{8,10},{9,11},{10,... | collective-permute-start | bytes 294920 | tf_op jit(solution)/shard_map/ppermute | solution.py:243
  959.4 17.7 %collective-permute-start.32 = (bf16[1,1,384,896]{2,3,1,0:T(8,128)(2,1)}, bf16[1,1,384,896]{2,3,1,0:T(8,128)(2,1)}, u32[]{:S(2)}, u32[]{:S(2)}) collective-permute-start(bf16[1,1,384,896]{2,3,1,0:T(8,128)(2,1)} %get-tuple-element.184), channel_id=1, source_target_pairs={{0,1},{1,0},{2,3},{3,2},{4,5},{5,4},{6,7},{7,6},{8,9},{9,8},{10,11... | collective-permute-start | bytes 2064392 | tf_op jit(solution)/shard_map/ppermute | solution.py:290
  960.7 17.6 %collective-permute-start.34 = (bf16[1,1,384,896]{2,3,1,0:T(8,128)(2,1)}, bf16[1,1,384,896]{2,3,1,0:T(8,128)(2,1)}, u32[]{:S(2)}, u32[]{:S(2)}) collective-permute-start(bf16[1,1,384,896]{2,3,1,0:T(8,128)(2,1)} %get-tuple-element.185), channel_id=1, source_target_pairs={{0,2},{1,3},{2,0},{3,1},{4,6},{5,7},{6,4},{7,5},{8,10},{9,11},{10,... | collective-permute-start | bytes 2064392 | tf_op jit(solution)/shard_map/ppermute | solution.py:290
  981.4 31.5 %collective-permute-start.35 = (bf16[2,1,384,896]{2,3,1,0:T(8,128)(2,1)}, bf16[2,1,384,896]{2,3,1,0:T(8,128)(2,1)}, u32[]{:S(2)}, u32[]{:S(2)}) collective-permute-start(bf16[2,1,384,896]{2,3,1,0:T(8,128)(2,1)} %pad_maximum_fusion.18), channel_id=1, source_target_pairs={{0,1},{1,0},{2,3},{3,2},{4,5},{5,4},{6,7},{7,6},{8,9},{9,8},{10,11... | collective-permute-start | bytes 4128776 | tf_op jit(solution)/shard_map/ppermute | solution.py:290
  983.5 37.4 %collective-permute-start.33 = (bf16[1,2,384,896]{2,3,1,0:T(8,128)(2,1)}, bf16[1,2,384,896]{2,3,1,0:T(8,128)(2,1)}, u32[]{:S(2)}, u32[]{:S(2)}) collective-permute-start(bf16[1,2,384,896]{2,3,1,0:T(8,128)(2,1)} %pad_maximum_fusion.17), channel_id=1, source_target_pairs={{0,2},{1,3},{2,0},{3,1},{4,6},{5,7},{6,4},{7,5},{8,10},{9,11},{10,... | collective-permute-start | bytes 4128776 | tf_op jit(solution)/shard_map/ppermute | solution.py:290
  1053.9 61.0 %all-to-all-start.14 = ((bf16[8,96,1536]{2,1,0:T(8,128)(2,1)}), bf16[8,96,1536]{2,1,0:T(8,128)(2,1)}, u32[]{:S(2)}, u32[]{:S(2)}) async-start(bf16[8,96,1536]{2,1,0:T(8,128)(2,1)} %bitcast.509), calls=%async_computation.14 | async-start | bytes 4718592 | tf_op jit(solution)/shard_map/all_to_all | solution.py:331
  1178.7 112.3 %all-to-all-start.15 = ((bf16[8,192,1536]{2,1,0:T(8,128)(2,1)}), bf16[8,192,1536]{2,1,0:T(8,128)(2,1)}, u32[]{:S(2)}, u32[]{:S(2)}) async-start(bf16[8,192,1536]{2,1,0:T(8,128)(2,1)} %bitcast.479), calls=%async_computation.15 | async-start | bytes 9437184 | tf_op jit(solution)/shard_map/all_to_all | solution.py:331
  1191.6 47.9 %collective-permute-start.71 = (f32[128,1536]{1,0:T(8,128)S(1)}, f32[128,1536]{1,0:T(8,128)S(1)}, u32[]{:S(2)}, u32[]{:S(2)}) collective-permute-start(f32[128,1536]{1,0:T(8,128)S(1)} %convolution_add_fusion.2), channel_id=1, source_target_pairs={{0,16},{1,17},{2,18},{3,19},{4,20},{5,21},{6,22},{7,23},{8,24},{9,... | collective-permute-start | bytes 2359304 | tf_op jit(solution)/shard_map/ppermute | solution.py:691
  1192.9 67.6 %collective-permute-start.64 = (bf16[2,4,384,896]{3,2,1,0:T(8,128)(2,1)}, bf16[2,4,384,896]{3,2,1,0:T(8,128)(2,1)}, u32[]{:S(2)}, u32[]{:S(2)}) collective-permute-start(bf16[2,4,384,896]{3,2,1,0:T(8,128)(2,1)} %pad_maximum_fusion.refs_1_), channel_id=1, source_target_pairs={{0,16},{1,17},{2,18},{3,19},{4,20},{5,21},{6,22},{7,23},{8,24},{9,... | collective-permute-start | bytes 16515080 | tf_op jit(solution)/shard_map/ppermute | solution.py:763
  1200.5 22.1 %collective-permute-start.68 = (bf16[2,1,416,512]{3,2,1,0:T(8,128)(2,1)S(1)}, bf16[2,1,416,512]{3,2,1,0:T(8,128)(2,1)S(1)}, u32[]{:S(2)}, u32[]{:S(2)}) collective-permute-start(bf16[2,1,416,512]{3,2,1,0:T(8,128)(2,1)S(1)} %pad_maximum_fusion.25), channel_id=1, source_target_pairs={{0,1},{1,0},{2,3},{3,2},{4,5},{5,4},{6,7},{7,6},{8,9},{9,8},{10,11... | collective-permute-start | bytes 2555912 | tf_op jit(solution)/shard_map/ppermute | solution.py:290
  1204.3 20.1 %collective-permute-start.66 = (bf16[1,2,416,512]{3,2,1,0:T(8,128)(2,1)S(1)}, bf16[1,2,416,512]{3,2,1,0:T(8,128)(2,1)S(1)}, u32[]{:S(2)}, u32[]{:S(2)}) collective-permute-start(bf16[1,2,416,512]{3,2,1,0:T(8,128)(2,1)S(1)} %pad_maximum_fusion.24), channel_id=1, source_target_pairs={{0,2},{1,3},{2,0},{3,1},{4,6},{5,7},{6,4},{7,5},{8,10},{9,11},{10,... | collective-permute-start | bytes 2555912 | tf_op jit(solution)/shard_map/ppermute | solution.py:290
  1206.6 28.6 %collective-permute-start.62 = (bf16[2,1,384,384]{3,2,1,0:T(8,128)(2,1)S(1)}, bf16[2,1,384,384]{3,2,1,0:T(8,128)(2,1)S(1)}, u32[]{:S(2)}, u32[]{:S(2)}) collective-permute-start(bf16[2,1,384,384]{3,2,1,0:T(8,128)(2,1)S(1)} %pad_maximum_fusion.32), channel_id=1, source_target_pairs={{0,1},{1,0},{2,3},{3,2},{4,5},{5,4},{6,7},{7,6},{8,9},{9,8},{10,11... | collective-permute-start | bytes 1769480 | tf_op jit(solution)/shard_map/ppermute | solution.py:290
  1222.5 18.3 %collective-permute-start.60 = (bf16[1,2,384,384]{3,2,1,0:T(8,128)(2,1)S(1)}, bf16[1,2,384,384]{3,2,1,0:T(8,128)(2,1)S(1)}, u32[]{:S(2)}, u32[]{:S(2)}) collective-permute-start(bf16[1,2,384,384]{3,2,1,0:T(8,128)(2,1)S(1)} %pad_maximum_fusion.31), channel_id=1, source_target_pairs={{0,2},{1,3},{2,0},{3,1},{4,6},{5,7},{6,4},{7,5},{8,10},{9,11},{10,... | collective-permute-start | bytes 1769480 | tf_op jit(solution)/shard_map/ppermute | solution.py:290
  1225.8 45.6 %collective-permute-start.69 = (bf16[2,4,416,512]{3,2,1,0:T(8,128)(2,1)S(1)}, bf16[2,4,416,512]{3,2,1,0:T(8,128)(2,1)}, u32[]{:S(2)}, u32[]{:S(2)}) collective-permute-start(bf16[2,4,416,512]{3,2,1,0:T(8,128)(2,1)S(1)} %pad_maximum_fusion.1.refs_0_), channel_id=1, source_target_pairs={{16,0},{17,1},{18,2},{19,3},{20,4},{21,5},{22,6},{23,7},{24,8},{25... | collective-permute-start | bytes 10223624 | tf_op jit(solution)/shard_map/ppermute | solution.py:771
  1250.3 53.5 %collective-permute-start.73 = (bf16[8,192,1536]{2,1,0:T(8,128)(2,1)}, bf16[8,192,1536]{2,1,0:T(8,128)(2,1)}, u32[]{:S(2)}, u32[]{:S(2)}) collective-permute-start(bf16[8,192,1536]{2,1,0:T(8,128)(2,1)} %all-to-all-done.13.refs_1_), channel_id=1, source_target_pairs={{0,16},{1,17},{2,18},{3,19},{4,20},{5,21},{6,22},{7,23},{8,24},{9,... | collective-permute-start | bytes 14155784 | tf_op jit(solution)/shard_map/ppermute | solution.py:161
  (223 other events, 2404.6 us)

commit v6 on v5

--- a/solution.py
+++ b/solution.py
@@ -223,7 +223,17 @@
     mine, others = two_parts(rows, lax.axis_index("section"), 1)
     half = mine.shape[1]
     joined = jnp.stack([mine.reshape(2, -1, half), swapped(others).reshape(2, -1, half)], 1)
-    return gathered(joined[:, None], 1, "expert").reshape(2, -1, half)
+    joined = joined[:, None]
+    for flip in reversed(flips("expert")):
+        others = lax.ppermute(joined, "expert", partners("expert", flip))
+        if flip == 1:
+            return joined, others
+        joined = jnp.concatenate([joined, others], 1)
+
+
+def early_join(pair):
+    joined = jnp.concatenate(pair, 1)
+    return joined.reshape(2, -1, joined.shape[-1])
 
 
 def late_operands(operands):
@@ -665,7 +675,7 @@
     second = attention_forward(
         state.astype(F32), visible, routed[1], dense_sets[1], lambda value: end("early", value)
     )
-    early_first = kept.early
+    early_first = early_join(kept.early)
     outgoing = jnp.concatenate(
         [t_dot(second.selector, second.hidden_two), t_dot(second.weighting, cotangent)], 1
     ).astype(BF)
@@ -700,21 +710,25 @@
         grad_router,
         grad_hidden,
         dense_sets[1],
-        lambda name, value: end("down1", value) if name == "kv_all" else value,
+        lambda name, value: value,
     )
     grad = later.input.astype(BF)
     branch, qkv, grad = tie(later.branch, later.qkv, grad)
     late = late_operands([branch, qkv])
     width = late[0].shape[1]
-    owed_first = send_out(t_dot(first.weighting, grad).astype(BF), experts_all)
+    outgoing = end("down1", t_dot(first.weighting, grad).astype(BF))
+    owed_first = send_out(outgoing, experts_all)
     late, owed_first = tie(late, owed_first)
-    hidden_early, mix_early = early_second
-    kept.dense = dense_rows(dense_partial([mix_early, hidden_early], late))
+    hidden_early, mix_early = early_join(early_second)
+    kept.dense = dense_partial([mix_early, hidden_early], late)
+    for flip in flips("dp")[:-1]:
+        kept.dense = dense_rows_step(kept.dense, flip)
     grad_pre = expert_backward(owed_first, *pres_first, down_first)
     grad_arrived = expert_input(grad_pre, gate_first, up_first).astype(BF)
     first_grads = [t_dot(arrived_first, grad_pre).astype(BF)]
     first_grads.append(t_dot(inner_first, owed_first).astype(BF))
     sent_first = send_back(end("dense", grad_arrived), experts_all)
+    kept.dense = dense_rows_step(kept.dense, flips("dp")[-1]).astype(BF)
     kept.dense, sent_first = tie(kept.dense, sent_first)
     kept.dense, gate_up_grad = tie(dense_line(kept.dense), gate_up_grad)
     kept.gate_up1 = expert_out(gate_up_grad, experts)
@@ -728,8 +742,9 @@
             value = end("late", value)
             kept.out = dense_partial([early_first[1]], kept.late)
             kept.dense = dense_groups(kept.dense)
-            value = end("dense", end("out", end("gate_up1", value)))
+            value = end("dense", end("out", value))
         if name == "kv":
+            value = end("gate_up1", value)
             kept.out = dense_rows_step(kept.out, flips("dp")[0])
             down_grad, value, kept.out = tie(first_grads[1], value, kept.out)
             kept.down0 = expert_out(down_grad, experts)
@@ -743,9 +758,9 @@
         jnp.where(is_first, later.small, earlier.small),
     )
     qkv_total = dense_partial([early_first[0]], late_operands([earlier.qkv]))
-    qkv_total, smalls, down_part, out_total = tie(qkv_total, smalls, kept.down0, kept.out)
     small_rows, small_columns = smalls.shape
     qkv_total = with_small(qkv_total, smalls)
+    qkv_total, down_part, out_total = tie(qkv_total, kept.down0, kept.out)
     steps = [(dense_rows_step, flip) for flip in flips("dp")]
     steps += [(dense_line_step, flip) for flip in reversed(flips("dp"))]
     turning = len(flips("dp"))

time: 1320 us -> 1300 us (0.985)
  blocking collectives: 119 us -> 76.1 us
  starting transfers between devices: 149 us -> 167 us
    all_to_all x2 -> x1, blocking collectives: 119 us -> 76.1 us  [exchange(): return lax.all_to_all(rows, axes, split_axis=0, concat_axis=0, tiled=True)]
    ppermute x8 -> x4, waiting for transfers between devices: 107 us -> 73.8 us  [gathered(): lax.ppermute(shard, over, partners(over, flip))]
    ppermute x0 -> x4, waiting for transfers between devices: none -> 32.6 us  [early_operand(): others = lax.ppermute(joined, 'expert', partners('expert', flip))]
    all_to_all x14 -> x15, waiting for transfers between devices: 330 us -> 301 us  [exchange(): return lax.all_to_all(rows, axes, split_axis=0, concat_axis=0, tiled=True)]
    ppermute x4, waiting for transfers between devices: 12 us -> 35.7 us  [sum_to_owner(): sent = lax.ppermute(sent.astype(sent_as), 'dp', partners('dp', flip))]
    ppermute x6, waiting for transfers between devices: 52.3 us -> 75.4 us  [dense_rows_step(): sent = lax.ppermute(sent.astype(BF), 'dp', partners('dp', flip))]
    all_to_all x14 -> x15, starting transfers between devices: 76.1 us -> 80.6 us  [exchange(): return lax.all_to_all(rows, axes, split_axis=0, concat_axis=0, tiled=True)]
  transfers between devices with their start and end apart: 88 -> 89, of which waited for: 47 -> 45; matrix products, arithmetic and copies ran while one was open for 22% -> 23% of each run, Pallas kernels for 3% -> 3%
where the time goes in v6:
time: 1300 us; the launch traced here: 1290 us
  waiting for transfers between devices  644 us (50%)
  starting transfers between devices  167 us (13%)
  matrix products  164 us (13%)
  other arithmetic  106 us (8%)
  local copies, waits for them, and re-layouts  81.9 us (6%)
  blocking collectives  76.1 us (6%)
  Pallas kernels  47.7 us (4%)
    all_to_all x15, waiting for transfers between devices, exchange(): return lax.all_to_all(rows, axes, split_axis=0, concat_axis=0, tiled=True)  301 us
    all_to_all x15, starting transfers between devices, exchange(): return lax.all_to_all(rows, axes, split_axis=0, concat_axis=0, tiled=True)  80.6 us
    all_to_all x1, blocking collectives, exchange(): return lax.all_to_all(rows, axes, split_axis=0, concat_axis=0, tiled=True)  76.1 us
    ppermute x6, waiting for transfers between devices, dense_rows_step(): sent = lax.ppermute(sent.astype(BF), 'dp', partners('dp', flip))  75.4 us
    ppermute x4, waiting for transfers between devices, gathered(): lax.ppermute(shard, over, partners(over, flip))  73.8 us
    dot_general x19, matrix products, dot_t(): lax.dot_general(left, right, (((1,), (1,)), ((), ())), preferred_element_...  58.6 us
    dot_general x24, matrix products, dot(): return jnp.dot(left, right, preferred_element_type=F32)  55.2 us
    pallas_call x5, Pallas kernels, pick_blocks(): pl.pallas_call(body, grid_spec=pltpu.PrefetchScalarGridSpec(num_scalar_pr...  47.7 us
  transfers between devices with their start and end apart: 89, of which 45 were waited for; matrix products, arithmetic and copies ran while one was open for 23% of the time, Pallas kernels for 3%

profile of v6, /device:TPU:1, one launch (start us, length us, event | category | flops | bytes accessed | tf_op | source)
XLA Modules:
  0.0 1291.0 jit_solution(12176348606240376127)
XLA Ops:
  9.2 5.7 slice_select_fusion.1
  14.9 6.4 all-to-all-start.2
  42.4 38.3 %collective-permute-done.4 = bf16[128,512]{1,0:T(8,128)(2,1)S(1)} collective-permute-done((bf16[128,512]{1,0:T(8,128)(2,1)S(1)}, bf16[128,512]{1,0:T(8,128)(2,1)S(1)}, u32[]{:S(2)}, u32[]{:S(2)}) %collective-permute-start.4) | collective-permute-done | bytes 131104 | tf_op jit(solution)/shard_map/ppermute | solution.py:113
  81.7 5.7 slice_select_fusion.2
  111.4 34.3 %all-to-all-done.1 = bf16[8,192,768]{2,1,0:T(8,128)(2,1)} async-done(((bf16[8,192,768]{2,1,0:T(8,128)(2,1)}), bf16[8,192,768]{2,1,0:T(8,128)(2,1)}, u32[]{:S(2)}, u32[]{:S(2)}) %all-to-all-start.1) | async-done | bytes 2359328 | tf_op jit(solution)/shard_map/all_to_all | solution.py:341
  149.8 5.7 slice_select_fusion
  155.5 32.6 %all-to-all-done = bf16[32,16,1536]{2,1,0:T(8,128)(2,1)S(1)} async-done(((bf16[32,16,1536]{2,1,0:T(8,128)(2,1)}), bf16[32,16,1536]{2,1,0:T(8,128)(2,1)S(1)}, u32[]{:S(2)}, u32[]{:S(2)}) %all-to-all-start) | async-done | bytes 1572896 | tf_op jit(solution)/shard_map/all_to_all | solution.py:341
  188.1 5.6 all-to-all-start.3
  202.4 45.2 %all-to-all-done.3 = bf16[8,96,1536]{2,1,0:T(8,128)(2,1)} async-done(((bf16[8,96,1536]{2,1,0:T(8,128)(2,1)}), bf16[8,96,1536]{2,1,0:T(8,128)(2,1)}, u32[]{:S(2)}, u32[]{:S(2)}) %all-to-all-start.3) | async-done | bytes 2359328 | tf_op jit(solution)/shard_map/all_to_all | solution.py:341
  259.6 34.1 %all-to-all-done.4 = bf16[32,16,1536]{2,1,0:T(8,128)(2,1)S(1)} async-done(((bf16[32,16,1536]{2,1,0:T(8,128)(2,1)}), bf16[32,16,1536]{2,1,0:T(8,128)(2,1)S(1)}, u32[]{:S(2)}, u32[]{:S(2)}) %all-to-all-start.4) | async-done | bytes 1572896 | tf_op jit(solution)/shard_map/all_to_all | solution.py:341
  304.5 18.0 %collective-permute-done.14 = bf16[2,1,2,128,768]{4,3,0,2,1:T(8,128)(2,1)S(1)} collective-permute-done((bf16[2,1,2,128,768]{4,3,0,2,1:T(8,128)(2,1)S(1)}, bf16[2,1,2,128,768]{4,3,0,2,1:T(8,128)(2,1)S(1)}, u32[]{:S(2)}, u32[]{:S(2)}) %collective-permute-start.14) | collective-permute-done | bytes 786464 | tf_op jit(solution)/shard_map/ppermute | solution.py:228
  326.4 32.1 %collective-permute-done.17 = bf16[128,512]{1,0:T(8,128)(2,1)S(1)} collective-permute-done((bf16[128,512]{1,0:T(8,128)(2,1)S(1)}, bf16[128,512]{1,0:T(8,128)(2,1)S(1)}, u32[]{:S(2)}, u32[]{:S(2)}) %collective-permute-start.17) | collective-permute-done | bytes 131104 | tf_op jit(solution)/shard_map/ppermute | solution.py:113
  368.7 6.2 all-to-all-start.8
  386.5 42.3 %all-to-all-done.8 = bf16[8,96,1536]{2,1,0:T(8,128)(2,1)} async-done(((bf16[8,96,1536]{2,1,0:T(8,128)(2,1)}), bf16[8,96,1536]{2,1,0:T(8,128)(2,1)}, u32[]{:S(2)}, u32[]{:S(2)}) %all-to-all-start.8) | async-done | bytes 2359328 | tf_op jit(solution)/shard_map/all_to_all | solution.py:341
  428.8 76.1 %all_to_all.80 = bf16[32,16,3072]{2,1,0:T(8,128)(2,1)} all-to-all(bf16[32,16,3072]{2,1,0:T(8,128)(2,1)} %pad_maximum_fusion.2), channel_id=1, replica_groups=mesh['section'=2,'dp'=4,'expert'=4] {'expert','dp','section'}, dimensions={0} | all-to-all | bytes 6291456 | tf_op jit(solution)/shard_map/all_to_all | solution.py:341
  504.9 5.5 all-to-all-start.7
  517.1 14.6 %collective-permute-done.20 = bf16[2,1,2,128,768]{4,3,0,2,1:T(8,128)(2,1)S(1)} collective-permute-done((bf16[2,1,2,128,768]{4,3,0,2,1:T(8,128)(2,1)S(1)}, bf16[2,1,2,128,768]{4,3,0,2,1:T(8,128)(2,1)S(1)}, u32[]{:S(2)}, u32[]{:S(2)}) %collective-permute-start.20) | collective-permute-done | bytes 786464 | tf_op jit(solution)/shard_map/ppermute | solution.py:228
  536.7 27.6 %all-to-all-done.7 = bf16[8,192,768]{2,1,0:T(8,128)(2,1)} async-done(((bf16[8,192,768]{2,1,0:T(8,128)(2,1)}), bf16[8,192,768]{2,1,0:T(8,128)(2,1)}, u32[]{:S(2)}, u32[]{:S(2)}) %all-to-all-start.7) | async-done | bytes 2359328 | tf_op jit(solution)/shard_map/all_to_all | solution.py:341
  594.1 63.5 %all-to-all-done.9 = bf16[32,16,3072]{2,1,0:T(8,128)(2,1)} async-done(((bf16[32,16,3072]{2,1,0:T(8,128)(2,1)}), bf16[32,16,3072]{2,1,0:T(8,128)(2,1)}, u32[]{:S(2)}, u32[]{:S(2)}) %all-to-all-start.9) | async-done | bytes 3145760 | tf_op jit(solution)/shard_map/all_to_all | solution.py:341
  694.7 17.0 %collective-permute-done.22 = bf16[256,512]{1,0:T(8,128)(2,1)S(1)} collective-permute-done((bf16[256,512]{1,0:T(8,128)(2,1)S(1)}, bf16[256,512]{1,0:T(8,128)(2,1)S(1)}, u32[]{:S(2)}, u32[]{:S(2)}) %collective-permute-start.22) | collective-permute-done | bytes 262176 | tf_op jit(solution)/shard_map/ppermute | solution.py:121
  718.8 8.3 collective-permute-done.23
  738.6 6.1 all-to-all-start.11
  749.9 13.3 %collective-permute-done.24 = bf16[128,896]{1,0:T(8,128)(2,1)S(1)} collective-permute-done((bf16[128,896]{1,0:T(8,128)(2,1)S(1)}, bf16[128,896]{1,0:T(8,128)(2,1)S(1)}, u32[]{:S(2)}, u32[]{:S(2)}) %collective-permute-start.24) | collective-permute-done | bytes 229408 | tf_op jit(solution)/shard_map/ppermute | solution.py:253
  763.2 9.3 collective-permute-done.26
  804.4 6.3 all-to-all-start.12
  815.3 52.0 %collective-permute-done.29 = bf16[192,896]{0,1:T(8,128)(2,1)} collective-permute-done((bf16[192,896]{0,1:T(8,128)(2,1)}, bf16[192,896]{0,1:T(8,128)(2,1)}, u32[]{:S(2)}, u32[]{:S(2)}) %collective-permute-start.29) | collective-permute-done | bytes 344096 | tf_op jit(solution)/shard_map/ppermute | solution.py:274
  873.0 19.2 %collective-permute-done.30 = bf16[192,896]{0,1:T(8,128)(2,1)} collective-permute-done((bf16[192,896]{0,1:T(8,128)(2,1)}, bf16[192,896]{0,1:T(8,128)(2,1)}, u32[]{:S(2)}, u32[]{:S(2)}) %collective-permute-start.30) | collective-permute-done | bytes 344096 | tf_op jit(solution)/shard_map/ppermute | solution.py:285
  899.1 11.2 collective-permute-done.31
  911.8 6.0 all-to-all-start.13
  926.9 6.2 convolution_convert_fusion.10
  947.2 12.0 collective-permute-done.32
  982.8 11.6 collective-permute-done.35
  1012.2 5.7 pad_maximum_fusion.refs_1_
  1030.3 6.2 collective-permute-done.41
  1046.6 7.2 fusion.58
  1081.6 14.5 %all-to-all-done.14.refs_0_ = bf16[8,96,1536]{2,1,0:T(8,128)(2,1)} async-done(((bf16[8,96,1536]{2,1,0:T(8,128)(2,1)}), bf16[8,96,1536]{2,1,0:T(8,128)(2,1)}, u32[]{:S(2)}, u32[]{:S(2)}) %all-to-all-start.14) | async-done | bytes 2359328 | tf_op jit(solution)/shard_map/all_to_all | solution.py:341
  1101.4 8.8 collective-permute-done.51
  1121.2 11.8 collective-permute-done.52
  1136.3 10.0 collective-permute-done.54
  1157.3 7.8 all-to-all-start.15
  1187.1 13.8 %collective-permute-done.68 = bf16[2,1,416,512]{3,2,1,0:T(8,128)(2,1)S(1)} collective-permute-done((bf16[2,1,416,512]{3,2,1,0:T(8,128)(2,1)S(1)}, bf16[2,1,416,512]{3,2,1,0:T(8,128)(2,1)S(1)}, u32[]{:S(2)}, u32[]{:S(2)}) %collective-permute-start.68) | collective-permute-done | bytes 852000 | tf_op jit(solution)/shard_map/ppermute | solution.py:300
  1205.0 6.8 collective-permute-start.69
  1230.5 7.8 shard_map.239
  1239.4 11.0 shard_map.240
  1250.4 12.3 shard_map.241
  1262.7 6.9 all-to-all-done.15.refs_0_
  1272.7 8.4 shard_map.242
  1282.4 8.2 shard_map.243
  (766 shorter events, 461.8 us)
Async XLA Ops:
  4.7 26.5 %collective-permute-start.7 = (s32[5,128]{1,0:T(8,128)}, s32[5,128]{1,0:T(8,128)S(1)}, u32[]{:S(2)}, u32[]{:S(2)}) collective-permute-start(s32[5,128]{1,0:T(8,128)} %select_bitcast_fusion.1), channel_id=1, source_target_pairs={{0,16},{16,0},{1,17},{17,1},{2,18},{18,2},{3,19},{19,3},{4,20},{20... | collective-permute-start | bytes 7688 | tf_op jit(solution)/shard_map/ppermute | solution.py:90
  5.8 27.2 %collective-permute-start.1 = (f32[1536]{0:T(1024)}, f32[1536]{0:T(1024)}, u32[]{:S(2)}, u32[]{:S(2)}) collective-permute-start(f32[1536]{0:T(1024)} %reduce), channel_id=1, source_target_pairs={{0,16},{16,0},{1,17},{17,1},{2,18},{18,2},{3,19},{19,3},{4,20},{20... | collective-permute-start | bytes 18440 | tf_op jit(solution)/shard_map/ppermute | solution.py:90
  6.7 28.3 %collective-permute-start = (bf16[128,1536]{1,0:T(8,128)(2,1)}, bf16[128,1536]{1,0:T(8,128)(2,1)S(1)}, u32[]{:S(2)}, u32[]{:S(2)}) collective-permute-start(bf16[128,1536]{1,0:T(8,128)(2,1)} %select_bitcast_fusion), channel_id=1, source_target_pairs={{0,16},{16,0},{1,17},{17,1},{2,18},{18,2},{3,19},{19,3},{4,20},{20... | collective-permute-start | bytes 1179656 | tf_op jit(solution)/shard_map/ppermute | solution.py:90
  7.1 30.1 %collective-permute-start.3 = (bf16[1536,256]{1,0:T(8,128)(2,1)S(1)}, bf16[1536,256]{1,0:T(8,128)(2,1)S(1)}, u32[]{:S(2)}, u32[]{:S(2)}) collective-permute-start(bf16[1536,256]{1,0:T(8,128)(2,1)S(1)} %bitcast.492), channel_id=1, source_target_pairs={{0,16},{16,0},{1,17},{17,1},{2,18},{18,2},{3,19},{19,3},{4,20},{20... | collective-permute-start | bytes 2359304 | tf_op jit(solution)/shard_map/ppermute | solution.py:90
  9.0 86.1 %collective-permute-start.6 = (bf16[1536,1536]{1,0:T(8,128)(2,1)}, bf16[1536,1536]{1,0:T(8,128)(2,1)}, u32[]{:S(2)}, u32[]{:S(2)}) collective-permute-start(bf16[1536,1536]{1,0:T(8,128)(2,1)} %bitcast.466), channel_id=1, source_target_pairs={{0,16},{16,0},{1,17},{17,1},{2,18},{18,2},{3,19},{19,3},{4,20},{20... | collective-permute-start | bytes 14155784 | tf_op jit(solution)/shard_map/ppermute | solution.py:90
  14.9 72.5 %all-to-all-start.2 = ((bf16[8,192,768]{2,1,0:T(8,128)(2,1)}), bf16[8,192,768]{2,1,0:T(8,128)(2,1)}, u32[]{:S(2)}, u32[]{:S(2)}) async-start(bf16[8,192,768]{2,1,0:T(8,128)(2,1)} %get-tuple-element.160), calls=%async_computation.2 | async-start | bytes 4718592 | tf_op jit(solution)/shard_map/all_to_all | solution.py:341
  31.2 50.3 %collective-permute-start.10 = (bf16[8,192,768]{2,1,0:T(8,128)(2,1)}, bf16[8,192,768]{2,1,0:T(8,128)(2,1)}, u32[]{:S(2)}, u32[]{:S(2)}) collective-permute-start(bf16[8,192,768]{2,1,0:T(8,128)(2,1)} %dynamic-slice_bitcast_fusion.2), channel_id=1, source_target_pairs={{0,16},{16,0},{1,17},{17,1},{2,18},{18,2},{3,19},{19,3},{4,20},{20... | collective-permute-start | bytes 7077896 | tf_op jit(solution)/shard_map/ppermute | solution.py:90
  35.7 68.6 %collective-permute-start.8 = (bf16[1536,1536]{1,0:T(8,128)(2,1)}, bf16[1536,1536]{1,0:T(8,128)(2,1)}, u32[]{:S(2)}, u32[]{:S(2)}) collective-permute-start(bf16[1536,1536]{1,0:T(8,128)(2,1)} %bitcast.445), channel_id=1, source_target_pairs={{0,16},{16,0},{1,17},{17,1},{2,18},{18,2},{3,19},{19,3},{4,20},{20... | collective-permute-start | bytes 14155784 | tf_op jit(solution)/shard_map/ppermute | solution.py:90
  37.3 54.6 %collective-permute-start.9 = (f32[1536]{0:T(1024)}, f32[1536]{0:T(1024)}, u32[]{:S(2)}, u32[]{:S(2)}) collective-permute-start(f32[1536]{0:T(1024)} %reduce.1), channel_id=1, source_target_pairs={{0,16},{16,0},{1,17},{17,1},{2,18},{18,2},{3,19},{19,3},{4,20},{20... | collective-permute-start | bytes 18440 | tf_op jit(solution)/shard_map/ppermute | solution.py:90
  38.6 42.1 %collective-permute-start.4 = (bf16[128,512]{1,0:T(8,128)(2,1)S(1)}, bf16[128,512]{1,0:T(8,128)(2,1)S(1)}, u32[]{:S(2)}, u32[]{:S(2)}) collective-permute-start(bf16[128,512]{1,0:T(8,128)(2,1)S(1)} %pad_maximum_fusion.45), channel_id=1, source_target_pairs={{0,8},{4,12},{8,0},{12,4},{1,9},{5,13},{9,1},{13,5},{2,10},{6,14},... | collective-permute-start | bytes 393224 | tf_op jit(solution)/shard_map/ppermute | solution.py:113
  80.7 69.1 %collective-permute-start.12 = (bf16[8,96,1536]{2,1,0:T(8,128)(2,1)}, bf16[8,96,1536]{2,1,0:T(8,128)(2,1)}, u32[]{:S(2)}, u32[]{:S(2)}) collective-permute-start(bf16[8,96,1536]{2,1,0:T(8,128)(2,1)} %dynamic-slice_bitcast_fusion), channel_id=1, source_target_pairs={{0,16},{16,0},{1,17},{17,1},{2,18},{18,2},{3,19},{19,3},{4,20},{20... | collective-permute-start | bytes 7077896 | tf_op jit(solution)/shard_map/ppermute | solution.py:90
  87.3 58.4 %all-to-all-start.1 = ((bf16[8,192,768]{2,1,0:T(8,128)(2,1)}), bf16[8,192,768]{2,1,0:T(8,128)(2,1)}, u32[]{:S(2)}, u32[]{:S(2)}) async-start(bf16[8,192,768]{2,1,0:T(8,128)(2,1)} %get-tuple-element.162), calls=%async_computation.1 | async-start | bytes 4718592 | tf_op jit(solution)/shard_map/all_to_all | solution.py:341
  145.7 42.4 %all-to-all-start = ((bf16[32,16,1536]{2,1,0:T(8,128)(2,1)}), bf16[32,16,1536]{2,1,0:T(8,128)(2,1)S(1)}, u32[]{:S(2)}, u32[]{:S(2)}) async-start(bf16[32,16,1536]{2,1,0:T(8,128)(2,1)} %bitcast.24), calls=%async_computation | async-start | bytes 3145728 | tf_op jit(solution)/shard_map/all_to_all | solution.py:341
  188.1 59.5 %all-to-all-start.3 = ((bf16[8,96,1536]{2,1,0:T(8,128)(2,1)}), bf16[8,96,1536]{2,1,0:T(8,128)(2,1)}, u32[]{:S(2)}, u32[]{:S(2)}) async-start(bf16[8,96,1536]{2,1,0:T(8,128)(2,1)} %get-tuple-element.164), calls=%async_computation.3 | async-start | bytes 4718592 | tf_op jit(solution)/shard_map/all_to_all | solution.py:341
  252.1 41.7 %all-to-all-start.4 = ((bf16[32,16,1536]{2,1,0:T(8,128)(2,1)}), bf16[32,16,1536]{2,1,0:T(8,128)(2,1)S(1)}, u32[]{:S(2)}, u32[]{:S(2)}) async-start(bf16[32,16,1536]{2,1,0:T(8,128)(2,1)} %bitcast.504), calls=%async_computation.4 | async-start | bytes 3145728 | tf_op jit(solution)/shard_map/all_to_all | solution.py:341
  255.4 43.7 %collective-permute-start.16 = (bf16[1536,32]{0,1:T(8,128)(2,1)}, bf16[1536,32]{0,1:T(8,128)(2,1)}, u32[]{:S(2)}, u32[]{:S(2)}) collective-permute-start(bf16[1536,32]{0,1:T(8,128)(2,1)} %bitcast.40), channel_id=1, source_target_pairs={{0,16},{16,0},{1,17},{17,1},{2,18},{18,2},{3,19},{19,3},{4,20},{20... | collective-permute-start | bytes 294920 | tf_op jit(solution)/shard_map/ppermute | solution.py:90
  293.8 74.9 %all-to-all-start.6 = ((bf16[8,192,768]{2,1,0:T(8,128)(2,1)}), bf16[8,192,768]{2,1,0:T(8,128)(2,1)}, u32[]{:S(2)}, u32[]{:S(2)}) async-start(bf16[8,192,768]{2,1,0:T(8,128)(2,1)} %get-tuple-element.161), calls=%async_computation.6 | async-start | bytes 4718592 | tf_op jit(solution)/shard_map/all_to_all | solution.py:341
  303.3 19.2 %collective-permute-start.14 = (bf16[2,1,2,128,768]{4,3,0,2,1:T(8,128)(2,1)S(1)}, bf16[2,1,2,128,768]{4,3,0,2,1:T(8,128)(2,1)S(1)}, u32[]{:S(2)}, u32[]{:S(2)}) collective-permute-start(bf16[2,1,2,128,768]{4,3,0,2,1:T(8,128)(2,1)S(1)} %maximum_bitcast_fusion), channel_id=1, source_target_pairs={{0,2},{1,3},{2,0},{3,1},{4,6},{5,7},{6,4},{7,5},{8,10},{9,11},{10,... | collective-permute-start | bytes 2359304 | tf_op jit(solution)/shard_map/ppermute | solution.py:228
  323.8 42.8 %collective-permute-start.15 = (bf16[2,2,2,128,768]{4,3,0,2,1:T(8,128)(2,1)}, bf16[2,2,2,128,768]{4,3,0,2,1:T(8,128)(2,1)}, u32[]{:S(2)}, u32[]{:S(2)}) collective-permute-start(bf16[2,2,2,128,768]{4,3,0,2,1:T(8,128)(2,1)} %pad_maximum_fusion.11), channel_id=1, source_target_pairs={{0,1},{1,0},{2,3},{3,2},{4,5},{5,4},{6,7},{7,6},{8,9},{9,8},{10,11... | collective-permute-start | bytes 4718600 | tf_op jit(solution)/shard_map/ppermute | solution.py:228
  324.3 34.2 %collective-permute-start.17 = (bf16[128,512]{1,0:T(8,128)(2,1)S(1)}, bf16[128,512]{1,0:T(8,128)(2,1)S(1)}, u32[]{:S(2)}, u32[]{:S(2)}) collective-permute-start(bf16[128,512]{1,0:T(8,128)(2,1)S(1)} %pad_maximum_fusion.46), channel_id=1, source_target_pairs={{0,8},{4,12},{8,0},{12,4},{1,9},{5,13},{9,1},{13,5},{2,10},{6,14},... | collective-permute-start | bytes 393224 | tf_op jit(solution)/shard_map/ppermute | solution.py:113
  368.7 60.1 %all-to-all-start.8 = ((bf16[8,96,1536]{2,1,0:T(8,128)(2,1)}), bf16[8,96,1536]{2,1,0:T(8,128)(2,1)}, u32[]{:S(2)}, u32[]{:S(2)}) async-start(bf16[8,96,1536]{2,1,0:T(8,128)(2,1)} %get-tuple-element.163), calls=%async_computation.8 | async-start | bytes 4718592 | tf_op jit(solution)/shard_map/all_to_all | solution.py:341
  504.9 59.4 %all-to-all-start.7 = ((bf16[8,192,768]{2,1,0:T(8,128)(2,1)}), bf16[8,192,768]{2,1,0:T(8,128)(2,1)}, u32[]{:S(2)}, u32[]{:S(2)}) async-start(bf16[8,192,768]{2,1,0:T(8,128)(2,1)} %get-tuple-element.159), calls=%async_computation.7 | async-start | bytes 4718592 | tf_op jit(solution)/shard_map/all_to_all | solution.py:341
  512.5 19.2 %collective-permute-start.20 = (bf16[2,1,2,128,768]{4,3,0,2,1:T(8,128)(2,1)S(1)}, bf16[2,1,2,128,768]{4,3,0,2,1:T(8,128)(2,1)S(1)}, u32[]{:S(2)}, u32[]{:S(2)}) collective-permute-start(bf16[2,1,2,128,768]{4,3,0,2,1:T(8,128)(2,1)S(1)} %maximum_bitcast_fusion.1), channel_id=1, source_target_pairs={{0,2},{1,3},{2,0},{3,1},{4,6},{5,7},{6,4},{7,5},{8,10},{9,11},{10,... | collective-permute-start | bytes 2359304 | tf_op jit(solution)/shard_map/ppermute | solution.py:228
  531.9 41.1 %collective-permute-start.21 = (bf16[2,2,2,128,768]{4,3,0,2,1:T(8,128)(2,1)S(1)}, bf16[2,2,2,128,768]{4,3,0,2,1:T(8,128)(2,1)}, u32[]{:S(2)}, u32[]{:S(2)}) collective-permute-start(bf16[2,2,2,128,768]{4,3,0,2,1:T(8,128)(2,1)S(1)} %pad_maximum_fusion.12), channel_id=1, source_target_pairs={{0,1},{1,0},{2,3},{3,2},{4,5},{5,4},{6,7},{7,6},{8,9},{9,8},{10,11... | collective-permute-start | bytes 4718600 | tf_op jit(solution)/shard_map/ppermute | solution.py:228
  581.3 76.3 %all-to-all-start.9 = ((bf16[32,16,3072]{2,1,0:T(8,128)(2,1)}), bf16[32,16,3072]{2,1,0:T(8,128)(2,1)}, u32[]{:S(2)}, u32[]{:S(2)}) async-start(bf16[32,16,3072]{2,1,0:T(8,128)(2,1)} %pad_maximum_fusion.3), calls=%async_computation.9 | async-start | bytes 6291456 | tf_op jit(solution)/shard_map/all_to_all | solution.py:341
  663.1 75.5 %all-to-all-start.10 = ((bf16[8,96,1536]{2,1,0:T(8,128)(2,1)}), bf16[8,96,1536]{2,1,0:T(8,128)(2,1)S(1)}, u32[]{:S(2)}, u32[]{:S(2)}) async-start(bf16[8,96,1536]{2,1,0:T(8,128)(2,1)} %bitcast.495), calls=%async_computation.10 | async-start | bytes 4718592 | tf_op jit(solution)/shard_map/all_to_all | solution.py:341
  738.6 44.5 %all-to-all-start.11 = ((bf16[32,16,1536]{2,1,0:T(8,128)(2,1)}), bf16[32,16,1536]{2,1,0:T(8,128)(2,1)}, u32[]{:S(2)}, u32[]{:S(2)}) async-start(bf16[32,16,1536]{2,1,0:T(8,128)(2,1)} %bitcast.463), calls=%async_computation.11 | async-start | bytes 3145728 | tf_op jit(solution)/shard_map/all_to_all | solution.py:341
  749.7 22.8 %collective-permute-start.26 = (bf16[128,896]{1,0:T(8,128)(2,1)S(1)}, bf16[128,896]{1,0:T(8,128)(2,1)S(1)}, u32[]{:S(2)}, u32[]{:S(2)}) collective-permute-start(bf16[128,896]{1,0:T(8,128)(2,1)S(1)} %pad_maximum_fusion.44), channel_id=1, source_target_pairs={{0,3},{1,2},{2,1},{3,0},{4,7},{5,6},{6,5},{7,4},{8,11},{9,10},{10,... | collective-permute-start | bytes 688136 | tf_op jit(solution)/shard_map/ppermute | solution.py:253
  804.4 65.5 %all-to-all-start.12 = ((bf16[32,16,1536]{2,1,0:T(8,128)(2,1)}), bf16[32,16,1536]{2,1,0:T(8,128)(2,1)}, u32[]{:S(2)}, u32[]{:S(2)}) async-start(bf16[32,16,1536]{2,1,0:T(8,128)(2,1)} %bitcast.503), calls=%async_computation.12 | async-start | bytes 3145728 | tf_op jit(solution)/shard_map/all_to_all | solution.py:341
  812.9 54.5 %collective-permute-start.29 = (bf16[192,896]{0,1:T(8,128)(2,1)}, bf16[192,896]{0,1:T(8,128)(2,1)}, u32[]{:S(2)}, u32[]{:S(2)}) collective-permute-start(bf16[192,896]{0,1:T(8,128)(2,1)} %dynamic-slice_convert_fusion), channel_id=1, source_target_pairs={{0,8},{4,12},{8,0},{12,4},{1,9},{5,13},{9,1},{13,5},{2,10},{6,14},... | collective-permute-start | bytes 1032200 | tf_op jit(solution)/shard_map/ppermute | solution.py:274
  869.9 22.3 %collective-permute-start.30 = (bf16[192,896]{0,1:T(8,128)(2,1)}, bf16[192,896]{0,1:T(8,128)(2,1)}, u32[]{:S(2)}, u32[]{:S(2)}) collective-permute-start(bf16[192,896]{0,1:T(8,128)(2,1)} %add_convert_fusion), channel_id=1, source_target_pairs={{0,8},{4,12},{8,0},{12,4},{1,9},{5,13},{9,1},{13,5},{2,10},{6,14},... | collective-permute-start | bytes 1032200 | tf_op jit(solution)/shard_map/ppermute | solution.py:285
  911.8 125.3 %all-to-all-start.13 = ((bf16[8,192,1536]{2,1,0:T(8,128)(2,1)}), bf16[8,192,1536]{2,1,0:T(8,128)(2,1)}, u32[]{:S(2)}, u32[]{:S(2)}) async-start(bf16[8,192,1536]{2,1,0:T(8,128)(2,1)} %bitcast.467), calls=%async_computation.13 | async-start | bytes 9437184 | tf_op jit(solution)/shard_map/all_to_all | solution.py:341
  937.0 29.7 %collective-permute-start.38 = (bf16[128,384]{1,0:T(8,128)(2,1)}, bf16[128,384]{1,0:T(8,128)(2,1)}, u32[]{:S(2)}, u32[]{:S(2)}) collective-permute-start(bf16[128,384]{1,0:T(8,128)(2,1)} %get-tuple-element.245), channel_id=1, source_target_pairs={{0,3},{1,2},{2,1},{3,0},{4,7},{5,6},{6,5},{7,4},{8,11},{9,10},{10,... | collective-permute-start | bytes 294920 | tf_op jit(solution)/shard_map/ppermute | solution.py:253
  939.4 27.4 %collective-permute-start.37 = (bf16[128,384]{1,0:T(8,128)(2,1)}, bf16[128,384]{1,0:T(8,128)(2,1)}, u32[]{:S(2)}, u32[]{:S(2)}) collective-permute-start(bf16[128,384]{1,0:T(8,128)(2,1)} %get-tuple-element.246), channel_id=1, source_target_pairs={{0,1},{1,0},{2,3},{3,2},{4,5},{5,4},{6,7},{7,6},{8,9},{9,8},{10,11... | collective-permute-start | bytes 294920 | tf_op jit(solution)/shard_map/ppermute | solution.py:253
  939.7 27.1 %collective-permute-start.36 = (bf16[128,384]{1,0:T(8,128)(2,1)}, bf16[128,384]{1,0:T(8,128)(2,1)}, u32[]{:S(2)}, u32[]{:S(2)}) collective-permute-start(bf16[128,384]{1,0:T(8,128)(2,1)} %get-tuple-element.247), channel_id=1, source_target_pairs={{0,2},{1,3},{2,0},{3,1},{4,6},{5,7},{6,4},{7,5},{8,10},{9,11},{10,... | collective-permute-start | bytes 294920 | tf_op jit(solution)/shard_map/ppermute | solution.py:253
  962.8 31.6 %collective-permute-start.35 = (bf16[2,1,384,896]{2,3,1,0:T(8,128)(2,1)}, bf16[2,1,384,896]{2,3,1,0:T(8,128)(2,1)}, u32[]{:S(2)}, u32[]{:S(2)}) collective-permute-start(bf16[2,1,384,896]{2,3,1,0:T(8,128)(2,1)} %pad_maximum_fusion.16), channel_id=1, source_target_pairs={{0,1},{1,0},{2,3},{3,2},{4,5},{5,4},{6,7},{7,6},{8,9},{9,8},{10,11... | collective-permute-start | bytes 4128776 | tf_op jit(solution)/shard_map/ppermute | solution.py:300
  971.8 31.9 %collective-permute-start.33 = (bf16[1,2,384,896]{2,3,1,0:T(8,128)(2,1)}, bf16[1,2,384,896]{2,3,1,0:T(8,128)(2,1)}, u32[]{:S(2)}, u32[]{:S(2)}) collective-permute-start(bf16[1,2,384,896]{2,3,1,0:T(8,128)(2,1)} %pad_maximum_fusion.15), channel_id=1, source_target_pairs={{0,2},{1,3},{2,0},{3,1},{4,6},{5,7},{6,4},{7,5},{8,10},{9,11},{10,... | collective-permute-start | bytes 4128776 | tf_op jit(solution)/shard_map/ppermute | solution.py:300
  981.2 47.2 %collective-permute-start.42 = (bf16[384,384]{1,0:T(8,128)(2,1)}, bf16[384,384]{1,0:T(8,128)(2,1)}, u32[]{:S(2)}, u32[]{:S(2)}) collective-permute-start(bf16[384,384]{1,0:T(8,128)(2,1)} %dynamic-slice_convert_fusion.2), channel_id=1, source_target_pairs={{0,4},{4,0},{8,12},{12,8},{1,5},{5,1},{9,13},{13,9},{2,6},{6,2},{1... | collective-permute-start | bytes 884744 | tf_op jit(solution)/shard_map/ppermute | solution.py:274
  1037.2 58.9 %all-to-all-start.14 = ((bf16[8,96,1536]{2,1,0:T(8,128)(2,1)}), bf16[8,96,1536]{2,1,0:T(8,128)(2,1)}, u32[]{:S(2)}, u32[]{:S(2)}) async-start(bf16[8,96,1536]{2,1,0:T(8,128)(2,1)} %bitcast.494), calls=%async_computation.14 | async-start | bytes 4718592 | tf_op jit(solution)/shard_map/all_to_all | solution.py:341
  1157.3 112.3 %all-to-all-start.15 = ((bf16[8,192,1536]{2,1,0:T(8,128)(2,1)}), bf16[8,192,1536]{2,1,0:T(8,128)(2,1)}, u32[]{:S(2)}, u32[]{:S(2)}) async-start(bf16[8,192,1536]{2,1,0:T(8,128)(2,1)} %bitcast.468), calls=%async_computation.15 | async-start | bytes 9437184 | tf_op jit(solution)/shard_map/all_to_all | solution.py:341
  1171.1 47.0 %collective-permute-start.71 = (f32[128,1536]{1,0:T(8,128)S(1)}, f32[128,1536]{1,0:T(8,128)S(1)}, u32[]{:S(2)}, u32[]{:S(2)}) collective-permute-start(f32[128,1536]{1,0:T(8,128)S(1)} %convolution_add_fusion.2), channel_id=1, source_target_pairs={{0,16},{1,17},{2,18},{3,19},{4,20},{5,21},{6,22},{7,23},{8,24},{9,... | collective-permute-start | bytes 2359304 | tf_op jit(solution)/shard_map/ppermute | solution.py:701
  1172.4 67.0 %collective-permute-start.64 = (bf16[2,4,384,896]{3,2,1,0:T(8,128)(2,1)}, bf16[2,4,384,896]{3,2,1,0:T(8,128)(2,1)}, u32[]{:S(2)}, u32[]{:S(2)}) collective-permute-start(bf16[2,4,384,896]{3,2,1,0:T(8,128)(2,1)} %pad_maximum_fusion.refs_1_), channel_id=1, source_target_pairs={{0,16},{1,17},{2,18},{3,19},{4,20},{5,21},{6,22},{7,23},{8,24},{9,... | collective-permute-start | bytes 16515080 | tf_op jit(solution)/shard_map/ppermute | solution.py:778
  1179.5 21.4 %collective-permute-start.68 = (bf16[2,1,416,512]{3,2,1,0:T(8,128)(2,1)S(1)}, bf16[2,1,416,512]{3,2,1,0:T(8,128)(2,1)S(1)}, u32[]{:S(2)}, u32[]{:S(2)}) collective-permute-start(bf16[2,1,416,512]{3,2,1,0:T(8,128)(2,1)S(1)} %pad_maximum_fusion.23), channel_id=1, source_target_pairs={{0,1},{1,0},{2,3},{3,2},{4,5},{5,4},{6,7},{7,6},{8,9},{9,8},{10,11... | collective-permute-start | bytes 2555912 | tf_op jit(solution)/shard_map/ppermute | solution.py:300
  1182.6 20.9 %collective-permute-start.66 = (bf16[1,2,416,512]{3,2,1,0:T(8,128)(2,1)S(1)}, bf16[1,2,416,512]{3,2,1,0:T(8,128)(2,1)S(1)}, u32[]{:S(2)}, u32[]{:S(2)}) collective-permute-start(bf16[1,2,416,512]{3,2,1,0:T(8,128)(2,1)S(1)} %pad_maximum_fusion.22), channel_id=1, source_target_pairs={{0,2},{1,3},{2,0},{3,1},{4,6},{5,7},{6,4},{7,5},{8,10},{9,11},{10,... | collective-permute-start | bytes 2555912 | tf_op jit(solution)/shard_map/ppermute | solution.py:300
  1185.2 28.3 %collective-permute-start.62 = (bf16[2,1,384,384]{3,2,1,0:T(8,128)(2,1)S(1)}, bf16[2,1,384,384]{3,2,1,0:T(8,128)(2,1)S(1)}, u32[]{:S(2)}, u32[]{:S(2)}) collective-permute-start(bf16[2,1,384,384]{3,2,1,0:T(8,128)(2,1)S(1)} %pad_maximum_fusion.30), channel_id=1, source_target_pairs={{0,1},{1,0},{2,3},{3,2},{4,5},{5,4},{6,7},{7,6},{8,9},{9,8},{10,11... | collective-permute-start | bytes 1769480 | tf_op jit(solution)/shard_map/ppermute | solution.py:300
  1200.9 18.8 %collective-permute-start.60 = (bf16[1,2,384,384]{3,2,1,0:T(8,128)(2,1)S(1)}, bf16[1,2,384,384]{3,2,1,0:T(8,128)(2,1)S(1)}, u32[]{:S(2)}, u32[]{:S(2)}) collective-permute-start(bf16[1,2,384,384]{3,2,1,0:T(8,128)(2,1)S(1)} %pad_maximum_fusion.29), channel_id=1, source_target_pairs={{0,2},{1,3},{2,0},{3,1},{4,6},{5,7},{6,4},{7,5},{8,10},{9,11},{10,... | collective-permute-start | bytes 1769480 | tf_op jit(solution)/shard_map/ppermute | solution.py:300
  1205.0 45.4 %collective-permute-start.69 = (bf16[2,4,416,512]{3,2,1,0:T(8,128)(2,1)S(1)}, bf16[2,4,416,512]{3,2,1,0:T(8,128)(2,1)}, u32[]{:S(2)}, u32[]{:S(2)}) collective-permute-start(bf16[2,4,416,512]{3,2,1,0:T(8,128)(2,1)S(1)} %pad_maximum_fusion.1.refs_0_), channel_id=1, source_target_pairs={{16,0},{17,1},{18,2},{19,3},{20,4},{21,5},{22,6},{23,7},{24,8},{25... | collective-permute-start | bytes 10223624 | tf_op jit(solution)/shard_map/ppermute | solution.py:786
  1229.2 53.2 %collective-permute-start.73 = (bf16[8,192,1536]{2,1,0:T(8,128)(2,1)}, bf16[8,192,1536]{2,1,0:T(8,128)(2,1)}, u32[]{:S(2)}, u32[]{:S(2)}) collective-permute-start(bf16[8,192,1536]{2,1,0:T(8,128)(2,1)} %all-to-all-done.13.refs_1_), channel_id=1, source_target_pairs={{0,16},{1,17},{2,18},{3,19},{4,20},{5,21},{6,22},{7,23},{8,24},{9,... | collective-permute-start | bytes 14155784 | tf_op jit(solution)/shard_map/ppermute | solution.py:161
  (220 other events, 2621.3 us)

commit v7 on v6

--- a/solution.py
+++ b/solution.py
@@ -477,8 +477,9 @@
     hidden_one = normed.astype(BF)
     key_rows = dot(hidden_one, w_key).astype(BF)
     value_rows = dot(hidden_one, w_value).astype(BF)
-    kv_all = hook(gathered(jnp.concatenate([key_rows, value_rows], 1), 0))
     queries = dot(hidden_one, w_query).astype(BF)
+    queries, kv_rows = tie(queries, jnp.concatenate([key_rows, value_rows], 1))
+    kv_all = hook(gathered(kv_rows, 0))
     key_width = w_key.shape[1]
     key_all = kv_all[:, :key_width].reshape(-1, heads_kv, HEAD_SIZE)
     value_all = kv_all[:, key_width:].reshape(-1, heads_kv, HEAD_SIZE)

time: 1300 us -> 1300 us (level)
  no operation moved by 1% of the time
where the time goes in v7:
time: 1300 us; the launch traced here: 1290 us
  waiting for transfers between devices  643 us (49%)
  starting transfers between devices  172 us (13%)
  matrix products  160 us (12%)
  other arithmetic  105 us (8%)
  local copies, waits for them, and re-layouts  79.1 us (6%)
  blocking collectives  76.1 us (6%)
  Pallas kernels  47.7 us (4%)
    all_to_all x15, waiting for transfers between devices, exchange(): return lax.all_to_all(rows, axes, split_axis=0, concat_axis=0, tiled=True)  296 us
    all_to_all x15, starting transfers between devices, exchange(): return lax.all_to_all(rows, axes, split_axis=0, concat_axis=0, tiled=True)  84 us
    ppermute x4, waiting for transfers between devices, gathered(): lax.ppermute(shard, over, partners(over, flip))  78.5 us
    all_to_all x1, blocking collectives, exchange(): return lax.all_to_all(rows, axes, split_axis=0, concat_axis=0, tiled=True)  76.1 us
    ppermute x6, waiting for transfers between devices, dense_rows_step(): sent = lax.ppermute(sent.astype(BF), 'dp', partners('dp', flip))  75.4 us
    dot_general x19, matrix products, dot_t(): lax.dot_general(left, right, (((1,), (1,)), ((), ())), preferred_element_...  58.6 us
    dot_general x24, matrix products, dot(): return jnp.dot(left, right, preferred_element_type=F32)  51.8 us
    pallas_call x5, Pallas kernels, pick_blocks(): pl.pallas_call(body, grid_spec=pltpu.PrefetchScalarGridSpec(num_scalar_pr...  47.7 us
  transfers between devices with their start and end apart: 89, of which 45 were waited for; matrix products, arithmetic and copies ran while one was open for 23% of the time, Pallas kernels for 3%

profile of v7, /device:TPU:1, one launch (start us, length us, event | category | flops | bytes accessed | tf_op | source)
XLA Modules:
  0.0 1286.3 jit_solution(3813618067562010798)
XLA Ops:
  16.8 6.4 all-to-all-start.2
  48.3 31.6 %all-to-all-done.2 = bf16[8,192,768]{2,1,0:T(8,128)(2,1)} async-done(((bf16[8,192,768]{2,1,0:T(8,128)(2,1)}), bf16[8,192,768]{2,1,0:T(8,128)(2,1)}, u32[]{:S(2)}, u32[]{:S(2)}) %all-to-all-start.2) | async-done | bytes 2359328 | tf_op jit(solution)/shard_map/all_to_all | solution.py:341
  79.9 5.7 all-to-all-start.1
  88.5 41.2 %collective-permute-done.6 = bf16[256,512]{1,0:T(8,128)(2,1)S(1)} collective-permute-done((bf16[256,512]{1,0:T(8,128)(2,1)S(1)}, bf16[256,512]{1,0:T(8,128)(2,1)S(1)}, u32[]{:S(2)}, u32[]{:S(2)}) %collective-permute-start.6) | collective-permute-done | bytes 262176 | tf_op jit(solution)/shard_map/ppermute | solution.py:113
  139.6 6.3 all-to-all-start
  145.9 5.7 slice_select_fusion
  151.5 32.6 %all-to-all-done = bf16[32,16,1536]{2,1,0:T(8,128)(2,1)S(1)} async-done(((bf16[32,16,1536]{2,1,0:T(8,128)(2,1)}), bf16[32,16,1536]{2,1,0:T(8,128)(2,1)S(1)}, u32[]{:S(2)}, u32[]{:S(2)}) %all-to-all-start) | async-done | bytes 1572896 | tf_op jit(solution)/shard_map/all_to_all | solution.py:341
  184.1 5.6 all-to-all-start.3
  198.5 45.2 %all-to-all-done.3 = bf16[8,96,1536]{2,1,0:T(8,128)(2,1)} async-done(((bf16[8,96,1536]{2,1,0:T(8,128)(2,1)}), bf16[8,96,1536]{2,1,0:T(8,128)(2,1)}, u32[]{:S(2)}, u32[]{:S(2)}) %all-to-all-start.3) | async-done | bytes 2359328 | tf_op jit(solution)/shard_map/all_to_all | solution.py:341
  257.2 32.6 %all-to-all-done.4 = bf16[32,16,1536]{2,1,0:T(8,128)(2,1)S(1)} async-done(((bf16[32,16,1536]{2,1,0:T(8,128)(2,1)}), bf16[32,16,1536]{2,1,0:T(8,128)(2,1)S(1)}, u32[]{:S(2)}, u32[]{:S(2)}) %all-to-all-start.4) | async-done | bytes 1572896 | tf_op jit(solution)/shard_map/all_to_all | solution.py:341
  299.3 17.2 %collective-permute-done.14 = bf16[2,1,2,128,768]{4,3,0,2,1:T(8,128)(2,1)S(1)} collective-permute-done((bf16[2,1,2,128,768]{4,3,0,2,1:T(8,128)(2,1)S(1)}, bf16[2,1,2,128,768]{4,3,0,2,1:T(8,128)(2,1)S(1)}, u32[]{:S(2)}, u32[]{:S(2)}) %collective-permute-start.14) | collective-permute-done | bytes 786464 | tf_op jit(solution)/shard_map/ppermute | solution.py:228
  323.1 31.5 %collective-permute-done.17 = bf16[128,512]{1,0:T(8,128)(2,1)S(1)} collective-permute-done((bf16[128,512]{1,0:T(8,128)(2,1)S(1)}, bf16[128,512]{1,0:T(8,128)(2,1)S(1)}, u32[]{:S(2)}, u32[]{:S(2)}) %collective-permute-start.17) | collective-permute-done | bytes 131104 | tf_op jit(solution)/shard_map/ppermute | solution.py:113
  356.7 5.8 collective-permute-done.18
  363.9 6.2 all-to-all-start.8
  382.2 41.8 %all-to-all-done.8 = bf16[8,96,1536]{2,1,0:T(8,128)(2,1)} async-done(((bf16[8,96,1536]{2,1,0:T(8,128)(2,1)}), bf16[8,96,1536]{2,1,0:T(8,128)(2,1)}, u32[]{:S(2)}, u32[]{:S(2)}) %all-to-all-start.8) | async-done | bytes 2359328 | tf_op jit(solution)/shard_map/all_to_all | solution.py:341
  424.1 76.1 %all_to_all.80 = bf16[32,16,3072]{2,1,0:T(8,128)(2,1)} all-to-all(bf16[32,16,3072]{2,1,0:T(8,128)(2,1)} %pad_maximum_fusion.2), channel_id=1, replica_groups=mesh['section'=2,'dp'=4,'expert'=4] {'expert','dp','section'}, dimensions={0} | all-to-all | bytes 6291456 | tf_op jit(solution)/shard_map/all_to_all | solution.py:341
  512.3 14.6 %collective-permute-done.20 = bf16[2,1,2,128,768]{4,3,0,2,1:T(8,128)(2,1)S(1)} collective-permute-done((bf16[2,1,2,128,768]{4,3,0,2,1:T(8,128)(2,1)S(1)}, bf16[2,1,2,128,768]{4,3,0,2,1:T(8,128)(2,1)S(1)}, u32[]{:S(2)}, u32[]{:S(2)}) %collective-permute-start.20) | collective-permute-done | bytes 786464 | tf_op jit(solution)/shard_map/ppermute | solution.py:228
  531.9 27.6 %all-to-all-done.7 = bf16[8,192,768]{2,1,0:T(8,128)(2,1)} async-done(((bf16[8,192,768]{2,1,0:T(8,128)(2,1)}), bf16[8,192,768]{2,1,0:T(8,128)(2,1)}, u32[]{:S(2)}, u32[]{:S(2)}) %all-to-all-start.7) | async-done | bytes 2359328 | tf_op jit(solution)/shard_map/all_to_all | solution.py:341
  589.3 63.6 %all-to-all-done.9 = bf16[32,16,3072]{2,1,0:T(8,128)(2,1)} async-done(((bf16[32,16,3072]{2,1,0:T(8,128)(2,1)}), bf16[32,16,3072]{2,1,0:T(8,128)(2,1)}, u32[]{:S(2)}, u32[]{:S(2)}) %all-to-all-start.9) | async-done | bytes 3145760 | tf_op jit(solution)/shard_map/all_to_all | solution.py:341
  689.9 17.0 %collective-permute-done.22 = bf16[256,512]{1,0:T(8,128)(2,1)S(1)} collective-permute-done((bf16[256,512]{1,0:T(8,128)(2,1)S(1)}, bf16[256,512]{1,0:T(8,128)(2,1)S(1)}, u32[]{:S(2)}, u32[]{:S(2)}) %collective-permute-start.22) | collective-permute-done | bytes 262176 | tf_op jit(solution)/shard_map/ppermute | solution.py:121
  714.1 8.3 collective-permute-done.23
  733.8 6.1 all-to-all-start.11
  745.1 13.3 %collective-permute-done.24 = bf16[128,896]{1,0:T(8,128)(2,1)S(1)} collective-permute-done((bf16[128,896]{1,0:T(8,128)(2,1)S(1)}, bf16[128,896]{1,0:T(8,128)(2,1)S(1)}, u32[]{:S(2)}, u32[]{:S(2)}) %collective-permute-start.24) | collective-permute-done | bytes 229408 | tf_op jit(solution)/shard_map/ppermute | solution.py:253
  758.4 9.3 collective-permute-done.26
  799.7 6.3 all-to-all-start.12
  810.6 52.0 %collective-permute-done.29 = bf16[192,896]{0,1:T(8,128)(2,1)} collective-permute-done((bf16[192,896]{0,1:T(8,128)(2,1)}, bf16[192,896]{0,1:T(8,128)(2,1)}, u32[]{:S(2)}, u32[]{:S(2)}) %collective-permute-start.29) | collective-permute-done | bytes 344096 | tf_op jit(solution)/shard_map/ppermute | solution.py:274
  868.3 19.2 %collective-permute-done.30 = bf16[192,896]{0,1:T(8,128)(2,1)} collective-permute-done((bf16[192,896]{0,1:T(8,128)(2,1)}, bf16[192,896]{0,1:T(8,128)(2,1)}, u32[]{:S(2)}, u32[]{:S(2)}) %collective-permute-start.30) | collective-permute-done | bytes 344096 | tf_op jit(solution)/shard_map/ppermute | solution.py:285
  894.3 11.2 collective-permute-done.31
  907.1 6.0 all-to-all-start.13
  922.2 6.2 convolution_convert_fusion.10
  942.5 12.0 collective-permute-done.32
  978.1 11.5 collective-permute-done.35
  1007.4 5.7 pad_maximum_fusion.refs_1_
  1025.5 6.2 collective-permute-done.41
  1041.8 7.2 fusion.58
  1077.0 14.4 %all-to-all-done.14.refs_0_ = bf16[8,96,1536]{2,1,0:T(8,128)(2,1)} async-done(((bf16[8,96,1536]{2,1,0:T(8,128)(2,1)}), bf16[8,96,1536]{2,1,0:T(8,128)(2,1)}, u32[]{:S(2)}, u32[]{:S(2)}) %all-to-all-start.14) | async-done | bytes 2359328 | tf_op jit(solution)/shard_map/all_to_all | solution.py:341
  1096.6 8.8 collective-permute-done.51
  1116.5 11.8 collective-permute-done.52
  1131.6 10.0 collective-permute-done.54
  1152.6 7.8 all-to-all-start.15
  1182.4 13.8 %collective-permute-done.68 = bf16[2,1,416,512]{3,2,1,0:T(8,128)(2,1)S(1)} collective-permute-done((bf16[2,1,416,512]{3,2,1,0:T(8,128)(2,1)S(1)}, bf16[2,1,416,512]{3,2,1,0:T(8,128)(2,1)S(1)}, u32[]{:S(2)}, u32[]{:S(2)}) %collective-permute-start.68) | collective-permute-done | bytes 852000 | tf_op jit(solution)/shard_map/ppermute | solution.py:300
  1200.2 6.8 collective-permute-start.69
  1225.7 7.8 shard_map.239
  1234.7 11.0 shard_map.240
  1245.6 12.3 shard_map.241
  1258.0 6.9 all-to-all-done.15.refs_0_
  1267.9 8.4 shard_map.242
  1277.6 8.2 shard_map.243
  (780 shorter events, 459.3 us)
Async XLA Ops:
  4.7 24.7 %collective-permute-start.7 = (s32[5,128]{1,0:T(8,128)}, s32[5,128]{1,0:T(8,128)S(1)}, u32[]{:S(2)}, u32[]{:S(2)}) collective-permute-start(s32[5,128]{1,0:T(8,128)} %select_bitcast_fusion.1), channel_id=1, source_target_pairs={{0,16},{16,0},{1,17},{17,1},{2,18},{18,2},{3,19},{19,3},{4,20},{20... | collective-permute-start | bytes 7688 | tf_op jit(solution)/shard_map/ppermute | solution.py:90
  5.8 25.5 %collective-permute-start.1 = (f32[1536]{0:T(1024)}, f32[1536]{0:T(1024)}, u32[]{:S(2)}, u32[]{:S(2)}) collective-permute-start(f32[1536]{0:T(1024)} %reduce), channel_id=1, source_target_pairs={{0,16},{16,0},{1,17},{17,1},{2,18},{18,2},{3,19},{19,3},{4,20},{20... | collective-permute-start | bytes 18440 | tf_op jit(solution)/shard_map/ppermute | solution.py:90
  6.6 26.6 %collective-permute-start = (bf16[128,1536]{1,0:T(8,128)(2,1)}, bf16[128,1536]{1,0:T(8,128)(2,1)S(1)}, u32[]{:S(2)}, u32[]{:S(2)}) collective-permute-start(bf16[128,1536]{1,0:T(8,128)(2,1)} %select_bitcast_fusion), channel_id=1, source_target_pairs={{0,16},{16,0},{1,17},{17,1},{2,18},{18,2},{3,19},{19,3},{4,20},{20... | collective-permute-start | bytes 1179656 | tf_op jit(solution)/shard_map/ppermute | solution.py:90
  7.1 35.0 %collective-permute-start.2 = (bf16[1536,1536]{1,0:T(8,128)(2,1)}, bf16[1536,1536]{1,0:T(8,128)(2,1)}, u32[]{:S(2)}, u32[]{:S(2)}) collective-permute-start(bf16[1536,1536]{1,0:T(8,128)(2,1)} %bitcast.466), channel_id=1, source_target_pairs={{0,16},{16,0},{1,17},{17,1},{2,18},{18,2},{3,19},{19,3},{4,20},{20... | collective-permute-start | bytes 14155784 | tf_op jit(solution)/shard_map/ppermute | solution.py:90
  12.1 23.4 %collective-permute-start.4 = (bf16[1536,256]{1,0:T(8,128)(2,1)S(1)}, bf16[1536,256]{1,0:T(8,128)(2,1)S(1)}, u32[]{:S(2)}, u32[]{:S(2)}) collective-permute-start(bf16[1536,256]{1,0:T(8,128)(2,1)S(1)} %bitcast.496), channel_id=1, source_target_pairs={{0,16},{16,0},{1,17},{17,1},{2,18},{18,2},{3,19},{19,3},{4,20},{20... | collective-permute-start | bytes 2359304 | tf_op jit(solution)/shard_map/ppermute | solution.py:90
  16.8 63.1 %all-to-all-start.2 = ((bf16[8,192,768]{2,1,0:T(8,128)(2,1)}), bf16[8,192,768]{2,1,0:T(8,128)(2,1)}, u32[]{:S(2)}, u32[]{:S(2)}) async-start(bf16[8,192,768]{2,1,0:T(8,128)(2,1)} %get-tuple-element.168), calls=%async_computation.2 | async-start | bytes 4718592 | tf_op jit(solution)/shard_map/all_to_all | solution.py:341
  33.9 98.6 %collective-permute-start.8 = (bf16[1536,1536]{1,0:T(8,128)(2,1)}, bf16[1536,1536]{1,0:T(8,128)(2,1)}, u32[]{:S(2)}, u32[]{:S(2)}) collective-permute-start(bf16[1536,1536]{1,0:T(8,128)(2,1)} %bitcast.445), channel_id=1, source_target_pairs={{0,16},{16,0},{1,17},{17,1},{2,18},{18,2},{3,19},{19,3},{4,20},{20... | collective-permute-start | bytes 14155784 | tf_op jit(solution)/shard_map/ppermute | solution.py:90
  35.5 52.2 %collective-permute-start.9 = (f32[1536]{0:T(1024)S(1)}, f32[1536]{0:T(1024)S(1)}, u32[]{:S(2)}, u32[]{:S(2)}) collective-permute-start(f32[1536]{0:T(1024)S(1)} %reduce.1), channel_id=1, source_target_pairs={{0,16},{16,0},{1,17},{17,1},{2,18},{18,2},{3,19},{19,3},{4,20},{20... | collective-permute-start | bytes 18440 | tf_op jit(solution)/shard_map/ppermute | solution.py:90
  35.9 110.0 %collective-permute-start.12 = (bf16[8,96,1536]{2,1,0:T(8,128)(2,1)}, bf16[8,96,1536]{2,1,0:T(8,128)(2,1)}, u32[]{:S(2)}, u32[]{:S(2)}) collective-permute-start(bf16[8,96,1536]{2,1,0:T(8,128)(2,1)} %dynamic-slice_bitcast_fusion), channel_id=1, source_target_pairs={{0,16},{16,0},{1,17},{17,1},{2,18},{18,2},{3,19},{19,3},{4,20},{20... | collective-permute-start | bytes 7077896 | tf_op jit(solution)/shard_map/ppermute | solution.py:90
  45.6 40.6 %collective-permute-start.5 = (bf16[128,512]{1,0:T(8,128)(2,1)S(1)}, bf16[128,512]{1,0:T(8,128)(2,1)S(1)}, u32[]{:S(2)}, u32[]{:S(2)}) collective-permute-start(bf16[128,512]{1,0:T(8,128)(2,1)S(1)} %pad_maximum_fusion.44), channel_id=1, source_target_pairs={{0,8},{4,12},{8,0},{12,4},{1,9},{5,13},{9,1},{13,5},{2,10},{6,14},... | collective-permute-start | bytes 393224 | tf_op jit(solution)/shard_map/ppermute | solution.py:113
  79.9 59.7 %all-to-all-start.1 = ((bf16[8,192,768]{2,1,0:T(8,128)(2,1)}), bf16[8,192,768]{2,1,0:T(8,128)(2,1)}, u32[]{:S(2)}, u32[]{:S(2)}) async-start(bf16[8,192,768]{2,1,0:T(8,128)(2,1)} %get-tuple-element.170), calls=%async_computation.1 | async-start | bytes 4718592 | tf_op jit(solution)/shard_map/all_to_all | solution.py:341
  86.2 43.6 %collective-permute-start.6 = (bf16[256,512]{1,0:T(8,128)(2,1)S(1)}, bf16[256,512]{1,0:T(8,128)(2,1)S(1)}, u32[]{:S(2)}, u32[]{:S(2)}) collective-permute-start(bf16[256,512]{1,0:T(8,128)(2,1)S(1)} %pad_maximum_fusion.39), channel_id=1, source_target_pairs={{0,4},{4,0},{8,12},{12,8},{1,5},{5,1},{9,13},{13,9},{2,6},{6,2},{1... | collective-permute-start | bytes 786440 | tf_op jit(solution)/shard_map/ppermute | solution.py:113
  139.6 44.5 %all-to-all-start = ((bf16[32,16,1536]{2,1,0:T(8,128)(2,1)}), bf16[32,16,1536]{2,1,0:T(8,128)(2,1)S(1)}, u32[]{:S(2)}, u32[]{:S(2)}) async-start(bf16[32,16,1536]{2,1,0:T(8,128)(2,1)} %bitcast.24), calls=%async_computation | async-start | bytes 3145728 | tf_op jit(solution)/shard_map/all_to_all | solution.py:341
  184.1 59.5 %all-to-all-start.3 = ((bf16[8,96,1536]{2,1,0:T(8,128)(2,1)}), bf16[8,96,1536]{2,1,0:T(8,128)(2,1)}, u32[]{:S(2)}, u32[]{:S(2)}) async-start(bf16[8,96,1536]{2,1,0:T(8,128)(2,1)} %get-tuple-element.172), calls=%async_computation.3 | async-start | bytes 4718592 | tf_op jit(solution)/shard_map/all_to_all | solution.py:341
  248.1 41.7 %all-to-all-start.4 = ((bf16[32,16,1536]{2,1,0:T(8,128)(2,1)}), bf16[32,16,1536]{2,1,0:T(8,128)(2,1)S(1)}, u32[]{:S(2)}, u32[]{:S(2)}) async-start(bf16[32,16,1536]{2,1,0:T(8,128)(2,1)} %bitcast.508), calls=%async_computation.4 | async-start | bytes 3145728 | tf_op jit(solution)/shard_map/all_to_all | solution.py:341
  289.8 74.1 %all-to-all-start.6 = ((bf16[8,192,768]{2,1,0:T(8,128)(2,1)}), bf16[8,192,768]{2,1,0:T(8,128)(2,1)}, u32[]{:S(2)}, u32[]{:S(2)}) async-start(bf16[8,192,768]{2,1,0:T(8,128)(2,1)} %get-tuple-element.169), calls=%async_computation.6 | async-start | bytes 4718592 | tf_op jit(solution)/shard_map/all_to_all | solution.py:341
  297.3 19.2 %collective-permute-start.14 = (bf16[2,1,2,128,768]{4,3,0,2,1:T(8,128)(2,1)S(1)}, bf16[2,1,2,128,768]{4,3,0,2,1:T(8,128)(2,1)S(1)}, u32[]{:S(2)}, u32[]{:S(2)}) collective-permute-start(bf16[2,1,2,128,768]{4,3,0,2,1:T(8,128)(2,1)S(1)} %maximum_bitcast_fusion), channel_id=1, source_target_pairs={{0,2},{1,3},{2,0},{3,1},{4,6},{5,7},{6,4},{7,5},{8,10},{9,11},{10,... | collective-permute-start | bytes 2359304 | tf_op jit(solution)/shard_map/ppermute | solution.py:228
  317.9 45.7 %collective-permute-start.15 = (bf16[2,2,2,128,768]{4,3,0,2,1:T(8,128)(2,1)}, bf16[2,2,2,128,768]{4,3,0,2,1:T(8,128)(2,1)}, u32[]{:S(2)}, u32[]{:S(2)}) collective-permute-start(bf16[2,2,2,128,768]{4,3,0,2,1:T(8,128)(2,1)} %pad_maximum_fusion.11), channel_id=1, source_target_pairs={{0,1},{1,0},{2,3},{3,2},{4,5},{5,4},{6,7},{7,6},{8,9},{9,8},{10,11... | collective-permute-start | bytes 4718600 | tf_op jit(solution)/shard_map/ppermute | solution.py:228
  320.0 34.5 %collective-permute-start.17 = (bf16[128,512]{1,0:T(8,128)(2,1)S(1)}, bf16[128,512]{1,0:T(8,128)(2,1)S(1)}, u32[]{:S(2)}, u32[]{:S(2)}) collective-permute-start(bf16[128,512]{1,0:T(8,128)(2,1)S(1)} %pad_maximum_fusion.45), channel_id=1, source_target_pairs={{0,8},{4,12},{8,0},{12,4},{1,9},{5,13},{9,1},{13,5},{2,10},{6,14},... | collective-permute-start | bytes 393224 | tf_op jit(solution)/shard_map/ppermute | solution.py:113
  363.9 60.1 %all-to-all-start.8 = ((bf16[8,96,1536]{2,1,0:T(8,128)(2,1)}), bf16[8,96,1536]{2,1,0:T(8,128)(2,1)}, u32[]{:S(2)}, u32[]{:S(2)}) async-start(bf16[8,96,1536]{2,1,0:T(8,128)(2,1)} %get-tuple-element.171), calls=%async_computation.8 | async-start | bytes 4718592 | tf_op jit(solution)/shard_map/all_to_all | solution.py:341
  500.1 59.3 %all-to-all-start.7 = ((bf16[8,192,768]{2,1,0:T(8,128)(2,1)}), bf16[8,192,768]{2,1,0:T(8,128)(2,1)}, u32[]{:S(2)}, u32[]{:S(2)}) async-start(bf16[8,192,768]{2,1,0:T(8,128)(2,1)} %get-tuple-element.167), calls=%async_computation.7 | async-start | bytes 4718592 | tf_op jit(solution)/shard_map/all_to_all | solution.py:341
  507.8 19.2 %collective-permute-start.20 = (bf16[2,1,2,128,768]{4,3,0,2,1:T(8,128)(2,1)S(1)}, bf16[2,1,2,128,768]{4,3,0,2,1:T(8,128)(2,1)S(1)}, u32[]{:S(2)}, u32[]{:S(2)}) collective-permute-start(bf16[2,1,2,128,768]{4,3,0,2,1:T(8,128)(2,1)S(1)} %maximum_bitcast_fusion.1), channel_id=1, source_target_pairs={{0,2},{1,3},{2,0},{3,1},{4,6},{5,7},{6,4},{7,5},{8,10},{9,11},{10,... | collective-permute-start | bytes 2359304 | tf_op jit(solution)/shard_map/ppermute | solution.py:228
  527.1 41.1 %collective-permute-start.21 = (bf16[2,2,2,128,768]{4,3,0,2,1:T(8,128)(2,1)S(1)}, bf16[2,2,2,128,768]{4,3,0,2,1:T(8,128)(2,1)}, u32[]{:S(2)}, u32[]{:S(2)}) collective-permute-start(bf16[2,2,2,128,768]{4,3,0,2,1:T(8,128)(2,1)S(1)} %pad_maximum_fusion.12), channel_id=1, source_target_pairs={{0,1},{1,0},{2,3},{3,2},{4,5},{5,4},{6,7},{7,6},{8,9},{9,8},{10,11... | collective-permute-start | bytes 4718600 | tf_op jit(solution)/shard_map/ppermute | solution.py:228
  576.5 76.3 %all-to-all-start.9 = ((bf16[32,16,3072]{2,1,0:T(8,128)(2,1)}), bf16[32,16,3072]{2,1,0:T(8,128)(2,1)}, u32[]{:S(2)}, u32[]{:S(2)}) async-start(bf16[32,16,3072]{2,1,0:T(8,128)(2,1)} %pad_maximum_fusion.3), calls=%async_computation.9 | async-start | bytes 6291456 | tf_op jit(solution)/shard_map/all_to_all | solution.py:341
  658.3 75.5 %all-to-all-start.10 = ((bf16[8,96,1536]{2,1,0:T(8,128)(2,1)}), bf16[8,96,1536]{2,1,0:T(8,128)(2,1)S(1)}, u32[]{:S(2)}, u32[]{:S(2)}) async-start(bf16[8,96,1536]{2,1,0:T(8,128)(2,1)} %bitcast.499), calls=%async_computation.10 | async-start | bytes 4718592 | tf_op jit(solution)/shard_map/all_to_all | solution.py:341
  688.5 18.5 %collective-permute-start.22 = (bf16[256,512]{1,0:T(8,128)(2,1)S(1)}, bf16[256,512]{1,0:T(8,128)(2,1)S(1)}, u32[]{:S(2)}, u32[]{:S(2)}) collective-permute-start(bf16[256,512]{1,0:T(8,128)(2,1)S(1)} %pad_maximum_fusion.38), channel_id=1, source_target_pairs={{0,4},{4,0},{8,12},{12,8},{1,5},{5,1},{9,13},{13,9},{2,6},{6,2},{1... | collective-permute-start | bytes 786440 | tf_op jit(solution)/shard_map/ppermute | solution.py:121
  733.8 44.5 %all-to-all-start.11 = ((bf16[32,16,1536]{2,1,0:T(8,128)(2,1)}), bf16[32,16,1536]{2,1,0:T(8,128)(2,1)}, u32[]{:S(2)}, u32[]{:S(2)}) async-start(bf16[32,16,1536]{2,1,0:T(8,128)(2,1)} %bitcast.463), calls=%async_computation.11 | async-start | bytes 3145728 | tf_op jit(solution)/shard_map/all_to_all | solution.py:341
  745.0 22.8 %collective-permute-start.26 = (bf16[128,896]{1,0:T(8,128)(2,1)S(1)}, bf16[128,896]{1,0:T(8,128)(2,1)S(1)}, u32[]{:S(2)}, u32[]{:S(2)}) collective-permute-start(bf16[128,896]{1,0:T(8,128)(2,1)S(1)} %pad_maximum_fusion.43), channel_id=1, source_target_pairs={{0,3},{1,2},{2,1},{3,0},{4,7},{5,6},{6,5},{7,4},{8,11},{9,10},{10,... | collective-permute-start | bytes 688136 | tf_op jit(solution)/shard_map/ppermute | solution.py:253
  799.7 65.5 %all-to-all-start.12 = ((bf16[32,16,1536]{2,1,0:T(8,128)(2,1)}), bf16[32,16,1536]{2,1,0:T(8,128)(2,1)}, u32[]{:S(2)}, u32[]{:S(2)}) async-start(bf16[32,16,1536]{2,1,0:T(8,128)(2,1)} %bitcast.507), calls=%async_computation.12 | async-start | bytes 3145728 | tf_op jit(solution)/shard_map/all_to_all | solution.py:341
  808.1 54.5 %collective-permute-start.29 = (bf16[192,896]{0,1:T(8,128)(2,1)}, bf16[192,896]{0,1:T(8,128)(2,1)}, u32[]{:S(2)}, u32[]{:S(2)}) collective-permute-start(bf16[192,896]{0,1:T(8,128)(2,1)} %dynamic-slice_convert_fusion), channel_id=1, source_target_pairs={{0,8},{4,12},{8,0},{12,4},{1,9},{5,13},{9,1},{13,5},{2,10},{6,14},... | collective-permute-start | bytes 1032200 | tf_op jit(solution)/shard_map/ppermute | solution.py:274
  865.2 22.3 %collective-permute-start.30 = (bf16[192,896]{0,1:T(8,128)(2,1)}, bf16[192,896]{0,1:T(8,128)(2,1)}, u32[]{:S(2)}, u32[]{:S(2)}) collective-permute-start(bf16[192,896]{0,1:T(8,128)(2,1)} %add_convert_fusion), channel_id=1, source_target_pairs={{0,8},{4,12},{8,0},{12,4},{1,9},{5,13},{9,1},{13,5},{2,10},{6,14},... | collective-permute-start | bytes 1032200 | tf_op jit(solution)/shard_map/ppermute | solution.py:285
  907.1 125.3 %all-to-all-start.13 = ((bf16[8,192,1536]{2,1,0:T(8,128)(2,1)}), bf16[8,192,1536]{2,1,0:T(8,128)(2,1)}, u32[]{:S(2)}, u32[]{:S(2)}) async-start(bf16[8,192,1536]{2,1,0:T(8,128)(2,1)} %bitcast.471), calls=%async_computation.13 | async-start | bytes 9437184 | tf_op jit(solution)/shard_map/all_to_all | solution.py:341
  932.3 29.7 %collective-permute-start.38 = (bf16[128,384]{1,0:T(8,128)(2,1)}, bf16[128,384]{1,0:T(8,128)(2,1)}, u32[]{:S(2)}, u32[]{:S(2)}) collective-permute-start(bf16[128,384]{1,0:T(8,128)(2,1)} %get-tuple-element.253), channel_id=1, source_target_pairs={{0,3},{1,2},{2,1},{3,0},{4,7},{5,6},{6,5},{7,4},{8,11},{9,10},{10,... | collective-permute-start | bytes 294920 | tf_op jit(solution)/shard_map/ppermute | solution.py:253
  934.7 27.4 %collective-permute-start.37 = (bf16[128,384]{1,0:T(8,128)(2,1)}, bf16[128,384]{1,0:T(8,128)(2,1)}, u32[]{:S(2)}, u32[]{:S(2)}) collective-permute-start(bf16[128,384]{1,0:T(8,128)(2,1)} %get-tuple-element.254), channel_id=1, source_target_pairs={{0,1},{1,0},{2,3},{3,2},{4,5},{5,4},{6,7},{7,6},{8,9},{9,8},{10,11... | collective-permute-start | bytes 294920 | tf_op jit(solution)/shard_map/ppermute | solution.py:253
  935.0 27.1 %collective-permute-start.36 = (bf16[128,384]{1,0:T(8,128)(2,1)}, bf16[128,384]{1,0:T(8,128)(2,1)}, u32[]{:S(2)}, u32[]{:S(2)}) collective-permute-start(bf16[128,384]{1,0:T(8,128)(2,1)} %get-tuple-element.255), channel_id=1, source_target_pairs={{0,2},{1,3},{2,0},{3,1},{4,6},{5,7},{6,4},{7,5},{8,10},{9,11},{10,... | collective-permute-start | bytes 294920 | tf_op jit(solution)/shard_map/ppermute | solution.py:253
  958.0 31.6 %collective-permute-start.35 = (bf16[2,1,384,896]{2,3,1,0:T(8,128)(2,1)}, bf16[2,1,384,896]{2,3,1,0:T(8,128)(2,1)}, u32[]{:S(2)}, u32[]{:S(2)}) collective-permute-start(bf16[2,1,384,896]{2,3,1,0:T(8,128)(2,1)} %pad_maximum_fusion.16), channel_id=1, source_target_pairs={{0,1},{1,0},{2,3},{3,2},{4,5},{5,4},{6,7},{7,6},{8,9},{9,8},{10,11... | collective-permute-start | bytes 4128776 | tf_op jit(solution)/shard_map/ppermute | solution.py:300
  967.1 32.0 %collective-permute-start.33 = (bf16[1,2,384,896]{2,3,1,0:T(8,128)(2,1)}, bf16[1,2,384,896]{2,3,1,0:T(8,128)(2,1)}, u32[]{:S(2)}, u32[]{:S(2)}) collective-permute-start(bf16[1,2,384,896]{2,3,1,0:T(8,128)(2,1)} %pad_maximum_fusion.15), channel_id=1, source_target_pairs={{0,2},{1,3},{2,0},{3,1},{4,6},{5,7},{6,4},{7,5},{8,10},{9,11},{10,... | collective-permute-start | bytes 4128776 | tf_op jit(solution)/shard_map/ppermute | solution.py:300
  976.5 47.2 %collective-permute-start.42 = (bf16[384,384]{1,0:T(8,128)(2,1)}, bf16[384,384]{1,0:T(8,128)(2,1)}, u32[]{:S(2)}, u32[]{:S(2)}) collective-permute-start(bf16[384,384]{1,0:T(8,128)(2,1)} %dynamic-slice_convert_fusion.2), channel_id=1, source_target_pairs={{0,4},{4,0},{8,12},{12,8},{1,5},{5,1},{9,13},{13,9},{2,6},{6,2},{1... | collective-permute-start | bytes 884744 | tf_op jit(solution)/shard_map/ppermute | solution.py:274
  1032.5 58.9 %all-to-all-start.14 = ((bf16[8,96,1536]{2,1,0:T(8,128)(2,1)}), bf16[8,96,1536]{2,1,0:T(8,128)(2,1)}, u32[]{:S(2)}, u32[]{:S(2)}) async-start(bf16[8,96,1536]{2,1,0:T(8,128)(2,1)} %bitcast.498), calls=%async_computation.14 | async-start | bytes 4718592 | tf_op jit(solution)/shard_map/all_to_all | solution.py:341
  1152.6 112.3 %all-to-all-start.15 = ((bf16[8,192,1536]{2,1,0:T(8,128)(2,1)}), bf16[8,192,1536]{2,1,0:T(8,128)(2,1)}, u32[]{:S(2)}, u32[]{:S(2)}) async-start(bf16[8,192,1536]{2,1,0:T(8,128)(2,1)} %bitcast.472), calls=%async_computation.15 | async-start | bytes 9437184 | tf_op jit(solution)/shard_map/all_to_all | solution.py:341
  1166.4 47.0 %collective-permute-start.71 = (f32[128,1536]{1,0:T(8,128)S(1)}, f32[128,1536]{1,0:T(8,128)S(1)}, u32[]{:S(2)}, u32[]{:S(2)}) collective-permute-start(f32[128,1536]{1,0:T(8,128)S(1)} %convolution_add_fusion.2), channel_id=1, source_target_pairs={{0,16},{1,17},{2,18},{3,19},{4,20},{5,21},{6,22},{7,23},{8,24},{9,... | collective-permute-start | bytes 2359304 | tf_op jit(solution)/shard_map/ppermute | solution.py:702
  1167.7 67.0 %collective-permute-start.64 = (bf16[2,4,384,896]{3,2,1,0:T(8,128)(2,1)}, bf16[2,4,384,896]{3,2,1,0:T(8,128)(2,1)}, u32[]{:S(2)}, u32[]{:S(2)}) collective-permute-start(bf16[2,4,384,896]{3,2,1,0:T(8,128)(2,1)} %pad_maximum_fusion.refs_1_), channel_id=1, source_target_pairs={{0,16},{1,17},{2,18},{3,19},{4,20},{5,21},{6,22},{7,23},{8,24},{9,... | collective-permute-start | bytes 16515080 | tf_op jit(solution)/shard_map/ppermute | solution.py:779
  1174.8 21.4 %collective-permute-start.68 = (bf16[2,1,416,512]{3,2,1,0:T(8,128)(2,1)S(1)}, bf16[2,1,416,512]{3,2,1,0:T(8,128)(2,1)S(1)}, u32[]{:S(2)}, u32[]{:S(2)}) collective-permute-start(bf16[2,1,416,512]{3,2,1,0:T(8,128)(2,1)S(1)} %pad_maximum_fusion.23), channel_id=1, source_target_pairs={{0,1},{1,0},{2,3},{3,2},{4,5},{5,4},{6,7},{7,6},{8,9},{9,8},{10,11... | collective-permute-start | bytes 2555912 | tf_op jit(solution)/shard_map/ppermute | solution.py:300
  1177.9 20.9 %collective-permute-start.66 = (bf16[1,2,416,512]{3,2,1,0:T(8,128)(2,1)S(1)}, bf16[1,2,416,512]{3,2,1,0:T(8,128)(2,1)S(1)}, u32[]{:S(2)}, u32[]{:S(2)}) collective-permute-start(bf16[1,2,416,512]{3,2,1,0:T(8,128)(2,1)S(1)} %pad_maximum_fusion.22), channel_id=1, source_target_pairs={{0,2},{1,3},{2,0},{3,1},{4,6},{5,7},{6,4},{7,5},{8,10},{9,11},{10,... | collective-permute-start | bytes 2555912 | tf_op jit(solution)/shard_map/ppermute | solution.py:300
  1180.5 28.3 %collective-permute-start.62 = (bf16[2,1,384,384]{3,2,1,0:T(8,128)(2,1)S(1)}, bf16[2,1,384,384]{3,2,1,0:T(8,128)(2,1)S(1)}, u32[]{:S(2)}, u32[]{:S(2)}) collective-permute-start(bf16[2,1,384,384]{3,2,1,0:T(8,128)(2,1)S(1)} %pad_maximum_fusion.30), channel_id=1, source_target_pairs={{0,1},{1,0},{2,3},{3,2},{4,5},{5,4},{6,7},{7,6},{8,9},{9,8},{10,11... | collective-permute-start | bytes 1769480 | tf_op jit(solution)/shard_map/ppermute | solution.py:300
  1196.2 18.8 %collective-permute-start.60 = (bf16[1,2,384,384]{3,2,1,0:T(8,128)(2,1)S(1)}, bf16[1,2,384,384]{3,2,1,0:T(8,128)(2,1)S(1)}, u32[]{:S(2)}, u32[]{:S(2)}) collective-permute-start(bf16[1,2,384,384]{3,2,1,0:T(8,128)(2,1)S(1)} %pad_maximum_fusion.29), channel_id=1, source_target_pairs={{0,2},{1,3},{2,0},{3,1},{4,6},{5,7},{6,4},{7,5},{8,10},{9,11},{10,... | collective-permute-start | bytes 1769480 | tf_op jit(solution)/shard_map/ppermute | solution.py:300
  1200.2 45.4 %collective-permute-start.69 = (bf16[2,4,416,512]{3,2,1,0:T(8,128)(2,1)S(1)}, bf16[2,4,416,512]{3,2,1,0:T(8,128)(2,1)}, u32[]{:S(2)}, u32[]{:S(2)}) collective-permute-start(bf16[2,4,416,512]{3,2,1,0:T(8,128)(2,1)S(1)} %pad_maximum_fusion.1.refs_0_), channel_id=1, source_target_pairs={{16,0},{17,1},{18,2},{19,3},{20,4},{21,5},{22,6},{23,7},{24,8},{25... | collective-permute-start | bytes 10223624 | tf_op jit(solution)/shard_map/ppermute | solution.py:787
  1224.4 53.2 %collective-permute-start.73 = (bf16[8,192,1536]{2,1,0:T(8,128)(2,1)}, bf16[8,192,1536]{2,1,0:T(8,128)(2,1)}, u32[]{:S(2)}, u32[]{:S(2)}) collective-permute-start(bf16[8,192,1536]{2,1,0:T(8,128)(2,1)} %all-to-all-done.13.refs_1_), channel_id=1, source_target_pairs={{0,16},{1,17},{2,18},{3,19},{4,20},{5,21},{6,22},{7,23},{8,24},{9,... | collective-permute-start | bytes 14155784 | tf_op jit(solution)/shard_map/ppermute | solution.py:161
  (225 other events, 2442.4 us)
